TPU v7x, 512 devices: a whole 4x8x8 slice. The times are simulated.
512 devices in a mesh: grp: 4 (over y_lo, core), dp: 32 (over z, x), mp: 4 (over y_hi).
Axes of the slice: x: 4, y: 8 (y_hi: 4, y_lo: 2; y = y_hi * 2 + y_lo), z: 8, core: 2. Of those that a mesh axis runs over, the one named last changes fastest.
Arguments:
- hidden: bfloat16 [14336, 4096], P('dp', ('grp', 'mp')), may hold values from -64 to 64
- wq: bfloat16 [4096, 4096], P('dp', ('grp', 'mp')), may hold values from -2 to 2
- kv_enc: bfloat16 [448, 2, 128, 4096], P('dp', None, 'mp', 'grp'), may hold values from -48 to 48
- group_neighbours: int32 [224, 2], replicated, may hold values from 0 to 447, as said below
- gain: float32 [4096], P(('grp', 'mp')), may hold values from 0.5 to 1.5
- d_mixed: bfloat16 [14336, 4096], P('dp', ('grp', 'mp')), may hold values from -6 to 6
Outputs:
- mixed: bfloat16 [14336, 4096], P('dp', ('grp', 'mp'))
- grad_queries: bfloat16 [14336, 4096], P('dp', ('grp', 'mp'))
- grad_kv: bfloat16 [448, 2, 128, 4096], P('dp', None, 'mp', 'grp')
- grad_wq: bfloat16 [4096, 4096], P('dp', ('grp', 'mp'))
Inputs may be any that keep to these rules, and one draw needn't show every extreme that they name: `group_neighbours`: every neighbour is named by exactly one slot. Number the blocks of 7 groups and the blocks of 14 neighbours alike, as many as dp devices; one block of groups takes either none or exactly 1 neighbours from one block of neighbours, and every block of neighbours gives some to at least one block of groups.
All inputs are finite; a program needn't handle non-finite values.
Results may differ from a plain program's by a relative error of at most 0.022.
Values may be sent and summed in bfloat16 or wider, within the bound.
No kernel may reach another device: no remote copies, remote signals or barrier semaphores. Data moves between devices by JAX's collectives and lax.ppermute only.
A program may use at most 64 MiB of HBM per device.

v0:
```python
import jax
import jax.numpy as jnp
from jax import lax
from jax.sharding import PartitionSpec as P

GROUP_LEN = 64
NEIGHBOURS = 2
HEADS = 32
HEAD_DIM = 128


def lookup(position, length, count):
    select = position[None, :] == jnp.arange(length, dtype=jnp.int32)[:, None]
    rows = jnp.sum(jnp.where(select, jnp.arange(count, dtype=jnp.int32)[None, :], 0), axis=1)
    return (rows, jnp.any(select, axis=1))


def relayout(block):
    shape = block.shape
    flat = block.reshape((shape[0] * shape[1],) + shape[2:])
    moved = lax.all_to_all(flat, ("dp", "mp"), split_axis=0, concat_axis=0, tiled=True)
    return moved.reshape(shape)


def shards(hidden, wq, kv_enc, group_neighbours, gain, d_mixed):
    n_dp = lax.axis_size("dp")
    n_mp = lax.axis_size("mp")
    me_dp = lax.axis_index("dp")
    neigh_dev, _, quarter, enc_width = kv_enc.shape
    dec_width = wq.shape[1]
    heads_here = dec_width // HEAD_DIM
    tok_dev = hidden.shape[0]
    groups_here = tok_dev // GROUP_LEN
    span = quarter * n_mp
    slot_cap = max(1, neigh_dev // n_dp)
    scale = HEAD_DIM ** (-0.5)
    width = HEADS * HEAD_DIM
    flat_ids = group_neighbours.reshape(-1)
    total = flat_ids.shape[0]
    counter = jnp.arange(neigh_dev, dtype=jnp.int32)
    full_rows = lax.all_gather(hidden, ("grp", "mp"), axis=1, tiled=True)
    columns = full_rows
    queries = jnp.dot(
        columns, lax.all_gather(wq, "dp", axis=0, tiled=True), preferred_element_type=jnp.float32
    ).astype(jnp.bfloat16)
    owned = me_dp * neigh_dev + counter
    matches = flat_ids[None, :] == owned[:, None]
    slot_of = jnp.sum(jnp.where(matches, jnp.arange(total, dtype=jnp.int32)[None, :], 0), axis=1)
    target = slot_of // neigh_dev
    send_rank = jnp.sum(
        (target[:, None] == target[None, :]) & (counter[None, :] < counter[:, None]), axis=1
    )
    send_pos = target * slot_cap + send_rank
    send_rows, send_used = lookup(send_pos, n_dp * slot_cap, neigh_dev)
    packed = jnp.where(
        send_used[:, None, None, None],
        jnp.take(kv_enc, send_rows, axis=0),
        jnp.zeros((), jnp.bfloat16),
    )
    packed = packed.reshape(n_dp, slot_cap, 2, quarter, n_mp, dec_width).transpose(0, 4, 1, 2, 3, 5)
    arrived = relayout(packed)
    arrived = arrived.transpose(0, 2, 3, 1, 4, 5).reshape(n_dp * slot_cap, 2, span, dec_width)
    mine = lax.dynamic_slice_in_dim(flat_ids, me_dp * neigh_dev, neigh_dev)
    source = mine // neigh_dev
    recv_rank = jnp.sum(
        (source[:, None] == source[None, :]) & (mine[None, :] < mine[:, None]), axis=1
    )
    recv_pos = source * slot_cap + recv_rank
    near = jnp.take(arrived, recv_pos, axis=0)
    keys = near[:, 0].reshape(groups_here, NEIGHBOURS * span, heads_here, HEAD_DIM)
    values = near[:, 1].reshape(groups_here, NEIGHBOURS * span, heads_here, HEAD_DIM)
    query_heads = queries.reshape(groups_here, GROUP_LEN, heads_here, HEAD_DIM)
    scores = (
        jnp.einsum("cihd,cthd->chit", query_heads, keys, preferred_element_type=jnp.float32) * scale
    )
    top = jnp.max(scores, axis=-1, keepdims=True)
    expo = jnp.exp(scores - top)
    probs = expo / jnp.sum(expo, axis=-1, keepdims=True)
    weights = probs.astype(jnp.bfloat16)
    heads_out = jnp.einsum("chit,cthd->cihd", weights, values, preferred_element_type=jnp.float32)
    attended = heads_out.reshape(tok_dev, dec_width)
    grad_in = d_mixed.astype(jnp.float32) * gain
    square_sum, grad_dot = lax.psum(
        (jnp.sum(attended * attended, axis=-1), jnp.sum(grad_in * attended, axis=-1)), ("grp", "mp")
    )
    inverse = lax.rsqrt(square_sum / width + 1e-06)
    mixed = (attended * inverse[:, None] * gain).astype(jnp.bfloat16)
    grad_att = inverse[:, None] * (
        grad_in - attended * (grad_dot * inverse * inverse / width)[:, None]
    )
    grad_b = grad_att.astype(jnp.bfloat16).reshape(groups_here, GROUP_LEN, heads_here, HEAD_DIM)
    grad_probs = jnp.einsum("cihd,cthd->chit", grad_b, values, preferred_element_type=jnp.float32)
    delta = jnp.swapaxes(jnp.sum(grad_b.astype(jnp.float32) * heads_out, axis=-1), 1, 2)
    grad_scores = (probs * (grad_probs - delta[..., None])).astype(jnp.bfloat16)
    grad_q = (
        jnp.einsum("chit,cthd->cihd", grad_scores, keys, preferred_element_type=jnp.float32) * scale
    )
    grad_q = grad_q.astype(jnp.bfloat16).reshape(tok_dev, dec_width)
    grad_k = (
        jnp.einsum("chit,cihd->cthd", grad_scores, query_heads, preferred_element_type=jnp.float32)
        * scale
    ).astype(jnp.bfloat16)
    grad_v = jnp.einsum(
        "chit,cihd->cthd", weights, grad_b, preferred_element_type=jnp.float32
    ).astype(jnp.bfloat16)
    back = jnp.stack(
        [grad_k.reshape(neigh_dev, span, dec_width), grad_v.reshape(neigh_dev, span, dec_width)],
        axis=1,
    )
    back_rows, back_used = lookup(recv_pos, n_dp * slot_cap, neigh_dev)
    outgoing = jnp.where(
        back_used[:, None, None, None],
        jnp.take(back, back_rows, axis=0),
        jnp.zeros((), jnp.bfloat16),
    )
    outgoing = outgoing.reshape(n_dp, slot_cap, 2, n_mp, quarter, dec_width).transpose(
        0, 3, 1, 2, 4, 5
    )
    returned = relayout(outgoing)
    returned = returned.transpose(0, 2, 3, 4, 1, 5).reshape(
        n_dp * slot_cap, 2, quarter, n_mp * dec_width
    )
    grad_kv = jnp.take(returned, send_pos, axis=0)
    columns = full_rows
    grad_wq = lax.psum_scatter(
        lax.dot_general(
            columns, grad_q, (((0,), (0,)), ((), ())), preferred_element_type=jnp.float32
        ).astype(jnp.bfloat16),
        "dp",
        scatter_dimension=0,
        tiled=True,
    )
    return (mixed, grad_q, grad_kv, grad_wq)


def solution(mesh):
    placed = (
        P("dp", ("grp", "mp")),
        P("dp", ("grp", "mp")),
        P("dp", None, "mp", "grp"),
        P(),
        P(("grp", "mp")),
        P("dp", ("grp", "mp")),
    )
    return jax.shard_map(
        shards,
        mesh=mesh,
        in_specs=placed,
        out_specs=(
            P("dp", ("grp", "mp")),
            P("dp", ("grp", "mp")),
            P("dp", None, "mp", "grp"),
            P("dp", ("grp", "mp")),
        ),
        check_vma=False,
    )
```

profile of v0, /device:TPU:1, one launch (start us, length us, event | category | flops | bytes accessed | tf_op | source)
XLA Modules:
  0.0 706.9 jit_solution(11017364050912992792)
XLA Ops:
  7.2 0.0 copy-start
  7.2 0.0 all-gather.5.cloned.1.call-start
  7.2 0.7 all-gather.5.cloned.1.call-update
  7.9 0.8 copy.91
  8.7 0.1 reshape.206
  8.9 0.2 select_reduce_fusion
  9.1 0.2 convert_reduce_fusion
  9.3 0.1 select_reduce_fusion.2
  9.4 2.7 gather_fusion
  12.2 7.8 %gather.21 = bf16[32,1,2,32,4,256]{5,4,3,2,0,1:T(4,128)(2,1)} reshape(bf16[32,2,32,1024]{3,2,1,0:T(8,128)(2,1)} %gather_fusion) | data formatting | bytes 8388608 | tf_op jit(solution)/shard_map/jit(_take)/gather | solution.py:57
  20.0 0.1 fusion.27
  20.1 4.3 select_bitcast_fusion
  24.4 2.9 copy.92
  27.3 21.4 %all-to-all-start = ((bf16[128,1,2,32,256]{4,3,2,1,0:T(8,128)(2,1)}), bf16[128,1,2,32,256]{4,3,2,1,0:T(8,128)(2,1)}, u32[]{:S(2)}, u32[]{:S(2)}) async-start(bf16[128,1,2,32,256]{4,3,2,1,0:T(8,128)(2,1)} %bitcast.95), calls=%async_computation | async-start | bytes 8388608 | tf_op jit(solution)/shard_map/all_to_all | solution.py:21
  48.7 0.0 all-gather.3.cloned.1.call-start
  48.7 0.7 all-gather.3.cloned.1.call-update
  49.4 0.1 and_select_fusion
  49.5 0.2 convert_reduce_fusion.1
  49.7 0.1 select_reduce_fusion.1
  49.8 0.1 fusion.26
  49.9 131.6 %all-gather.5.cloned.1.call-done = bf16[4096,256]{1,0:T(8,128)(2,1)} async-done(((bf16[128,256]{1,0:T(8,128)(2,1)}), bf16[4096,256]{1,0:T(8,128)(2,1)}) %all-gather.5.cloned.1.call-update) | async-done | bytes 2097168 | tf_op jit(solution)/shard_map/all_gather | solution.py:44
  181.5 125.1 %all-gather.3.cloned.1.call-done = bf16[448,4096]{1,0:T(8,128)(2,1)} async-done(((bf16[448,256]{1,0:T(8,128)(2,1)}), bf16[448,4096]{1,0:T(8,128)(2,1)}) %all-gather.3.cloned.1.call-update) | async-done | bytes 3670032 | tf_op jit(solution)/shard_map/all_gather | solution.py:41
  306.6 3.8 convolution_convert_fusion.2
  310.4 0.1 reshape.210
  310.5 4.8 copy.94
  315.3 4.1 gather_fusion.1
  319.4 1.7 broadcast_select_fusion.1
  321.2 1.1 fusion.36
  322.3 2.2 reshape_squeeze.7
  324.4 1.2 reshape_squeeze.6
  325.7 0.4 convolution_multiply_fusion
  326.1 1.1 fusion.37
  327.3 1.7 multiply_reduce_fusion.1
  329.0 0.1 reduce_sum.96
  329.1 0.4 copy.98
  329.5 0.2 fusion.17
  329.6 31.6 %all-reduce = (f32[448]{0:T(512)S(1)}, f32[448]{0:T(512)S(1)}) all-reduce(f32[448]{0:T(512)S(1)} %reduce_sum.96, f32[448]{0:T(512)S(1)} %fusion.17), channel_id=1, replica_groups=mesh['grp'=4,'dp'=32,'mp'=4] {'grp','mp'}, use_global_device_ids=true, to_apply=%region_8.9 | all-reduce | flops 896 | bytes 7168 | tf_op jit(solution)/shard_map/psum | solution.py:83
  361.2 0.9 fusion.20
  362.1 0.1 reshape.212
  362.1 0.2 multiply_reduce_fusion
  362.3 1.8 fusion.5
  364.2 1.3 copy.107
  365.5 0.6 stack_reshape.7
  366.1 1.6 fusion.8
  367.8 0.8 copy-done.8
  368.6 0.4 fusion.4
  369.0 1.3 copy.105
  370.3 1.5 stack_reshape.6
  371.8 1.3 pad_maximum_fusion
  373.2 2.7 gather_fusion.2
  375.9 3.9 fusion.2
  379.8 18.1 %all-to-all-start.1 = ((bf16[128,1,2,32,256]{4,3,2,1,0:T(8,128)(2,1)}), bf16[128,1,2,32,256]{4,3,2,1,0:T(8,128)(2,1)}, u32[]{:S(2)}, u32[]{:S(2)}) async-start(bf16[128,1,2,32,256]{4,3,2,1,0:T(8,128)(2,1)} %bitcast.96), calls=%async_computation.1 | async-start | bytes 8388608 | tf_op jit(solution)/shard_map/all_to_all | solution.py:21
  397.9 0.0 reduce-scatter.4.cloned.1.call-start
  398.0 0.3 fusion.10
  398.3 0.2 copy.103
  398.6 4.8 fusion.1
  403.4 4.1 copy.112
  407.4 0.0 reduce-scatter.4.cloned.1.call-update
  407.5 86.9 %all-to-all-done.1 = bf16[128,1,2,32,256]{4,3,2,1,0:T(8,128)(2,1)} async-done(((bf16[128,1,2,32,256]{4,3,2,1,0:T(8,128)(2,1)}), bf16[128,1,2,32,256]{4,3,2,1,0:T(8,128)(2,1)}, u32[]{:S(2)}, u32[]{:S(2)}) %all-to-all-start.1) | async-done | bytes 4194336 | tf_op jit(solution)/shard_map/all_to_all | solution.py:21
  494.4 12.5 %copy.143 = bf16[32,4,1,2,32,256]{5,1,4,3,0,2:T(4,128)(2,1)} copy(bf16[32,4,1,2,32,256]{5,4,3,1,0,2:T(8,128)(2,1)} %bitcast.19) | data formatting | bytes 8388608 | tf_op jit(solution)/shard_map/reshape | solution.py:22
  506.9 7.7 %reshape.216 = bf16[32,2,32,1024]{3,2,1,0:T(8,128)(2,1)} reshape(bf16[32,1,2,32,4,256]{5,4,3,2,0,1:T(4,128)(2,1)} %bitcast.98) | data formatting | bytes 8388608 | tf_op jit(solution)/shard_map/reshape | solution.py:120
  514.6 4.3 gather_fusion.3
  518.9 3.0 broadcast_select_fusion
  521.9 178.5 %reduce-scatter.4.cloned.1.call-done = bf16[128,256]{1,0:T(8,128)(2,1)} async-done(((bf16[4096,256]{1,0:T(8,128)(2,1)}), bf16[128,256]{1,0:T(8,128)(2,1)}) %reduce-scatter.4.cloned.1.call-update) | async-done | bytes 65552
  (37 shorter events, 0.2 us)
Async XLA Ops:
  7.2 2.2 copy-start
  7.2 174.4 %all-gather.5.cloned.1.call-start = ((), (), s32[]{:S(2)}) async-start(), calls=%async_computation.4 | async-start | bytes 2162688 | tf_op jit(solution)/shard_map/all_gather | solution.py:44
  27.3 283.2 %all-to-all-start = ((bf16[128,1,2,32,256]{4,3,2,1,0:T(8,128)(2,1)}), bf16[128,1,2,32,256]{4,3,2,1,0:T(8,128)(2,1)}, u32[]{:S(2)}, u32[]{:S(2)}) async-start(bf16[128,1,2,32,256]{4,3,2,1,0:T(8,128)(2,1)} %bitcast.95), calls=%async_computation | async-start | bytes 8388608 | tf_op jit(solution)/shard_map/all_to_all | solution.py:21
  48.7 257.9 %all-gather.3.cloned.1.call-start = ((), (), s32[]{:S(2)}) async-start(), calls=%async_computation.3 | async-start | bytes 3899392 | tf_op jit(solution)/shard_map/all_gather | solution.py:41
  324.4 2.8 copy-start.2
  325.7 1.6 copy-start.4
  327.2 2.2 copy-start.7
  327.3 2.2 copy-start.10
  364.2 1.9 copy-start.5
  367.7 0.8 copy-start.8
  379.8 18.2 %copy-start.3 = (bf16[7,256,2,128]{3,2,1,0:T(2,128)(2,1)S(1)}, bf16[7,256,2,128]{3,2,1,0:T(2,128)(2,1)}, u32[]{:S(2)}) copy-start(bf16[7,256,2,128]{3,2,1,0:T(2,128)(2,1)} %copy-done.2) | copy-start | bytes 2752516
  379.8 18.2 %copy-start.9 = (bf16[7,2,64,256]{3,2,1,0:T(8,128)(2,1)S(1)}, bf16[7,2,64,256]{3,2,1,0:T(8,128)(2,1)}, u32[]{:S(2)}) copy-start(bf16[7,2,64,256]{3,2,1,0:T(8,128)(2,1)} %copy-done.8) | copy-start | bytes 1376260
  379.8 114.5 %all-to-all-start.1 = ((bf16[128,1,2,32,256]{4,3,2,1,0:T(8,128)(2,1)}), bf16[128,1,2,32,256]{4,3,2,1,0:T(8,128)(2,1)}, u32[]{:S(2)}, u32[]{:S(2)}) async-start(bf16[128,1,2,32,256]{4,3,2,1,0:T(8,128)(2,1)} %bitcast.96), calls=%async_computation.1 | async-start | bytes 8388608 | tf_op jit(solution)/shard_map/all_to_all | solution.py:21
  397.9 302.4 %reduce-scatter.4.cloned.1.call-start = ((), (), s32[]{:S(2)}) async-start(), calls=%async_computation.5 | async-start | bytes 2162688
  398.6 4.8 copy-start.6
  514.6 185.7 %copy-start.1 = (bf16[14,2,32,1024]{3,2,1,0:T(8,128)(2,1)S(1)}, bf16[14,2,32,1024]{3,2,1,0:T(8,128)(2,1)}, u32[]{:S(2)}) copy-start(bf16[14,2,32,1024]{3,2,1,0:T(8,128)(2,1)} %param.8) | copy-start | bytes 5505028
Sparse Core Ops, SparseCore 0:
  11.2 170.3 all-gather.4
  183.6 123.0 all-gather.2
  407.6 292.7 reduce-scatter.3
where the time goes:
time: 712 us; the launch traced here: 707 us
  waiting for transfers between devices  523 us (73%)
  local copies, waits for them, and re-layouts  65.6 us (9%)
  starting transfers between devices  39.6 us (6%)
  blocking collectives  31.6 us (4%)
  other arithmetic  17.8 us (2%)
  matrix products  15 us (2%)
  between operations  14.1 us (2%)
    unnamed x4, waiting for transfers between devices  180 us
    all_gather x1, waiting for transfers between devices, shards(): lax.all_gather(wq, 'dp', axis=0, tiled=True)  132 us
    all_gather x1, waiting for transfers between devices, shards(): full_rows = lax.all_gather(hidden, ('grp', 'mp'), axis=1, tiled=True)  125 us
    all_to_all x2, waiting for transfers between devices, relayout(): lax.all_to_all(flat, ('dp', 'mp'), split_axis=0, concat_axis=0, tiled=True)  86.9 us
    all_to_all x2, starting transfers between devices, relayout(): lax.all_to_all(flat, ('dp', 'mp'), split_axis=0, concat_axis=0, tiled=True)  39.4 us
    psum x1, blocking collectives, shards(): lax.psum((jnp.sum(attended * attended, axis=-1), jnp.sum(grad_in * attend...  31.6 us
  transfers between devices with their start and end apart: 5, of which 4 were waited for; matrix products, arithmetic and copies ran while one was open for 9% of the time, Pallas kernels for 0%

commit v1 on v0

--- a/solution.py
+++ b/solution.py
@@ -1,12 +1,15 @@
 import jax
 import jax.numpy as jnp
 from jax import lax
+from jax.sharding import Mesh
 from jax.sharding import PartitionSpec as P
 
 GROUP_LEN = 64
 NEIGHBOURS = 2
 HEADS = 32
 HEAD_DIM = 128
+DP = ("dz", "dx")
+GRP = ("yl", "co")
 
 
 def lookup(position, length, count):
@@ -18,14 +21,46 @@
 def relayout(block):
     shape = block.shape
     flat = block.reshape((shape[0] * shape[1],) + shape[2:])
-    moved = lax.all_to_all(flat, ("dp", "mp"), split_axis=0, concat_axis=0, tiled=True)
+    moved = lax.all_to_all(flat, DP + ("mp",), split_axis=0, concat_axis=0, tiled=True)
     return moved.reshape(shape)
 
 
+def gather_weight(wq):
+    near = lax.all_gather(wq, "dz", axis=0)
+    both = lax.all_gather(near, "dx", axis=1)
+    return both.reshape(-1, wq.shape[1])
+
+
+def gather_hidden(hidden):
+    line = lax.all_gather(hidden, ("yl", "mp"), axis=0)
+    both = lax.all_gather(line, "co", axis=0)
+    rows, width = hidden.shape
+    n_co, n_line = both.shape[:2]
+    n_yl = lax.axis_size("yl")
+    blocks = both.reshape(n_co, n_yl, n_line // n_yl, rows, width)
+    return blocks.transpose(3, 1, 0, 2, 4).reshape(rows, -1)
+
+
+def total_over_heads(pair):
+    axes = GRP + ("mp",)
+    count = lax.axis_size(axes)
+    flat = jnp.stack(pair).reshape(-1, 128)
+    spread = jnp.broadcast_to(flat[None], (count,) + flat.shape)
+    moved = lax.all_to_all(spread, axes, split_axis=0, concat_axis=0, tiled=True)
+    return jnp.sum(moved, axis=0).reshape(2, -1)
+
+
+def scatter_weight(partial):
+    n_z, n_x = lax.axis_size("dz"), lax.axis_size("dx")
+    blocks = partial.reshape(n_z, n_x, -1, partial.shape[1])
+    column = lax.psum_scatter(blocks, "dx", scatter_dimension=1, tiled=False)
+    return lax.psum_scatter(column, "dz", scatter_dimension=0, tiled=False)
+
+
 def shards(hidden, wq, kv_enc, group_neighbours, gain, d_mixed):
-    n_dp = lax.axis_size("dp")
+    n_dp = lax.axis_size(DP)
     n_mp = lax.axis_size("mp")
-    me_dp = lax.axis_index("dp")
+    me_dp = lax.axis_index(DP)
     neigh_dev, _, quarter, enc_width = kv_enc.shape
     dec_width = wq.shape[1]
     heads_here = dec_width // HEAD_DIM
@@ -38,10 +73,10 @@
     flat_ids = group_neighbours.reshape(-1)
     total = flat_ids.shape[0]
     counter = jnp.arange(neigh_dev, dtype=jnp.int32)
-    full_rows = lax.all_gather(hidden, ("grp", "mp"), axis=1, tiled=True)
+    full_rows = gather_hidden(hidden)
     columns = full_rows
     queries = jnp.dot(
-        columns, lax.all_gather(wq, "dp", axis=0, tiled=True), preferred_element_type=jnp.float32
+        columns, gather_weight(wq), preferred_element_type=jnp.float32
     ).astype(jnp.bfloat16)
     owned = me_dp * neigh_dev + counter
     matches = flat_ids[None, :] == owned[:, None]
@@ -80,8 +115,8 @@
     heads_out = jnp.einsum("chit,cthd->cihd", weights, values, preferred_element_type=jnp.float32)
     attended = heads_out.reshape(tok_dev, dec_width)
     grad_in = d_mixed.astype(jnp.float32) * gain
-    square_sum, grad_dot = lax.psum(
-        (jnp.sum(attended * attended, axis=-1), jnp.sum(grad_in * attended, axis=-1)), ("grp", "mp")
+    square_sum, grad_dot = total_over_heads(
+        (jnp.sum(attended * attended, axis=-1), jnp.sum(grad_in * attended, axis=-1))
     )
     inverse = lax.rsqrt(square_sum / width + 1e-06)
     mixed = (attended * inverse[:, None] * gain).astype(jnp.bfloat16)
@@ -122,35 +157,22 @@
     )
     grad_kv = jnp.take(returned, send_pos, axis=0)
     columns = full_rows
-    grad_wq = lax.psum_scatter(
+    grad_wq = scatter_weight(
         lax.dot_general(
             columns, grad_q, (((0,), (0,)), ((), ())), preferred_element_type=jnp.float32
-        ).astype(jnp.bfloat16),
-        "dp",
-        scatter_dimension=0,
-        tiled=True,
+        ).astype(jnp.bfloat16)
     )
     return (mixed, grad_q, grad_kv, grad_wq)
 
 
 def solution(mesh):
-    placed = (
-        P("dp", ("grp", "mp")),
-        P("dp", ("grp", "mp")),
-        P("dp", None, "mp", "grp"),
-        P(),
-        P(("grp", "mp")),
-        P("dp", ("grp", "mp")),
-    )
+    cut = Mesh(mesh.devices.reshape(2, 2, 8, 4, 4), GRP + DP + ("mp",))
+    heads = GRP + ("mp",)
+    placed = (P(DP, heads), P(DP, heads), P(DP, None, "mp", GRP), P(), P(heads), P(DP, heads))
     return jax.shard_map(
         shards,
-        mesh=mesh,
+        mesh=cut,
         in_specs=placed,
-        out_specs=(
-            P("dp", ("grp", "mp")),
-            P("dp", ("grp", "mp")),
-            P("dp", None, "mp", "grp"),
-            P("dp", ("grp", "mp")),
-        ),
+        out_specs=(P(DP, heads), P(DP, heads), P(DP, None, "mp", GRP), P(DP, heads)),
         check_vma=False,
     )

time: 712 us -> 429 us (0.60)
  the two profiles are of different devices: /device:TPU:1 before, /device:TPU:24 now
where the time goes in v1:
time: 429 us; the launch traced here: 427 us
  waiting for transfers between devices  186 us (43%)
  local copies, waits for them, and re-layouts  84.8 us (20%)
  blocking collectives  70.1 us (16%)
  starting transfers between devices  40.1 us (9%)
  other arithmetic  17.8 us (4%)
  matrix products  15 us (3%)
  between operations  14.2 us (3%)
    all_gather x1, blocking collectives, gather_weight(): near = lax.all_gather(wq, 'dz', axis=0)  70.1 us
    all_to_all x2, waiting for transfers between devices, relayout(): lax.all_to_all(flat, DP + ('mp',), split_axis=0, concat_axis=0, tiled=True)  67.8 us
    reduce_scatter x1, waiting for transfers between devices, scatter_weight(): column = lax.psum_scatter(blocks, 'dx', scatter_dimension=1, tiled=False)  46.8 us
    all_gather x1, waiting for transfers between devices, gather_hidden(): line = lax.all_gather(hidden, ('yl', 'mp'), axis=0)  43 us
    all_to_all x2, starting transfers between devices, relayout(): lax.all_to_all(flat, DP + ('mp',), split_axis=0, concat_axis=0, tiled=True)  33.1 us
    all_gather x1, waiting for transfers between devices, gather_weight(): both = lax.all_gather(near, 'dx', axis=1)  22.1 us
    reshape x1, local copies, waits for them, and re-layouts, relayout(): return moved.reshape(shape)  12.5 us
    gather x2, local copies, waits for them, and re-layouts, shards(): jnp.take(kv_enc, send_rows, axis=0)  10.6 us
  transfers between devices with their start and end apart: 8, of which 5 were waited for; matrix products, arithmetic and copies ran while one was open for 18% of the time, Pallas kernels for 0%

profile of v1, /device:TPU:24, one launch (start us, length us, event | category | flops | bytes accessed | tf_op | source)
XLA Modules:
  0.0 427.5 jit_solution(18371506608995683395)
XLA Ops:
  7.2 0.7 all-gather.8.cloned.1.call-update
  7.9 0.8 copy.116
  8.7 0.1 reshape.243
  8.9 0.2 select_reduce_fusion
  9.1 0.2 convert_reduce_fusion
  9.3 0.1 select_reduce_fusion.2
  9.4 2.7 gather_fusion
  12.2 7.8 %gather.21 = bf16[32,1,2,32,4,256]{5,4,3,2,0,1:T(4,128)(2,1)} reshape(bf16[32,2,32,1024]{3,2,1,0:T(8,128)(2,1)} %gather_fusion) | data formatting | bytes 8388608 | tf_op jit(solution)/shard_map/jit(_take)/gather | solution.py:92
  20.0 0.1 fusion.27
  20.1 4.3 %select_bitcast_fusion = bf16[32,4,1,2,32,256]{5,1,4,3,0,2:T(4,128)(2,1)S(1)} fusion(bf16[32,1,2,32,4,256]{5,4,3,2,0,1:T(4,128)(2,1)} %gather.21, pred[32]{0:T(512)(128)(4,1)S(1)} %compare_and_fusion.2, pred[32]{0:T(512)(128)(4,1)S(1)} %fusion.27), kind=kLoop, calls=%fused_computation.10 | loop fusion | flops 4194304 | bytes 8388672 | tf_op jit(solution)/shard_map/transpose | solution.py:95
  24.4 2.9 copy.117
  27.3 19.4 %all-to-all-start = ((bf16[128,1,2,32,256]{4,3,2,1,0:T(8,128)(2,1)}), bf16[128,1,2,32,256]{4,3,2,1,0:T(8,128)(2,1)}, u32[]{:S(2)}, u32[]{:S(2)}) async-start(bf16[128,1,2,32,256]{4,3,2,1,0:T(8,128)(2,1)} %bitcast.107), calls=%async_computation | async-start | bytes 8388608 | tf_op jit(solution)/shard_map/all_to_all | solution.py:24
  46.8 43.0 %all-gather.8.cloned.1.call-done = bf16[3584,256]{1,0:T(8,128)(2,1)} async-done(((bf16[448,256]{1,0:T(8,128)(2,1)}), bf16[3584,256]{1,0:T(8,128)(2,1)}) %all-gather.8.cloned.1.call-update) | async-done | bytes 1835024 | tf_op jit(solution)/shard_map/all_gather | solution.py:35
  89.8 70.1 %all-gather.2 = bf16[1024,256]{1,0:T(8,128)(2,1)} all-gather(bf16[128,256]{1,0:T(8,128)(2,1)S(1)} %copy-done.10), channel_id=4, replica_groups=mesh['yl'=2,'co'=2,'dz'=8,'dx'=4,'mp'=4] {'dz'}, dimensions={0}, use_global_device_ids=true | all-gather | bytes 589824 | tf_op jit(solution)/shard_map/all_gather | solution.py:29
  159.9 0.1 and_select_fusion
  160.0 0.2 convert_reduce_fusion.1
  160.2 0.1 select_reduce_fusion.1
  160.3 0.1 fusion.26
  160.5 6.7 %copy.120 = bf16[448,2,2,4,256]{4,3,2,1,0:T(4,128)(2,1)} copy(bf16[448,2,2,4,256]{4,0,3,1,2:T(8,128)(2,1)} %bitcast.114) | data formatting | bytes 7340032 | tf_op jit(solution)/shard_map/transpose | solution.py:41
  167.2 7.1 %reshape.248 = bf16[448,4096]{1,0:T(8,128)(2,1)} reshape(bf16[448,2,2,4,256]{4,3,2,1,0:T(4,128)(2,1)} %copy.120) | data formatting | bytes 7340032 | tf_op jit(solution)/shard_map/reshape | solution.py:41
  174.3 22.1 %all-gather.12.cloned.1.call-done = bf16[8,512,256]{2,1,0:T(8,128)(2,1)} async-done(((bf16[8,128,256]{2,1,0:T(8,128)(2,1)}), bf16[8,512,256]{2,1,0:T(8,128)(2,1)}) %all-gather.12.cloned.1.call-update) | async-done | bytes 2097168 | tf_op jit(solution)/shard_map/all_gather | solution.py:30
  196.4 3.8 convolution_convert_fusion.2
  200.3 4.8 %copy.119 = bf16[32,1,2,4,32,256]{5,4,3,2,0,1:T(8,128)(2,1)} copy(bf16[32,1,2,4,32,256]{5,4,2,3,0,1:T(8,128)(2,1)} %bitcast.6) | data formatting | bytes 8388608 | tf_op jit(solution)/shard_map/transpose | solution.py:97
  205.1 4.1 gather_fusion.1
  209.2 1.7 broadcast_select_fusion.1
  211.0 1.1 fusion.38
  212.0 2.2 reshape_squeeze.7
  214.2 1.2 reshape_squeeze.6
  215.4 0.4 convolution_multiply_fusion
  215.9 1.1 fusion.40
  217.0 1.7 multiply_reduce_fusion.1
  218.8 0.1 stack.12
  218.9 0.4 copy.124
  219.2 0.2 fusion.15
  219.5 0.6 broadcast_in_dim.141
  220.1 6.5 %all-to-all-start.1 = ((f32[16,7,128]{2,1,0:T(8,128)}), f32[16,7,128]{2,1,0:T(8,128)S(1)}, u32[]{:S(2)}, u32[]{:S(2)}) async-start(f32[16,7,128]{2,1,0:T(8,128)} %broadcast_in_dim.141), calls=%async_computation.1 | async-start | bytes 131072 | tf_op jit(solution)/shard_map/all_to_all | solution.py:49
  226.7 5.2 %all-to-all-done.1 = f32[16,7,128]{2,1,0:T(8,128)S(1)} async-done(((f32[16,7,128]{2,1,0:T(8,128)}), f32[16,7,128]{2,1,0:T(8,128)S(1)}, u32[]{:S(2)}, u32[]{:S(2)}) %all-to-all-start.1) | async-done | bytes 57376 | tf_op jit(solution)/shard_map/all_to_all | solution.py:49
  231.9 0.1 reshape.252
  232.0 0.9 fusion.20
  233.0 0.2 multiply_reduce_fusion
  233.2 1.8 fusion.5
  235.0 1.3 copy.134
  236.4 0.6 stack_reshape.7
  237.0 1.6 fusion.8
  238.6 0.8 copy-done.8
  239.4 0.4 fusion.4
  239.9 1.3 copy.132
  241.2 1.5 stack_reshape.6
  242.7 1.3 pad_maximum_fusion
  244.0 2.7 gather_fusion.2
  246.8 3.9 fusion.2
  250.7 13.7 %all-to-all-start.2 = ((bf16[128,1,2,32,256]{4,3,2,1,0:T(8,128)(2,1)}), bf16[128,1,2,32,256]{4,3,2,1,0:T(8,128)(2,1)}, u32[]{:S(2)}, u32[]{:S(2)}) async-start(bf16[128,1,2,32,256]{4,3,2,1,0:T(8,128)(2,1)} %bitcast.108), calls=%async_computation.2 | async-start | bytes 8388608 | tf_op jit(solution)/shard_map/all_to_all | solution.py:24
  264.4 0.3 fusion.10
  264.7 0.2 copy.130
  265.0 4.8 %fusion.1 = bf16[4096,256]{0,1:T(8,128)(2,1)} fusion(bf16[448,256]{1,0:T(8,128)(2,1)S(1)} %bitcast.118, bf16[448,4096]{1,0:T(8,128)(2,1)} %reshape.248), kind=kOutput, calls=%fused_computation.6 | convolution fusion | flops 940572672 | bytes 5996544 | tf_op jit(solution)/shard_map/dot_general | solution.py:161
  269.8 4.5 %reshape.258 = bf16[8,4,128,256]{2,1,0,3:T(4,128)(2,1)} reshape(bf16[4096,256]{0,1:T(8,128)(2,1)} %fusion.1) | data formatting | bytes 4194304 | tf_op jit(solution)/shard_map/reshape | solution.py:55
  274.3 4.3 copy.138
  278.6 0.3 reduce-scatter.5.cloned.1.call-start
  278.9 46.8 %reduce-scatter.3.cloned.1.call-done = bf16[8,1,128,256]{3,2,0,1:T(8,128)(2,1)} async-done(((bf16[8,4,128,256]{3,2,0,1:T(8,128)(2,1)}), bf16[8,1,128,256]{3,2,0,1:T(8,128)(2,1)}) %reduce-scatter.3.cloned.1.call-update) | async-done | bytes 524304 | tf_op jit(solution)/shard_map/reduce_scatter | solution.py:56
  325.7 67.8 %all-to-all-done.2 = bf16[128,1,2,32,256]{4,3,2,1,0:T(8,128)(2,1)} async-done(((bf16[128,1,2,32,256]{4,3,2,1,0:T(8,128)(2,1)}), bf16[128,1,2,32,256]{4,3,2,1,0:T(8,128)(2,1)}, u32[]{:S(2)}, u32[]{:S(2)}) %all-to-all-start.2) | async-done | bytes 4194336 | tf_op jit(solution)/shard_map/all_to_all | solution.py:24
  393.5 12.5 %copy.169 = bf16[32,4,1,2,32,256]{5,1,4,3,0,2:T(4,128)(2,1)} copy(bf16[32,4,1,2,32,256]{5,4,3,1,0,2:T(8,128)(2,1)} %bitcast.27) | data formatting | bytes 8388608 | tf_op jit(solution)/shard_map/reshape | solution.py:25
  406.0 7.7 %reshape.257 = bf16[32,2,32,1024]{3,2,1,0:T(8,128)(2,1)} reshape(bf16[32,1,2,32,4,256]{5,4,3,2,0,1:T(4,128)(2,1)} %bitcast.110) | data formatting | bytes 8388608 | tf_op jit(solution)/shard_map/reshape | solution.py:155
  413.8 4.2 gather_fusion.3
  418.0 3.0 broadcast_select_fusion
  (56 shorter events, 0.7 us)
Async XLA Ops:
  7.2 2.2 copy-start
  7.2 82.6 %all-gather.8.cloned.1.call-start = ((), (), s32[]{:S(2)}) async-start(), calls=%async_computation.7 | async-start | bytes 2064384 | tf_op jit(solution)/shard_map/all_gather | solution.py:35
  27.3 62.5 %copy-start.10 = (bf16[128,256]{1,0:T(8,128)(2,1)S(1)}, bf16[128,256]{1,0:T(8,128)(2,1)}, u32[]{:S(2)}) copy-start(bf16[128,256]{1,0:T(8,128)(2,1)} %param.7) | copy-start | bytes 196612
  27.3 172.9 %all-to-all-start = ((bf16[128,1,2,32,256]{4,3,2,1,0:T(8,128)(2,1)}), bf16[128,1,2,32,256]{4,3,2,1,0:T(8,128)(2,1)}, u32[]{:S(2)}, u32[]{:S(2)}) async-start(bf16[128,1,2,32,256]{4,3,2,1,0:T(8,128)(2,1)} %bitcast.107), calls=%async_computation | async-start | bytes 8388608 | tf_op jit(solution)/shard_map/all_to_all | solution.py:24
  46.7 113.7 %all-gather.10.cloned.1.call-start = ((), (), s32[]{:S(2)}) async-start(), calls=%async_computation.8 | async-start | bytes 5505024 | tf_op jit(solution)/shard_map/all_gather | solution.py:36
  89.8 106.6 %all-gather.12.cloned.1.call-start = ((), (), s32[]{:S(2)}) async-start(), calls=%async_computation.9 | async-start | bytes 2621440 | tf_op jit(solution)/shard_map/all_gather | solution.py:30
  214.2 2.8 copy-start.2
  215.4 1.6 copy-start.4
  217.0 2.2 copy-start.7
  217.0 2.2 copy-start.11
  220.1 11.8 %all-to-all-start.1 = ((f32[16,7,128]{2,1,0:T(8,128)}), f32[16,7,128]{2,1,0:T(8,128)S(1)}, u32[]{:S(2)}, u32[]{:S(2)}) async-start(f32[16,7,128]{2,1,0:T(8,128)} %broadcast_in_dim.141), calls=%async_computation.1 | async-start | bytes 131072 | tf_op jit(solution)/shard_map/all_to_all | solution.py:49
  235.0 1.9 copy-start.5
  238.6 0.8 copy-start.8
  250.7 13.7 %copy-start.3 = (bf16[7,256,2,128]{3,2,1,0:T(2,128)(2,1)S(1)}, bf16[7,256,2,128]{3,2,1,0:T(2,128)(2,1)}, u32[]{:S(2)}) copy-start(bf16[7,256,2,128]{3,2,1,0:T(2,128)(2,1)} %copy-done.2) | copy-start | bytes 2752516
  250.7 13.7 %copy-start.9 = (bf16[7,2,64,256]{3,2,1,0:T(8,128)(2,1)S(1)}, bf16[7,2,64,256]{3,2,1,0:T(8,128)(2,1)}, u32[]{:S(2)}) copy-start(bf16[7,2,64,256]{3,2,1,0:T(8,128)(2,1)} %copy-done.8) | copy-start | bytes 1376260
  250.7 142.9 %all-to-all-start.2 = ((bf16[128,1,2,32,256]{4,3,2,1,0:T(8,128)(2,1)}), bf16[128,1,2,32,256]{4,3,2,1,0:T(8,128)(2,1)}, u32[]{:S(2)}, u32[]{:S(2)}) async-start(bf16[128,1,2,32,256]{4,3,2,1,0:T(8,128)(2,1)} %bitcast.108), calls=%async_computation.2 | async-start | bytes 8388608 | tf_op jit(solution)/shard_map/all_to_all | solution.py:24
  264.3 61.3 %reduce-scatter.3.cloned.1.call-start = ((), (), s32[]{:S(2)}) async-start(), calls=%async_computation.5 | async-start | bytes 2621440 | tf_op jit(solution)/shard_map/reduce_scatter | solution.py:56
  265.0 4.8 %copy-start.6 = (bf16[56,8,2,128]{3,1,2,0:T(8,128)(2,1)}, bf16[56,8,2,128]{3,1,2,0:T(8,128)(2,1)S(1)}, u32[]{:S(2)}) copy-start(bf16[56,8,2,128]{3,1,2,0:T(8,128)(2,1)S(1)} %copy.170) | copy-start | bytes 688132
  278.6 142.4 %reduce-scatter.5.cloned.1.call-start = ((), (), s32[]{:S(2)}) async-start(), calls=%async_computation.6 | async-start | bytes 589824 | tf_op jit(solution)/shard_map/reduce_scatter | solution.py:57
  413.8 7.2 %copy-start.1 = (bf16[14,2,32,1024]{3,2,1,0:T(8,128)(2,1)S(1)}, bf16[14,2,32,1024]{3,2,1,0:T(8,128)(2,1)}, u32[]{:S(2)}) copy-start(bf16[14,2,32,1024]{3,2,1,0:T(8,128)(2,1)} %param.8) | copy-start | bytes 5505028
Sparse Core Ops, SparseCore 0:
  10.1 79.6 all-gather.7
  91.9 33.8 all-gather.9
  160.0 36.2 all-gather.11
  278.7 46.9 reduce-scatter.2
  329.1 63.1 reduce-scatter.4

commit v2 on v1

v2 whole, which is shorter than its diff:
```python
import functools

import jax
import jax.numpy as jnp
from jax import lax
from jax.experimental import pallas as pl
from jax.experimental.pallas import tpu as pltpu
from jax.sharding import Mesh
from jax.sharding import PartitionSpec as P

GROUP_LEN = 64
NEIGHBOURS = 2
HEAD_DIM = 128
EXTRA = 16
EPS = 1e-06
SCALE = HEAD_DIM ** (-0.5)
DP = ("dz", "dx")
GRP = ("yl", "co")
LINE = ("yl", "mp")
BF = jnp.bfloat16
F32 = jnp.float32
SMEM = pl.BlockSpec(memory_space=pltpu.SMEM)
VMEM = pl.BlockSpec(memory_space=pltpu.VMEM)
PARAMS = pltpu.CompilerParams(vmem_limit_bytes=40 << 20)
LAST = (((1,), (1,)), ((), ()))
FIRST = (((0,), (0,)), ((), ()))
PLAIN = (((1,), (0,)), ((), ()))


def call(kernel, scalars, arrays, outs):
    return pl.pallas_call(
        kernel,
        in_specs=[SMEM] * len(scalars) + [VMEM] * len(arrays),
        out_specs=[VMEM] * len(outs),
        out_shape=[jax.ShapeDtypeStruct(shape, kind) for shape, kind in outs],
        compiler_params=PARAMS,
    )(*scalars, *arrays)


def exchange(array, axes):
    return lax.all_to_all(array, axes, split_axis=0, concat_axis=0, tiled=True)


def copies(array, count):
    return jnp.broadcast_to(array[None], (count,) + array.shape)


def shift(array, axis, step):
    size = lax.axis_size(axis)
    return lax.ppermute(array, axis, [(i, (i + step) % size) for i in range(size)])


def dot(a, b, dims):
    return lax.dot_general(a, b, dims, preferred_element_type=F32)


def eye(size):
    rows = lax.broadcasted_iota(jnp.int32, (size, size), 0)
    return rows == lax.broadcasted_iota(jnp.int32, (size, size), 1)


def as_column(row):
    return jnp.sum(jnp.where(eye(row.shape[1]), row, 0.0), axis=1, keepdims=True)


def as_row(column):
    return jnp.sum(jnp.where(eye(column.shape[0]), column, 0.0), axis=0, keepdims=True)


def by_head(block):
    blank = jnp.zeros((block.shape[0], HEAD_DIM), block.dtype)
    upper = jnp.concatenate([block[:, :HEAD_DIM], blank], axis=1)
    lower = jnp.concatenate([blank, block[:, HEAD_DIM:]], axis=1)
    return jnp.concatenate([upper, lower], axis=0)


def own_head(both):
    half = both.shape[0] // 2
    return jnp.concatenate([both[:half, :HEAD_DIM], both[half:, HEAD_DIM:]], axis=1)


def pieces(row, count, width):
    index = lax.broadcasted_iota(jnp.int32, (EXTRA, row.shape[1]), 0)
    tile = jnp.zeros((EXTRA, row.shape[1]), F32)
    rest = row
    for i in range(count):
        part = rest.astype(BF).astype(F32)
        tile = jnp.where(index == i, part, tile)
        rest = rest - part
    blank = jnp.zeros((EXTRA, width - row.shape[1]), F32)
    return jnp.concatenate([tile, blank], axis=1).astype(BF)


def joined(tile, count, width):
    tile = tile.astype(F32)[:, :width]
    index = lax.broadcasted_iota(jnp.int32, tile.shape, 0)
    return jnp.sum(jnp.where(index < count, tile, 0.0), axis=0, keepdims=True)


def split_kernel(place, *refs):
    for block, out in zip(refs[:4], refs[4:]):
        out[...] = block[...]


def weight_rows(line, co, n_co, n_mp):
    return (line // n_mp * n_co + co) * n_mp + line % n_mp


def query_kernel(sizes, place, source, mine, other, weight, slots, total):
    n_co, n_mp, n_x = sizes
    rows = weight.shape[2]
    per = mine.shape[2] // rows
    for part, block in enumerate((mine, other)):
        co = lax.rem(place[1] + part, n_co)
        for line in range(mine.shape[0]):
            first = weight_rows(line, co, n_co, n_mp) * per
            w = jnp.concatenate(
                [weight[lax.rem(first + i, n_x), lax.div(first + i, n_x)] for i in range(per)], axis=0
            )
            product = dot(block[line], w, PLAIN)
            if part == 0 and line == 0:
                total[...] = product
            else:
                total[...] += product
    for k in range(source.shape[0]):
        c = k // NEIGHBOURS
        slots[source[k]] = total[c * GROUP_LEN : (c + 1) * GROUP_LEN].astype(BF)


def owner_forward_kernel(target, arrived, kv0, kv1, kv2, kv3, slots, probs):
    for n in range(target.shape[0]):
        t = target[n]
        keys = jnp.concatenate([kv[n, 0] for kv in (kv0, kv1, kv2, kv3)], axis=0)
        values = jnp.concatenate([kv[n, 1] for kv in (kv0, kv1, kv2, kv3)], axis=0)
        scores = dot(keys, by_head(arrived[t]), LAST) * SCALE
        top = jnp.max(scores, axis=0, keepdims=True)
        expo = jnp.exp(scores - top)
        total = jnp.sum(expo, axis=0, keepdims=True)
        prob = expo / total
        probs[n] = prob
        out = own_head(dot(prob.astype(BF), values, FIRST))
        slots[t, :GROUP_LEN, :] = out.astype(BF)
        slots[t, GROUP_LEN:, :] = pieces(top + jnp.log(total), 3, out.shape[1])


def combine_kernel(source, arrived, d_mixed, gain, attended, shares, stats):
    stats[...] = jnp.zeros_like(stats)
    shares[...] = jnp.zeros_like(shares)
    lanes = NEIGHBOURS * GROUP_LEN
    for c in range(source.shape[0] // NEIGHBOURS):
        here = slice(c * GROUP_LEN, (c + 1) * GROUP_LEN)
        tiles = [arrived[source[NEIGHBOURS * c + k]] for k in range(NEIGHBOURS)]
        logs = [joined(tile[GROUP_LEN:], 3, lanes) for tile in tiles]
        top = jnp.maximum(logs[0], logs[1])
        expos = [jnp.exp(log - top) for log in logs]
        rest = 1.0 / (expos[0] + expos[1])
        out = jnp.zeros((GROUP_LEN, 2 * HEAD_DIM), F32)
        for k in range(NEIGHBOURS):
            share = expos[k] * rest
            shares[NEIGHBOURS * c + k : NEIGHBOURS * c + k + 1, :] = share
            column = as_column(share)
            value = tiles[k][:GROUP_LEN].astype(F32)
            out = out + jnp.concatenate(
                [
                    value[:, :HEAD_DIM] * column[:GROUP_LEN],
                    value[:, HEAD_DIM:] * column[GROUP_LEN:],
                ],
                axis=1,
            )
        attended[here, :] = out
        grad_in = d_mixed[here, :].astype(F32) * gain[...]
        column = jnp.concatenate(
            [
                jnp.sum(out * out, axis=1, keepdims=True),
                jnp.sum(grad_in * out, axis=1, keepdims=True),
            ],
            axis=0,
        )
        stats[c : c + 1, :] = as_row(column)


def grad_kernel(width, source, moved, attended, shares, d_mixed, gain, mixed, slots):
    total = jnp.sum(moved[...], axis=0)
    for c in range(source.shape[0] // NEIGHBOURS):
        here = slice(c * GROUP_LEN, (c + 1) * GROUP_LEN)
        column = as_column(total[c : c + 1, :])
        inverse = lax.rsqrt(column[:GROUP_LEN] / width + EPS)
        out = attended[here, :]
        grad_in = d_mixed[here, :].astype(F32) * gain[...]
        mixed[here, :] = (out * inverse * gain[...]).astype(BF)
        factor = column[GROUP_LEN:] * inverse * inverse / width
        grad = (inverse * (grad_in - out * factor)).astype(BF).astype(F32)
        inner = grad * out
        delta = jnp.concatenate(
            [
                jnp.sum(inner[:, :HEAD_DIM], axis=1, keepdims=True),
                jnp.sum(inner[:, HEAD_DIM:], axis=1, keepdims=True),
            ],
            axis=0,
        )
        for k in range(NEIGHBOURS):
            slot = source[NEIGHBOURS * c + k]
            share = as_column(shares[NEIGHBOURS * c + k : NEIGHBOURS * c + k + 1, :])
            scaled = jnp.concatenate(
                [grad[:, :HEAD_DIM] * share[:GROUP_LEN], grad[:, HEAD_DIM:] * share[GROUP_LEN:]],
                axis=1,
            )
            slots[slot, :GROUP_LEN, :] = scaled.astype(BF)
            slots[slot, GROUP_LEN:, :] = pieces(as_row(delta * share), 2, scaled.shape[1])


def owner_backward_kernel(target, arrived, queries, probs, *refs):
    kv_refs, slots, outs = refs[:4], refs[4], refs[5:]
    for n in range(target.shape[0]):
        t = target[n]
        keys = jnp.concatenate([kv[n, 0] for kv in kv_refs], axis=0)
        values = jnp.concatenate([kv[n, 1] for kv in kv_refs], axis=0)
        grad = by_head(arrived[t, :GROUP_LEN, :])
        query = by_head(queries[t])
        prob = probs[n]
        delta = joined(arrived[t, GROUP_LEN:, :], 2, prob.shape[1])
        grad_scores = (prob * (dot(values, grad, LAST) - delta)).astype(BF)
        slots[t] = (own_head(dot(grad_scores, keys, FIRST)) * SCALE).astype(BF)
        grad_keys = (dot(grad_scores, query, PLAIN) * SCALE).astype(BF)
        grad_values = dot(prob.astype(BF), grad, PLAIN).astype(BF)
        rows = grad_keys.shape[0] // 4
        for d in range(4):
            outs[d][n, 0] = grad_keys[d * rows : (d + 1) * rows]
            outs[d][n, 1] = grad_values[d * rows : (d + 1) * rows]


def weight_kernel(sizes, place, source, arrived, mine, other, grad_q, partial):
    n_co, n_mp, n_x = sizes
    for c in range(source.shape[0] // NEIGHBOURS):
        both = sum(arrived[source[NEIGHBOURS * c + k]].astype(F32) for k in range(NEIGHBOURS))
        grad_q[c * GROUP_LEN : (c + 1) * GROUP_LEN, :] = both.astype(BF)
    rows = partial.shape[2]
    per = mine.shape[2] // rows
    for part, block in enumerate((mine, other)):
        co = lax.rem(place[1] + part, n_co)
        for line in range(mine.shape[0]):
            first = weight_rows(line, co, n_co, n_mp) * per
            product = dot(block[line], grad_q[...], FIRST).astype(BF)
            for i in range(per):
                partial[lax.rem(first + i, n_x), lax.div(first + i, n_x)] = product[
                    i * rows : (i + 1) * rows
                ]


def merge_kernel(place, *refs):
    pieces_in, out = refs[:-1], refs[-1]
    for d in range(4):

        @pl.when(pl.program_id(0) == d)
        def _():
            out[...] = pieces_in[d][...]


def split_by_quarter(place, kv):
    n, _, quarter, width = kv.shape
    part = width // 4
    take = [
        pl.BlockSpec((n, 2, quarter, part), functools.partial(block_at, d)) for d in range(4)
    ]
    whole = pl.BlockSpec((n, 2, quarter, part), lambda i, place: (0, 0, 0, 0))
    return pl.pallas_call(
        split_kernel,
        grid_spec=pltpu.PrefetchScalarGridSpec(
            num_scalar_prefetch=1, grid=(1,), in_specs=take, out_specs=[whole] * 4
        ),
        out_shape=[jax.ShapeDtypeStruct((n, 2, quarter, part), kv.dtype)] * 4,
        compiler_params=PARAMS,
    )(place, kv, kv, kv, kv)


def block_at(d, i, place):
    return (0, 0, 0, lax.rem(place[0] + d, 4))


def merge_quarters(place, parts):
    n, _, quarter, part = parts[0].shape
    whole = pl.BlockSpec((n, 2, quarter, part), lambda i, place: (0, 0, 0, 0))
    return pl.pallas_call(
        merge_kernel,
        grid_spec=pltpu.PrefetchScalarGridSpec(
            num_scalar_prefetch=1,
            grid=(4,),
            in_specs=[whole] * 4,
            out_specs=pl.BlockSpec(
                (n, 2, quarter, part), lambda i, place: (0, 0, 0, lax.rem(place[0] + i, 4))
            ),
        ),
        out_shape=jax.ShapeDtypeStruct((n, 2, quarter, 4 * part), parts[0].dtype),
        compiler_params=PARAMS,
    )(place, *parts)


def shards(hidden, wq, kv_enc, group_neighbours, gain, d_mixed):
    n_z, n_x = lax.axis_size("dz"), lax.axis_size("dx")
    n_co, n_mp = lax.axis_size("co"), lax.axis_size("mp")
    n_dp = n_z * n_x
    heads = GRP + ("mp",)
    n_heads = lax.axis_size(heads)
    sizes = (n_co, n_mp, n_x)
    me_dp = lax.axis_index(DP)
    neigh_dev = kv_enc.shape[0]
    tok_dev, dec_width = hidden.shape[0], wq.shape[1]
    model = wq.shape[0] * n_dp
    gain = gain.reshape(1, dec_width)
    place = jnp.stack([lax.axis_index("mp"), lax.axis_index("co")]).astype(jnp.int32)
    flat_ids = group_neighbours.reshape(-1)
    slot_block = jnp.arange(flat_ids.shape[0], dtype=jnp.int32) // neigh_dev
    owned = me_dp * neigh_dev + jnp.arange(neigh_dev, dtype=jnp.int32)
    matches = flat_ids[None, :] == owned[:, None]
    target = jnp.sum(jnp.where(matches, slot_block[None, :], 0), axis=1)
    source = lax.dynamic_slice_in_dim(flat_ids, me_dp * neigh_dev, neigh_dev) // neigh_dev

    line = lax.all_gather(hidden, LINE, axis=0)
    near = exchange(copies(wq, n_z), "dz").reshape(n_z, -1, dec_width)
    weight = exchange(copies(near, n_x).reshape(n_x * n_z, -1, dec_width), "dx")
    weight = weight.reshape(n_x, n_z, -1, dec_width)
    other = shift(line, "co", 1)

    split = split_by_quarter(place, kv_enc)
    kv = [shift(part, "mp", d) if d else part for d, part in enumerate(split)]

    (slots,) = pl.pallas_call(
        functools.partial(query_kernel, sizes),
        in_specs=[SMEM, SMEM, VMEM, VMEM, VMEM],
        out_specs=[VMEM],
        out_shape=[jax.ShapeDtypeStruct((n_dp, GROUP_LEN, dec_width), BF)],
        scratch_shapes=[pltpu.VMEM((tok_dev, dec_width), F32)],
        compiler_params=PARAMS,
    )(place, source, line, other, weight)
    queries = exchange(slots, DP)

    wide = (n_dp, GROUP_LEN + EXTRA, dec_width)
    span = kv_enc.shape[2] * n_mp
    slots, probs = call(
        owner_forward_kernel,
        (target,),
        (queries, *kv),
        [(wide, BF), ((neigh_dev, span, 2 * GROUP_LEN), F32)],
    )
    arrived = exchange(slots, DP)
    attended, shares, stats = call(
        combine_kernel,
        (source,),
        (arrived, d_mixed, gain),
        [((tok_dev, dec_width), F32), ((16, 128), F32), ((8, 128), F32)],
    )
    moved = exchange(copies(stats, n_heads), heads)
    mixed, slots = call(
        functools.partial(grad_kernel, model),
        (source,),
        (moved, attended, shares, d_mixed, gain),
        [((tok_dev, dec_width), BF), (wide, BF)],
    )
    arrived = exchange(slots, DP)
    slots, *parts = call(
        owner_backward_kernel,
        (target,),
        (arrived, queries, probs, *kv),
        [((n_dp, GROUP_LEN, dec_width), BF)] + [(kv[0].shape, BF)] * 4,
    )
    arrived = exchange(slots, DP)
    grad_q, partial = call(
        functools.partial(weight_kernel, sizes),
        (place, source),
        (arrived, line, other),
        [((tok_dev, dec_width), BF), (weight.shape, BF)],
    )
    parts = [shift(part, "mp", -d) if d else part for d, part in enumerate(parts)]
    column = exchange(partial.reshape(n_x * n_z, -1, dec_width), "dx").reshape(weight.shape)
    column = jnp.sum(column, axis=0, dtype=F32).astype(BF)
    grad_wq = jnp.sum(exchange(column, "dz"), axis=0, dtype=F32).astype(BF)
    grad_kv = merge_quarters(place, parts)
    return (mixed, grad_q, grad_kv, grad_wq)


def solution(mesh):
    cut = Mesh(mesh.devices.reshape(2, 2, 8, 4, 4), GRP + DP + ("mp",))
    heads = GRP + ("mp",)
    placed = (P(DP, heads), P(DP, heads), P(DP, None, "mp", GRP), P(), P(heads), P(DP, heads))
    return jax.shard_map(
        shards,
        mesh=cut,
        in_specs=placed,
        out_specs=(P(DP, heads), P(DP, heads), P(DP, None, "mp", GRP), P(DP, heads)),
        check_vma=False,
    )
```

time: 429 us -> 405 us (0.944)
  the two profiles are of different devices: /device:TPU:24 before, /device:TPU:9 now
where the time goes in v2:
time: 405 us; the launch traced here: 404 us
  blocking collectives  162 us (40%)
  waiting for transfers between devices  145 us (36%)
  starting transfers between devices  52.8 us (13%)
  Pallas kernels  17.8 us (4%)
  between operations  14.2 us (4%)
  local copies, waits for them, and re-layouts  8.35 us (2%)
    all_to_all x5, blocking collectives, exchange(): return lax.all_to_all(array, axes, split_axis=0, concat_axis=0, tiled=True)  162 us
    ppermute x7, waiting for transfers between devices, shift(): lax.ppermute(array, axis, [(i, (i + step) % size) for i in range(size)])  69 us
    all_gather x1, waiting for transfers between devices, shards(): line = lax.all_gather(hidden, LINE, axis=0)  49.1 us
    all_to_all x4, starting transfers between devices, exchange(): return lax.all_to_all(array, axes, split_axis=0, concat_axis=0, tiled=True)  28.1 us
    all_to_all x4, waiting for transfers between devices, exchange(): return lax.all_to_all(array, axes, split_axis=0, concat_axis=0, tiled=True)  25.7 us
    ppermute x7, starting transfers between devices, shift(): lax.ppermute(array, axis, [(i, (i + step) % size) for i in range(size)])  24.7 us
    pallas_call x5, Pallas kernels, call(): pl.pallas_call(kernel, in_specs=[SMEM] * len(scalars) + [VMEM] * len(arra...  12 us
  transfers between devices with their start and end apart: 12, of which 8 were waited for; matrix products, arithmetic and copies ran while one was open for 1% of the time, Pallas kernels for 1%

profile of v2, /device:TPU:9, one launch (start us, length us, event | category | flops | bytes accessed | tf_op | source)
XLA Modules:
  0.0 403.6 jit_solution(12043633446065102356)
XLA Ops:
  7.2 0.0 all-gather.3.cloned.1.call-start
  7.2 0.7 all-gather.3.cloned.1.call-update
  7.9 1.7 broadcast_in_dim.20
  9.6 10.0 %all-to-all-start = ((bf16[8,128,256]{2,1,0:T(8,128)(2,1)}), bf16[8,128,256]{2,1,0:T(8,128)(2,1)S(1)}, u32[]{:S(2)}, u32[]{:S(2)}) async-start(bf16[8,128,256]{2,1,0:T(8,128)(2,1)} %broadcast_in_dim.20), calls=%async_computation | async-start | bytes 1048576 | tf_op jit(solution)/shard_map/all_to_all | solution.py:41
  19.6 49.1 %all-gather.3.cloned.1.call-done = bf16[3584,256]{1,0:T(8,128)(2,1)} async-done(((bf16[448,256]{1,0:T(8,128)(2,1)}), bf16[3584,256]{1,0:T(8,128)(2,1)}) %all-gather.3.cloned.1.call-update) | async-done | bytes 1835024 | tf_op jit(solution)/shard_map/all_gather | solution.py:318
  68.7 4.0 collective-permute-start
  72.7 0.0 all-to-all-done
  72.7 1.6 broadcast_in_dim.21
  74.3 4.1 %all-to-all-start.1 = ((bf16[32,128,256]{2,1,0:T(8,128)(2,1)}), bf16[32,128,256]{2,1,0:T(8,128)(2,1)S(1)}, u32[]{:S(2)}, u32[]{:S(2)}) async-start(bf16[32,128,256]{2,1,0:T(8,128)(2,1)} %bitcast.15), calls=%async_computation.1 | async-start | bytes 4194304 | tf_op jit(solution)/shard_map/all_to_all | solution.py:41
  78.3 0.0 copy-done.12
  78.3 0.1 copy.11
  78.5 0.1 reshape.47
  78.6 0.1 pad_add_fusion.place
  78.7 0.1 and_select_fusion.source
  78.8 25.7 %all-to-all-done.1 = bf16[32,128,256]{2,1,0:T(8,128)(2,1)S(1)} async-done(((bf16[32,128,256]{2,1,0:T(8,128)(2,1)}), bf16[32,128,256]{2,1,0:T(8,128)(2,1)S(1)}, u32[]{:S(2)}, u32[]{:S(2)}) %all-to-all-start.1) | async-done | bytes 2097184 | tf_op jit(solution)/shard_map/all_to_all | solution.py:41
  104.5 0.0 collective-permute-done.other
  104.5 1.5 copy-done.1
  106.0 2.6 shard_map.93
  108.7 0.0 copy-start.3
  108.7 1.0 copy-done.3
  109.6 8.4 %all-to-all-start.2 = ((bf16[32,64,256]{2,1,0:T(8,128)(2,1)}), bf16[32,64,256]{2,1,0:T(8,128)(2,1)S(1)}, u32[]{:S(2)}, u32[]{:S(2)}) async-start(bf16[32,64,256]{2,1,0:T(8,128)(2,1)} %copy-done.3), calls=%async_computation.2 | async-start | bytes 2097152 | tf_op jit(solution)/shard_map/all_to_all | solution.py:41
  118.1 0.0 copy-done
  118.1 0.8 shard_map.94
  118.9 2.9 collective-permute-start.1
  121.8 4.2 %collective-permute-start.2 = (bf16[14,2,32,256]{3,2,1,0:T(8,128)(2,1)S(1)}, bf16[14,2,32,256]{3,2,1,0:T(8,128)(2,1)S(1)}, u32[]{:S(2)}, u32[]{:S(2)}) collective-permute-start(bf16[14,2,32,256]{3,2,1,0:T(8,128)(2,1)S(1)} %get-tuple-element.24), channel_id=1, source_target_pairs={{0,2},{1,3},{2,0},{3,1},{4,6},{5,7},{6,4},{7,5},{8,10},{9,11},{10,... | collective-permute-start | bytes 1376264 | tf_op jit(solution)/shard_map/ppermute | solution.py:50
  125.9 4.3 %collective-permute-start.3 = (bf16[14,2,32,256]{3,2,1,0:T(8,128)(2,1)S(1)}, bf16[14,2,32,256]{3,2,1,0:T(8,128)(2,1)S(1)}, u32[]{:S(2)}, u32[]{:S(2)}) collective-permute-start(bf16[14,2,32,256]{3,2,1,0:T(8,128)(2,1)S(1)} %get-tuple-element.25), channel_id=1, source_target_pairs={{0,3},{1,0},{2,1},{3,2},{4,7},{5,4},{6,5},{7,6},{8,11},{9,8},{10,9... | collective-permute-start | bytes 1376264 | tf_op jit(solution)/shard_map/ppermute | solution.py:50
  130.3 0.2 select_reduce_fusion.target
  130.5 9.5 %collective-permute-done.1.kv1.refs_1_ = bf16[14,2,32,256]{3,2,1,0:T(8,128)(2,1)S(1)} collective-permute-done((bf16[14,2,32,256]{3,2,1,0:T(8,128)(2,1)S(1)}, bf16[14,2,32,256]{3,2,1,0:T(8,128)(2,1)S(1)}, u32[]{:S(2)}, u32[]{:S(2)}) %collective-permute-start.1) | collective-permute-done | bytes 458784 | tf_op jit(solution)/shard_map/ppermute | solution.py:50
  140.0 3.4 collective-permute-done.2.kv2.refs_2_
  143.4 14.8 %collective-permute-done.3.kv3.refs_3_ = bf16[14,2,32,256]{3,2,1,0:T(8,128)(2,1)S(1)} collective-permute-done((bf16[14,2,32,256]{3,2,1,0:T(8,128)(2,1)S(1)}, bf16[14,2,32,256]{3,2,1,0:T(8,128)(2,1)S(1)}, u32[]{:S(2)}, u32[]{:S(2)}) %collective-permute-start.3) | collective-permute-done | bytes 458784 | tf_op jit(solution)/shard_map/ppermute | solution.py:50
  158.2 0.0 all-to-all-done.2.arrived.queries
  158.2 1.7 shard_map.95
  159.9 0.0 copy-start.4
  159.9 0.0 copy-start.5
  159.9 36.3 %all_to_all.45.arrived = bf16[32,80,256]{2,1,0:T(8,128)(2,1)S(1)} all-to-all(bf16[32,80,256]{2,1,0:T(8,128)(2,1)S(1)} %get-tuple-element.26), channel_id=1, replica_groups=mesh['yl'=2,'co'=2,'dz'=8,'dx'=4,'mp'=4] {'dz','dx'}, dimensions={0} | all-to-all | bytes 2621440 | tf_op jit(solution)/shard_map/all_to_all | solution.py:41
  196.2 0.0 copy-done.4
  196.2 0.0 copy-done.5
  196.2 1.6 shard_map.96
  197.8 31.0 %all_to_all.46.moved = f32[16,8,128]{2,1,0:T(8,128)S(1)} all-to-all(f32[16,8,128]{2,1,0:T(8,128)S(1)} %broadcast_in_dim.36), channel_id=1, replica_groups=mesh['yl'=2,'co'=2,'dz'=8,'dx'=4,'mp'=4] {'yl','co','mp'}, dimensions={0} | all-to-all | bytes 131072 | tf_op jit(solution)/shard_map/all_to_all | solution.py:41
  228.8 2.5 shard_map.97
  231.3 37.6 %all_to_all.47.arrived = bf16[32,80,256]{2,1,0:T(8,128)(2,1)S(1)} all-to-all(bf16[32,80,256]{2,1,0:T(8,128)(2,1)S(1)} %get-tuple-element.31), channel_id=1, replica_groups=mesh['yl'=2,'co'=2,'dz'=8,'dx'=4,'mp'=4] {'dz','dx'}, dimensions={0} | all-to-all | bytes 2621440 | tf_op jit(solution)/shard_map/all_to_all | solution.py:41
  268.9 3.1 shard_map.98
  272.0 0.0 copy-start.6
  272.0 0.8 copy-done.6
  272.8 0.8 copy-done.8
  273.6 0.8 copy-done.10
  274.3 30.1 %all_to_all.48.arrived = bf16[32,64,256]{2,1,0:T(8,128)(2,1)S(1)} all-to-all(bf16[32,64,256]{2,1,0:T(8,128)(2,1)S(1)} %get-tuple-element.33), channel_id=1, replica_groups=mesh['yl'=2,'co'=2,'dz'=8,'dx'=4,'mp'=4] {'dz','dx'}, dimensions={0} | all-to-all | bytes 2097152 | tf_op jit(solution)/shard_map/all_to_all | solution.py:41
  304.4 0.0 copy-done.2
  304.4 3.3 shard_map.99
  307.7 26.9 %all_to_all.49 = bf16[32,128,256]{2,1,0:T(8,128)(2,1)} all-to-all(bf16[32,128,256]{2,1,0:T(8,128)(2,1)S(1)} %bitcast.12), channel_id=1, replica_groups=mesh['yl'=2,'co'=2,'dz'=8,'dx'=4,'mp'=4] {'dx'}, dimensions={0} | all-to-all | bytes 4194304 | tf_op jit(solution)/shard_map/all_to_all | solution.py:41
  334.6 3.0 reduce_sum.34
  337.5 5.5 %all-to-all-start.8 = ((bf16[8,128,256]{2,1,0:T(8,128)(2,1)}), bf16[8,128,256]{2,1,0:T(8,128)(2,1)S(1)}, u32[]{:S(2)}, u32[]{:S(2)}) async-start(bf16[8,128,256]{2,1,0:T(8,128)(2,1)} %reduce_sum.34), calls=%async_computation.8 | async-start | bytes 1048576 | tf_op jit(solution)/shard_map/all_to_all | solution.py:41
  343.1 0.0 copy-done.11
  343.1 3.0 collective-permute-start.4
  346.1 0.0 copy-done.9
  346.1 3.7 collective-permute-start.5
  349.9 0.0 copy-done.7
  349.9 2.6 collective-permute-start.6
  352.4 5.8 %collective-permute-done.4.refs_1_ = bf16[14,2,32,256]{3,2,1,0:T(8,128)(2,1)S(1)} collective-permute-done((bf16[14,2,32,256]{3,2,1,0:T(8,128)(2,1)S(1)}, bf16[14,2,32,256]{3,2,1,0:T(8,128)(2,1)S(1)}, u32[]{:S(2)}, u32[]{:S(2)}) %collective-permute-start.4) | collective-permute-done | bytes 458784 | tf_op jit(solution)/shard_map/ppermute | solution.py:50
  358.2 27.8 %collective-permute-done.5.refs_2_ = bf16[14,2,32,256]{3,2,1,0:T(8,128)(2,1)S(1)} collective-permute-done((bf16[14,2,32,256]{3,2,1,0:T(8,128)(2,1)S(1)}, bf16[14,2,32,256]{3,2,1,0:T(8,128)(2,1)S(1)}, u32[]{:S(2)}, u32[]{:S(2)}) %collective-permute-start.5) | collective-permute-done | bytes 458784 | tf_op jit(solution)/shard_map/ppermute | solution.py:50
  386.0 7.7 %collective-permute-done.6.refs_3_ = bf16[14,2,32,256]{3,2,1,0:T(8,128)(2,1)S(1)} collective-permute-done((bf16[14,2,32,256]{3,2,1,0:T(8,128)(2,1)S(1)}, bf16[14,2,32,256]{3,2,1,0:T(8,128)(2,1)S(1)}, u32[]{:S(2)}, u32[]{:S(2)}) %collective-permute-start.6) | collective-permute-done | bytes 458784 | tf_op jit(solution)/shard_map/ppermute | solution.py:50
  393.7 2.3 shard_map.100
  396.1 0.0 all-to-all-done.8
  396.1 0.7 reduce_sum.35
  (12 shorter events, 0.0 us)
Async XLA Ops:
  7.2 61.5 %all-gather.3.cloned.1.call-start = ((), (), s32[]{:S(2)}) async-start(), calls=%async_computation.9 | async-start | bytes 2064384 | tf_op jit(solution)/shard_map/all_gather | solution.py:318
  9.6 63.1 %all-to-all-start = ((bf16[8,128,256]{2,1,0:T(8,128)(2,1)}), bf16[8,128,256]{2,1,0:T(8,128)(2,1)S(1)}, u32[]{:S(2)}, u32[]{:S(2)}) async-start(bf16[8,128,256]{2,1,0:T(8,128)(2,1)} %broadcast_in_dim.20), calls=%async_computation | async-start | bytes 1048576 | tf_op jit(solution)/shard_map/all_to_all | solution.py:41
  68.7 35.8 %collective-permute-start = (bf16[8,448,256]{2,1,0:T(8,128)(2,1)}, bf16[8,448,256]{2,1,0:T(8,128)(2,1)}, u32[]{:S(2)}, u32[]{:S(2)}) collective-permute-start(bf16[8,448,256]{2,1,0:T(8,128)(2,1)} %bitcast.9), channel_id=1, source_target_pairs={{0,128},{128,0},{1,129},{129,1},{2,130},{130,2},{3,131},{131,3},{4... | collective-permute-start | bytes 5505032 | tf_op jit(solution)/shard_map/ppermute | solution.py:50
  74.3 4.1 %copy-start.12 = (s32[224,2]{0,1:T(2,128)S(1)}, s32[224,2]{0,1:T(2,128)}, u32[]{:S(2)}) copy-start(s32[224,2]{0,1:T(2,128)} %param.9) | copy-start | bytes 5380
  74.3 30.2 %all-to-all-start.1 = ((bf16[32,128,256]{2,1,0:T(8,128)(2,1)}), bf16[32,128,256]{2,1,0:T(8,128)(2,1)S(1)}, u32[]{:S(2)}, u32[]{:S(2)}) async-start(bf16[32,128,256]{2,1,0:T(8,128)(2,1)} %bitcast.15), calls=%async_computation.1 | async-start | bytes 4194304 | tf_op jit(solution)/shard_map/all_to_all | solution.py:41
  104.5 1.5 copy-start.1
  108.7 1.0 copy-start.3
  109.6 8.5 %copy-start = (bf16[14,2,32,1024]{3,2,1,0:T(8,128)(2,1)S(1)}, bf16[14,2,32,1024]{3,2,1,0:T(8,128)(2,1)}, u32[]{:S(2)}) copy-start(bf16[14,2,32,1024]{3,2,1,0:T(8,128)(2,1)} %refs_3_.1) | copy-start | bytes 5505028
  109.6 48.6 %all-to-all-start.2 = ((bf16[32,64,256]{2,1,0:T(8,128)(2,1)}), bf16[32,64,256]{2,1,0:T(8,128)(2,1)S(1)}, u32[]{:S(2)}, u32[]{:S(2)}) async-start(bf16[32,64,256]{2,1,0:T(8,128)(2,1)} %copy-done.3), calls=%async_computation.2 | async-start | bytes 2097152 | tf_op jit(solution)/shard_map/all_to_all | solution.py:41
  118.9 21.1 %collective-permute-start.1 = (bf16[14,2,32,256]{3,2,1,0:T(8,128)(2,1)S(1)}, bf16[14,2,32,256]{3,2,1,0:T(8,128)(2,1)S(1)}, u32[]{:S(2)}, u32[]{:S(2)}) collective-permute-start(bf16[14,2,32,256]{3,2,1,0:T(8,128)(2,1)S(1)} %get-tuple-element.23), channel_id=1, source_target_pairs={{0,1},{1,2},{2,3},{3,0},{4,5},{5,6},{6,7},{7,4},{8,9},{9,10},{10,1... | collective-permute-start | bytes 1376264 | tf_op jit(solution)/shard_map/ppermute | solution.py:50
  121.8 21.6 %collective-permute-start.2 = (bf16[14,2,32,256]{3,2,1,0:T(8,128)(2,1)S(1)}, bf16[14,2,32,256]{3,2,1,0:T(8,128)(2,1)S(1)}, u32[]{:S(2)}, u32[]{:S(2)}) collective-permute-start(bf16[14,2,32,256]{3,2,1,0:T(8,128)(2,1)S(1)} %get-tuple-element.24), channel_id=1, source_target_pairs={{0,2},{1,3},{2,0},{3,1},{4,6},{5,7},{6,4},{7,5},{8,10},{9,11},{10,... | collective-permute-start | bytes 1376264 | tf_op jit(solution)/shard_map/ppermute | solution.py:50
  125.9 32.3 %collective-permute-start.3 = (bf16[14,2,32,256]{3,2,1,0:T(8,128)(2,1)S(1)}, bf16[14,2,32,256]{3,2,1,0:T(8,128)(2,1)S(1)}, u32[]{:S(2)}, u32[]{:S(2)}) collective-permute-start(bf16[14,2,32,256]{3,2,1,0:T(8,128)(2,1)S(1)} %get-tuple-element.25), channel_id=1, source_target_pairs={{0,3},{1,0},{2,1},{3,2},{4,7},{5,4},{6,5},{7,6},{8,11},{9,8},{10,9... | collective-permute-start | bytes 1376264 | tf_op jit(solution)/shard_map/ppermute | solution.py:50
  159.9 36.3 %copy-start.4 = (bf16[448,256]{1,0:T(8,128)(2,1)S(1)}, bf16[448,256]{1,0:T(8,128)(2,1)}, u32[]{:S(2)}) copy-start(bf16[448,256]{1,0:T(8,128)(2,1)} %d_mixed.3) | copy-start | bytes 688132
  159.9 36.3 %copy-start.5 = (f32[256]{0:T(256)S(1)}, f32[256]{0:T(256)}, u32[]{:S(2)}) copy-start(f32[256]{0:T(256)} %param.10) | copy-start | bytes 3076
  272.0 0.8 copy-start.6
  272.8 0.8 copy-start.8
  273.6 0.8 copy-start.10
  274.3 30.1 %copy-start.2 = (bf16[3584,256]{1,0:T(8,128)(2,1)S(1)}, bf16[3584,256]{1,0:T(8,128)(2,1)}, u32[]{:S(2)}) copy-start(bf16[3584,256]{1,0:T(8,128)(2,1)} %all-gather.3.cloned.1.call-done) | copy-start | bytes 5505028
  334.6 8.5 %copy-start.11 = (bf16[14,2,32,256]{3,2,1,0:T(8,128)(2,1)S(1)}, bf16[14,2,32,256]{3,2,1,0:T(8,128)(2,1)}, u32[]{:S(2)}) copy-start(bf16[14,2,32,256]{3,2,1,0:T(8,128)(2,1)} %copy-done.10) | copy-start | bytes 1376260
  334.6 11.6 %copy-start.9 = (bf16[14,2,32,256]{3,2,1,0:T(8,128)(2,1)S(1)}, bf16[14,2,32,256]{3,2,1,0:T(8,128)(2,1)}, u32[]{:S(2)}) copy-start(bf16[14,2,32,256]{3,2,1,0:T(8,128)(2,1)} %copy-done.8) | copy-start | bytes 1376260
  334.6 15.3 %copy-start.7 = (bf16[14,2,32,256]{3,2,1,0:T(8,128)(2,1)S(1)}, bf16[14,2,32,256]{3,2,1,0:T(8,128)(2,1)}, u32[]{:S(2)}) copy-start(bf16[14,2,32,256]{3,2,1,0:T(8,128)(2,1)} %copy-done.6) | copy-start | bytes 1376260
  337.5 58.5 %all-to-all-start.8 = ((bf16[8,128,256]{2,1,0:T(8,128)(2,1)}), bf16[8,128,256]{2,1,0:T(8,128)(2,1)S(1)}, u32[]{:S(2)}, u32[]{:S(2)}) async-start(bf16[8,128,256]{2,1,0:T(8,128)(2,1)} %reduce_sum.34), calls=%async_computation.8 | async-start | bytes 1048576 | tf_op jit(solution)/shard_map/all_to_all | solution.py:41
  343.1 15.2 %collective-permute-start.4 = (bf16[14,2,32,256]{3,2,1,0:T(8,128)(2,1)S(1)}, bf16[14,2,32,256]{3,2,1,0:T(8,128)(2,1)S(1)}, u32[]{:S(2)}, u32[]{:S(2)}) collective-permute-start(bf16[14,2,32,256]{3,2,1,0:T(8,128)(2,1)S(1)} %copy-done.11), channel_id=1, source_target_pairs={{0,3},{1,0},{2,1},{3,2},{4,7},{5,4},{6,5},{7,6},{8,11},{9,8},{10,9... | collective-permute-start | bytes 1376264 | tf_op jit(solution)/shard_map/ppermute | solution.py:50
  346.1 39.9 %collective-permute-start.5 = (bf16[14,2,32,256]{3,2,1,0:T(8,128)(2,1)S(1)}, bf16[14,2,32,256]{3,2,1,0:T(8,128)(2,1)S(1)}, u32[]{:S(2)}, u32[]{:S(2)}) collective-permute-start(bf16[14,2,32,256]{3,2,1,0:T(8,128)(2,1)S(1)} %copy-done.9), channel_id=1, source_target_pairs={{0,2},{1,3},{2,0},{3,1},{4,6},{5,7},{6,4},{7,5},{8,10},{9,11},{10,... | collective-permute-start | bytes 1376264 | tf_op jit(solution)/shard_map/ppermute | solution.py:50
  349.9 43.9 %collective-permute-start.6 = (bf16[14,2,32,256]{3,2,1,0:T(8,128)(2,1)S(1)}, bf16[14,2,32,256]{3,2,1,0:T(8,128)(2,1)S(1)}, u32[]{:S(2)}, u32[]{:S(2)}) collective-permute-start(bf16[14,2,32,256]{3,2,1,0:T(8,128)(2,1)S(1)} %copy-done.7), channel_id=1, source_target_pairs={{0,1},{1,2},{2,3},{3,0},{4,5},{5,6},{6,7},{7,4},{8,9},{9,10},{10,1... | collective-permute-start | bytes 1376264 | tf_op jit(solution)/shard_map/ppermute | solution.py:50
Sparse Core Ops, SparseCore 0:
  10.1 58.5 all-gather.2

commit v3 on v2

--- a/solution.py
+++ b/solution.py
@@ -79,7 +79,7 @@
     return jnp.concatenate([both[:half, :HEAD_DIM], both[half:, HEAD_DIM:]], axis=1)
 
 
-def pieces(row, count, width):
+def pieces(row, count):
     index = lax.broadcasted_iota(jnp.int32, (EXTRA, row.shape[1]), 0)
     tile = jnp.zeros((EXTRA, row.shape[1]), F32)
     rest = row
@@ -87,19 +87,42 @@
         part = rest.astype(BF).astype(F32)
         tile = jnp.where(index == i, part, tile)
         rest = rest - part
-    blank = jnp.zeros((EXTRA, width - row.shape[1]), F32)
-    return jnp.concatenate([tile, blank], axis=1).astype(BF)
-
-
-def joined(tile, count, width):
-    tile = tile.astype(F32)[:, :width]
+    return tile.astype(BF)
+
+
+def write_slot(slots, slot, block, row, count):
+    width = block.shape[1]
+    for i in range(GROUP_LEN // EXTRA):
+        slots[slot, :, i * width : (i + 1) * width] = block[i * EXTRA : (i + 1) * EXTRA]
+    slots[slot, :, GROUP_LEN // EXTRA * width :] = pieces(row, count)
+
+
+def read_slot(slots, slot, width, count):
+    folds = GROUP_LEN // EXTRA
+    tile = slots[slot]
+    block = jnp.concatenate([tile[:, i * width : (i + 1) * width] for i in range(folds)], axis=0)
+    return block, joined(tile[:, folds * width :], count)
+
+
+def joined(tile, count):
+    tile = tile.astype(F32)
     index = lax.broadcasted_iota(jnp.int32, tile.shape, 0)
     return jnp.sum(jnp.where(index < count, tile, 0.0), axis=0, keepdims=True)
 
 
-def split_kernel(place, *refs):
-    for block, out in zip(refs[:4], refs[4:]):
-        out[...] = block[...]
+def split_kernel(place, block0, block1, block2, block3, own, up, down):
+    own[...] = block0[...]
+    up[:, :2] = block1[...]
+    up[:, 2] = block2[:, 0]
+    down[:, :2] = block3[...]
+    down[:, 2] = block2[:, 1]
+
+
+def whole_rows(n, own, first, far_keys, far_values, last):
+    return [
+        jnp.concatenate([own[n, i], first[n, i], far[n], last[n, i]], axis=0)
+        for i, far in enumerate((far_keys, far_values))
+    ]
 
 
 def weight_rows(line, co, n_co, n_mp):
@@ -127,11 +150,10 @@
         slots[source[k]] = total[c * GROUP_LEN : (c + 1) * GROUP_LEN].astype(BF)
 
 
-def owner_forward_kernel(target, arrived, kv0, kv1, kv2, kv3, slots, probs):
+def owner_forward_kernel(target, arrived, own, first, far_keys, far_values, last, slots, probs):
     for n in range(target.shape[0]):
         t = target[n]
-        keys = jnp.concatenate([kv[n, 0] for kv in (kv0, kv1, kv2, kv3)], axis=0)
-        values = jnp.concatenate([kv[n, 1] for kv in (kv0, kv1, kv2, kv3)], axis=0)
+        keys, values = whole_rows(n, own, first, far_keys, far_values, last)
         scores = dot(keys, by_head(arrived[t]), LAST) * SCALE
         top = jnp.max(scores, axis=0, keepdims=True)
         expo = jnp.exp(scores - top)
@@ -139,18 +161,18 @@
         prob = expo / total
         probs[n] = prob
         out = own_head(dot(prob.astype(BF), values, FIRST))
-        slots[t, :GROUP_LEN, :] = out.astype(BF)
-        slots[t, GROUP_LEN:, :] = pieces(top + jnp.log(total), 3, out.shape[1])
+        write_slot(slots, t, out.astype(BF), top + jnp.log(total), 3)
 
 
 def combine_kernel(source, arrived, d_mixed, gain, attended, shares, stats):
     stats[...] = jnp.zeros_like(stats)
     shares[...] = jnp.zeros_like(shares)
-    lanes = NEIGHBOURS * GROUP_LEN
+    width = attended.shape[1]
     for c in range(source.shape[0] // NEIGHBOURS):
         here = slice(c * GROUP_LEN, (c + 1) * GROUP_LEN)
-        tiles = [arrived[source[NEIGHBOURS * c + k]] for k in range(NEIGHBOURS)]
-        logs = [joined(tile[GROUP_LEN:], 3, lanes) for tile in tiles]
+        values, logs = zip(
+            *[read_slot(arrived, source[NEIGHBOURS * c + k], width, 3) for k in range(NEIGHBOURS)]
+        )
         top = jnp.maximum(logs[0], logs[1])
         expos = [jnp.exp(log - top) for log in logs]
         rest = 1.0 / (expos[0] + expos[1])
@@ -159,7 +181,7 @@
             share = expos[k] * rest
             shares[NEIGHBOURS * c + k : NEIGHBOURS * c + k + 1, :] = share
             column = as_column(share)
-            value = tiles[k][:GROUP_LEN].astype(F32)
+            value = values[k].astype(F32)
             out = out + jnp.concatenate(
                 [
                     value[:, :HEAD_DIM] * column[:GROUP_LEN],
@@ -205,28 +227,28 @@
                 [grad[:, :HEAD_DIM] * share[:GROUP_LEN], grad[:, HEAD_DIM:] * share[GROUP_LEN:]],
                 axis=1,
             )
-            slots[slot, :GROUP_LEN, :] = scaled.astype(BF)
-            slots[slot, GROUP_LEN:, :] = pieces(as_row(delta * share), 2, scaled.shape[1])
+            write_slot(slots, slot, scaled.astype(BF), as_row(delta * share), 2)
 
 
 def owner_backward_kernel(target, arrived, queries, probs, *refs):
-    kv_refs, slots, outs = refs[:4], refs[4], refs[5:]
+    kv_refs, (slots, own, down, up) = refs[:5], refs[5:]
     for n in range(target.shape[0]):
         t = target[n]
-        keys = jnp.concatenate([kv[n, 0] for kv in kv_refs], axis=0)
-        values = jnp.concatenate([kv[n, 1] for kv in kv_refs], axis=0)
-        grad = by_head(arrived[t, :GROUP_LEN, :])
+        keys, values = whole_rows(n, *kv_refs)
+        block, delta = read_slot(arrived, t, keys.shape[1], 2)
+        grad = by_head(block)
         query = by_head(queries[t])
         prob = probs[n]
-        delta = joined(arrived[t, GROUP_LEN:, :], 2, prob.shape[1])
         grad_scores = (prob * (dot(values, grad, LAST) - delta)).astype(BF)
         slots[t] = (own_head(dot(grad_scores, keys, FIRST)) * SCALE).astype(BF)
         grad_keys = (dot(grad_scores, query, PLAIN) * SCALE).astype(BF)
         grad_values = dot(prob.astype(BF), grad, PLAIN).astype(BF)
         rows = grad_keys.shape[0] // 4
-        for d in range(4):
-            outs[d][n, 0] = grad_keys[d * rows : (d + 1) * rows]
-            outs[d][n, 1] = grad_values[d * rows : (d + 1) * rows]
+        for i, grads in enumerate((grad_keys, grad_values)):
+            own[n, i] = grads[:rows]
+            down[n, i] = grads[rows : 2 * rows]
+            (down, up)[i][n, 2] = grads[2 * rows : 3 * rows]
+            up[n, i] = grads[3 * rows :]
 
 
 def weight_kernel(sizes, place, source, arrived, mine, other, grad_q, partial):
@@ -247,13 +269,25 @@
                 ]
 
 
-def merge_kernel(place, *refs):
-    pieces_in, out = refs[:-1], refs[-1]
-    for d in range(4):
-
-        @pl.when(pl.program_id(0) == d)
-        def _():
-            out[...] = pieces_in[d][...]
+def merge_kernel(place, own, first, far_keys, far_values, last, out):
+    step = pl.program_id(0)
+
+    @pl.when(step == 0)
+    def _():
+        out[...] = own[...]
+
+    @pl.when(step == 1)
+    def _():
+        out[...] = first[:, :2]
+
+    @pl.when(step == 2)
+    def _():
+        out[:, 0] = far_keys[...]
+        out[:, 1] = far_values[...]
+
+    @pl.when(step == 3)
+    def _():
+        out[...] = last[:, :2]
 
 
 def split_by_quarter(place, kv):
@@ -262,13 +296,16 @@
     take = [
         pl.BlockSpec((n, 2, quarter, part), functools.partial(block_at, d)) for d in range(4)
     ]
-    whole = pl.BlockSpec((n, 2, quarter, part), lambda i, place: (0, 0, 0, 0))
+    shapes = [(n, 2, quarter, part), (n, 3, quarter, part), (n, 3, quarter, part)]
     return pl.pallas_call(
         split_kernel,
         grid_spec=pltpu.PrefetchScalarGridSpec(
-            num_scalar_prefetch=1, grid=(1,), in_specs=take, out_specs=[whole] * 4
+            num_scalar_prefetch=1,
+            grid=(1,),
+            in_specs=take,
+            out_specs=[pl.BlockSpec(shape, lambda i, place: (0, 0, 0, 0)) for shape in shapes],
         ),
-        out_shape=[jax.ShapeDtypeStruct((n, 2, quarter, part), kv.dtype)] * 4,
+        out_shape=[jax.ShapeDtypeStruct(shape, kv.dtype) for shape in shapes],
         compiler_params=PARAMS,
     )(place, kv, kv, kv, kv)
 
@@ -279,13 +316,14 @@
 
 def merge_quarters(place, parts):
     n, _, quarter, part = parts[0].shape
-    whole = pl.BlockSpec((n, 2, quarter, part), lambda i, place: (0, 0, 0, 0))
     return pl.pallas_call(
         merge_kernel,
         grid_spec=pltpu.PrefetchScalarGridSpec(
             num_scalar_prefetch=1,
             grid=(4,),
-            in_specs=[whole] * 4,
+            in_specs=[
+                pl.BlockSpec(x.shape, functools.partial(origin, x.ndim)) for x in parts
+            ],
             out_specs=pl.BlockSpec(
                 (n, 2, quarter, part), lambda i, place: (0, 0, 0, lax.rem(place[0] + i, 4))
             ),
@@ -293,6 +331,10 @@
         out_shape=jax.ShapeDtypeStruct((n, 2, quarter, 4 * part), parts[0].dtype),
         compiler_params=PARAMS,
     )(place, *parts)
+
+
+def origin(ndim, i, place):
+    return (0,) * ndim
 
 
 def shards(hidden, wq, kv_enc, group_neighbours, gain, d_mixed):
@@ -316,13 +358,18 @@
     source = lax.dynamic_slice_in_dim(flat_ids, me_dp * neigh_dev, neigh_dev) // neigh_dev
 
     line = lax.all_gather(hidden, LINE, axis=0)
+    own, up, down = split_by_quarter(place, kv_enc)
+    first, last = shift(up, "mp", 1), shift(down, "mp", -1)
     near = exchange(copies(wq, n_z), "dz").reshape(n_z, -1, dec_width)
+    near, first, last = lax.optimization_barrier((near, first, last))
+    far_keys, far_values = shift(first[:, 2], "mp", 1), shift(last[:, 2], "mp", -1)
     weight = exchange(copies(near, n_x).reshape(n_x * n_z, -1, dec_width), "dx")
     weight = weight.reshape(n_x, n_z, -1, dec_width)
+    line, weight, far_keys, far_values = lax.optimization_barrier(
+        (line, weight, far_keys, far_values)
+    )
     other = shift(line, "co", 1)
-
-    split = split_by_quarter(place, kv_enc)
-    kv = [shift(part, "mp", d) if d else part for d, part in enumerate(split)]
+    kv = (own, first, far_keys, far_values, last)
 
     (slots,) = pl.pallas_call(
         functools.partial(query_kernel, sizes),
@@ -334,7 +381,7 @@
     )(place, source, line, other, weight)
     queries = exchange(slots, DP)
 
-    wide = (n_dp, GROUP_LEN + EXTRA, dec_width)
+    wide = (n_dp, EXTRA, GROUP_LEN // EXTRA * dec_width + NEIGHBOURS * GROUP_LEN)
     span = kv_enc.shape[2] * n_mp
     slots, probs = call(
         owner_forward_kernel,
@@ -357,24 +404,27 @@
         [((tok_dev, dec_width), BF), (wide, BF)],
     )
     arrived = exchange(slots, DP)
-    slots, *parts = call(
+    slots, own, down, up = call(
         owner_backward_kernel,
         (target,),
         (arrived, queries, probs, *kv),
-        [((n_dp, GROUP_LEN, dec_width), BF)] + [(kv[0].shape, BF)] * 4,
-    )
+        [((n_dp, GROUP_LEN, dec_width), BF)] + [(x.shape, BF) for x in (own, first, last)],
+    )
+    first, last = shift(down, "mp", -1), shift(up, "mp", 1)
     arrived = exchange(slots, DP)
+    arrived, first, last = lax.optimization_barrier((arrived, first, last))
+    far_keys, far_values = shift(first[:, 2], "mp", -1), shift(last[:, 2], "mp", 1)
     grad_q, partial = call(
         functools.partial(weight_kernel, sizes),
         (place, source),
         (arrived, line, other),
         [((tok_dev, dec_width), BF), (weight.shape, BF)],
     )
-    parts = [shift(part, "mp", -d) if d else part for d, part in enumerate(parts)]
     column = exchange(partial.reshape(n_x * n_z, -1, dec_width), "dx").reshape(weight.shape)
+    column, far_keys, far_values = lax.optimization_barrier((column, far_keys, far_values))
+    grad_kv = merge_quarters(place, (own, first, far_keys, far_values, last))
     column = jnp.sum(column, axis=0, dtype=F32).astype(BF)
     grad_wq = jnp.sum(exchange(column, "dz"), axis=0, dtype=F32).astype(BF)
-    grad_kv = merge_quarters(place, parts)
     return (mixed, grad_q, grad_kv, grad_wq)
 
 

time: 405 us -> 382 us (0.943)
  the two profiles are of different devices: /device:TPU:9 before, /device:TPU:1 now
where the time goes in v3:
time: 382 us; the launch traced here: 378 us
  waiting for transfers between devices  162 us (42%)
  blocking collectives  89 us (23%)
  starting transfers between devices  69.6 us (18%)
  local copies, waits for them, and re-layouts  20.4 us (5%)
  Pallas kernels  19.8 us (5%)
  between operations  14.3 us (4%)
    ppermute x9, waiting for transfers between devices, shift(): lax.ppermute(array, axis, [(i, (i + step) % size) for i in range(size)])  109 us
    all_to_all x3, blocking collectives, exchange(): return lax.all_to_all(array, axes, split_axis=0, concat_axis=0, tiled=True)  89 us
    all_to_all x6, waiting for transfers between devices, exchange(): return lax.all_to_all(array, axes, split_axis=0, concat_axis=0, tiled=True)  53.2 us
    all_to_all x6, starting transfers between devices, exchange(): return lax.all_to_all(array, axes, split_axis=0, concat_axis=0, tiled=True)  37.2 us
    ppermute x9, starting transfers between devices, shift(): lax.ppermute(array, axis, [(i, (i + step) % size) for i in range(size)])  32.3 us
    pallas_call x5, Pallas kernels, call(): pl.pallas_call(kernel, in_specs=[SMEM] * len(scalars) + [VMEM] * len(arra...  12 us
    unnamed x33, local copies, waits for them, and re-layouts  8.7 us
  transfers between devices with their start and end apart: 16, of which 11 were waited for; matrix products, arithmetic and copies ran while one was open for 3% of the time, Pallas kernels for 1%

profile of v3, /device:TPU:1, one launch (start us, length us, event | category | flops | bytes accessed | tf_op | source)
XLA Modules:
  0.0 377.9 jit_solution(2021841644351695328)
XLA Ops:
  7.2 0.0 all-gather.3.cloned.1.call-start
  7.2 0.7 all-gather.3.cloned.1.call-update
  7.9 1.7 broadcast_in_dim.20
  9.6 10.9 %all-to-all-start = ((bf16[8,128,256]{2,1,0:T(8,128)(2,1)}), bf16[8,128,256]{2,1,0:T(8,128)(2,1)}, u32[]{:S(2)}, u32[]{:S(2)}) async-start(bf16[8,128,256]{2,1,0:T(8,128)(2,1)} %broadcast_in_dim.20), calls=%async_computation | async-start | bytes 1048576 | tf_op jit(solution)/shard_map/all_to_all | solution.py:41
  20.4 0.1 pad_add_fusion.place
  20.5 0.8 shard_map.93
  21.4 4.2 %collective-permute-start = (bf16[14,3,32,256]{3,2,0,1:T(8,128)(2,1)S(1)}, bf16[14,3,32,256]{3,2,0,1:T(8,128)(2,1)S(1)}, u32[]{:S(2)}, u32[]{:S(2)}) collective-permute-start(bf16[14,3,32,256]{3,2,0,1:T(8,128)(2,1)S(1)} %copy.22), channel_id=1, source_target_pairs={{0,1},{1,2},{2,3},{3,0},{4,5},{5,6},{6,7},{7,4},{8,9},{9,10},{10,1... | collective-permute-start | bytes 2064392 | tf_op jit(solution)/shard_map/ppermute | solution.py:50
  25.6 3.6 collective-permute-start.1
  29.2 43.4 %collective-permute-done = bf16[14,3,32,256]{3,2,0,1:T(8,128)(2,1)S(1)} collective-permute-done((bf16[14,3,32,256]{3,2,0,1:T(8,128)(2,1)S(1)}, bf16[14,3,32,256]{3,2,0,1:T(8,128)(2,1)S(1)}, u32[]{:S(2)}, u32[]{:S(2)}) %collective-permute-start) | collective-permute-done | bytes 688160 | tf_op jit(solution)/shard_map/ppermute | solution.py:50
  72.6 18.8 %collective-permute-done.1.last.refs_4_ = bf16[14,3,32,256]{3,2,1,0:T(8,128)(2,1)S(1)} collective-permute-done((bf16[14,3,32,256]{3,2,1,0:T(8,128)(2,1)S(1)}, bf16[14,3,32,256]{3,2,1,0:T(8,128)(2,1)S(1)}, u32[]{:S(2)}, u32[]{:S(2)}) %collective-permute-start.1) | collective-permute-done | bytes 688160 | tf_op jit(solution)/shard_map/ppermute | solution.py:50
  91.5 2.7 broadcast_in_dim.21
  94.1 4.3 %all-to-all-start.1 = ((bf16[32,128,256]{2,1,0:T(8,128)(2,1)}), bf16[32,128,256]{2,1,0:T(8,128)(2,1)S(1)}, u32[]{:S(2)}, u32[]{:S(2)}) async-start(bf16[32,128,256]{2,1,0:T(8,128)(2,1)} %bitcast.23), calls=%async_computation.1 | async-start | bytes 4194304 | tf_op jit(solution)/shard_map/all_to_all | solution.py:41
  98.4 1.0 slice_bitcast_fusion.3
  99.4 4.7 %collective-permute-start.3 = (bf16[14,32,256]{2,1,0:T(8,128)(2,1)S(1)}, bf16[14,32,256]{2,1,0:T(8,128)(2,1)S(1)}, u32[]{:S(2)}, u32[]{:S(2)}) collective-permute-start(bf16[14,32,256]{2,1,0:T(8,128)(2,1)S(1)} %slice_bitcast_fusion.2), channel_id=1, source_target_pairs={{0,3},{1,0},{2,1},{3,2},{4,7},{5,4},{6,5},{7,6},{8,11},{9,8},{10,9... | collective-permute-start | bytes 688136 | tf_op jit(solution)/shard_map/ppermute | solution.py:50
  104.1 1.9 collective-permute-start.2
  106.0 2.3 collective-permute-done.3.far_values.refs_3_
  108.3 5.5 %collective-permute-done.2.far_keys.refs_2_ = bf16[14,32,256]{2,1,0:T(8,128)(2,1)S(1)} collective-permute-done((bf16[14,32,256]{2,1,0:T(8,128)(2,1)S(1)}, bf16[14,32,256]{2,1,0:T(8,128)(2,1)S(1)}, u32[]{:S(2)}, u32[]{:S(2)}) %collective-permute-start.2) | collective-permute-done | bytes 229408 | tf_op jit(solution)/shard_map/ppermute | solution.py:50
  113.8 0.7 copy-done.6
  114.5 8.8 %all-to-all-done.1 = bf16[32,128,256]{2,1,0:T(8,128)(2,1)S(1)} async-done(((bf16[32,128,256]{2,1,0:T(8,128)(2,1)}), bf16[32,128,256]{2,1,0:T(8,128)(2,1)S(1)}, u32[]{:S(2)}, u32[]{:S(2)}) %all-to-all-start.1) | async-done | bytes 2097184 | tf_op jit(solution)/shard_map/all_to_all | solution.py:41
  123.3 4.3 %collective-permute-start.4 = (bf16[8,448,256]{2,1,0:T(8,128)(2,1)}, bf16[8,448,256]{2,1,0:T(8,128)(2,1)}, u32[]{:S(2)}, u32[]{:S(2)}) collective-permute-start(bf16[8,448,256]{2,1,0:T(8,128)(2,1)} %bitcast.17), channel_id=1, source_target_pairs={{0,128},{128,0},{1,129},{129,1},{2,130},{130,2},{3,131},{131,3},{4... | collective-permute-start | bytes 5505032 | tf_op jit(solution)/shard_map/ppermute | solution.py:50
  127.6 0.8 copy.21
  128.4 1.0 reshape.47
  129.4 0.1 and_select_fusion.source
  129.5 1.8 collective-permute-done.4.other
  131.3 1.5 copy-done.1
  132.8 3.6 shard_map.94
  136.4 7.5 %all-to-all-start.2 = ((bf16[32,64,256]{2,1,0:T(8,128)(2,1)}), bf16[32,64,256]{2,1,0:T(8,128)(2,1)S(1)}, u32[]{:S(2)}, u32[]{:S(2)}) async-start(bf16[32,64,256]{2,1,0:T(8,128)(2,1)} %shard_map.94), calls=%async_computation.2 | async-start | bytes 2097152 | tf_op jit(solution)/shard_map/all_to_all | solution.py:41
  144.0 0.2 select_reduce_fusion.target
  144.2 1.1 copy.23.first.refs_1_
  145.3 25.0 %all-to-all-done.2.arrived.queries = bf16[32,64,256]{2,1,0:T(8,128)(2,1)S(1)} async-done(((bf16[32,64,256]{2,1,0:T(8,128)(2,1)}), bf16[32,64,256]{2,1,0:T(8,128)(2,1)S(1)}, u32[]{:S(2)}, u32[]{:S(2)}) %all-to-all-start.2) | async-done | bytes 1048608 | tf_op jit(solution)/shard_map/all_to_all | solution.py:41
  170.3 1.7 shard_map.95
  172.0 0.0 copy-start.5
  172.0 0.0 copy-start.11
  172.0 37.2 %all_to_all.45.arrived = bf16[32,16,1152]{2,1,0:T(8,128)(2,1)S(1)} all-to-all(bf16[32,16,1152]{2,1,0:T(8,128)(2,1)S(1)} %get-tuple-element.43), channel_id=1, replica_groups=mesh['yl'=2,'co'=2,'dz'=8,'dx'=4,'mp'=4] {'dz','dx'}, dimensions={0} | all-to-all | bytes 2359296 | tf_op jit(solution)/shard_map/all_to_all | solution.py:41
  209.2 1.6 shard_map.96
  210.8 16.6 %all_to_all.46.moved = f32[16,8,128]{2,1,0:T(8,128)S(1)} all-to-all(f32[16,8,128]{2,1,0:T(8,128)S(1)} %broadcast_in_dim.36), channel_id=1, replica_groups=mesh['yl'=2,'co'=2,'dz'=8,'dx'=4,'mp'=4] {'yl','co','mp'}, dimensions={0} | all-to-all | bytes 131072 | tf_op jit(solution)/shard_map/all_to_all | solution.py:41
  227.4 2.5 shard_map.97
  229.8 35.2 %all_to_all.47.arrived = bf16[32,16,1152]{2,1,0:T(8,128)(2,1)S(1)} all-to-all(bf16[32,16,1152]{2,1,0:T(8,128)(2,1)S(1)} %get-tuple-element.48), channel_id=1, replica_groups=mesh['yl'=2,'co'=2,'dz'=8,'dx'=4,'mp'=4] {'dz','dx'}, dimensions={0} | all-to-all | bytes 2359296 | tf_op jit(solution)/shard_map/all_to_all | solution.py:41
  265.0 3.1 shard_map.98
  268.1 1.0 copy-done.4
  269.1 0.9 copy-done.8
  269.9 0.8 copy-done.9
  270.7 0.9 copy-done.12
  271.6 4.1 %all-to-all-start.6 = ((bf16[32,64,256]{2,1,0:T(8,128)(2,1)}), bf16[32,64,256]{2,1,0:T(8,128)(2,1)S(1)}, u32[]{:S(2)}, u32[]{:S(2)}) async-start(bf16[32,64,256]{2,1,0:T(8,128)(2,1)} %copy-done.4), calls=%async_computation.6 | async-start | bytes 2097152 | tf_op jit(solution)/shard_map/all_to_all | solution.py:41
  275.7 1.1 copy.25
  276.8 1.9 collective-permute-start.5
  278.7 4.3 %collective-permute-start.6 = (bf16[14,3,32,256]{3,2,1,0:T(8,128)(2,1)}, bf16[14,3,32,256]{3,2,1,0:T(8,128)(2,1)}, u32[]{:S(2)}, u32[]{:S(2)}) collective-permute-start(bf16[14,3,32,256]{3,2,1,0:T(8,128)(2,1)} %copy-done.12), channel_id=1, source_target_pairs={{0,1},{1,2},{2,3},{3,0},{4,5},{5,6},{6,7},{7,4},{8,9},{9,10},{10,1... | collective-permute-start | bytes 2064392 | tf_op jit(solution)/shard_map/ppermute | solution.py:50
  283.0 28.8 %collective-permute-done.5 = bf16[14,3,32,256]{3,2,0,1:T(8,128)(2,1)S(1)} collective-permute-done((bf16[14,3,32,256]{3,2,0,1:T(8,128)(2,1)S(1)}, bf16[14,3,32,256]{3,2,0,1:T(8,128)(2,1)S(1)}, u32[]{:S(2)}, u32[]{:S(2)}) %collective-permute-start.5) | collective-permute-done | bytes 688160 | tf_op jit(solution)/shard_map/ppermute | solution.py:50
  311.8 0.9 copy-done.14
  312.7 3.3 shard_map.99
  315.9 1.4 copy-done.3
  317.3 3.9 %all-to-all-start.7 = ((bf16[32,128,256]{2,1,0:T(8,128)(2,1)}), bf16[32,128,256]{2,1,0:T(8,128)(2,1)S(1)}, u32[]{:S(2)}, u32[]{:S(2)}) async-start(bf16[32,128,256]{2,1,0:T(8,128)(2,1)} %bitcast.20), calls=%async_computation.7 | async-start | bytes 4194304 | tf_op jit(solution)/shard_map/all_to_all | solution.py:41
  321.2 1.0 slice_bitcast_fusion.1
  322.1 1.0 slice_bitcast_fusion
  323.1 2.4 collective-permute-start.8
  325.5 5.0 %collective-permute-start.7 = (bf16[14,32,256]{2,1,0:T(8,128)(2,1)S(1)}, bf16[14,32,256]{2,1,0:T(8,128)(2,1)S(1)}, u32[]{:S(2)}, u32[]{:S(2)}) collective-permute-start(bf16[14,32,256]{2,1,0:T(8,128)(2,1)S(1)} %slice_bitcast_fusion.1), channel_id=1, source_target_pairs={{0,3},{1,0},{2,1},{3,2},{4,7},{5,4},{6,5},{7,6},{8,11},{9,8},{10,9... | collective-permute-start | bytes 688136 | tf_op jit(solution)/shard_map/ppermute | solution.py:50
  330.5 8.0 %collective-permute-done.8.far_values = bf16[14,32,256]{2,1,0:T(8,128)(2,1)S(1)} collective-permute-done((bf16[14,32,256]{2,1,0:T(8,128)(2,1)S(1)}, bf16[14,32,256]{2,1,0:T(8,128)(2,1)S(1)}, u32[]{:S(2)}, u32[]{:S(2)}) %collective-permute-start.8) | collective-permute-done | bytes 229408 | tf_op jit(solution)/shard_map/ppermute | solution.py:50
  338.5 8.3 %all-to-all-done.7 = bf16[32,128,256]{2,1,0:T(8,128)(2,1)S(1)} async-done(((bf16[32,128,256]{2,1,0:T(8,128)(2,1)}), bf16[32,128,256]{2,1,0:T(8,128)(2,1)S(1)}, u32[]{:S(2)}, u32[]{:S(2)}) %all-to-all-start.7) | async-done | bytes 2097184 | tf_op jit(solution)/shard_map/all_to_all | solution.py:41
  346.7 1.3 reduce_sum.34
  348.0 6.6 %all-to-all-start.8 = ((bf16[8,128,256]{2,1,0:T(8,128)(2,1)}), bf16[8,128,256]{2,1,0:T(8,128)(2,1)S(1)}, u32[]{:S(2)}, u32[]{:S(2)}) async-start(bf16[8,128,256]{2,1,0:T(8,128)(2,1)} %reduce_sum.34), calls=%async_computation.8 | async-start | bytes 1048576 | tf_op jit(solution)/shard_map/all_to_all | solution.py:41
  354.6 1.1 copy.26.first
  355.8 3.4 shard_map.100
  359.2 11.2 %all-to-all-done.8 = bf16[8,128,256]{2,1,0:T(8,128)(2,1)S(1)} async-done(((bf16[8,128,256]{2,1,0:T(8,128)(2,1)}), bf16[8,128,256]{2,1,0:T(8,128)(2,1)S(1)}, u32[]{:S(2)}, u32[]{:S(2)}) %all-to-all-start.8) | async-done | bytes 524320 | tf_op jit(solution)/shard_map/all_to_all | solution.py:41
  370.4 0.7 reduce_sum.35
  (32 shorter events, 0.1 us)
Async XLA Ops:
  7.2 13.4 %copy-start = (bf16[14,2,32,1024]{3,2,1,0:T(8,128)(2,1)S(1)}, bf16[14,2,32,1024]{3,2,1,0:T(8,128)(2,1)}, u32[]{:S(2)}) copy-start(bf16[14,2,32,1024]{3,2,1,0:T(8,128)(2,1)} %block3.1) | copy-start | bytes 5505028
  7.2 116.1 %all-gather.3.cloned.1.call-start = ((), (), s32[]{:S(2)}) async-start(), calls=%async_computation.9 | async-start | bytes 2064384 | tf_op jit(solution)/shard_map/all_gather | solution.py:360
  9.6 81.9 %all-to-all-start = ((bf16[8,128,256]{2,1,0:T(8,128)(2,1)}), bf16[8,128,256]{2,1,0:T(8,128)(2,1)}, u32[]{:S(2)}, u32[]{:S(2)}) async-start(bf16[8,128,256]{2,1,0:T(8,128)(2,1)} %broadcast_in_dim.20), calls=%async_computation | async-start | bytes 1048576 | tf_op jit(solution)/shard_map/all_to_all | solution.py:41
  21.4 51.2 %collective-permute-start = (bf16[14,3,32,256]{3,2,0,1:T(8,128)(2,1)S(1)}, bf16[14,3,32,256]{3,2,0,1:T(8,128)(2,1)S(1)}, u32[]{:S(2)}, u32[]{:S(2)}) collective-permute-start(bf16[14,3,32,256]{3,2,0,1:T(8,128)(2,1)S(1)} %copy.22), channel_id=1, source_target_pairs={{0,1},{1,2},{2,3},{3,0},{4,5},{5,6},{6,7},{7,4},{8,9},{9,10},{10,1... | collective-permute-start | bytes 2064392 | tf_op jit(solution)/shard_map/ppermute | solution.py:50
  25.6 65.9 %collective-permute-start.1 = (bf16[14,3,32,256]{3,2,1,0:T(8,128)(2,1)S(1)}, bf16[14,3,32,256]{3,2,1,0:T(8,128)(2,1)S(1)}, u32[]{:S(2)}, u32[]{:S(2)}) collective-permute-start(bf16[14,3,32,256]{3,2,1,0:T(8,128)(2,1)S(1)} %get-tuple-element.34), channel_id=1, source_target_pairs={{0,3},{1,0},{2,1},{3,2},{4,7},{5,4},{6,5},{7,6},{8,11},{9,8},{10,9... | collective-permute-start | bytes 2064392 | tf_op jit(solution)/shard_map/ppermute | solution.py:50
  72.6 21.5 %copy-start.13 = (bf16[14,3,32,256]{3,2,0,1:T(8,128)(2,1)}, bf16[14,3,32,256]{3,2,0,1:T(8,128)(2,1)S(1)}, u32[]{:S(2)}) copy-start(bf16[14,3,32,256]{3,2,0,1:T(8,128)(2,1)S(1)} %collective-permute-done) | copy-start | bytes 2064388
  94.1 33.5 %copy-start.15 = (s32[224,2]{0,1:T(2,128)S(1)}, s32[224,2]{0,1:T(2,128)}, u32[]{:S(2)}) copy-start(s32[224,2]{0,1:T(2,128)} %param.9) | copy-start | bytes 5380
  94.1 29.2 %all-to-all-start.1 = ((bf16[32,128,256]{2,1,0:T(8,128)(2,1)}), bf16[32,128,256]{2,1,0:T(8,128)(2,1)S(1)}, u32[]{:S(2)}, u32[]{:S(2)}) async-start(bf16[32,128,256]{2,1,0:T(8,128)(2,1)} %bitcast.23), calls=%async_computation.1 | async-start | bytes 4194304 | tf_op jit(solution)/shard_map/all_to_all | solution.py:41
  99.4 8.9 %collective-permute-start.3 = (bf16[14,32,256]{2,1,0:T(8,128)(2,1)S(1)}, bf16[14,32,256]{2,1,0:T(8,128)(2,1)S(1)}, u32[]{:S(2)}, u32[]{:S(2)}) collective-permute-start(bf16[14,32,256]{2,1,0:T(8,128)(2,1)S(1)} %slice_bitcast_fusion.2), channel_id=1, source_target_pairs={{0,3},{1,0},{2,1},{3,2},{4,7},{5,4},{6,5},{7,6},{8,11},{9,8},{10,9... | collective-permute-start | bytes 688136 | tf_op jit(solution)/shard_map/ppermute | solution.py:50
  104.1 9.7 %collective-permute-start.2 = (bf16[14,32,256]{2,1,0:T(8,128)(2,1)S(1)}, bf16[14,32,256]{2,1,0:T(8,128)(2,1)S(1)}, u32[]{:S(2)}, u32[]{:S(2)}) collective-permute-start(bf16[14,32,256]{2,1,0:T(8,128)(2,1)S(1)} %slice_bitcast_fusion.3), channel_id=1, source_target_pairs={{0,1},{1,2},{2,3},{3,0},{4,5},{5,6},{6,7},{7,4},{8,9},{9,10},{10,1... | collective-permute-start | bytes 688136 | tf_op jit(solution)/shard_map/ppermute | solution.py:50
  113.8 0.7 copy-start.6
  123.3 8.0 %collective-permute-start.4 = (bf16[8,448,256]{2,1,0:T(8,128)(2,1)}, bf16[8,448,256]{2,1,0:T(8,128)(2,1)}, u32[]{:S(2)}, u32[]{:S(2)}) collective-permute-start(bf16[8,448,256]{2,1,0:T(8,128)(2,1)} %bitcast.17), channel_id=1, source_target_pairs={{0,128},{128,0},{1,129},{129,1},{2,130},{130,2},{3,131},{131,3},{4... | collective-permute-start | bytes 5505032 | tf_op jit(solution)/shard_map/ppermute | solution.py:50
  131.3 1.5 copy-start.1
  136.4 33.9 %copy-start.7 = (bf16[14,32,256]{2,1,0:T(8,128)(2,1)S(1)}, bf16[14,32,256]{2,1,0:T(8,128)(2,1)}, u32[]{:S(2)}) copy-start(bf16[14,32,256]{2,1,0:T(8,128)(2,1)} %copy-done.6) | copy-start | bytes 688132
  136.4 33.9 %all-to-all-start.2 = ((bf16[32,64,256]{2,1,0:T(8,128)(2,1)}), bf16[32,64,256]{2,1,0:T(8,128)(2,1)S(1)}, u32[]{:S(2)}, u32[]{:S(2)}) async-start(bf16[32,64,256]{2,1,0:T(8,128)(2,1)} %shard_map.94), calls=%async_computation.2 | async-start | bytes 2097152 | tf_op jit(solution)/shard_map/all_to_all | solution.py:41
  172.0 37.2 %copy-start.5 = (bf16[448,256]{1,0:T(8,128)(2,1)S(1)}, bf16[448,256]{1,0:T(8,128)(2,1)}, u32[]{:S(2)}) copy-start(bf16[448,256]{1,0:T(8,128)(2,1)} %d_mixed.3) | copy-start | bytes 688132
  172.0 37.2 %copy-start.11 = (f32[256]{0:T(256)S(1)}, f32[256]{0:T(256)}, u32[]{:S(2)}) copy-start(f32[256]{0:T(256)} %param.10) | copy-start | bytes 3076
  268.1 1.0 copy-start.4
  269.1 0.9 copy-start.8
  269.9 0.8 copy-start.9
  270.7 0.9 copy-start.12
  271.6 41.1 %copy-start.2 = (bf16[3584,256]{1,0:T(8,128)(2,1)S(1)}, bf16[3584,256]{1,0:T(8,128)(2,1)}, u32[]{:S(2)}) copy-start(bf16[3584,256]{1,0:T(8,128)(2,1)} %all-gather.3.cloned.1.call-done) | copy-start | bytes 5505028
  271.6 41.1 %all-to-all-start.6 = ((bf16[32,64,256]{2,1,0:T(8,128)(2,1)}), bf16[32,64,256]{2,1,0:T(8,128)(2,1)S(1)}, u32[]{:S(2)}, u32[]{:S(2)}) async-start(bf16[32,64,256]{2,1,0:T(8,128)(2,1)} %copy-done.4), calls=%async_computation.6 | async-start | bytes 2097152 | tf_op jit(solution)/shard_map/all_to_all | solution.py:41
  276.8 35.0 %collective-permute-start.5 = (bf16[14,3,32,256]{3,2,0,1:T(8,128)(2,1)S(1)}, bf16[14,3,32,256]{3,2,0,1:T(8,128)(2,1)S(1)}, u32[]{:S(2)}, u32[]{:S(2)}) collective-permute-start(bf16[14,3,32,256]{3,2,0,1:T(8,128)(2,1)S(1)} %copy.25), channel_id=1, source_target_pairs={{0,3},{1,0},{2,1},{3,2},{4,7},{5,4},{6,5},{7,6},{8,11},{9,8},{10,9... | collective-permute-start | bytes 2064392 | tf_op jit(solution)/shard_map/ppermute | solution.py:50
  278.7 33.9 %collective-permute-start.6 = (bf16[14,3,32,256]{3,2,1,0:T(8,128)(2,1)}, bf16[14,3,32,256]{3,2,1,0:T(8,128)(2,1)}, u32[]{:S(2)}, u32[]{:S(2)}) collective-permute-start(bf16[14,3,32,256]{3,2,1,0:T(8,128)(2,1)} %copy-done.12), channel_id=1, source_target_pairs={{0,1},{1,2},{2,3},{3,0},{4,5},{5,6},{6,7},{7,4},{8,9},{9,10},{10,1... | collective-permute-start | bytes 2064392 | tf_op jit(solution)/shard_map/ppermute | solution.py:50
  311.8 0.9 copy-start.14
  315.9 1.4 copy-start.3
  317.3 29.4 %all-to-all-start.7 = ((bf16[32,128,256]{2,1,0:T(8,128)(2,1)}), bf16[32,128,256]{2,1,0:T(8,128)(2,1)S(1)}, u32[]{:S(2)}, u32[]{:S(2)}) async-start(bf16[32,128,256]{2,1,0:T(8,128)(2,1)} %bitcast.20), calls=%async_computation.7 | async-start | bytes 4194304 | tf_op jit(solution)/shard_map/all_to_all | solution.py:41
  323.1 15.4 %collective-permute-start.8 = (bf16[14,32,256]{2,1,0:T(8,128)(2,1)S(1)}, bf16[14,32,256]{2,1,0:T(8,128)(2,1)S(1)}, u32[]{:S(2)}, u32[]{:S(2)}) collective-permute-start(bf16[14,32,256]{2,1,0:T(8,128)(2,1)S(1)} %slice_bitcast_fusion), channel_id=1, source_target_pairs={{0,1},{1,2},{2,3},{3,0},{4,5},{5,6},{6,7},{7,4},{8,9},{9,10},{10,1... | collective-permute-start | bytes 688136 | tf_op jit(solution)/shard_map/ppermute | solution.py:50
  325.5 13.0 %collective-permute-start.7 = (bf16[14,32,256]{2,1,0:T(8,128)(2,1)S(1)}, bf16[14,32,256]{2,1,0:T(8,128)(2,1)S(1)}, u32[]{:S(2)}, u32[]{:S(2)}) collective-permute-start(bf16[14,32,256]{2,1,0:T(8,128)(2,1)S(1)} %slice_bitcast_fusion.1), channel_id=1, source_target_pairs={{0,3},{1,0},{2,1},{3,2},{4,7},{5,4},{6,5},{7,6},{8,11},{9,8},{10,9... | collective-permute-start | bytes 688136 | tf_op jit(solution)/shard_map/ppermute | solution.py:50
  348.0 7.8 %copy-start.10 = (bf16[14,2,32,256]{3,2,1,0:T(8,128)(2,1)S(1)}, bf16[14,2,32,256]{3,2,1,0:T(8,128)(2,1)}, u32[]{:S(2)}) copy-start(bf16[14,2,32,256]{3,2,1,0:T(8,128)(2,1)} %copy-done.9) | copy-start | bytes 1376260
  348.0 22.4 %all-to-all-start.8 = ((bf16[8,128,256]{2,1,0:T(8,128)(2,1)}), bf16[8,128,256]{2,1,0:T(8,128)(2,1)S(1)}, u32[]{:S(2)}, u32[]{:S(2)}) async-start(bf16[8,128,256]{2,1,0:T(8,128)(2,1)} %reduce_sum.34), calls=%async_computation.8 | async-start | bytes 1048576 | tf_op jit(solution)/shard_map/all_to_all | solution.py:41
Sparse Core Ops, SparseCore 0:
  10.1 86.4 all-gather.2

commit v4 on v3

--- a/solution.py
+++ b/solution.py
@@ -16,12 +16,12 @@
 SCALE = HEAD_DIM ** (-0.5)
 DP = ("dz", "dx")
 GRP = ("yl", "co")
-LINE = ("yl", "mp")
+LINE = ("mp", "yl")
 BF = jnp.bfloat16
 F32 = jnp.float32
 SMEM = pl.BlockSpec(memory_space=pltpu.SMEM)
 VMEM = pl.BlockSpec(memory_space=pltpu.VMEM)
-PARAMS = pltpu.CompilerParams(vmem_limit_bytes=40 << 20)
+PARAMS = pltpu.CompilerParams(vmem_limit_bytes=24 << 20)
 LAST = (((1,), (1,)), ((), ()))
 FIRST = (((0,), (0,)), ((), ()))
 PLAIN = (((1,), (0,)), ((), ()))
@@ -125,18 +125,18 @@
     ]
 
 
-def weight_rows(line, co, n_co, n_mp):
-    return (line // n_mp * n_co + co) * n_mp + line % n_mp
+def weight_rows(line, co, n_yl, n_co, n_mp):
+    return (line % n_yl * n_co + co) * n_mp + line // n_yl
 
 
 def query_kernel(sizes, place, source, mine, other, weight, slots, total):
-    n_co, n_mp, n_x = sizes
+    n_yl, n_co, n_mp, n_x = sizes
     rows = weight.shape[2]
     per = mine.shape[2] // rows
     for part, block in enumerate((mine, other)):
         co = lax.rem(place[1] + part, n_co)
         for line in range(mine.shape[0]):
-            first = weight_rows(line, co, n_co, n_mp) * per
+            first = weight_rows(line, co, n_yl, n_co, n_mp) * per
             w = jnp.concatenate(
                 [weight[lax.rem(first + i, n_x), lax.div(first + i, n_x)] for i in range(per)], axis=0
             )
@@ -252,7 +252,7 @@
 
 
 def weight_kernel(sizes, place, source, arrived, mine, other, grad_q, partial):
-    n_co, n_mp, n_x = sizes
+    n_yl, n_co, n_mp, n_x = sizes
     for c in range(source.shape[0] // NEIGHBOURS):
         both = sum(arrived[source[NEIGHBOURS * c + k]].astype(F32) for k in range(NEIGHBOURS))
         grad_q[c * GROUP_LEN : (c + 1) * GROUP_LEN, :] = both.astype(BF)
@@ -261,7 +261,7 @@
     for part, block in enumerate((mine, other)):
         co = lax.rem(place[1] + part, n_co)
         for line in range(mine.shape[0]):
-            first = weight_rows(line, co, n_co, n_mp) * per
+            first = weight_rows(line, co, n_yl, n_co, n_mp) * per
             product = dot(block[line], grad_q[...], FIRST).astype(BF)
             for i in range(per):
                 partial[lax.rem(first + i, n_x), lax.div(first + i, n_x)] = product[
@@ -343,7 +343,7 @@
     n_dp = n_z * n_x
     heads = GRP + ("mp",)
     n_heads = lax.axis_size(heads)
-    sizes = (n_co, n_mp, n_x)
+    sizes = (lax.axis_size("yl"), n_co, n_mp, n_x)
     me_dp = lax.axis_index(DP)
     neigh_dev = kv_enc.shape[0]
     tok_dev, dec_width = hidden.shape[0], wq.shape[1]
@@ -359,15 +359,13 @@
 
     line = lax.all_gather(hidden, LINE, axis=0)
     own, up, down = split_by_quarter(place, kv_enc)
+    near = exchange(copies(wq, n_z), "dz").reshape(n_z, -1, dec_width)
+    near, up, down = lax.optimization_barrier((near, up, down))
     first, last = shift(up, "mp", 1), shift(down, "mp", -1)
-    near = exchange(copies(wq, n_z), "dz").reshape(n_z, -1, dec_width)
-    near, first, last = lax.optimization_barrier((near, first, last))
-    far_keys, far_values = shift(first[:, 2], "mp", 1), shift(last[:, 2], "mp", -1)
     weight = exchange(copies(near, n_x).reshape(n_x * n_z, -1, dec_width), "dx")
     weight = weight.reshape(n_x, n_z, -1, dec_width)
-    line, weight, far_keys, far_values = lax.optimization_barrier(
-        (line, weight, far_keys, far_values)
-    )
+    line, weight, first, last = lax.optimization_barrier((line, weight, first, last))
+    far_keys, far_values = shift(first[:, 2], "mp", 1), shift(last[:, 2], "mp", -1)
     other = shift(line, "co", 1)
     kv = (own, first, far_keys, far_values, last)
 
@@ -412,14 +410,14 @@
     )
     first, last = shift(down, "mp", -1), shift(up, "mp", 1)
     arrived = exchange(slots, DP)
-    arrived, first, last = lax.optimization_barrier((arrived, first, last))
-    far_keys, far_values = shift(first[:, 2], "mp", -1), shift(last[:, 2], "mp", 1)
     grad_q, partial = call(
         functools.partial(weight_kernel, sizes),
         (place, source),
         (arrived, line, other),
         [((tok_dev, dec_width), BF), (weight.shape, BF)],
     )
+    partial, first, last = lax.optimization_barrier((partial, first, last))
+    far_keys, far_values = shift(first[:, 2], "mp", -1), shift(last[:, 2], "mp", 1)
     column = exchange(partial.reshape(n_x * n_z, -1, dec_width), "dx").reshape(weight.shape)
     column, far_keys, far_values = lax.optimization_barrier((column, far_keys, far_values))
     grad_kv = merge_quarters(place, (own, first, far_keys, far_values, last))

time: 382 us -> 338 us (0.88)
  waiting for transfers between devices: 162 us -> 121 us
    ppermute x9, waiting for transfers between devices: 109 us -> 61.7 us  [shift(): lax.ppermute(array, axis, [(i, (i + step) % size) for i in range(size)])]
    all_to_all x6, waiting for transfers between devices: 53.2 us -> 58.3 us  [exchange(): return lax.all_to_all(array, axes, split_axis=0, concat_axis=0, tiled=True)]
  transfers between devices with their start and end apart: 16 -> 16, of which waited for: 11 -> 12; matrix products, arithmetic and copies ran while one was open for 3% -> 4% of each run, Pallas kernels for 1% -> 2%
where the time goes in v4:
time: 338 us; the launch traced here: 332 us
  waiting for transfers between devices  121 us (36%)
  blocking collectives  87.8 us (26%)
  starting transfers between devices  67.4 us (20%)
  local copies, waits for them, and re-layouts  19.9 us (6%)
  Pallas kernels  19.8 us (6%)
  between operations  14.3 us (4%)
    all_to_all x3, blocking collectives, exchange(): return lax.all_to_all(array, axes, split_axis=0, concat_axis=0, tiled=True)  87.8 us
    ppermute x9, waiting for transfers between devices, shift(): lax.ppermute(array, axis, [(i, (i + step) % size) for i in range(size)])  61.7 us
    all_to_all x6, waiting for transfers between devices, exchange(): return lax.all_to_all(array, axes, split_axis=0, concat_axis=0, tiled=True)  58.3 us
    all_to_all x6, starting transfers between devices, exchange(): return lax.all_to_all(array, axes, split_axis=0, concat_axis=0, tiled=True)  36.6 us
    ppermute x9, starting transfers between devices, shift(): lax.ppermute(array, axis, [(i, (i + step) % size) for i in range(size)])  30.7 us
    pallas_call x5, Pallas kernels, call(): pl.pallas_call(kernel, in_specs=[SMEM] * len(scalars) + [VMEM] * len(arra...  12 us
    unnamed x33, local copies, waits for them, and re-layouts  8.2 us
  transfers between devices with their start and end apart: 16, of which 12 were waited for; matrix products, arithmetic and copies ran while one was open for 4% of the time, Pallas kernels for 2%

profile of v4, /device:TPU:1, one launch (start us, length us, event | category | flops | bytes accessed | tf_op | source)
XLA Modules:
  0.0 332.2 jit_solution(11821047066907210221)
XLA Ops:
  7.2 0.0 all-gather.3.cloned.1.call-start
  7.2 0.7 all-gather.3.cloned.1.call-update
  7.9 1.7 broadcast_in_dim.20
  9.6 10.9 %all-to-all-start = ((bf16[8,128,256]{2,1,0:T(8,128)(2,1)}), bf16[8,128,256]{2,1,0:T(8,128)(2,1)}, u32[]{:S(2)}, u32[]{:S(2)}) async-start(bf16[8,128,256]{2,1,0:T(8,128)(2,1)} %broadcast_in_dim.20), calls=%async_computation | async-start | bytes 1048576 | tf_op jit(solution)/shard_map/all_to_all | solution.py:41
  20.4 0.1 pad_add_fusion.place
  20.5 0.8 shard_map.93
  21.3 0.8 copy-done.7
  22.2 16.3 %all-to-all-done = bf16[8,128,256]{2,1,0:T(8,128)(2,1)} async-done(((bf16[8,128,256]{2,1,0:T(8,128)(2,1)}), bf16[8,128,256]{2,1,0:T(8,128)(2,1)}, u32[]{:S(2)}, u32[]{:S(2)}) %all-to-all-start) | async-done | bytes 524320 | tf_op jit(solution)/shard_map/all_to_all | solution.py:41
  38.5 2.7 broadcast_in_dim.21
  41.2 4.1 %all-to-all-start.1 = ((bf16[32,128,256]{2,1,0:T(8,128)(2,1)}), bf16[32,128,256]{2,1,0:T(8,128)(2,1)S(1)}, u32[]{:S(2)}, u32[]{:S(2)}) async-start(bf16[32,128,256]{2,1,0:T(8,128)(2,1)} %bitcast.23), calls=%async_computation.1 | async-start | bytes 4194304 | tf_op jit(solution)/shard_map/all_to_all | solution.py:41
  45.4 4.2 %collective-permute-start = (bf16[14,3,32,256]{3,2,0,1:T(8,128)(2,1)S(1)}, bf16[14,3,32,256]{3,2,0,1:T(8,128)(2,1)S(1)}, u32[]{:S(2)}, u32[]{:S(2)}) collective-permute-start(bf16[14,3,32,256]{3,2,0,1:T(8,128)(2,1)S(1)} %copy.22), channel_id=1, source_target_pairs={{0,1},{1,2},{2,3},{3,0},{4,5},{5,6},{6,7},{7,4},{8,9},{9,10},{10,1... | collective-permute-start | bytes 2064392 | tf_op jit(solution)/shard_map/ppermute | solution.py:50
  49.6 3.6 %collective-permute-start.1 = (bf16[14,3,32,256]{3,2,1,0:T(8,128)(2,1)}, bf16[14,3,32,256]{3,2,1,0:T(8,128)(2,1)S(1)}, u32[]{:S(2)}, u32[]{:S(2)}) collective-permute-start(bf16[14,3,32,256]{3,2,1,0:T(8,128)(2,1)} %copy-done.13), channel_id=1, source_target_pairs={{0,3},{1,0},{2,1},{3,2},{4,7},{5,4},{6,5},{7,6},{8,11},{9,8},{10,9... | collective-permute-start | bytes 2064392 | tf_op jit(solution)/shard_map/ppermute | solution.py:50
  53.2 24.8 %collective-permute-done = bf16[14,3,32,256]{3,2,0,1:T(8,128)(2,1)S(1)} collective-permute-done((bf16[14,3,32,256]{3,2,0,1:T(8,128)(2,1)S(1)}, bf16[14,3,32,256]{3,2,0,1:T(8,128)(2,1)S(1)}, u32[]{:S(2)}, u32[]{:S(2)}) %collective-permute-start) | collective-permute-done | bytes 688160 | tf_op jit(solution)/shard_map/ppermute | solution.py:50
  78.0 0.9 copy-done.14
  78.8 7.6 %collective-permute-done.1.last.refs_4_ = bf16[14,3,32,256]{3,2,1,0:T(8,128)(2,1)S(1)} collective-permute-done((bf16[14,3,32,256]{3,2,1,0:T(8,128)(2,1)}, bf16[14,3,32,256]{3,2,1,0:T(8,128)(2,1)S(1)}, u32[]{:S(2)}, u32[]{:S(2)}) %collective-permute-start.1) | collective-permute-done | bytes 688160 | tf_op jit(solution)/shard_map/ppermute | solution.py:50
  86.5 2.7 collective-permute-start.2
  89.2 0.1 copy.21
  89.3 0.1 reshape.47
  89.5 0.1 and_select_fusion.source
  89.6 3.3 %collective-permute-done.2.other = bf16[8,448,256]{2,1,0:T(8,128)(2,1)} collective-permute-done((bf16[8,448,256]{2,1,0:T(8,128)(2,1)}, bf16[8,448,256]{2,1,0:T(8,128)(2,1)}, u32[]{:S(2)}, u32[]{:S(2)}) %collective-permute-start.2) | collective-permute-done | bytes 1835040 | tf_op jit(solution)/shard_map/ppermute | solution.py:50
  92.9 1.5 copy-done.1
  94.4 3.6 %shard_map.94 = bf16[32,64,256]{2,1,0:T(8,128)(2,1)} custom-call(s32[2]{0:T(128)S(1)} %pad_add_fusion.place, s32[14]{0:T(128)S(1)} %and_select_fusion.source, bf16[8,448,256]{2,1,0:T(8,128)(2,1)S(1)} %bitcast.18, bf16[8,448,256]{2,1,0:T(8,128)(2,1)} %collective-permute-done.2.other, bf16[4,8,128,256]{3,2,1,0:T(8,128)(2,1)S(1)} %bitcast.16), custom_call_target="tpu_custom_call" | custom-call | tf_op jit(solution)/shard_map/pallas_call | solution.py:372
  98.0 7.3 %all-to-all-start.2 = ((bf16[32,64,256]{2,1,0:T(8,128)(2,1)}), bf16[32,64,256]{2,1,0:T(8,128)(2,1)S(1)}, u32[]{:S(2)}, u32[]{:S(2)}) async-start(bf16[32,64,256]{2,1,0:T(8,128)(2,1)} %shard_map.94), calls=%async_computation.2 | async-start | bytes 2097152 | tf_op jit(solution)/shard_map/all_to_all | solution.py:41
  105.4 4.1 %collective-permute-start.4 = (bf16[14,32,256]{2,1,0:T(8,128)(2,1)S(1)}, bf16[14,32,256]{2,1,0:T(8,128)(2,1)S(1)}, u32[]{:S(2)}, u32[]{:S(2)}) collective-permute-start(bf16[14,32,256]{2,1,0:T(8,128)(2,1)S(1)} %slice_bitcast_fusion.2), channel_id=1, source_target_pairs={{0,3},{1,0},{2,1},{3,2},{4,7},{5,4},{6,5},{7,6},{8,11},{9,8},{10,9... | collective-permute-start | bytes 688136 | tf_op jit(solution)/shard_map/ppermute | solution.py:50
  109.5 1.0 slice_bitcast_fusion.3
  110.5 2.5 collective-permute-start.3
  113.1 0.2 select_reduce_fusion.target
  113.3 1.1 copy.23.first.refs_1_
  114.4 6.7 %collective-permute-done.4.far_values.refs_3_ = bf16[14,32,256]{2,1,0:T(8,128)(2,1)S(1)} collective-permute-done((bf16[14,32,256]{2,1,0:T(8,128)(2,1)S(1)}, bf16[14,32,256]{2,1,0:T(8,128)(2,1)S(1)}, u32[]{:S(2)}, u32[]{:S(2)}) %collective-permute-start.4) | collective-permute-done | bytes 229408 | tf_op jit(solution)/shard_map/ppermute | solution.py:50
  121.1 4.6 %collective-permute-done.3.far_keys.refs_2_ = bf16[14,32,256]{2,1,0:T(8,128)(2,1)S(1)} collective-permute-done((bf16[14,32,256]{2,1,0:T(8,128)(2,1)S(1)}, bf16[14,32,256]{2,1,0:T(8,128)(2,1)S(1)}, u32[]{:S(2)}, u32[]{:S(2)}) %collective-permute-start.3) | collective-permute-done | bytes 229408 | tf_op jit(solution)/shard_map/ppermute | solution.py:50
  125.7 6.0 %all-to-all-done.2.arrived.queries = bf16[32,64,256]{2,1,0:T(8,128)(2,1)S(1)} async-done(((bf16[32,64,256]{2,1,0:T(8,128)(2,1)}), bf16[32,64,256]{2,1,0:T(8,128)(2,1)S(1)}, u32[]{:S(2)}, u32[]{:S(2)}) %all-to-all-start.2) | async-done | bytes 1048608 | tf_op jit(solution)/shard_map/all_to_all | solution.py:41
  131.7 1.7 shard_map.95
  133.4 0.0 copy-start.5
  133.4 37.2 %all_to_all.45.arrived = bf16[32,16,1152]{2,1,0:T(8,128)(2,1)S(1)} all-to-all(bf16[32,16,1152]{2,1,0:T(8,128)(2,1)S(1)} %get-tuple-element.43), channel_id=1, replica_groups=mesh['yl'=2,'co'=2,'dz'=8,'dx'=4,'mp'=4] {'dz','dx'}, dimensions={0} | all-to-all | bytes 2359296 | tf_op jit(solution)/shard_map/all_to_all | solution.py:41
  170.6 1.6 shard_map.96
  172.2 15.4 %all_to_all.46.moved = f32[16,8,128]{2,1,0:T(8,128)S(1)} all-to-all(f32[16,8,128]{2,1,0:T(8,128)S(1)} %broadcast_in_dim.36), channel_id=1, replica_groups=mesh['yl'=2,'co'=2,'dz'=8,'dx'=4,'mp'=4] {'yl','co','mp'}, dimensions={0} | all-to-all | bytes 131072 | tf_op jit(solution)/shard_map/all_to_all | solution.py:41
  187.6 2.5 shard_map.97
  190.0 35.2 %all_to_all.47.arrived = bf16[32,16,1152]{2,1,0:T(8,128)(2,1)S(1)} all-to-all(bf16[32,16,1152]{2,1,0:T(8,128)(2,1)S(1)} %get-tuple-element.48), channel_id=1, replica_groups=mesh['yl'=2,'co'=2,'dz'=8,'dx'=4,'mp'=4] {'dz','dx'}, dimensions={0} | all-to-all | bytes 2359296 | tf_op jit(solution)/shard_map/all_to_all | solution.py:41
  225.3 3.1 shard_map.98
  228.3 1.0 copy-done.4
  229.3 0.9 copy-done.6
  230.2 0.8 copy-done.9
  230.9 0.9 copy-done.12
  231.8 4.1 %all-to-all-start.6 = ((bf16[32,64,256]{2,1,0:T(8,128)(2,1)}), bf16[32,64,256]{2,1,0:T(8,128)(2,1)S(1)}, u32[]{:S(2)}, u32[]{:S(2)}) async-start(bf16[32,64,256]{2,1,0:T(8,128)(2,1)} %copy-done.4), calls=%async_computation.6 | async-start | bytes 2097152 | tf_op jit(solution)/shard_map/all_to_all | solution.py:41
  235.9 2.0 copy.25
  237.9 1.9 collective-permute-start.5
  239.8 4.3 %collective-permute-start.6 = (bf16[14,3,32,256]{3,2,1,0:T(8,128)(2,1)}, bf16[14,3,32,256]{3,2,1,0:T(8,128)(2,1)}, u32[]{:S(2)}, u32[]{:S(2)}) collective-permute-start(bf16[14,3,32,256]{3,2,1,0:T(8,128)(2,1)} %copy-done.12), channel_id=1, source_target_pairs={{0,1},{1,2},{2,3},{3,0},{4,5},{5,6},{6,7},{7,4},{8,9},{9,10},{10,1... | collective-permute-start | bytes 2064392 | tf_op jit(solution)/shard_map/ppermute | solution.py:50
  244.1 17.4 %all-to-all-done.6.arrived = bf16[32,64,256]{2,1,0:T(8,128)(2,1)S(1)} async-done(((bf16[32,64,256]{2,1,0:T(8,128)(2,1)}), bf16[32,64,256]{2,1,0:T(8,128)(2,1)S(1)}, u32[]{:S(2)}, u32[]{:S(2)}) %all-to-all-start.6) | async-done | bytes 1048608 | tf_op jit(solution)/shard_map/all_to_all | solution.py:41
  261.5 3.3 shard_map.99
  264.8 1.4 copy-done.3
  266.2 6.9 %collective-permute-done.5 = bf16[14,3,32,256]{3,2,0,1:T(8,128)(2,1)} collective-permute-done((bf16[14,3,32,256]{3,2,0,1:T(8,128)(2,1)}, bf16[14,3,32,256]{3,2,0,1:T(8,128)(2,1)}, u32[]{:S(2)}, u32[]{:S(2)}) %collective-permute-start.5) | collective-permute-done | bytes 688160 | tf_op jit(solution)/shard_map/ppermute | solution.py:50
  273.1 3.9 %all-to-all-start.7 = ((bf16[32,128,256]{2,1,0:T(8,128)(2,1)}), bf16[32,128,256]{2,1,0:T(8,128)(2,1)S(1)}, u32[]{:S(2)}, u32[]{:S(2)}) async-start(bf16[32,128,256]{2,1,0:T(8,128)(2,1)} %bitcast.20), calls=%async_computation.7 | async-start | bytes 4194304 | tf_op jit(solution)/shard_map/all_to_all | solution.py:41
  277.0 1.0 slice_bitcast_fusion.1
  277.9 1.0 slice_bitcast_fusion
  278.9 2.5 collective-permute-start.8
  281.4 4.9 %collective-permute-start.7 = (bf16[14,32,256]{2,1,0:T(8,128)(2,1)S(1)}, bf16[14,32,256]{2,1,0:T(8,128)(2,1)S(1)}, u32[]{:S(2)}, u32[]{:S(2)}) collective-permute-start(bf16[14,32,256]{2,1,0:T(8,128)(2,1)S(1)} %slice_bitcast_fusion.1), channel_id=1, source_target_pairs={{0,3},{1,0},{2,1},{3,2},{4,7},{5,4},{6,5},{7,6},{8,11},{9,8},{10,9... | collective-permute-start | bytes 688136 | tf_op jit(solution)/shard_map/ppermute | solution.py:50
  286.3 7.7 %collective-permute-done.8.far_values = bf16[14,32,256]{2,1,0:T(8,128)(2,1)S(1)} collective-permute-done((bf16[14,32,256]{2,1,0:T(8,128)(2,1)S(1)}, bf16[14,32,256]{2,1,0:T(8,128)(2,1)S(1)}, u32[]{:S(2)}, u32[]{:S(2)}) %collective-permute-start.8) | collective-permute-done | bytes 229408 | tf_op jit(solution)/shard_map/ppermute | solution.py:50
  293.9 8.2 %all-to-all-done.7 = bf16[32,128,256]{2,1,0:T(8,128)(2,1)S(1)} async-done(((bf16[32,128,256]{2,1,0:T(8,128)(2,1)}), bf16[32,128,256]{2,1,0:T(8,128)(2,1)S(1)}, u32[]{:S(2)}, u32[]{:S(2)}) %all-to-all-start.7) | async-done | bytes 2097184 | tf_op jit(solution)/shard_map/all_to_all | solution.py:41
  302.2 1.3 reduce_sum.34
  303.5 6.3 %all-to-all-start.8 = ((bf16[8,128,256]{2,1,0:T(8,128)(2,1)}), bf16[8,128,256]{2,1,0:T(8,128)(2,1)S(1)}, u32[]{:S(2)}, u32[]{:S(2)}) async-start(bf16[8,128,256]{2,1,0:T(8,128)(2,1)} %reduce_sum.34), calls=%async_computation.8 | async-start | bytes 1048576 | tf_op jit(solution)/shard_map/all_to_all | solution.py:41
  309.8 1.1 copy.26.first
  311.0 3.4 %shard_map.100 = bf16[14,2,32,1024]{3,2,1,0:T(8,128)(2,1)} custom-call(s32[2]{0:T(128)S(1)} %pad_add_fusion.place, bf16[14,2,32,256]{3,2,1,0:T(8,128)(2,1)S(1)} %copy-done.10, bf16[14,3,32,256]{3,2,1,0:T(8,128)(2,1)S(1)} %copy.26.first, bf16[14,32,256]{2,1,0:T(8,128)(2,1)S(1)} %collective-permute-done.7.far_keys, ...), custom_call_target="tpu_custom_call" | custom-call | tf_op jit(solution)/shard_map/pallas_call | solution.py:319
  314.4 10.3 %all-to-all-done.8 = bf16[8,128,256]{2,1,0:T(8,128)(2,1)S(1)} async-done(((bf16[8,128,256]{2,1,0:T(8,128)(2,1)}), bf16[8,128,256]{2,1,0:T(8,128)(2,1)S(1)}, u32[]{:S(2)}, u32[]{:S(2)}) %all-to-all-start.8) | async-done | bytes 524320 | tf_op jit(solution)/shard_map/all_to_all | solution.py:41
  324.7 0.7 reduce_sum.35
  (32 shorter events, 0.1 us)
Async XLA Ops:
  7.2 13.4 %copy-start = (bf16[14,2,32,1024]{3,2,1,0:T(8,128)(2,1)S(1)}, bf16[14,2,32,1024]{3,2,1,0:T(8,128)(2,1)}, u32[]{:S(2)}) copy-start(bf16[14,2,32,1024]{3,2,1,0:T(8,128)(2,1)} %block3.1) | copy-start | bytes 5505028
  7.2 79.3 %all-gather.3.cloned.1.call-start = ((), (), s32[]{:S(2)}) async-start(), calls=%async_computation.9 | async-start | bytes 2064384 | tf_op jit(solution)/shard_map/all_gather | solution.py:360
  9.6 28.9 %all-to-all-start = ((bf16[8,128,256]{2,1,0:T(8,128)(2,1)}), bf16[8,128,256]{2,1,0:T(8,128)(2,1)}, u32[]{:S(2)}, u32[]{:S(2)}) async-start(bf16[8,128,256]{2,1,0:T(8,128)(2,1)} %broadcast_in_dim.20), calls=%async_computation | async-start | bytes 1048576 | tf_op jit(solution)/shard_map/all_to_all | solution.py:41
  21.3 0.8 copy-start.7
  22.2 19.0 %copy-start.13 = (bf16[14,3,32,256]{3,2,1,0:T(8,128)(2,1)}, bf16[14,3,32,256]{3,2,1,0:T(8,128)(2,1)S(1)}, u32[]{:S(2)}) copy-start(bf16[14,3,32,256]{3,2,1,0:T(8,128)(2,1)S(1)} %get-tuple-element.37) | copy-start | bytes 2064388
  41.2 4.2 %copy-start.8 = (bf16[14,3,32,256]{3,2,1,0:T(8,128)(2,1)S(1)}, bf16[14,3,32,256]{3,2,1,0:T(8,128)(2,1)}, u32[]{:S(2)}) copy-start(bf16[14,3,32,256]{3,2,1,0:T(8,128)(2,1)} %copy-done.7) | copy-start | bytes 2064388
  41.2 48.0 %copy-start.15 = (s32[224,2]{0,1:T(2,128)S(1)}, s32[224,2]{0,1:T(2,128)}, u32[]{:S(2)}) copy-start(s32[224,2]{0,1:T(2,128)} %param.9) | copy-start | bytes 5380
  41.2 45.3 %all-to-all-start.1 = ((bf16[32,128,256]{2,1,0:T(8,128)(2,1)}), bf16[32,128,256]{2,1,0:T(8,128)(2,1)S(1)}, u32[]{:S(2)}, u32[]{:S(2)}) async-start(bf16[32,128,256]{2,1,0:T(8,128)(2,1)} %bitcast.23), calls=%async_computation.1 | async-start | bytes 4194304 | tf_op jit(solution)/shard_map/all_to_all | solution.py:41
  45.4 32.6 %collective-permute-start = (bf16[14,3,32,256]{3,2,0,1:T(8,128)(2,1)S(1)}, bf16[14,3,32,256]{3,2,0,1:T(8,128)(2,1)S(1)}, u32[]{:S(2)}, u32[]{:S(2)}) collective-permute-start(bf16[14,3,32,256]{3,2,0,1:T(8,128)(2,1)S(1)} %copy.22), channel_id=1, source_target_pairs={{0,1},{1,2},{2,3},{3,0},{4,5},{5,6},{6,7},{7,4},{8,9},{9,10},{10,1... | collective-permute-start | bytes 2064392 | tf_op jit(solution)/shard_map/ppermute | solution.py:50
  49.6 36.9 %collective-permute-start.1 = (bf16[14,3,32,256]{3,2,1,0:T(8,128)(2,1)}, bf16[14,3,32,256]{3,2,1,0:T(8,128)(2,1)S(1)}, u32[]{:S(2)}, u32[]{:S(2)}) collective-permute-start(bf16[14,3,32,256]{3,2,1,0:T(8,128)(2,1)} %copy-done.13), channel_id=1, source_target_pairs={{0,3},{1,0},{2,1},{3,2},{4,7},{5,4},{6,5},{7,6},{8,11},{9,8},{10,9... | collective-permute-start | bytes 2064392 | tf_op jit(solution)/shard_map/ppermute | solution.py:50
  78.0 0.9 copy-start.14
  86.5 6.4 %collective-permute-start.2 = (bf16[8,448,256]{2,1,0:T(8,128)(2,1)}, bf16[8,448,256]{2,1,0:T(8,128)(2,1)}, u32[]{:S(2)}, u32[]{:S(2)}) collective-permute-start(bf16[8,448,256]{2,1,0:T(8,128)(2,1)} %bitcast.17), channel_id=1, source_target_pairs={{0,128},{128,0},{1,129},{129,1},{2,130},{130,2},{3,131},{131,3},{4... | collective-permute-start | bytes 5505032 | tf_op jit(solution)/shard_map/ppermute | solution.py:50
  92.9 1.5 copy-start.1
  98.0 33.7 %all-to-all-start.2 = ((bf16[32,64,256]{2,1,0:T(8,128)(2,1)}), bf16[32,64,256]{2,1,0:T(8,128)(2,1)S(1)}, u32[]{:S(2)}, u32[]{:S(2)}) async-start(bf16[32,64,256]{2,1,0:T(8,128)(2,1)} %shard_map.94), calls=%async_computation.2 | async-start | bytes 2097152 | tf_op jit(solution)/shard_map/all_to_all | solution.py:41
  105.4 15.7 %collective-permute-start.4 = (bf16[14,32,256]{2,1,0:T(8,128)(2,1)S(1)}, bf16[14,32,256]{2,1,0:T(8,128)(2,1)S(1)}, u32[]{:S(2)}, u32[]{:S(2)}) collective-permute-start(bf16[14,32,256]{2,1,0:T(8,128)(2,1)S(1)} %slice_bitcast_fusion.2), channel_id=1, source_target_pairs={{0,3},{1,0},{2,1},{3,2},{4,7},{5,4},{6,5},{7,6},{8,11},{9,8},{10,9... | collective-permute-start | bytes 688136 | tf_op jit(solution)/shard_map/ppermute | solution.py:50
  110.5 15.2 %collective-permute-start.3 = (bf16[14,32,256]{2,1,0:T(8,128)(2,1)S(1)}, bf16[14,32,256]{2,1,0:T(8,128)(2,1)S(1)}, u32[]{:S(2)}, u32[]{:S(2)}) collective-permute-start(bf16[14,32,256]{2,1,0:T(8,128)(2,1)S(1)} %slice_bitcast_fusion.3), channel_id=1, source_target_pairs={{0,1},{1,2},{2,3},{3,0},{4,5},{5,6},{6,7},{7,4},{8,9},{9,10},{10,1... | collective-permute-start | bytes 688136 | tf_op jit(solution)/shard_map/ppermute | solution.py:50
  133.4 37.2 %copy-start.5 = (bf16[448,256]{1,0:T(8,128)(2,1)S(1)}, bf16[448,256]{1,0:T(8,128)(2,1)}, u32[]{:S(2)}) copy-start(bf16[448,256]{1,0:T(8,128)(2,1)} %d_mixed.3) | copy-start | bytes 688132
  133.4 37.2 %copy-start.11 = (f32[256]{0:T(256)S(1)}, f32[256]{0:T(256)}, u32[]{:S(2)}) copy-start(f32[256]{0:T(256)} %param.10) | copy-start | bytes 3076
  228.3 1.0 copy-start.4
  229.3 0.9 copy-start.6
  230.2 0.8 copy-start.9
  230.9 0.9 copy-start.12
  231.8 29.7 %copy-start.2 = (bf16[3584,256]{1,0:T(8,128)(2,1)S(1)}, bf16[3584,256]{1,0:T(8,128)(2,1)}, u32[]{:S(2)}) copy-start(bf16[3584,256]{1,0:T(8,128)(2,1)} %all-gather.3.cloned.1.call-done) | copy-start | bytes 5505028
  231.8 29.7 %all-to-all-start.6 = ((bf16[32,64,256]{2,1,0:T(8,128)(2,1)}), bf16[32,64,256]{2,1,0:T(8,128)(2,1)S(1)}, u32[]{:S(2)}, u32[]{:S(2)}) async-start(bf16[32,64,256]{2,1,0:T(8,128)(2,1)} %copy-done.4), calls=%async_computation.6 | async-start | bytes 2097152 | tf_op jit(solution)/shard_map/all_to_all | solution.py:41
  237.9 35.2 %collective-permute-start.5 = (bf16[14,3,32,256]{3,2,0,1:T(8,128)(2,1)}, bf16[14,3,32,256]{3,2,0,1:T(8,128)(2,1)}, u32[]{:S(2)}, u32[]{:S(2)}) collective-permute-start(bf16[14,3,32,256]{3,2,0,1:T(8,128)(2,1)} %copy.25), channel_id=1, source_target_pairs={{0,3},{1,0},{2,1},{3,2},{4,7},{5,4},{6,5},{7,6},{8,11},{9,8},{10,9... | collective-permute-start | bytes 2064392 | tf_op jit(solution)/shard_map/ppermute | solution.py:50
  239.8 33.3 %collective-permute-start.6 = (bf16[14,3,32,256]{3,2,1,0:T(8,128)(2,1)}, bf16[14,3,32,256]{3,2,1,0:T(8,128)(2,1)}, u32[]{:S(2)}, u32[]{:S(2)}) collective-permute-start(bf16[14,3,32,256]{3,2,1,0:T(8,128)(2,1)} %copy-done.12), channel_id=1, source_target_pairs={{0,1},{1,2},{2,3},{3,0},{4,5},{5,6},{6,7},{7,4},{8,9},{9,10},{10,1... | collective-permute-start | bytes 2064392 | tf_op jit(solution)/shard_map/ppermute | solution.py:50
  264.8 1.4 copy-start.3
  273.1 29.1 %all-to-all-start.7 = ((bf16[32,128,256]{2,1,0:T(8,128)(2,1)}), bf16[32,128,256]{2,1,0:T(8,128)(2,1)S(1)}, u32[]{:S(2)}, u32[]{:S(2)}) async-start(bf16[32,128,256]{2,1,0:T(8,128)(2,1)} %bitcast.20), calls=%async_computation.7 | async-start | bytes 4194304 | tf_op jit(solution)/shard_map/all_to_all | solution.py:41
  278.9 15.1 %collective-permute-start.8 = (bf16[14,32,256]{2,1,0:T(8,128)(2,1)S(1)}, bf16[14,32,256]{2,1,0:T(8,128)(2,1)S(1)}, u32[]{:S(2)}, u32[]{:S(2)}) collective-permute-start(bf16[14,32,256]{2,1,0:T(8,128)(2,1)S(1)} %slice_bitcast_fusion), channel_id=1, source_target_pairs={{0,1},{1,2},{2,3},{3,0},{4,5},{5,6},{6,7},{7,4},{8,9},{9,10},{10,1... | collective-permute-start | bytes 688136 | tf_op jit(solution)/shard_map/ppermute | solution.py:50
  281.4 12.5 %collective-permute-start.7 = (bf16[14,32,256]{2,1,0:T(8,128)(2,1)S(1)}, bf16[14,32,256]{2,1,0:T(8,128)(2,1)S(1)}, u32[]{:S(2)}, u32[]{:S(2)}) collective-permute-start(bf16[14,32,256]{2,1,0:T(8,128)(2,1)S(1)} %slice_bitcast_fusion.1), channel_id=1, source_target_pairs={{0,3},{1,0},{2,1},{3,2},{4,7},{5,4},{6,5},{7,6},{8,11},{9,8},{10,9... | collective-permute-start | bytes 688136 | tf_op jit(solution)/shard_map/ppermute | solution.py:50
  303.5 7.5 %copy-start.10 = (bf16[14,2,32,256]{3,2,1,0:T(8,128)(2,1)S(1)}, bf16[14,2,32,256]{3,2,1,0:T(8,128)(2,1)}, u32[]{:S(2)}) copy-start(bf16[14,2,32,256]{3,2,1,0:T(8,128)(2,1)} %copy-done.9) | copy-start | bytes 1376260
  303.5 21.2 %all-to-all-start.8 = ((bf16[8,128,256]{2,1,0:T(8,128)(2,1)}), bf16[8,128,256]{2,1,0:T(8,128)(2,1)S(1)}, u32[]{:S(2)}, u32[]{:S(2)}) async-start(bf16[8,128,256]{2,1,0:T(8,128)(2,1)} %reduce_sum.34), calls=%async_computation.8 | async-start | bytes 1048576 | tf_op jit(solution)/shard_map/all_to_all | solution.py:41
Sparse Core Ops, SparseCore 0:
  10.1 47.2 all-gather.2

commit v5 on v4

--- a/solution.py
+++ b/solution.py
@@ -110,12 +110,12 @@
     return jnp.sum(jnp.where(index < count, tile, 0.0), axis=0, keepdims=True)
 
 
-def split_kernel(place, block0, block1, block2, block3, own, up, down):
+def split_kernel(place, block0, block1, block2, block3, own, first, far_keys, far_values, last):
     own[...] = block0[...]
-    up[:, :2] = block1[...]
-    up[:, 2] = block2[:, 0]
-    down[:, :2] = block3[...]
-    down[:, 2] = block2[:, 1]
+    first[...] = block1[...]
+    far_keys[...] = block2[:, 0]
+    far_values[...] = block2[:, 1]
+    last[...] = block3[...]
 
 
 def whole_rows(n, own, first, far_keys, far_values, last):
@@ -231,7 +231,7 @@
 
 
 def owner_backward_kernel(target, arrived, queries, probs, *refs):
-    kv_refs, (slots, own, down, up) = refs[:5], refs[5:]
+    kv_refs, (slots, own, first, far_keys, far_values, last) = refs[:5], refs[5:]
     for n in range(target.shape[0]):
         t = target[n]
         keys, values = whole_rows(n, *kv_refs)
@@ -246,9 +246,9 @@
         rows = grad_keys.shape[0] // 4
         for i, grads in enumerate((grad_keys, grad_values)):
             own[n, i] = grads[:rows]
-            down[n, i] = grads[rows : 2 * rows]
-            (down, up)[i][n, 2] = grads[2 * rows : 3 * rows]
-            up[n, i] = grads[3 * rows :]
+            first[n, i] = grads[rows : 2 * rows]
+            (far_keys, far_values)[i][n] = grads[2 * rows : 3 * rows]
+            last[n, i] = grads[3 * rows :]
 
 
 def weight_kernel(sizes, place, source, arrived, mine, other, grad_q, partial):
@@ -278,7 +278,7 @@
 
     @pl.when(step == 1)
     def _():
-        out[...] = first[:, :2]
+        out[...] = first[...]
 
     @pl.when(step == 2)
     def _():
@@ -287,7 +287,7 @@
 
     @pl.when(step == 3)
     def _():
-        out[...] = last[:, :2]
+        out[...] = last[...]
 
 
 def split_by_quarter(place, kv):
@@ -296,14 +296,17 @@
     take = [
         pl.BlockSpec((n, 2, quarter, part), functools.partial(block_at, d)) for d in range(4)
     ]
-    shapes = [(n, 2, quarter, part), (n, 3, quarter, part), (n, 3, quarter, part)]
+    pair, single = (n, 2, quarter, part), (n, quarter, part)
+    shapes = [pair, pair, single, single, pair]
     return pl.pallas_call(
         split_kernel,
         grid_spec=pltpu.PrefetchScalarGridSpec(
             num_scalar_prefetch=1,
             grid=(1,),
             in_specs=take,
-            out_specs=[pl.BlockSpec(shape, lambda i, place: (0, 0, 0, 0)) for shape in shapes],
+            out_specs=[
+                pl.BlockSpec(shape, functools.partial(origin, len(shape))) for shape in shapes
+            ],
         ),
         out_shape=[jax.ShapeDtypeStruct(shape, kv.dtype) for shape in shapes],
         compiler_params=PARAMS,
@@ -358,15 +361,18 @@
     source = lax.dynamic_slice_in_dim(flat_ids, me_dp * neigh_dev, neigh_dev) // neigh_dev
 
     line = lax.all_gather(hidden, LINE, axis=0)
-    own, up, down = split_by_quarter(place, kv_enc)
+    own, first, far_keys, far_values, last = split_by_quarter(place, kv_enc)
     near = exchange(copies(wq, n_z), "dz").reshape(n_z, -1, dec_width)
-    near, up, down = lax.optimization_barrier((near, up, down))
-    first, last = shift(up, "mp", 1), shift(down, "mp", -1)
+    near, far_keys, far_values = lax.optimization_barrier((near, far_keys, far_values))
+    far_keys, far_values = shift(far_keys, "mp", 1), shift(far_values, "mp", -1)
     weight = exchange(copies(near, n_x).reshape(n_x * n_z, -1, dec_width), "dx")
     weight = weight.reshape(n_x, n_z, -1, dec_width)
-    line, weight, first, last = lax.optimization_barrier((line, weight, first, last))
-    far_keys, far_values = shift(first[:, 2], "mp", 1), shift(last[:, 2], "mp", -1)
+    line, weight, far_keys, far_values, first, last = lax.optimization_barrier(
+        (line, weight, far_keys, far_values, first, last)
+    )
     other = shift(line, "co", 1)
+    first, last = shift(first, "mp", 1), shift(last, "mp", -1)
+    far_keys, far_values = shift(far_keys, "mp", 1), shift(far_values, "mp", -1)
     kv = (own, first, far_keys, far_values, last)
 
     (slots,) = pl.pallas_call(
@@ -402,13 +408,14 @@
         [((tok_dev, dec_width), BF), (wide, BF)],
     )
     arrived = exchange(slots, DP)
-    slots, own, down, up = call(
+    slots, own, first, far_keys, far_values, last = call(
         owner_backward_kernel,
         (target,),
         (arrived, queries, probs, *kv),
-        [((n_dp, GROUP_LEN, dec_width), BF)] + [(x.shape, BF) for x in (own, first, last)],
-    )
-    first, last = shift(down, "mp", -1), shift(up, "mp", 1)
+        [((n_dp, GROUP_LEN, dec_width), BF)] + [(x.shape, BF) for x in kv],
+    )
+    far_keys, far_values = shift(far_keys, "mp", -1), shift(far_values, "mp", 1)
+    first, last = shift(first, "mp", -1), shift(last, "mp", 1)
     arrived = exchange(slots, DP)
     grad_q, partial = call(
         functools.partial(weight_kernel, sizes),
@@ -416,8 +423,10 @@
         (arrived, line, other),
         [((tok_dev, dec_width), BF), (weight.shape, BF)],
     )
-    partial, first, last = lax.optimization_barrier((partial, first, last))
-    far_keys, far_values = shift(first[:, 2], "mp", -1), shift(last[:, 2], "mp", 1)
+    partial, first, far_keys, far_values, last = lax.optimization_barrier(
+        (partial, first, far_keys, far_values, last)
+    )
+    far_keys, far_values = shift(far_keys, "mp", -1), shift(far_values, "mp", 1)
     column = exchange(partial.reshape(n_x * n_z, -1, dec_width), "dx").reshape(weight.shape)
     column, far_keys, far_values = lax.optimization_barrier((column, far_keys, far_values))
     grad_kv = merge_quarters(place, (own, first, far_keys, far_values, last))

time: 338 us -> 334 us (0.988)
  starting transfers between devices: 67.4 us -> 78.3 us
  waiting for transfers between devices: 121 us -> 112 us
  local copies, waits for them, and re-layouts: 19.9 us -> 11.4 us
    ppermute x9 -> x13, starting transfers between devices: 30.7 us -> 45.1 us  [shift(): lax.ppermute(array, axis, [(i, (i + step) % size) for i in range(size)])]
    ppermute x9 -> x13, waiting for transfers between devices: 61.7 us -> 51.3 us  [shift(): lax.ppermute(array, axis, [(i, (i + step) % size) for i in range(size)])]
    all_to_all x6, starting transfers between devices: 36.6 us -> 33.1 us  [exchange(): return lax.all_to_all(array, axes, split_axis=0, concat_axis=0, tiled=True)]
    unnamed x33 -> x27, local copies, waits for them, and re-layouts: 8.2 us -> 6.97 us
  transfers between devices with their start and end apart: 16 -> 20, of which waited for: 12 -> 13; matrix products, arithmetic and copies ran while one was open for 4% -> 2% of each run, Pallas kernels for 2% -> 3%
where the time goes in v5:
time: 334 us; the launch traced here: 328 us
  waiting for transfers between devices  112 us (34%)
  blocking collectives  89.8 us (27%)
  starting transfers between devices  78.3 us (23%)
  Pallas kernels  20.7 us (6%)
  between operations  14.3 us (4%)
  local copies, waits for them, and re-layouts  11.4 us (3%)
    all_to_all x3, blocking collectives, exchange(): return lax.all_to_all(array, axes, split_axis=0, concat_axis=0, tiled=True)  89.8 us
    all_to_all x6, waiting for transfers between devices, exchange(): return lax.all_to_all(array, axes, split_axis=0, concat_axis=0, tiled=True)  59.5 us
    ppermute x13, waiting for transfers between devices, shift(): lax.ppermute(array, axis, [(i, (i + step) % size) for i in range(size)])  51.3 us
    ppermute x13, starting transfers between devices, shift(): lax.ppermute(array, axis, [(i, (i + step) % size) for i in range(size)])  45.1 us
    all_to_all x6, starting transfers between devices, exchange(): return lax.all_to_all(array, axes, split_axis=0, concat_axis=0, tiled=True)  33.1 us
    pallas_call x5, Pallas kernels, call(): pl.pallas_call(kernel, in_specs=[SMEM] * len(scalars) + [VMEM] * len(arra...  12 us
    unnamed x27, local copies, waits for them, and re-layouts  6.97 us
  transfers between devices with their start and end apart: 20, of which 13 were waited for; matrix products, arithmetic and copies ran while one was open for 2% of the time, Pallas kernels for 3%

profile of v5, /device:TPU:1, one launch (start us, length us, event | category | flops | bytes accessed | tf_op | source)
XLA Modules:
  0.0 328.4 jit_solution(2522964704460076654)
XLA Ops:
  7.2 0.0 all-gather.3.cloned.1.call-start
  7.2 0.7 all-gather.3.cloned.1.call-update
  7.9 1.7 broadcast_in_dim.20
  9.6 10.9 %all-to-all-start = ((bf16[8,128,256]{2,1,0:T(8,128)(2,1)}), bf16[8,128,256]{2,1,0:T(8,128)(2,1)}, u32[]{:S(2)}, u32[]{:S(2)}) async-start(bf16[8,128,256]{2,1,0:T(8,128)(2,1)} %broadcast_in_dim.20), calls=%async_computation | async-start | bytes 1048576 | tf_op jit(solution)/shard_map/all_to_all | solution.py:41
  20.4 0.1 pad_add_fusion.place
  20.5 1.6 shard_map.93
  22.1 16.4 %all-to-all-done = bf16[8,128,256]{2,1,0:T(8,128)(2,1)} async-done(((bf16[8,128,256]{2,1,0:T(8,128)(2,1)}), bf16[8,128,256]{2,1,0:T(8,128)(2,1)}, u32[]{:S(2)}, u32[]{:S(2)}) %all-to-all-start) | async-done | bytes 524320 | tf_op jit(solution)/shard_map/all_to_all | solution.py:41
  38.5 2.7 broadcast_in_dim.21
  41.2 4.1 %all-to-all-start.1 = ((bf16[32,128,256]{2,1,0:T(8,128)(2,1)}), bf16[32,128,256]{2,1,0:T(8,128)(2,1)S(1)}, u32[]{:S(2)}, u32[]{:S(2)}) async-start(bf16[32,128,256]{2,1,0:T(8,128)(2,1)} %bitcast.15), calls=%async_computation.1 | async-start | bytes 4194304 | tf_op jit(solution)/shard_map/all_to_all | solution.py:41
  45.3 4.2 %collective-permute-start = (bf16[14,32,256]{2,1,0:T(8,128)(2,1)}, bf16[14,32,256]{2,1,0:T(8,128)(2,1)}, u32[]{:S(2)}, u32[]{:S(2)}) collective-permute-start(bf16[14,32,256]{2,1,0:T(8,128)(2,1)} %copy-done.11), channel_id=1, source_target_pairs={{0,1},{1,2},{2,3},{3,0},{4,5},{5,6},{6,7},{7,4},{8,9},{9,10},{10,1... | collective-permute-start | bytes 688136 | tf_op jit(solution)/shard_map/ppermute | solution.py:50
  49.5 3.6 %collective-permute-start.1 = (bf16[14,32,256]{2,1,0:T(8,128)(2,1)S(1)}, bf16[14,32,256]{2,1,0:T(8,128)(2,1)}, u32[]{:S(2)}, u32[]{:S(2)}) collective-permute-start(bf16[14,32,256]{2,1,0:T(8,128)(2,1)S(1)} %get-tuple-element.45), channel_id=1, source_target_pairs={{0,3},{1,0},{2,1},{3,2},{4,7},{5,4},{6,5},{7,6},{8,11},{9,8},{10,9... | collective-permute-start | bytes 688136 | tf_op jit(solution)/shard_map/ppermute | solution.py:50
  53.1 10.5 %collective-permute-done = bf16[14,32,256]{2,1,0:T(8,128)(2,1)} collective-permute-done((bf16[14,32,256]{2,1,0:T(8,128)(2,1)}, bf16[14,32,256]{2,1,0:T(8,128)(2,1)}, u32[]{:S(2)}, u32[]{:S(2)}) %collective-permute-start) | collective-permute-done | bytes 229408 | tf_op jit(solution)/shard_map/ppermute | solution.py:50
  63.7 3.0 collective-permute-done.1
  66.7 4.3 %all-to-all-done.1 = bf16[32,128,256]{2,1,0:T(8,128)(2,1)S(1)} async-done(((bf16[32,128,256]{2,1,0:T(8,128)(2,1)}), bf16[32,128,256]{2,1,0:T(8,128)(2,1)S(1)}, u32[]{:S(2)}, u32[]{:S(2)}) %all-to-all-start.1) | async-done | bytes 2097184 | tf_op jit(solution)/shard_map/all_to_all | solution.py:41
  70.9 3.6 %collective-permute-start.2 = (bf16[8,448,256]{2,1,0:T(8,128)(2,1)}, bf16[8,448,256]{2,1,0:T(8,128)(2,1)}, u32[]{:S(2)}, u32[]{:S(2)}) collective-permute-start(bf16[8,448,256]{2,1,0:T(8,128)(2,1)} %bitcast.9), channel_id=1, source_target_pairs={{0,128},{128,0},{1,129},{129,1},{2,130},{130,2},{3,131},{131,3},{4... | collective-permute-start | bytes 5505032 | tf_op jit(solution)/shard_map/ppermute | solution.py:50
  74.5 0.1 copy.11
  74.7 0.1 reshape.47
  74.8 0.1 and_select_fusion.source
  74.9 3.3 %collective-permute-done.2.other = bf16[8,448,256]{2,1,0:T(8,128)(2,1)} collective-permute-done((bf16[8,448,256]{2,1,0:T(8,128)(2,1)}, bf16[8,448,256]{2,1,0:T(8,128)(2,1)}, u32[]{:S(2)}, u32[]{:S(2)}) %collective-permute-start.2) | collective-permute-done | bytes 1835040 | tf_op jit(solution)/shard_map/ppermute | solution.py:50
  78.2 1.5 copy-done.1
  79.7 3.6 %shard_map.94 = bf16[32,64,256]{2,1,0:T(8,128)(2,1)} custom-call(s32[2]{0:T(128)S(1)} %pad_add_fusion.place, s32[14]{0:T(128)S(1)} %and_select_fusion.source, bf16[8,448,256]{2,1,0:T(8,128)(2,1)S(1)} %bitcast.10, bf16[8,448,256]{2,1,0:T(8,128)(2,1)} %collective-permute-done.2.other, bf16[4,8,128,256]{3,2,1,0:T(8,128)(2,1)S(1)} %bitcast.8), custom_call_target="tpu_custom_call" | custom-call | tf_op jit(solution)/shard_map/pallas_call | solution.py:378
  83.4 3.9 %all-to-all-start.2 = ((bf16[32,64,256]{2,1,0:T(8,128)(2,1)}), bf16[32,64,256]{2,1,0:T(8,128)(2,1)S(1)}, u32[]{:S(2)}, u32[]{:S(2)}) async-start(bf16[32,64,256]{2,1,0:T(8,128)(2,1)} %shard_map.94), calls=%async_computation.2 | async-start | bytes 2097152 | tf_op jit(solution)/shard_map/all_to_all | solution.py:41
  87.3 4.2 %collective-permute-start.3 = (bf16[14,2,32,256]{3,2,1,0:T(8,128)(2,1)}, bf16[14,2,32,256]{3,2,1,0:T(8,128)(2,1)S(1)}, u32[]{:S(2)}, u32[]{:S(2)}) collective-permute-start(bf16[14,2,32,256]{3,2,1,0:T(8,128)(2,1)} %get-tuple-element.51), channel_id=1, source_target_pairs={{0,1},{1,2},{2,3},{3,0},{4,5},{5,6},{6,7},{7,4},{8,9},{9,10},{10,1... | collective-permute-start | bytes 1376264 | tf_op jit(solution)/shard_map/ppermute | solution.py:50
  91.5 3.6 %collective-permute-start.6 = (bf16[14,2,32,256]{3,2,1,0:T(8,128)(2,1)S(1)}, bf16[14,2,32,256]{3,2,1,0:T(8,128)(2,1)S(1)}, u32[]{:S(2)}, u32[]{:S(2)}) collective-permute-start(bf16[14,2,32,256]{3,2,1,0:T(8,128)(2,1)S(1)} %get-tuple-element.54), channel_id=1, source_target_pairs={{0,3},{1,0},{2,1},{3,2},{4,7},{5,4},{6,5},{7,6},{8,11},{9,8},{10,9... | collective-permute-start | bytes 1376264 | tf_op jit(solution)/shard_map/ppermute | solution.py:50
  95.1 3.8 %collective-permute-start.4 = (bf16[14,32,256]{2,1,0:T(8,128)(2,1)}, bf16[14,32,256]{2,1,0:T(8,128)(2,1)S(1)}, u32[]{:S(2)}, u32[]{:S(2)}) collective-permute-start(bf16[14,32,256]{2,1,0:T(8,128)(2,1)} %collective-permute-done), channel_id=1, source_target_pairs={{0,1},{1,2},{2,3},{3,0},{4,5},{5,6},{6,7},{7,4},{8,9},{9,10},{10,1... | collective-permute-start | bytes 688136 | tf_op jit(solution)/shard_map/ppermute | solution.py:50
  98.9 3.6 %collective-permute-start.5 = (bf16[14,32,256]{2,1,0:T(8,128)(2,1)}, bf16[14,32,256]{2,1,0:T(8,128)(2,1)S(1)}, u32[]{:S(2)}, u32[]{:S(2)}) collective-permute-start(bf16[14,32,256]{2,1,0:T(8,128)(2,1)} %collective-permute-done.1), channel_id=1, source_target_pairs={{0,3},{1,0},{2,1},{3,2},{4,7},{5,4},{6,5},{7,6},{8,11},{9,8},{10,9... | collective-permute-start | bytes 688136 | tf_op jit(solution)/shard_map/ppermute | solution.py:50
  102.6 0.2 select_reduce_fusion.target
  102.7 15.7 %collective-permute-done.4.far_keys.refs_2_ = bf16[14,32,256]{2,1,0:T(8,128)(2,1)S(1)} collective-permute-done((bf16[14,32,256]{2,1,0:T(8,128)(2,1)}, bf16[14,32,256]{2,1,0:T(8,128)(2,1)S(1)}, u32[]{:S(2)}, u32[]{:S(2)}) %collective-permute-start.4) | collective-permute-done | bytes 229408 | tf_op jit(solution)/shard_map/ppermute | solution.py:50
  118.5 9.0 %collective-permute-done.5.far_values.refs_3_ = bf16[14,32,256]{2,1,0:T(8,128)(2,1)S(1)} collective-permute-done((bf16[14,32,256]{2,1,0:T(8,128)(2,1)}, bf16[14,32,256]{2,1,0:T(8,128)(2,1)S(1)}, u32[]{:S(2)}, u32[]{:S(2)}) %collective-permute-start.5) | collective-permute-done | bytes 229408 | tf_op jit(solution)/shard_map/ppermute | solution.py:50
  127.5 1.7 shard_map.95
  129.2 0.0 copy-start.5
  129.2 0.0 copy-start.6
  129.2 40.3 %all_to_all.45.arrived = bf16[32,16,1152]{2,1,0:T(8,128)(2,1)S(1)} all-to-all(bf16[32,16,1152]{2,1,0:T(8,128)(2,1)S(1)} %get-tuple-element.55), channel_id=1, replica_groups=mesh['yl'=2,'co'=2,'dz'=8,'dx'=4,'mp'=4] {'dz','dx'}, dimensions={0} | all-to-all | bytes 2359296 | tf_op jit(solution)/shard_map/all_to_all | solution.py:41
  169.5 1.6 shard_map.96
  171.1 14.3 %all_to_all.46.moved = f32[16,8,128]{2,1,0:T(8,128)S(1)} all-to-all(f32[16,8,128]{2,1,0:T(8,128)S(1)} %broadcast_in_dim.36), channel_id=1, replica_groups=mesh['yl'=2,'co'=2,'dz'=8,'dx'=4,'mp'=4] {'yl','co','mp'}, dimensions={0} | all-to-all | bytes 131072 | tf_op jit(solution)/shard_map/all_to_all | solution.py:41
  185.4 2.5 shard_map.97
  187.9 35.2 %all_to_all.47.arrived = bf16[32,16,1152]{2,1,0:T(8,128)(2,1)S(1)} all-to-all(bf16[32,16,1152]{2,1,0:T(8,128)(2,1)S(1)} %get-tuple-element.60), channel_id=1, replica_groups=mesh['yl'=2,'co'=2,'dz'=8,'dx'=4,'mp'=4] {'dz','dx'}, dimensions={0} | all-to-all | bytes 2359296 | tf_op jit(solution)/shard_map/all_to_all | solution.py:41
  223.1 3.1 shard_map.98
  226.1 0.0 copy-start.4
  226.2 1.0 copy-done.4
  227.1 0.8 copy-done.7
  227.9 0.8 copy-done.8
  228.7 0.7 copy-done.9
  229.4 0.7 copy-done.10
  230.1 4.1 %all-to-all-start.6 = ((bf16[32,64,256]{2,1,0:T(8,128)(2,1)}), bf16[32,64,256]{2,1,0:T(8,128)(2,1)S(1)}, u32[]{:S(2)}, u32[]{:S(2)}) async-start(bf16[32,64,256]{2,1,0:T(8,128)(2,1)} %copy-done.4), calls=%async_computation.6 | async-start | bytes 2097152 | tf_op jit(solution)/shard_map/all_to_all | solution.py:41
  234.2 1.9 collective-permute-start.7
  236.1 4.3 %collective-permute-start.10 = (bf16[14,2,32,256]{3,2,1,0:T(8,128)(2,1)}, bf16[14,2,32,256]{3,2,1,0:T(8,128)(2,1)}, u32[]{:S(2)}, u32[]{:S(2)}) collective-permute-start(bf16[14,2,32,256]{3,2,1,0:T(8,128)(2,1)} %copy-done.7), channel_id=1, source_target_pairs={{0,1},{1,2},{2,3},{3,0},{4,5},{5,6},{6,7},{7,4},{8,9},{9,10},{10,1... | collective-permute-start | bytes 1376264 | tf_op jit(solution)/shard_map/ppermute | solution.py:50
  240.4 3.1 collective-permute-start.8
  243.5 3.1 collective-permute-start.9
  246.6 13.2 %all-to-all-done.6.arrived = bf16[32,64,256]{2,1,0:T(8,128)(2,1)S(1)} async-done(((bf16[32,64,256]{2,1,0:T(8,128)(2,1)}), bf16[32,64,256]{2,1,0:T(8,128)(2,1)S(1)}, u32[]{:S(2)}, u32[]{:S(2)}) %all-to-all-start.6) | async-done | bytes 1048608 | tf_op jit(solution)/shard_map/all_to_all | solution.py:41
  259.8 3.3 shard_map.99
  263.1 1.4 copy-done.3
  264.5 4.9 %collective-permute-done.8 = bf16[14,32,256]{2,1,0:T(8,128)(2,1)} collective-permute-done((bf16[14,32,256]{2,1,0:T(8,128)(2,1)}, bf16[14,32,256]{2,1,0:T(8,128)(2,1)}, u32[]{:S(2)}, u32[]{:S(2)}) %collective-permute-start.8) | collective-permute-done | bytes 229408 | tf_op jit(solution)/shard_map/ppermute | solution.py:50
  269.4 3.9 %all-to-all-start.7 = ((bf16[32,128,256]{2,1,0:T(8,128)(2,1)}), bf16[32,128,256]{2,1,0:T(8,128)(2,1)S(1)}, u32[]{:S(2)}, u32[]{:S(2)}) async-start(bf16[32,128,256]{2,1,0:T(8,128)(2,1)} %bitcast.12), calls=%async_computation.7 | async-start | bytes 4194304 | tf_op jit(solution)/shard_map/all_to_all | solution.py:41
  273.3 1.9 collective-permute-start.11
  275.2 4.3 %collective-permute-start.12 = (bf16[14,32,256]{2,1,0:T(8,128)(2,1)}, bf16[14,32,256]{2,1,0:T(8,128)(2,1)S(1)}, u32[]{:S(2)}, u32[]{:S(2)}) collective-permute-start(bf16[14,32,256]{2,1,0:T(8,128)(2,1)} %collective-permute-done.9), channel_id=1, source_target_pairs={{0,1},{1,2},{2,3},{3,0},{4,5},{5,6},{6,7},{7,4},{8,9},{9,10},{10,1... | collective-permute-start | bytes 688136 | tf_op jit(solution)/shard_map/ppermute | solution.py:50
  279.4 2.8 collective-permute-done.11.far_keys
  282.2 2.1 collective-permute-done.12.far_values
  284.3 14.2 %all-to-all-done.7 = bf16[32,128,256]{2,1,0:T(8,128)(2,1)S(1)} async-done(((bf16[32,128,256]{2,1,0:T(8,128)(2,1)}), bf16[32,128,256]{2,1,0:T(8,128)(2,1)S(1)}, u32[]{:S(2)}, u32[]{:S(2)}) %all-to-all-start.7) | async-done | bytes 2097184 | tf_op jit(solution)/shard_map/all_to_all | solution.py:41
  298.5 1.3 reduce_sum.34
  299.7 6.2 %all-to-all-start.8 = ((bf16[8,128,256]{2,1,0:T(8,128)(2,1)}), bf16[8,128,256]{2,1,0:T(8,128)(2,1)S(1)}, u32[]{:S(2)}, u32[]{:S(2)}) async-start(bf16[8,128,256]{2,1,0:T(8,128)(2,1)} %reduce_sum.34), calls=%async_computation.8 | async-start | bytes 1048576 | tf_op jit(solution)/shard_map/all_to_all | solution.py:41
  306.0 3.5 %shard_map.100 = bf16[14,2,32,1024]{3,2,1,0:T(8,128)(2,1)} custom-call(s32[2]{0:T(128)S(1)} %pad_add_fusion.place, bf16[14,2,32,256]{3,2,1,0:T(8,128)(2,1)S(1)} %get-tuple-element.64.own, bf16[14,2,32,256]{3,2,1,0:T(8,128)(2,1)} %collective-permute-done.7.first, bf16[14,32,256]{2,1,0:T(8,128)(2,1)S(1)} %collective-permute-done.11.far_keys, ...), custom_call_target="tpu_custom_call" | custom-call | tf_op jit(solution)/shard_map/pallas_call | solution.py:322
  309.5 11.4 %all-to-all-done.8 = bf16[8,128,256]{2,1,0:T(8,128)(2,1)S(1)} async-done(((bf16[8,128,256]{2,1,0:T(8,128)(2,1)}), bf16[8,128,256]{2,1,0:T(8,128)(2,1)S(1)}, u32[]{:S(2)}, u32[]{:S(2)}) %all-to-all-start.8) | async-done | bytes 524320 | tf_op jit(solution)/shard_map/all_to_all | solution.py:41
  320.9 0.7 reduce_sum.35
  (26 shorter events, 0.1 us)
Async XLA Ops:
  7.2 13.4 %copy-start = (bf16[14,2,32,1024]{3,2,1,0:T(8,128)(2,1)S(1)}, bf16[14,2,32,1024]{3,2,1,0:T(8,128)(2,1)}, u32[]{:S(2)}) copy-start(bf16[14,2,32,1024]{3,2,1,0:T(8,128)(2,1)} %block3.1) | copy-start | bytes 5505028
  7.2 63.8 %all-gather.3.cloned.1.call-start = ((), (), s32[]{:S(2)}) async-start(), calls=%async_computation.9 | async-start | bytes 2064384 | tf_op jit(solution)/shard_map/all_gather | solution.py:363
  9.6 28.9 %all-to-all-start = ((bf16[8,128,256]{2,1,0:T(8,128)(2,1)}), bf16[8,128,256]{2,1,0:T(8,128)(2,1)}, u32[]{:S(2)}, u32[]{:S(2)}) async-start(bf16[8,128,256]{2,1,0:T(8,128)(2,1)} %broadcast_in_dim.20), calls=%async_computation | async-start | bytes 1048576 | tf_op jit(solution)/shard_map/all_to_all | solution.py:41
  22.1 19.1 %copy-start.11 = (bf16[14,32,256]{2,1,0:T(8,128)(2,1)}, bf16[14,32,256]{2,1,0:T(8,128)(2,1)S(1)}, u32[]{:S(2)}) copy-start(bf16[14,32,256]{2,1,0:T(8,128)(2,1)S(1)} %get-tuple-element.44) | copy-start | bytes 688132
  41.2 33.4 %copy-start.12 = (s32[224,2]{0,1:T(2,128)S(1)}, s32[224,2]{0,1:T(2,128)}, u32[]{:S(2)}) copy-start(s32[224,2]{0,1:T(2,128)} %param.9) | copy-start | bytes 5380
  41.2 29.8 %all-to-all-start.1 = ((bf16[32,128,256]{2,1,0:T(8,128)(2,1)}), bf16[32,128,256]{2,1,0:T(8,128)(2,1)S(1)}, u32[]{:S(2)}, u32[]{:S(2)}) async-start(bf16[32,128,256]{2,1,0:T(8,128)(2,1)} %bitcast.15), calls=%async_computation.1 | async-start | bytes 4194304 | tf_op jit(solution)/shard_map/all_to_all | solution.py:41
  45.3 18.4 %collective-permute-start = (bf16[14,32,256]{2,1,0:T(8,128)(2,1)}, bf16[14,32,256]{2,1,0:T(8,128)(2,1)}, u32[]{:S(2)}, u32[]{:S(2)}) collective-permute-start(bf16[14,32,256]{2,1,0:T(8,128)(2,1)} %copy-done.11), channel_id=1, source_target_pairs={{0,1},{1,2},{2,3},{3,0},{4,5},{5,6},{6,7},{7,4},{8,9},{9,10},{10,1... | collective-permute-start | bytes 688136 | tf_op jit(solution)/shard_map/ppermute | solution.py:50
  49.5 17.1 %collective-permute-start.1 = (bf16[14,32,256]{2,1,0:T(8,128)(2,1)S(1)}, bf16[14,32,256]{2,1,0:T(8,128)(2,1)}, u32[]{:S(2)}, u32[]{:S(2)}) collective-permute-start(bf16[14,32,256]{2,1,0:T(8,128)(2,1)S(1)} %get-tuple-element.45), channel_id=1, source_target_pairs={{0,3},{1,0},{2,1},{3,2},{4,7},{5,4},{6,5},{7,6},{8,11},{9,8},{10,9... | collective-permute-start | bytes 688136 | tf_op jit(solution)/shard_map/ppermute | solution.py:50
  70.9 7.3 %collective-permute-start.2 = (bf16[8,448,256]{2,1,0:T(8,128)(2,1)}, bf16[8,448,256]{2,1,0:T(8,128)(2,1)}, u32[]{:S(2)}, u32[]{:S(2)}) collective-permute-start(bf16[8,448,256]{2,1,0:T(8,128)(2,1)} %bitcast.9), channel_id=1, source_target_pairs={{0,128},{128,0},{1,129},{129,1},{2,130},{130,2},{3,131},{131,3},{4... | collective-permute-start | bytes 5505032 | tf_op jit(solution)/shard_map/ppermute | solution.py:50
  78.2 1.5 copy-start.1
  83.4 44.1 %all-to-all-start.2 = ((bf16[32,64,256]{2,1,0:T(8,128)(2,1)}), bf16[32,64,256]{2,1,0:T(8,128)(2,1)S(1)}, u32[]{:S(2)}, u32[]{:S(2)}) async-start(bf16[32,64,256]{2,1,0:T(8,128)(2,1)} %shard_map.94), calls=%async_computation.2 | async-start | bytes 2097152 | tf_op jit(solution)/shard_map/all_to_all | solution.py:41
  87.3 40.2 %collective-permute-start.3 = (bf16[14,2,32,256]{3,2,1,0:T(8,128)(2,1)}, bf16[14,2,32,256]{3,2,1,0:T(8,128)(2,1)S(1)}, u32[]{:S(2)}, u32[]{:S(2)}) collective-permute-start(bf16[14,2,32,256]{3,2,1,0:T(8,128)(2,1)} %get-tuple-element.51), channel_id=1, source_target_pairs={{0,1},{1,2},{2,3},{3,0},{4,5},{5,6},{6,7},{7,4},{8,9},{9,10},{10,1... | collective-permute-start | bytes 1376264 | tf_op jit(solution)/shard_map/ppermute | solution.py:50
  91.5 35.9 %collective-permute-start.6 = (bf16[14,2,32,256]{3,2,1,0:T(8,128)(2,1)S(1)}, bf16[14,2,32,256]{3,2,1,0:T(8,128)(2,1)S(1)}, u32[]{:S(2)}, u32[]{:S(2)}) collective-permute-start(bf16[14,2,32,256]{3,2,1,0:T(8,128)(2,1)S(1)} %get-tuple-element.54), channel_id=1, source_target_pairs={{0,3},{1,0},{2,1},{3,2},{4,7},{5,4},{6,5},{7,6},{8,11},{9,8},{10,9... | collective-permute-start | bytes 1376264 | tf_op jit(solution)/shard_map/ppermute | solution.py:50
  95.1 23.4 %collective-permute-start.4 = (bf16[14,32,256]{2,1,0:T(8,128)(2,1)}, bf16[14,32,256]{2,1,0:T(8,128)(2,1)S(1)}, u32[]{:S(2)}, u32[]{:S(2)}) collective-permute-start(bf16[14,32,256]{2,1,0:T(8,128)(2,1)} %collective-permute-done), channel_id=1, source_target_pairs={{0,1},{1,2},{2,3},{3,0},{4,5},{5,6},{6,7},{7,4},{8,9},{9,10},{10,1... | collective-permute-start | bytes 688136 | tf_op jit(solution)/shard_map/ppermute | solution.py:50
  98.9 28.6 %collective-permute-start.5 = (bf16[14,32,256]{2,1,0:T(8,128)(2,1)}, bf16[14,32,256]{2,1,0:T(8,128)(2,1)S(1)}, u32[]{:S(2)}, u32[]{:S(2)}) collective-permute-start(bf16[14,32,256]{2,1,0:T(8,128)(2,1)} %collective-permute-done.1), channel_id=1, source_target_pairs={{0,3},{1,0},{2,1},{3,2},{4,7},{5,4},{6,5},{7,6},{8,11},{9,8},{10,9... | collective-permute-start | bytes 688136 | tf_op jit(solution)/shard_map/ppermute | solution.py:50
  129.2 40.4 %copy-start.5 = (bf16[448,256]{1,0:T(8,128)(2,1)S(1)}, bf16[448,256]{1,0:T(8,128)(2,1)}, u32[]{:S(2)}) copy-start(bf16[448,256]{1,0:T(8,128)(2,1)} %d_mixed.3) | copy-start | bytes 688132
  129.2 40.3 %copy-start.6 = (f32[256]{0:T(256)S(1)}, f32[256]{0:T(256)}, u32[]{:S(2)}) copy-start(f32[256]{0:T(256)} %param.10) | copy-start | bytes 3076
  226.1 1.0 copy-start.4
  227.1 0.8 copy-start.7
  227.9 0.8 copy-start.8
  228.7 0.7 copy-start.9
  229.4 0.7 copy-start.10
  230.1 29.7 %copy-start.2 = (bf16[3584,256]{1,0:T(8,128)(2,1)S(1)}, bf16[3584,256]{1,0:T(8,128)(2,1)}, u32[]{:S(2)}) copy-start(bf16[3584,256]{1,0:T(8,128)(2,1)} %all-gather.3.cloned.1.call-done) | copy-start | bytes 5505028
  230.1 29.7 %all-to-all-start.6 = ((bf16[32,64,256]{2,1,0:T(8,128)(2,1)}), bf16[32,64,256]{2,1,0:T(8,128)(2,1)S(1)}, u32[]{:S(2)}, u32[]{:S(2)}) async-start(bf16[32,64,256]{2,1,0:T(8,128)(2,1)} %copy-done.4), calls=%async_computation.6 | async-start | bytes 2097152 | tf_op jit(solution)/shard_map/all_to_all | solution.py:41
  234.2 35.2 %collective-permute-start.7 = (bf16[14,2,32,256]{3,2,1,0:T(8,128)(2,1)}, bf16[14,2,32,256]{3,2,1,0:T(8,128)(2,1)}, u32[]{:S(2)}, u32[]{:S(2)}) collective-permute-start(bf16[14,2,32,256]{3,2,1,0:T(8,128)(2,1)} %copy-done.8), channel_id=1, source_target_pairs={{0,3},{1,0},{2,1},{3,2},{4,7},{5,4},{6,5},{7,6},{8,11},{9,8},{10,9... | collective-permute-start | bytes 1376264 | tf_op jit(solution)/shard_map/ppermute | solution.py:50
  236.1 33.3 %collective-permute-start.10 = (bf16[14,2,32,256]{3,2,1,0:T(8,128)(2,1)}, bf16[14,2,32,256]{3,2,1,0:T(8,128)(2,1)}, u32[]{:S(2)}, u32[]{:S(2)}) collective-permute-start(bf16[14,2,32,256]{3,2,1,0:T(8,128)(2,1)} %copy-done.7), channel_id=1, source_target_pairs={{0,1},{1,2},{2,3},{3,0},{4,5},{5,6},{6,7},{7,4},{8,9},{9,10},{10,1... | collective-permute-start | bytes 1376264 | tf_op jit(solution)/shard_map/ppermute | solution.py:50
  240.4 29.0 %collective-permute-start.8 = (bf16[14,32,256]{2,1,0:T(8,128)(2,1)}, bf16[14,32,256]{2,1,0:T(8,128)(2,1)}, u32[]{:S(2)}, u32[]{:S(2)}) collective-permute-start(bf16[14,32,256]{2,1,0:T(8,128)(2,1)} %copy-done.10), channel_id=1, source_target_pairs={{0,3},{1,0},{2,1},{3,2},{4,7},{5,4},{6,5},{7,6},{8,11},{9,8},{10,9... | collective-permute-start | bytes 688136 | tf_op jit(solution)/shard_map/ppermute | solution.py:50
  243.5 25.9 %collective-permute-start.9 = (bf16[14,32,256]{2,1,0:T(8,128)(2,1)}, bf16[14,32,256]{2,1,0:T(8,128)(2,1)}, u32[]{:S(2)}, u32[]{:S(2)}) collective-permute-start(bf16[14,32,256]{2,1,0:T(8,128)(2,1)} %copy-done.9), channel_id=1, source_target_pairs={{0,1},{1,2},{2,3},{3,0},{4,5},{5,6},{6,7},{7,4},{8,9},{9,10},{10,1... | collective-permute-start | bytes 688136 | tf_op jit(solution)/shard_map/ppermute | solution.py:50
  263.1 1.4 copy-start.3
  269.4 29.1 %all-to-all-start.7 = ((bf16[32,128,256]{2,1,0:T(8,128)(2,1)}), bf16[32,128,256]{2,1,0:T(8,128)(2,1)S(1)}, u32[]{:S(2)}, u32[]{:S(2)}) async-start(bf16[32,128,256]{2,1,0:T(8,128)(2,1)} %bitcast.12), calls=%async_computation.7 | async-start | bytes 4194304 | tf_op jit(solution)/shard_map/all_to_all | solution.py:41
  273.3 8.9 %collective-permute-start.11 = (bf16[14,32,256]{2,1,0:T(8,128)(2,1)}, bf16[14,32,256]{2,1,0:T(8,128)(2,1)S(1)}, u32[]{:S(2)}, u32[]{:S(2)}) collective-permute-start(bf16[14,32,256]{2,1,0:T(8,128)(2,1)} %collective-permute-done.8), channel_id=1, source_target_pairs={{0,3},{1,0},{2,1},{3,2},{4,7},{5,4},{6,5},{7,6},{8,11},{9,8},{10,9... | collective-permute-start | bytes 688136 | tf_op jit(solution)/shard_map/ppermute | solution.py:50
  275.2 9.1 %collective-permute-start.12 = (bf16[14,32,256]{2,1,0:T(8,128)(2,1)}, bf16[14,32,256]{2,1,0:T(8,128)(2,1)S(1)}, u32[]{:S(2)}, u32[]{:S(2)}) collective-permute-start(bf16[14,32,256]{2,1,0:T(8,128)(2,1)} %collective-permute-done.9), channel_id=1, source_target_pairs={{0,1},{1,2},{2,3},{3,0},{4,5},{5,6},{6,7},{7,4},{8,9},{9,10},{10,1... | collective-permute-start | bytes 688136 | tf_op jit(solution)/shard_map/ppermute | solution.py:50
  299.7 21.1 %all-to-all-start.8 = ((bf16[8,128,256]{2,1,0:T(8,128)(2,1)}), bf16[8,128,256]{2,1,0:T(8,128)(2,1)S(1)}, u32[]{:S(2)}, u32[]{:S(2)}) async-start(bf16[8,128,256]{2,1,0:T(8,128)(2,1)} %reduce_sum.34), calls=%async_computation.8 | async-start | bytes 1048576 | tf_op jit(solution)/shard_map/all_to_all | solution.py:41
Sparse Core Ops, SparseCore 0:
  10.1 47.5 all-gather.2

commit v6 on v4

--- a/solution.py
+++ b/solution.py
@@ -110,19 +110,25 @@
     return jnp.sum(jnp.where(index < count, tile, 0.0), axis=0, keepdims=True)
 
 
-def split_kernel(place, block0, block1, block2, block3, own, up, down):
+def split_kernel(place, block0, block1, block2, block3, own, up, down, first, last):
     own[...] = block0[...]
-    up[:, :2] = block1[...]
-    up[:, 2] = block2[:, 0]
-    down[:, :2] = block3[...]
-    down[:, 2] = block2[:, 1]
-
-
-def whole_rows(n, own, first, far_keys, far_values, last):
+    up[:, 0] = block1[:, 0]
+    up[:, 1] = block2[:, 0]
+    down[:, 0] = block3[:, 0]
+    down[:, 1] = block2[:, 1]
+    first[...] = block1[:, 1]
+    last[...] = block3[:, 1]
+
+
+def whole_rows(n, own, up, down, far_up, far_down):
     return [
-        jnp.concatenate([own[n, i], first[n, i], far[n], last[n, i]], axis=0)
-        for i, far in enumerate((far_keys, far_values))
+        jnp.concatenate([own[n, 0], up[n, 0], far_up[n, 1], down[n, 0]], axis=0),
+        jnp.concatenate([own[n, 1], far_up[n, 0], far_down[n, 1], far_down[n, 0]], axis=0),
     ]
+
+
+def second_step(first, arrived):
+    return jnp.stack([first, arrived[:, 1]], axis=1)
 
 
 def weight_rows(line, co, n_yl, n_co, n_mp):
@@ -131,16 +137,12 @@
 
 def query_kernel(sizes, place, source, mine, other, weight, slots, total):
     n_yl, n_co, n_mp, n_x = sizes
-    rows = weight.shape[2]
-    per = mine.shape[2] // rows
+    span = mine.shape[2]
     for part, block in enumerate((mine, other)):
         co = lax.rem(place[1] + part, n_co)
         for line in range(mine.shape[0]):
-            first = weight_rows(line, co, n_yl, n_co, n_mp) * per
-            w = jnp.concatenate(
-                [weight[lax.rem(first + i, n_x), lax.div(first + i, n_x)] for i in range(per)], axis=0
-            )
-            product = dot(block[line], w, PLAIN)
+            first = pl.multiple_of(weight_rows(line, co, n_yl, n_co, n_mp) * span, span)
+            product = dot(block[line], weight[pl.ds(first, span), :], PLAIN)
             if part == 0 and line == 0:
                 total[...] = product
             else:
@@ -150,10 +152,10 @@
         slots[source[k]] = total[c * GROUP_LEN : (c + 1) * GROUP_LEN].astype(BF)
 
 
-def owner_forward_kernel(target, arrived, own, first, far_keys, far_values, last, slots, probs):
+def owner_forward_kernel(target, arrived, own, up, down, far_up, far_down, slots, probs):
     for n in range(target.shape[0]):
         t = target[n]
-        keys, values = whole_rows(n, own, first, far_keys, far_values, last)
+        keys, values = whole_rows(n, own, up, down, far_up, far_down)
         scores = dot(keys, by_head(arrived[t]), LAST) * SCALE
         top = jnp.max(scores, axis=0, keepdims=True)
         expo = jnp.exp(scores - top)
@@ -231,7 +233,7 @@
 
 
 def owner_backward_kernel(target, arrived, queries, probs, *refs):
-    kv_refs, (slots, own, down, up) = refs[:5], refs[5:]
+    kv_refs, (slots, own, up, down, first, last) = refs[:5], refs[5:]
     for n in range(target.shape[0]):
         t = target[n]
         keys, values = whole_rows(n, *kv_refs)
@@ -244,11 +246,10 @@
         grad_keys = (dot(grad_scores, query, PLAIN) * SCALE).astype(BF)
         grad_values = dot(prob.astype(BF), grad, PLAIN).astype(BF)
         rows = grad_keys.shape[0] // 4
-        for i, grads in enumerate((grad_keys, grad_values)):
-            own[n, i] = grads[:rows]
-            down[n, i] = grads[rows : 2 * rows]
-            (down, up)[i][n, 2] = grads[2 * rows : 3 * rows]
-            up[n, i] = grads[3 * rows :]
+        own[n, 0], own[n, 1] = grad_keys[:rows], grad_values[:rows]
+        up[n, 0], first[n] = grad_keys[rows : 2 * rows], grad_values[rows : 2 * rows]
+        up[n, 1], down[n, 1] = grad_keys[2 * rows : 3 * rows], grad_values[2 * rows : 3 * rows]
+        down[n, 0], last[n] = grad_keys[3 * rows :], grad_values[3 * rows :]
 
 
 def weight_kernel(sizes, place, source, arrived, mine, other, grad_q, partial):
@@ -269,7 +270,7 @@
                 ]
 
 
-def merge_kernel(place, own, first, far_keys, far_values, last, out):
+def merge_kernel(place, own, up, down, far_up, far_down, out):
     step = pl.program_id(0)
 
     @pl.when(step == 0)
@@ -278,16 +279,18 @@
 
     @pl.when(step == 1)
     def _():
-        out[...] = first[:, :2]
+        out[:, 0] = up[:, 0]
+        out[:, 1] = far_up[:, 0]
 
     @pl.when(step == 2)
     def _():
-        out[:, 0] = far_keys[...]
-        out[:, 1] = far_values[...]
+        out[:, 0] = far_up[:, 1]
+        out[:, 1] = far_down[:, 1]
 
     @pl.when(step == 3)
     def _():
-        out[...] = last[:, :2]
+        out[:, 0] = down[:, 0]
+        out[:, 1] = far_down[:, 0]
 
 
 def split_by_quarter(place, kv):
@@ -296,14 +299,17 @@
     take = [
         pl.BlockSpec((n, 2, quarter, part), functools.partial(block_at, d)) for d in range(4)
     ]
-    shapes = [(n, 2, quarter, part), (n, 3, quarter, part), (n, 3, quarter, part)]
+    pair, single = (n, 2, quarter, part), (n, quarter, part)
+    shapes = [pair, pair, pair, single, single]
     return pl.pallas_call(
         split_kernel,
         grid_spec=pltpu.PrefetchScalarGridSpec(
             num_scalar_prefetch=1,
             grid=(1,),
             in_specs=take,
-            out_specs=[pl.BlockSpec(shape, lambda i, place: (0, 0, 0, 0)) for shape in shapes],
+            out_specs=[
+                pl.BlockSpec(shape, functools.partial(origin, len(shape))) for shape in shapes
+            ],
         ),
         out_shape=[jax.ShapeDtypeStruct(shape, kv.dtype) for shape in shapes],
         compiler_params=PARAMS,
@@ -358,16 +364,14 @@
     source = lax.dynamic_slice_in_dim(flat_ids, me_dp * neigh_dev, neigh_dev) // neigh_dev
 
     line = lax.all_gather(hidden, LINE, axis=0)
-    own, up, down = split_by_quarter(place, kv_enc)
-    near = exchange(copies(wq, n_z), "dz").reshape(n_z, -1, dec_width)
-    near, up, down = lax.optimization_barrier((near, up, down))
-    first, last = shift(up, "mp", 1), shift(down, "mp", -1)
-    weight = exchange(copies(near, n_x).reshape(n_x * n_z, -1, dec_width), "dx")
-    weight = weight.reshape(n_x, n_z, -1, dec_width)
-    line, weight, first, last = lax.optimization_barrier((line, weight, first, last))
-    far_keys, far_values = shift(first[:, 2], "mp", 1), shift(last[:, 2], "mp", -1)
+    own, up, down, first, last = split_by_quarter(place, kv_enc)
+    weight = exchange(copies(wq, n_dp), DP).reshape(-1, dec_width)
+    up, down = shift(up, "mp", 1), shift(down, "mp", -1)
+    line, up, down = lax.optimization_barrier((line, up, down))
     other = shift(line, "co", 1)
-    kv = (own, first, far_keys, far_values, last)
+    far_up = shift(second_step(first, up), "mp", 1)
+    far_down = shift(second_step(last, down), "mp", -1)
+    kv = (own, up, down, far_up, far_down)
 
     (slots,) = pl.pallas_call(
         functools.partial(query_kernel, sizes),
@@ -402,25 +406,28 @@
         [((tok_dev, dec_width), BF), (wide, BF)],
     )
     arrived = exchange(slots, DP)
-    slots, own, down, up = call(
+    slots, own, up, down, first, last = call(
         owner_backward_kernel,
         (target,),
         (arrived, queries, probs, *kv),
-        [((n_dp, GROUP_LEN, dec_width), BF)] + [(x.shape, BF) for x in (own, first, last)],
-    )
-    first, last = shift(down, "mp", -1), shift(up, "mp", 1)
+        [((n_dp, GROUP_LEN, dec_width), BF)]
+        + [(x.shape, BF) for x in (own, up, down, first, last)],
+    )
+    up, down = shift(up, "mp", -1), shift(down, "mp", 1)
     arrived = exchange(slots, DP)
+    blocks = (n_x, n_z, wq.shape[0], dec_width)
     grad_q, partial = call(
         functools.partial(weight_kernel, sizes),
         (place, source),
         (arrived, line, other),
-        [((tok_dev, dec_width), BF), (weight.shape, BF)],
-    )
-    partial, first, last = lax.optimization_barrier((partial, first, last))
-    far_keys, far_values = shift(first[:, 2], "mp", -1), shift(last[:, 2], "mp", 1)
-    column = exchange(partial.reshape(n_x * n_z, -1, dec_width), "dx").reshape(weight.shape)
-    column, far_keys, far_values = lax.optimization_barrier((column, far_keys, far_values))
-    grad_kv = merge_quarters(place, (own, first, far_keys, far_values, last))
+        [((tok_dev, dec_width), BF), (blocks, BF)],
+    )
+    partial, up, down = lax.optimization_barrier((partial, up, down))
+    far_up = shift(second_step(first, up), "mp", -1)
+    far_down = shift(second_step(last, down), "mp", 1)
+    column = exchange(partial.reshape(n_x * n_z, -1, dec_width), "dx").reshape(blocks)
+    column, far_up, far_down = lax.optimization_barrier((column, far_up, far_down))
+    grad_kv = merge_quarters(place, (own, up, down, far_up, far_down))
     column = jnp.sum(column, axis=0, dtype=F32).astype(BF)
     grad_wq = jnp.sum(exchange(column, "dz"), axis=0, dtype=F32).astype(BF)
     return (mixed, grad_q, grad_kv, grad_wq)

time: 338 us -> 331 us (0.979); the launches traced: 332 us -> 330 us
  waiting for transfers between devices: 121 us -> 114 us
    all_to_all x6 -> x5, waiting for transfers between devices: 58.3 us -> 34 us  [exchange(): return lax.all_to_all(array, axes, split_axis=0, concat_axis=0, tiled=True)]
    ppermute x9, waiting for transfers between devices: 61.7 us -> 73.2 us  [shift(): lax.ppermute(array, axis, [(i, (i + step) % size) for i in range(size)])]
    all_gather x1, waiting for transfers between devices: 0.01 us -> 6.29 us  [shards(): line = lax.all_gather(hidden, LINE, axis=0)]
    unnamed x33 -> x45, local copies, waits for them, and re-layouts: 8.2 us -> 13 us
    all_to_all x6 -> x5, starting transfers between devices: 36.6 us -> 37 us  [exchange(): return lax.all_to_all(array, axes, split_axis=0, concat_axis=0, tiled=True)]
  transfers between devices with their start and end apart: 16 -> 15, of which waited for: 12 -> 10; matrix products, arithmetic and copies ran while one was open for 4% -> 2% of each run, Pallas kernels for 2% -> 2%
where the time goes in v6:
time: 331 us; the launch traced here: 330 us
  waiting for transfers between devices  114 us (34%)
  blocking collectives  90.9 us (27%)
  starting transfers between devices  68.8 us (21%)
  Pallas kernels  19 us (6%)
  local copies, waits for them, and re-layouts  17.5 us (5%)
  between operations  14.4 us (4%)
  other arithmetic  5.09 us (2%)
    all_to_all x3, blocking collectives, exchange(): return lax.all_to_all(array, axes, split_axis=0, concat_axis=0, tiled=True)  90.9 us
    ppermute x9, waiting for transfers between devices, shift(): lax.ppermute(array, axis, [(i, (i + step) % size) for i in range(size)])  73.2 us
    all_to_all x5, starting transfers between devices, exchange(): return lax.all_to_all(array, axes, split_axis=0, concat_axis=0, tiled=True)  37 us
    all_to_all x5, waiting for transfers between devices, exchange(): return lax.all_to_all(array, axes, split_axis=0, concat_axis=0, tiled=True)  34 us
    ppermute x9, starting transfers between devices, shift(): lax.ppermute(array, axis, [(i, (i + step) % size) for i in range(size)])  31.7 us
    unnamed x45, local copies, waits for them, and re-layouts  13 us
    pallas_call x5, Pallas kernels, call(): pl.pallas_call(kernel, in_specs=[SMEM] * len(scalars) + [VMEM] * len(arra...  11.2 us
  transfers between devices with their start and end apart: 15, of which 10 were waited for; matrix products, arithmetic and copies ran while one was open for 2% of the time, Pallas kernels for 2%

profile of v6, /device:TPU:1, one launch (start us, length us, event | category | flops | bytes accessed | tf_op | source)
XLA Modules:
  0.0 329.9 jit_solution(12260950039581303325)
XLA Ops:
  7.2 0.0 all-gather.3.cloned.1.call-start
  7.2 0.7 all-gather.3.cloned.1.call-update
  7.9 2.4 broadcast_in_dim.28
  10.3 14.0 %all-to-all-start = ((bf16[32,128,256]{2,1,0:T(8,128)(2,1)}), bf16[32,128,256]{2,1,0:T(8,128)(2,1)}, u32[]{:S(2)}, u32[]{:S(2)}) async-start(bf16[32,128,256]{2,1,0:T(8,128)(2,1)} %broadcast_in_dim.28), calls=%async_computation | async-start | bytes 4194304 | tf_op jit(solution)/shard_map/all_to_all | solution.py:41
  24.3 0.1 pad_add_fusion.place
  24.4 0.8 shard_map.93
  25.2 0.0 copy-start.13
  25.2 0.7 copy-done.13
  25.9 4.2 %collective-permute-start = (bf16[14,2,32,256]{3,2,1,0:T(8,128)(2,1)S(1)}, bf16[14,2,32,256]{3,2,1,0:T(8,128)(2,1)S(1)}, u32[]{:S(2)}, u32[]{:S(2)}) collective-permute-start(bf16[14,2,32,256]{3,2,1,0:T(8,128)(2,1)S(1)} %get-tuple-element.33), channel_id=1, source_target_pairs={{0,1},{1,2},{2,3},{3,0},{4,5},{5,6},{6,7},{7,4},{8,9},{9,10},{10,1... | collective-permute-start | bytes 1376264 | tf_op jit(solution)/shard_map/ppermute | solution.py:50
  30.1 3.6 %collective-permute-start.1 = (bf16[14,2,32,256]{3,2,1,0:T(8,128)(2,1)S(1)}, bf16[14,2,32,256]{3,2,1,0:T(8,128)(2,1)S(1)}, u32[]{:S(2)}, u32[]{:S(2)}) collective-permute-start(bf16[14,2,32,256]{3,2,1,0:T(8,128)(2,1)S(1)} %get-tuple-element.34), channel_id=1, source_target_pairs={{0,3},{1,0},{2,1},{3,2},{4,7},{5,4},{6,5},{7,6},{8,11},{9,8},{10,9... | collective-permute-start | bytes 1376264 | tf_op jit(solution)/shard_map/ppermute | solution.py:50
  33.7 24.0 %collective-permute-done.up.refs_1_ = bf16[14,2,32,256]{3,2,1,0:T(8,128)(2,1)S(1)} collective-permute-done((bf16[14,2,32,256]{3,2,1,0:T(8,128)(2,1)S(1)}, bf16[14,2,32,256]{3,2,1,0:T(8,128)(2,1)S(1)}, u32[]{:S(2)}, u32[]{:S(2)}) %collective-permute-start) | collective-permute-done | bytes 458784 | tf_op jit(solution)/shard_map/ppermute | solution.py:50
  57.7 7.7 %collective-permute-done.1.down.refs_2_ = bf16[14,2,32,256]{3,2,1,0:T(8,128)(2,1)S(1)} collective-permute-done((bf16[14,2,32,256]{3,2,1,0:T(8,128)(2,1)S(1)}, bf16[14,2,32,256]{3,2,1,0:T(8,128)(2,1)S(1)}, u32[]{:S(2)}, u32[]{:S(2)}) %collective-permute-start.1) | collective-permute-done | bytes 458784 | tf_op jit(solution)/shard_map/ppermute | solution.py:50
  65.4 6.3 %all-gather.3.cloned.1.call-done = bf16[3584,256]{1,0:T(8,128)(2,1)} async-done(((bf16[448,256]{1,0:T(8,128)(2,1)}), bf16[3584,256]{1,0:T(8,128)(2,1)}) %all-gather.3.cloned.1.call-update) | async-done | bytes 1835024 | tf_op jit(solution)/shard_map/all_gather | solution.py:366
  71.7 3.1 collective-permute-start.2
  74.9 0.8 copy.11
  75.6 1.0 reshape.43
  76.7 0.1 and_select_fusion.source
  76.8 0.0 all-to-all-done
  76.8 1.7 collective-permute-done.2.other
  78.5 2.2 copy-done.1
  80.6 3.7 %shard_map.94 = bf16[32,64,256]{2,1,0:T(8,128)(2,1)} custom-call(s32[2]{0:T(128)S(1)} %pad_add_fusion.place, s32[14]{0:T(128)S(1)} %and_select_fusion.source, bf16[8,448,256]{2,1,0:T(8,128)(2,1)S(1)} %bitcast.12, bf16[8,448,256]{2,1,0:T(8,128)(2,1)S(1)} %collective-permute-done.2.other, bf16[4096,256]{1,0:T(8,128)(2,1)} %bitcast.3.weight), custom_call_target="tpu_custom_call" | custom-call | tf_op jit(solution)/shard_map/pallas_call | solution.py:376
  84.3 9.3 %all-to-all-start.1 = ((bf16[32,64,256]{2,1,0:T(8,128)(2,1)}), bf16[32,64,256]{2,1,0:T(8,128)(2,1)S(1)}, u32[]{:S(2)}, u32[]{:S(2)}) async-start(bf16[32,64,256]{2,1,0:T(8,128)(2,1)} %shard_map.94), calls=%async_computation.1 | async-start | bytes 2097152 | tf_op jit(solution)/shard_map/all_to_all | solution.py:41
  93.7 1.0 pad_maximum_fusion.1
  94.7 4.5 %collective-permute-start.4 = (bf16[14,2,32,256]{3,2,1,0:T(8,128)(2,1)S(1)}, bf16[14,2,32,256]{3,2,1,0:T(8,128)(2,1)S(1)}, u32[]{:S(2)}, u32[]{:S(2)}) collective-permute-start(bf16[14,2,32,256]{3,2,1,0:T(8,128)(2,1)S(1)} %pad_maximum_fusion.1), channel_id=1, source_target_pairs={{0,3},{1,0},{2,1},{3,2},{4,7},{5,4},{6,5},{7,6},{8,11},{9,8},{10,9... | collective-permute-start | bytes 1376264 | tf_op jit(solution)/shard_map/ppermute | solution.py:50
  99.3 2.7 collective-permute-start.3
  102.0 0.2 select_reduce_fusion.target
  102.2 17.9 %collective-permute-done.4.far_down.refs_4_ = bf16[14,2,32,256]{3,2,1,0:T(8,128)(2,1)S(1)} collective-permute-done((bf16[14,2,32,256]{3,2,1,0:T(8,128)(2,1)S(1)}, bf16[14,2,32,256]{3,2,1,0:T(8,128)(2,1)S(1)}, u32[]{:S(2)}, u32[]{:S(2)}) %collective-permute-start.4) | collective-permute-done | bytes 458784 | tf_op jit(solution)/shard_map/ppermute | solution.py:50
  120.1 2.9 collective-permute-done.3.far_up.refs_3_
  123.0 0.8 copy-done.6
  123.8 1.0 copy-done.7
  124.8 1.7 shard_map.95
  126.5 0.0 copy-start.10
  126.5 0.0 copy-start.18
  126.5 37.8 %all_to_all.40.arrived = bf16[32,16,1152]{2,1,0:T(8,128)(2,1)S(1)} all-to-all(bf16[32,16,1152]{2,1,0:T(8,128)(2,1)S(1)} %get-tuple-element.41), channel_id=1, replica_groups=mesh['yl'=2,'co'=2,'dz'=8,'dx'=4,'mp'=4] {'dz','dx'}, dimensions={0} | all-to-all | bytes 2359296 | tf_op jit(solution)/shard_map/all_to_all | solution.py:41
  164.3 1.6 shard_map.96
  165.9 17.9 %all_to_all.41.moved = f32[16,8,128]{2,1,0:T(8,128)S(1)} all-to-all(f32[16,8,128]{2,1,0:T(8,128)S(1)} %broadcast_in_dim.29), channel_id=1, replica_groups=mesh['yl'=2,'co'=2,'dz'=8,'dx'=4,'mp'=4] {'yl','co','mp'}, dimensions={0} | all-to-all | bytes 131072 | tf_op jit(solution)/shard_map/all_to_all | solution.py:41
  183.8 2.5 shard_map.97
  186.3 35.2 %all_to_all.42.arrived = bf16[32,16,1152]{2,1,0:T(8,128)(2,1)S(1)} all-to-all(bf16[32,16,1152]{2,1,0:T(8,128)(2,1)S(1)} %get-tuple-element.46), channel_id=1, replica_groups=mesh['yl'=2,'co'=2,'dz'=8,'dx'=4,'mp'=4] {'dz','dx'}, dimensions={0} | all-to-all | bytes 2359296 | tf_op jit(solution)/shard_map/all_to_all | solution.py:41
  221.5 3.1 shard_map.98
  224.6 1.0 copy-done.9
  225.5 0.8 copy-done.11
  226.3 0.7 copy-done.14
  227.0 0.7 copy-done.16
  227.7 0.8 copy-done.19
  228.5 0.8 copy-done.20
  229.2 4.1 %all-to-all-start.5 = ((bf16[32,64,256]{2,1,0:T(8,128)(2,1)}), bf16[32,64,256]{2,1,0:T(8,128)(2,1)S(1)}, u32[]{:S(2)}, u32[]{:S(2)}) async-start(bf16[32,64,256]{2,1,0:T(8,128)(2,1)} %copy-done.9), calls=%async_computation.5 | async-start | bytes 2097152 | tf_op jit(solution)/shard_map/all_to_all | solution.py:41
  233.3 1.9 collective-permute-start.5
  235.2 4.3 %collective-permute-start.6 = (bf16[14,2,32,256]{3,2,1,0:T(8,128)(2,1)}, bf16[14,2,32,256]{3,2,1,0:T(8,128)(2,1)}, u32[]{:S(2)}, u32[]{:S(2)}) collective-permute-start(bf16[14,2,32,256]{3,2,1,0:T(8,128)(2,1)} %copy-done.19), channel_id=1, source_target_pairs={{0,1},{1,2},{2,3},{3,0},{4,5},{5,6},{6,7},{7,4},{8,9},{9,10},{10,1... | collective-permute-start | bytes 1376264 | tf_op jit(solution)/shard_map/ppermute | solution.py:50
  239.5 19.4 %all-to-all-done.5.arrived = bf16[32,64,256]{2,1,0:T(8,128)(2,1)S(1)} async-done(((bf16[32,64,256]{2,1,0:T(8,128)(2,1)}), bf16[32,64,256]{2,1,0:T(8,128)(2,1)S(1)}, u32[]{:S(2)}, u32[]{:S(2)}) %all-to-all-start.5) | async-done | bytes 1048608 | tf_op jit(solution)/shard_map/all_to_all | solution.py:41
  258.9 1.5 copy-done.4
  260.4 2.4 shard_map.99
  262.8 1.4 copy-done.5
  264.2 4.6 %all-to-all-start.6 = ((bf16[32,128,256]{2,1,0:T(8,128)(2,1)}), bf16[32,128,256]{2,1,0:T(8,128)(2,1)}, u32[]{:S(2)}, u32[]{:S(2)}) async-start(bf16[32,128,256]{2,1,0:T(8,128)(2,1)} %bitcast.14), calls=%async_computation.6 | async-start | bytes 4194304 | tf_op jit(solution)/shard_map/all_to_all | solution.py:41
  268.8 1.0 slice.15
  269.9 2.4 collective-permute-start.8
  272.3 0.1 pad_maximum_fusion.2
  272.4 5.0 %collective-permute-start.7 = (bf16[14,2,32,256]{3,2,1,0:T(8,128)(2,1)S(1)}, bf16[14,2,32,256]{3,2,1,0:T(8,128)(2,1)S(1)}, u32[]{:S(2)}, u32[]{:S(2)}) collective-permute-start(bf16[14,2,32,256]{3,2,1,0:T(8,128)(2,1)S(1)} %pad_maximum_fusion.2), channel_id=1, source_target_pairs={{0,3},{1,0},{2,1},{3,2},{4,7},{5,4},{6,5},{7,6},{8,11},{9,8},{10,9... | collective-permute-start | bytes 1376264 | tf_op jit(solution)/shard_map/ppermute | solution.py:50
  277.4 13.5 %collective-permute-done.8.far_down = bf16[14,2,32,256]{3,2,1,0:T(8,128)(2,1)S(1)} collective-permute-done((bf16[14,2,32,256]{3,2,1,0:T(8,128)(2,1)S(1)}, bf16[14,2,32,256]{3,2,1,0:T(8,128)(2,1)S(1)}, u32[]{:S(2)}, u32[]{:S(2)}) %collective-permute-start.8) | collective-permute-done | bytes 458784 | tf_op jit(solution)/shard_map/ppermute | solution.py:50
  290.8 5.5 %collective-permute-done.7.far_up = bf16[14,2,32,256]{3,2,1,0:T(8,128)(2,1)S(1)} collective-permute-done((bf16[14,2,32,256]{3,2,1,0:T(8,128)(2,1)S(1)}, bf16[14,2,32,256]{3,2,1,0:T(8,128)(2,1)S(1)}, u32[]{:S(2)}, u32[]{:S(2)}) %collective-permute-start.7) | collective-permute-done | bytes 458784 | tf_op jit(solution)/shard_map/ppermute | solution.py:50
  296.4 2.9 reduce_sum.34
  299.3 5.1 %all-to-all-start.7 = ((bf16[8,128,256]{2,1,0:T(8,128)(2,1)}), bf16[8,128,256]{2,1,0:T(8,128)(2,1)S(1)}, u32[]{:S(2)}, u32[]{:S(2)}) async-start(bf16[8,128,256]{2,1,0:T(8,128)(2,1)} %reduce_sum.34), calls=%async_computation.7 | async-start | bytes 1048576 | tf_op jit(solution)/shard_map/all_to_all | solution.py:41
  304.4 3.4 %shard_map.100 = bf16[14,2,32,1024]{3,2,1,0:T(8,128)(2,1)} custom-call(s32[2]{0:T(128)S(1)} %pad_add_fusion.place, bf16[14,2,32,256]{3,2,1,0:T(8,128)(2,1)S(1)} %copy-done.12, bf16[14,2,32,256]{3,2,1,0:T(8,128)(2,1)S(1)} %collective-permute-done.5.up, bf16[14,2,32,256]{3,2,1,0:T(8,128)(2,1)} %collective-permute-done.6.down, ...), custom_call_target="tpu_custom_call" | custom-call | tf_op jit(solution)/shard_map/pallas_call | solution.py:325
  307.7 14.6 %all-to-all-done.7 = bf16[8,128,256]{2,1,0:T(8,128)(2,1)S(1)} async-done(((bf16[8,128,256]{2,1,0:T(8,128)(2,1)}), bf16[8,128,256]{2,1,0:T(8,128)(2,1)S(1)}, u32[]{:S(2)}, u32[]{:S(2)}) %all-to-all-start.7) | async-done | bytes 524320 | tf_op jit(solution)/shard_map/all_to_all | solution.py:41
  322.3 0.7 reduce_sum.35
  (41 shorter events, 0.2 us)
Async XLA Ops:
  7.2 64.5 %all-gather.3.cloned.1.call-start = ((), (), s32[]{:S(2)}) async-start(), calls=%async_computation.8 | async-start | bytes 2064384 | tf_op jit(solution)/shard_map/all_gather | solution.py:366
  10.3 14.1 %copy-start = (bf16[14,2,32,1024]{3,2,1,0:T(8,128)(2,1)S(1)}, bf16[14,2,32,1024]{3,2,1,0:T(8,128)(2,1)}, u32[]{:S(2)}) copy-start(bf16[14,2,32,1024]{3,2,1,0:T(8,128)(2,1)} %block3.1) | copy-start | bytes 5505028
  10.3 66.5 %all-to-all-start = ((bf16[32,128,256]{2,1,0:T(8,128)(2,1)}), bf16[32,128,256]{2,1,0:T(8,128)(2,1)}, u32[]{:S(2)}, u32[]{:S(2)}) async-start(bf16[32,128,256]{2,1,0:T(8,128)(2,1)} %broadcast_in_dim.28), calls=%async_computation | async-start | bytes 4194304 | tf_op jit(solution)/shard_map/all_to_all | solution.py:41
  24.4 50.5 %copy-start.21 = (s32[224,2]{0,1:T(2,128)S(1)}, s32[224,2]{0,1:T(2,128)}, u32[]{:S(2)}) copy-start(s32[224,2]{0,1:T(2,128)} %param.9) | copy-start | bytes 5380
  25.2 0.7 copy-start.13
  25.9 31.8 %collective-permute-start = (bf16[14,2,32,256]{3,2,1,0:T(8,128)(2,1)S(1)}, bf16[14,2,32,256]{3,2,1,0:T(8,128)(2,1)S(1)}, u32[]{:S(2)}, u32[]{:S(2)}) collective-permute-start(bf16[14,2,32,256]{3,2,1,0:T(8,128)(2,1)S(1)} %get-tuple-element.33), channel_id=1, source_target_pairs={{0,1},{1,2},{2,3},{3,0},{4,5},{5,6},{6,7},{7,4},{8,9},{9,10},{10,1... | collective-permute-start | bytes 1376264 | tf_op jit(solution)/shard_map/ppermute | solution.py:50
  30.1 35.3 %collective-permute-start.1 = (bf16[14,2,32,256]{3,2,1,0:T(8,128)(2,1)S(1)}, bf16[14,2,32,256]{3,2,1,0:T(8,128)(2,1)S(1)}, u32[]{:S(2)}, u32[]{:S(2)}) collective-permute-start(bf16[14,2,32,256]{3,2,1,0:T(8,128)(2,1)S(1)} %get-tuple-element.34), channel_id=1, source_target_pairs={{0,3},{1,0},{2,1},{3,2},{4,7},{5,4},{6,5},{7,6},{8,11},{9,8},{10,9... | collective-permute-start | bytes 1376264 | tf_op jit(solution)/shard_map/ppermute | solution.py:50
  71.7 6.7 %collective-permute-start.2 = (bf16[8,448,256]{2,1,0:T(8,128)(2,1)}, bf16[8,448,256]{2,1,0:T(8,128)(2,1)S(1)}, u32[]{:S(2)}, u32[]{:S(2)}) collective-permute-start(bf16[8,448,256]{2,1,0:T(8,128)(2,1)} %bitcast.11), channel_id=1, source_target_pairs={{0,128},{128,0},{1,129},{129,1},{2,130},{130,2},{3,131},{131,3},{4... | collective-permute-start | bytes 5505032 | tf_op jit(solution)/shard_map/ppermute | solution.py:50
  78.4 5.9 %copy-start.3 = (bf16[8,448,256]{2,1,0:T(8,128)(2,1)}, bf16[8,448,256]{2,1,0:T(8,128)(2,1)S(1)}, u32[]{:S(2)}) copy-start(bf16[8,448,256]{2,1,0:T(8,128)(2,1)S(1)} %collective-permute-done.2.other) | copy-start | bytes 5505028
  78.4 2.2 copy-start.1
  84.3 39.5 %all-to-all-start.1 = ((bf16[32,64,256]{2,1,0:T(8,128)(2,1)}), bf16[32,64,256]{2,1,0:T(8,128)(2,1)S(1)}, u32[]{:S(2)}, u32[]{:S(2)}) async-start(bf16[32,64,256]{2,1,0:T(8,128)(2,1)} %shard_map.94), calls=%async_computation.1 | async-start | bytes 2097152 | tf_op jit(solution)/shard_map/all_to_all | solution.py:41
  94.7 25.4 %collective-permute-start.4 = (bf16[14,2,32,256]{3,2,1,0:T(8,128)(2,1)S(1)}, bf16[14,2,32,256]{3,2,1,0:T(8,128)(2,1)S(1)}, u32[]{:S(2)}, u32[]{:S(2)}) collective-permute-start(bf16[14,2,32,256]{3,2,1,0:T(8,128)(2,1)S(1)} %pad_maximum_fusion.1), channel_id=1, source_target_pairs={{0,3},{1,0},{2,1},{3,2},{4,7},{5,4},{6,5},{7,6},{8,11},{9,8},{10,9... | collective-permute-start | bytes 1376264 | tf_op jit(solution)/shard_map/ppermute | solution.py:50
  99.3 23.8 %collective-permute-start.3 = (bf16[14,2,32,256]{3,2,1,0:T(8,128)(2,1)S(1)}, bf16[14,2,32,256]{3,2,1,0:T(8,128)(2,1)S(1)}, u32[]{:S(2)}, u32[]{:S(2)}) collective-permute-start(bf16[14,2,32,256]{3,2,1,0:T(8,128)(2,1)S(1)} %pad_maximum_fusion), channel_id=1, source_target_pairs={{0,1},{1,2},{2,3},{3,0},{4,5},{5,6},{6,7},{7,4},{8,9},{9,10},{10,1... | collective-permute-start | bytes 1376264 | tf_op jit(solution)/shard_map/ppermute | solution.py:50
  123.0 0.8 copy-start.6
  123.8 1.0 copy-start.7
  126.5 37.8 %copy-start.10 = (bf16[448,256]{1,0:T(8,128)(2,1)S(1)}, bf16[448,256]{1,0:T(8,128)(2,1)}, u32[]{:S(2)}) copy-start(bf16[448,256]{1,0:T(8,128)(2,1)} %d_mixed.3) | copy-start | bytes 688132
  126.5 37.8 %copy-start.18 = (f32[256]{0:T(256)S(1)}, f32[256]{0:T(256)}, u32[]{:S(2)}) copy-start(f32[256]{0:T(256)} %param.10) | copy-start | bytes 3076
  165.9 55.6 %copy-start.8 = (bf16[14,2,32,256]{3,2,1,0:T(8,128)(2,1)S(1)}, bf16[14,2,32,256]{3,2,1,0:T(8,128)(2,1)}, u32[]{:S(2)}) copy-start(bf16[14,2,32,256]{3,2,1,0:T(8,128)(2,1)} %copy-done.6) | copy-start | bytes 1376260
  224.6 1.0 copy-start.9
  225.5 0.8 copy-start.11
  226.3 0.7 copy-start.14
  227.0 0.7 copy-start.16
  227.7 0.8 copy-start.19
  228.5 0.8 copy-start.20
  229.2 29.7 %copy-start.2 = (bf16[3584,256]{1,0:T(8,128)(2,1)S(1)}, bf16[3584,256]{1,0:T(8,128)(2,1)}, u32[]{:S(2)}) copy-start(bf16[3584,256]{1,0:T(8,128)(2,1)} %all-gather.3.cloned.1.call-done) | copy-start | bytes 5505028
  229.2 29.7 %all-to-all-start.5 = ((bf16[32,64,256]{2,1,0:T(8,128)(2,1)}), bf16[32,64,256]{2,1,0:T(8,128)(2,1)S(1)}, u32[]{:S(2)}, u32[]{:S(2)}) async-start(bf16[32,64,256]{2,1,0:T(8,128)(2,1)} %copy-done.9), calls=%async_computation.5 | async-start | bytes 2097152 | tf_op jit(solution)/shard_map/all_to_all | solution.py:41
  233.3 30.9 %collective-permute-start.5 = (bf16[14,2,32,256]{3,2,1,0:T(8,128)(2,1)}, bf16[14,2,32,256]{3,2,1,0:T(8,128)(2,1)S(1)}, u32[]{:S(2)}, u32[]{:S(2)}) collective-permute-start(bf16[14,2,32,256]{3,2,1,0:T(8,128)(2,1)} %copy-done.20), channel_id=1, source_target_pairs={{0,3},{1,0},{2,1},{3,2},{4,7},{5,4},{6,5},{7,6},{8,11},{9,8},{10,9... | collective-permute-start | bytes 1376264 | tf_op jit(solution)/shard_map/ppermute | solution.py:50
  235.2 29.0 %collective-permute-start.6 = (bf16[14,2,32,256]{3,2,1,0:T(8,128)(2,1)}, bf16[14,2,32,256]{3,2,1,0:T(8,128)(2,1)}, u32[]{:S(2)}, u32[]{:S(2)}) collective-permute-start(bf16[14,2,32,256]{3,2,1,0:T(8,128)(2,1)} %copy-done.19), channel_id=1, source_target_pairs={{0,1},{1,2},{2,3},{3,0},{4,5},{5,6},{6,7},{7,4},{8,9},{9,10},{10,1... | collective-permute-start | bytes 1376264 | tf_op jit(solution)/shard_map/ppermute | solution.py:50
  258.9 1.5 copy-start.4
  262.8 1.4 copy-start.5
  264.2 5.7 %copy-start.17 = (bf16[14,32,256]{2,1,0:T(8,128)(2,1)S(1)}, bf16[14,32,256]{2,1,0:T(8,128)(2,1)}, u32[]{:S(2)}) copy-start(bf16[14,32,256]{2,1,0:T(8,128)(2,1)} %copy-done.16) | copy-start | bytes 688132
  264.2 32.2 %all-to-all-start.6 = ((bf16[32,128,256]{2,1,0:T(8,128)(2,1)}), bf16[32,128,256]{2,1,0:T(8,128)(2,1)}, u32[]{:S(2)}, u32[]{:S(2)}) async-start(bf16[32,128,256]{2,1,0:T(8,128)(2,1)} %bitcast.14), calls=%async_computation.6 | async-start | bytes 4194304 | tf_op jit(solution)/shard_map/all_to_all | solution.py:41
  268.8 3.5 %copy-start.15 = (bf16[14,32,256]{2,1,0:T(8,128)(2,1)S(1)}, bf16[14,32,256]{2,1,0:T(8,128)(2,1)}, u32[]{:S(2)}) copy-start(bf16[14,32,256]{2,1,0:T(8,128)(2,1)} %copy-done.14) | copy-start | bytes 688132
  269.9 20.9 %collective-permute-start.8 = (bf16[14,2,32,256]{3,2,1,0:T(8,128)(2,1)S(1)}, bf16[14,2,32,256]{3,2,1,0:T(8,128)(2,1)S(1)}, u32[]{:S(2)}, u32[]{:S(2)}) collective-permute-start(bf16[14,2,32,256]{3,2,1,0:T(8,128)(2,1)S(1)} %pad_maximum_fusion.3), channel_id=1, source_target_pairs={{0,1},{1,2},{2,3},{3,0},{4,5},{5,6},{6,7},{7,4},{8,9},{9,10},{10,1... | collective-permute-start | bytes 1376264 | tf_op jit(solution)/shard_map/ppermute | solution.py:50
  272.4 24.0 %collective-permute-start.7 = (bf16[14,2,32,256]{3,2,1,0:T(8,128)(2,1)S(1)}, bf16[14,2,32,256]{3,2,1,0:T(8,128)(2,1)S(1)}, u32[]{:S(2)}, u32[]{:S(2)}) collective-permute-start(bf16[14,2,32,256]{3,2,1,0:T(8,128)(2,1)S(1)} %pad_maximum_fusion.2), channel_id=1, source_target_pairs={{0,3},{1,0},{2,1},{3,2},{4,7},{5,4},{6,5},{7,6},{8,11},{9,8},{10,9... | collective-permute-start | bytes 1376264 | tf_op jit(solution)/shard_map/ppermute | solution.py:50
  296.4 8.0 %copy-start.12 = (bf16[14,2,32,256]{3,2,1,0:T(8,128)(2,1)S(1)}, bf16[14,2,32,256]{3,2,1,0:T(8,128)(2,1)}, u32[]{:S(2)}) copy-start(bf16[14,2,32,256]{3,2,1,0:T(8,128)(2,1)} %copy-done.11) | copy-start | bytes 1376260
  299.3 23.1 %all-to-all-start.7 = ((bf16[8,128,256]{2,1,0:T(8,128)(2,1)}), bf16[8,128,256]{2,1,0:T(8,128)(2,1)S(1)}, u32[]{:S(2)}, u32[]{:S(2)}) async-start(bf16[8,128,256]{2,1,0:T(8,128)(2,1)} %reduce_sum.34), calls=%async_computation.7 | async-start | bytes 1048576 | tf_op jit(solution)/shard_map/all_to_all | solution.py:41
Sparse Core Ops, SparseCore 0:
  10.1 61.5 all-gather.2

commit v7 on v6

--- a/solution.py
+++ b/solution.py
@@ -27,13 +27,13 @@
 PLAIN = (((1,), (0,)), ((), ()))
 
 
-def call(kernel, scalars, arrays, outs):
+def call(kernel, scalars, arrays, outs, params=PARAMS):
     return pl.pallas_call(
         kernel,
         in_specs=[SMEM] * len(scalars) + [VMEM] * len(arrays),
         out_specs=[VMEM] * len(outs),
         out_shape=[jax.ShapeDtypeStruct(shape, kind) for shape, kind in outs],
-        compiler_params=PARAMS,
+        compiler_params=params,
     )(*scalars, *arrays)
 
 
@@ -110,20 +110,18 @@
     return jnp.sum(jnp.where(index < count, tile, 0.0), axis=0, keepdims=True)
 
 
-def split_kernel(place, block0, block1, block2, block3, own, up, down, first, last):
+def split_kernel(place, block0, block1, block2, block3, own, first, last, far_keys, far_values):
     own[...] = block0[...]
-    up[:, 0] = block1[:, 0]
-    up[:, 1] = block2[:, 0]
-    down[:, 0] = block3[:, 0]
-    down[:, 1] = block2[:, 1]
-    first[...] = block1[:, 1]
-    last[...] = block3[:, 1]
-
-
-def whole_rows(n, own, up, down, far_up, far_down):
+    first[...] = block1[...]
+    last[...] = block3[...]
+    far_keys[...] = block2[:, 0]
+    far_values[...] = block2[:, 1]
+
+
+def whole_rows(n, own, up, down):
     return [
-        jnp.concatenate([own[n, 0], up[n, 0], far_up[n, 1], down[n, 0]], axis=0),
-        jnp.concatenate([own[n, 1], far_up[n, 0], far_down[n, 1], far_down[n, 0]], axis=0),
+        jnp.concatenate([own[n, 0], up[n, 0], up[n, 2], down[n, 0]], axis=0),
+        jnp.concatenate([own[n, 1], up[n, 1], down[n, 2], down[n, 1]], axis=0),
     ]
 
 
@@ -152,10 +150,10 @@
         slots[source[k]] = total[c * GROUP_LEN : (c + 1) * GROUP_LEN].astype(BF)
 
 
-def owner_forward_kernel(target, arrived, own, up, down, far_up, far_down, slots, probs):
+def owner_forward_kernel(target, arrived, own, up, down, slots, probs):
     for n in range(target.shape[0]):
         t = target[n]
-        keys, values = whole_rows(n, own, up, down, far_up, far_down)
+        keys, values = whole_rows(n, own, up, down)
         scores = dot(keys, by_head(arrived[t]), LAST) * SCALE
         top = jnp.max(scores, axis=0, keepdims=True)
         expo = jnp.exp(scores - top)
@@ -233,7 +231,7 @@
 
 
 def owner_backward_kernel(target, arrived, queries, probs, *refs):
-    kv_refs, (slots, own, up, down, first, last) = refs[:5], refs[5:]
+    kv_refs, (slots, own, up, down, first, last) = refs[:3], refs[3:]
     for n in range(target.shape[0]):
         t = target[n]
         keys, values = whole_rows(n, *kv_refs)
@@ -364,14 +362,13 @@
     source = lax.dynamic_slice_in_dim(flat_ids, me_dp * neigh_dev, neigh_dev) // neigh_dev
 
     line = lax.all_gather(hidden, LINE, axis=0)
-    own, up, down, first, last = split_by_quarter(place, kv_enc)
+    own, first, last, far_keys, far_values = split_by_quarter(place, kv_enc)
     weight = exchange(copies(wq, n_dp), DP).reshape(-1, dec_width)
-    up, down = shift(up, "mp", 1), shift(down, "mp", -1)
+    up = jnp.concatenate([first, shift(far_keys, "mp", 1)[:, None]], axis=1)
+    down = jnp.concatenate([last, shift(far_values, "mp", -1)[:, None]], axis=1)
     line, up, down = lax.optimization_barrier((line, up, down))
     other = shift(line, "co", 1)
-    far_up = shift(second_step(first, up), "mp", 1)
-    far_down = shift(second_step(last, down), "mp", -1)
-    kv = (own, up, down, far_up, far_down)
+    kv = (own, shift(up, "mp", 1), shift(down, "mp", -1))
 
     (slots,) = pl.pallas_call(
         functools.partial(query_kernel, sizes),
@@ -411,7 +408,9 @@
         (target,),
         (arrived, queries, probs, *kv),
         [((n_dp, GROUP_LEN, dec_width), BF)]
-        + [(x.shape, BF) for x in (own, up, down, first, last)],
+        + [(own.shape, BF)] * 3
+        + [(far_keys.shape, BF)] * 2,
+        pltpu.CompilerParams(vmem_limit_bytes=60 << 20),
     )
     up, down = shift(up, "mp", -1), shift(down, "mp", 1)
     arrived = exchange(slots, DP)

time: 331 us -> 332 us (level)
  local copies, waits for them, and re-layouts: 17.5 us -> 11.1 us
  Pallas kernels: 19 us -> 22.4 us
    ppermute x9, waiting for transfers between devices: 73.2 us -> 64.9 us  [shift(): lax.ppermute(array, axis, [(i, (i + step) % size) for i in range(size)])]
    all_gather x1, waiting for transfers between devices: 6.29 us -> 12.5 us  [shards(): line = lax.all_gather(hidden, LINE, axis=0)]
    unnamed x45 -> x39, local copies, waits for them, and re-layouts: 13 us -> 7.5 us
    pallas_call x5, Pallas kernels: 11.2 us -> 14.6 us  [call(): pl.pallas_call(kernel, in_specs=[SMEM] * len(scalars) + [VMEM] * len(arra...]
where the time goes in v7:
time: 332 us; the launch traced here: 329 us
  waiting for transfers between devices  113 us (34%)
  blocking collectives  92.1 us (28%)
  starting transfers between devices  69.3 us (21%)
  Pallas kernels  22.4 us (7%)
  between operations  14.3 us (4%)
  local copies, waits for them, and re-layouts  11.1 us (3%)
  other arithmetic  5.93 us (2%)
    all_to_all x3, blocking collectives, exchange(): return lax.all_to_all(array, axes, split_axis=0, concat_axis=0, tiled=True)  92.1 us
    ppermute x9, waiting for transfers between devices, shift(): lax.ppermute(array, axis, [(i, (i + step) % size) for i in range(size)])  64.9 us
    all_to_all x5, waiting for transfers between devices, exchange(): return lax.all_to_all(array, axes, split_axis=0, concat_axis=0, tiled=True)  35.3 us
    all_to_all x5, starting transfers between devices, exchange(): return lax.all_to_all(array, axes, split_axis=0, concat_axis=0, tiled=True)  35 us
    ppermute x9, starting transfers between devices, shift(): lax.ppermute(array, axis, [(i, (i + step) % size) for i in range(size)])  34.2 us
    pallas_call x5, Pallas kernels, call(): pl.pallas_call(kernel, in_specs=[SMEM] * len(scalars) + [VMEM] * len(arra...  14.6 us
    all_gather x1, waiting for transfers between devices, shards(): line = lax.all_gather(hidden, LINE, axis=0)  12.5 us
    unnamed x39, local copies, waits for them, and re-layouts  7.5 us
  transfers between devices with their start and end apart: 15, of which 10 were waited for; matrix products, arithmetic and copies ran while one was open for 2% of the time, Pallas kernels for 2%

profile of v7, /device:TPU:1, one launch (start us, length us, event | category | flops | bytes accessed | tf_op | source)
XLA Modules:
  0.0 328.5 jit_solution(14619102644002078030)
XLA Ops:
  7.2 0.0 all-gather.3.cloned.1.call-start
  7.2 0.7 all-gather.3.cloned.1.call-update
  7.9 2.4 broadcast_in_dim.36
  10.3 14.0 %all-to-all-start = ((bf16[32,128,256]{2,1,0:T(8,128)(2,1)}), bf16[32,128,256]{2,1,0:T(8,128)(2,1)}, u32[]{:S(2)}, u32[]{:S(2)}) async-start(bf16[32,128,256]{2,1,0:T(8,128)(2,1)} %broadcast_in_dim.36), calls=%async_computation | async-start | bytes 4194304 | tf_op jit(solution)/shard_map/all_to_all | solution.py:41
  24.3 0.1 pad_add_fusion.place
  24.4 0.0 copy-done
  24.4 0.8 shard_map.93
  25.2 0.0 copy-start.9
  25.2 0.0 copy-start.18
  25.2 4.3 %collective-permute-start = (bf16[14,32,256]{2,1,0:T(8,128)(2,1)S(1)}, bf16[14,32,256]{2,1,0:T(8,128)(2,1)S(1)}, u32[]{:S(2)}, u32[]{:S(2)}) collective-permute-start(bf16[14,32,256]{2,1,0:T(8,128)(2,1)S(1)} %get-tuple-element.34), channel_id=1, source_target_pairs={{0,1},{1,2},{2,3},{3,0},{4,5},{5,6},{6,7},{7,4},{8,9},{9,10},{10,1... | collective-permute-start | bytes 688136 | tf_op jit(solution)/shard_map/ppermute | solution.py:50
  29.5 3.6 %collective-permute-start.1 = (bf16[14,32,256]{2,1,0:T(8,128)(2,1)S(1)}, bf16[14,32,256]{2,1,0:T(8,128)(2,1)S(1)}, u32[]{:S(2)}, u32[]{:S(2)}) collective-permute-start(bf16[14,32,256]{2,1,0:T(8,128)(2,1)S(1)} %get-tuple-element.36), channel_id=1, source_target_pairs={{0,3},{1,0},{2,1},{3,2},{4,7},{5,4},{6,5},{7,6},{8,11},{9,8},{10,9... | collective-permute-start | bytes 688136 | tf_op jit(solution)/shard_map/ppermute | solution.py:50
  33.1 8.5 %collective-permute-done = bf16[14,32,256]{2,1,0:T(8,128)(2,1)S(1)} collective-permute-done((bf16[14,32,256]{2,1,0:T(8,128)(2,1)S(1)}, bf16[14,32,256]{2,1,0:T(8,128)(2,1)S(1)}, u32[]{:S(2)}, u32[]{:S(2)}) %collective-permute-start) | collective-permute-done | bytes 229408 | tf_op jit(solution)/shard_map/ppermute | solution.py:50
  41.6 0.9 pad_maximum_fusion
  42.6 7.6 %collective-permute-done.1 = bf16[14,32,256]{2,1,0:T(8,128)(2,1)S(1)} collective-permute-done((bf16[14,32,256]{2,1,0:T(8,128)(2,1)S(1)}, bf16[14,32,256]{2,1,0:T(8,128)(2,1)S(1)}, u32[]{:S(2)}, u32[]{:S(2)}) %collective-permute-start.1) | collective-permute-done | bytes 229408 | tf_op jit(solution)/shard_map/ppermute | solution.py:50
  50.2 0.9 pad_maximum_fusion.1
  51.1 12.5 %all-gather.3.cloned.1.call-done = bf16[3584,256]{1,0:T(8,128)(2,1)} async-done(((bf16[448,256]{1,0:T(8,128)(2,1)}), bf16[3584,256]{1,0:T(8,128)(2,1)}) %all-gather.3.cloned.1.call-update) | async-done | bytes 1835024 | tf_op jit(solution)/shard_map/all_gather | solution.py:364
  63.7 5.3 %collective-permute-start.2 = (bf16[8,448,256]{2,1,0:T(8,128)(2,1)}, bf16[8,448,256]{2,1,0:T(8,128)(2,1)S(1)}, u32[]{:S(2)}, u32[]{:S(2)}) collective-permute-start(bf16[8,448,256]{2,1,0:T(8,128)(2,1)} %bitcast.11), channel_id=1, source_target_pairs={{0,128},{128,0},{1,129},{129,1},{2,130},{130,2},{3,131},{131,3},{4... | collective-permute-start | bytes 5505032 | tf_op jit(solution)/shard_map/ppermute | solution.py:50
  69.0 0.1 copy.11
  69.1 0.1 reshape.43
  69.2 0.1 and_select_fusion.source
  69.3 3.4 %all-to-all-done = bf16[32,128,256]{2,1,0:T(8,128)(2,1)} async-done(((bf16[32,128,256]{2,1,0:T(8,128)(2,1)}), bf16[32,128,256]{2,1,0:T(8,128)(2,1)}, u32[]{:S(2)}, u32[]{:S(2)}) %all-to-all-start) | async-done | bytes 2097184 | tf_op jit(solution)/shard_map/all_to_all | solution.py:41
  72.7 0.0 collective-permute-done.2.other
  72.8 2.2 copy-done.2
  74.9 3.7 %shard_map.94 = bf16[32,64,256]{2,1,0:T(8,128)(2,1)} custom-call(s32[2]{0:T(128)S(1)} %pad_add_fusion.place, s32[14]{0:T(128)S(1)} %and_select_fusion.source, bf16[8,448,256]{2,1,0:T(8,128)(2,1)S(1)} %bitcast.12, bf16[8,448,256]{2,1,0:T(8,128)(2,1)S(1)} %collective-permute-done.2.other, bf16[4096,256]{1,0:T(8,128)(2,1)} %bitcast.5.weight), custom_call_target="tpu_custom_call" | custom-call | tf_op jit(solution)/shard_map/pallas_call | solution.py:373
  78.6 8.9 %all-to-all-start.1 = ((bf16[32,64,256]{2,1,0:T(8,128)(2,1)}), bf16[32,64,256]{2,1,0:T(8,128)(2,1)S(1)}, u32[]{:S(2)}, u32[]{:S(2)}) async-start(bf16[32,64,256]{2,1,0:T(8,128)(2,1)} %shard_map.94), calls=%async_computation.1 | async-start | bytes 2097152 | tf_op jit(solution)/shard_map/all_to_all | solution.py:41
  87.6 3.0 collective-permute-start.3
  90.6 4.4 %collective-permute-start.4 = (bf16[14,3,32,256]{3,2,1,0:T(8,128)(2,1)}, bf16[14,3,32,256]{3,2,1,0:T(8,128)(2,1)S(1)}, u32[]{:S(2)}, u32[]{:S(2)}) collective-permute-start(bf16[14,3,32,256]{3,2,1,0:T(8,128)(2,1)} %pad_maximum_fusion.1), channel_id=1, source_target_pairs={{0,3},{1,0},{2,1},{3,2},{4,7},{5,4},{6,5},{7,6},{8,11},{9,8},{10,9... | collective-permute-start | bytes 2064392 | tf_op jit(solution)/shard_map/ppermute | solution.py:50
  95.0 0.2 select_reduce_fusion.target
  95.2 21.5 %collective-permute-done.3.up.refs_1_ = bf16[14,3,32,256]{3,2,1,0:T(8,128)(2,1)S(1)} collective-permute-done((bf16[14,3,32,256]{3,2,1,0:T(8,128)(2,1)}, bf16[14,3,32,256]{3,2,1,0:T(8,128)(2,1)S(1)}, u32[]{:S(2)}, u32[]{:S(2)}) %collective-permute-start.3) | collective-permute-done | bytes 688160 | tf_op jit(solution)/shard_map/ppermute | solution.py:50
  116.7 8.9 %collective-permute-done.4.down.refs_2_ = bf16[14,3,32,256]{3,2,1,0:T(8,128)(2,1)S(1)} collective-permute-done((bf16[14,3,32,256]{3,2,1,0:T(8,128)(2,1)}, bf16[14,3,32,256]{3,2,1,0:T(8,128)(2,1)S(1)}, u32[]{:S(2)}, u32[]{:S(2)}) %collective-permute-start.4) | collective-permute-done | bytes 688160 | tf_op jit(solution)/shard_map/ppermute | solution.py:50
  125.7 0.0 all-to-all-done.1.arrived.queries
  125.7 1.7 shard_map.95
  127.4 0.9 copy-done.10
  128.3 40.2 %all_to_all.40.arrived = bf16[32,16,1152]{2,1,0:T(8,128)(2,1)S(1)} all-to-all(bf16[32,16,1152]{2,1,0:T(8,128)(2,1)S(1)} %get-tuple-element.41), channel_id=1, replica_groups=mesh['yl'=2,'co'=2,'dz'=8,'dx'=4,'mp'=4] {'dz','dx'}, dimensions={0} | all-to-all | bytes 2359296 | tf_op jit(solution)/shard_map/all_to_all | solution.py:41
  168.5 0.0 copy-done.13
  168.5 0.0 copy-done.7
  168.5 1.6 shard_map.96
  170.1 15.7 %all_to_all.41.moved = f32[16,8,128]{2,1,0:T(8,128)S(1)} all-to-all(f32[16,8,128]{2,1,0:T(8,128)S(1)} %broadcast_in_dim.37), channel_id=1, replica_groups=mesh['yl'=2,'co'=2,'dz'=8,'dx'=4,'mp'=4] {'yl','co','mp'}, dimensions={0} | all-to-all | bytes 131072 | tf_op jit(solution)/shard_map/all_to_all | solution.py:41
  185.8 2.5 shard_map.97
  188.3 36.2 %all_to_all.42.arrived = bf16[32,16,1152]{2,1,0:T(8,128)(2,1)} all-to-all(bf16[32,16,1152]{2,1,0:T(8,128)(2,1)S(1)} %get-tuple-element.46), channel_id=1, replica_groups=mesh['yl'=2,'co'=2,'dz'=8,'dx'=4,'mp'=4] {'dz','dx'}, dimensions={0} | all-to-all | bytes 2359296 | tf_op jit(solution)/shard_map/all_to_all | solution.py:41
  224.5 6.5 %shard_map.98 = (bf16[32,64,256]{2,1,0:T(8,128)(2,1)}, bf16[14,2,32,256]{3,2,1,0:T(8,128)(2,1)}, bf16[14,2,32,256]{3,2,1,0:T(8,128)(2,1)}, bf16[14,2,32,256]{3,2...) custom-call(s32[14]{0:T(128)} %copy-done.13, bf16[32,16,1152]{2,1,0:T(8,128)(2,1)} %all_to_all.42.arrived, ...), custom_call_target="tpu_custom_call" | custom-call | tf_op jit(solution)/shard_map/pallas_call | solution.py:31
  230.9 4.1 %all-to-all-start.5 = ((bf16[32,64,256]{2,1,0:T(8,128)(2,1)}), bf16[32,64,256]{2,1,0:T(8,128)(2,1)S(1)}, u32[]{:S(2)}, u32[]{:S(2)}) async-start(bf16[32,64,256]{2,1,0:T(8,128)(2,1)} %get-tuple-element.48), calls=%async_computation.5 | async-start | bytes 2097152 | tf_op jit(solution)/shard_map/all_to_all | solution.py:41
  235.0 1.9 collective-permute-start.5
  236.9 4.3 %collective-permute-start.6 = (bf16[14,2,32,256]{3,2,1,0:T(8,128)(2,1)}, bf16[14,2,32,256]{3,2,1,0:T(8,128)(2,1)}, u32[]{:S(2)}, u32[]{:S(2)}) collective-permute-start(bf16[14,2,32,256]{3,2,1,0:T(8,128)(2,1)} %get-tuple-element.53), channel_id=1, source_target_pairs={{0,1},{1,2},{2,3},{3,0},{4,5},{5,6},{6,7},{7,4},{8,9},{9,10},{10,1... | collective-permute-start | bytes 1376264 | tf_op jit(solution)/shard_map/ppermute | solution.py:50
  241.2 19.9 %all-to-all-done.5.arrived = bf16[32,64,256]{2,1,0:T(8,128)(2,1)S(1)} async-done(((bf16[32,64,256]{2,1,0:T(8,128)(2,1)}), bf16[32,64,256]{2,1,0:T(8,128)(2,1)S(1)}, u32[]{:S(2)}, u32[]{:S(2)}) %all-to-all-start.5) | async-done | bytes 1048608 | tf_op jit(solution)/shard_map/all_to_all | solution.py:41
  261.1 1.5 copy-done.5
  262.6 2.4 shard_map.99
  265.0 1.4 copy-done.8
  266.3 0.0 collective-permute-done.5.up
  266.3 0.0 collective-permute-done.6.down
  266.4 4.6 %all-to-all-start.6 = ((bf16[32,128,256]{2,1,0:T(8,128)(2,1)}), bf16[32,128,256]{2,1,0:T(8,128)(2,1)S(1)}, u32[]{:S(2)}, u32[]{:S(2)}) async-start(bf16[32,128,256]{2,1,0:T(8,128)(2,1)} %bitcast.14), calls=%async_computation.6 | async-start | bytes 4194304 | tf_op jit(solution)/shard_map/all_to_all | solution.py:41
  271.0 1.0 slice.7
  272.0 0.0 copy-done.17
  272.0 2.0 collective-permute-start.8
  274.1 5.4 %collective-permute-start.7 = (bf16[14,2,32,256]{3,2,1,0:T(8,128)(2,1)S(1)}, bf16[14,2,32,256]{3,2,1,0:T(8,128)(2,1)S(1)}, u32[]{:S(2)}, u32[]{:S(2)}) collective-permute-start(bf16[14,2,32,256]{3,2,1,0:T(8,128)(2,1)S(1)} %pad_maximum_fusion.2), channel_id=1, source_target_pairs={{0,3},{1,0},{2,1},{3,2},{4,7},{5,4},{6,5},{7,6},{8,11},{9,8},{10,9... | collective-permute-start | bytes 1376264 | tf_op jit(solution)/shard_map/ppermute | solution.py:50
  279.5 16.7 %collective-permute-done.8.far_down = bf16[14,2,32,256]{3,2,1,0:T(8,128)(2,1)S(1)} collective-permute-done((bf16[14,2,32,256]{3,2,1,0:T(8,128)(2,1)S(1)}, bf16[14,2,32,256]{3,2,1,0:T(8,128)(2,1)S(1)}, u32[]{:S(2)}, u32[]{:S(2)}) %collective-permute-start.8) | collective-permute-done | bytes 458784 | tf_op jit(solution)/shard_map/ppermute | solution.py:50
  296.2 1.6 collective-permute-done.7.far_up
  297.8 0.0 all-to-all-done.6
  297.8 1.4 copy-done.15
  299.2 2.9 reduce_sum.34
  302.1 3.5 %all-to-all-start.7 = ((bf16[8,128,256]{2,1,0:T(8,128)(2,1)}), bf16[8,128,256]{2,1,0:T(8,128)(2,1)S(1)}, u32[]{:S(2)}, u32[]{:S(2)}) async-start(bf16[8,128,256]{2,1,0:T(8,128)(2,1)} %reduce_sum.34), calls=%async_computation.7 | async-start | bytes 1048576 | tf_op jit(solution)/shard_map/all_to_all | solution.py:41
  305.6 3.4 %shard_map.100 = bf16[14,2,32,1024]{3,2,1,0:T(8,128)(2,1)} custom-call(s32[2]{0:T(128)S(1)} %pad_add_fusion.place, bf16[14,2,32,256]{3,2,1,0:T(8,128)(2,1)S(1)} %copy-done.12, bf16[14,2,32,256]{3,2,1,0:T(8,128)(2,1)S(1)} %collective-permute-done.5.up, bf16[14,2,32,256]{3,2,1,0:T(8,128)(2,1)} %collective-permute-done.6.down, ...), custom_call_target="tpu_custom_call" | custom-call | tf_op jit(solution)/shard_map/pallas_call | solution.py:323
  309.0 12.0 %all-to-all-done.7 = bf16[8,128,256]{2,1,0:T(8,128)(2,1)S(1)} async-done(((bf16[8,128,256]{2,1,0:T(8,128)(2,1)}), bf16[8,128,256]{2,1,0:T(8,128)(2,1)S(1)}, u32[]{:S(2)}, u32[]{:S(2)}) %all-to-all-start.7) | async-done | bytes 524320 | tf_op jit(solution)/shard_map/all_to_all | solution.py:41
  321.0 0.7 reduce_sum.35
  (33 shorter events, 0.2 us)
Async XLA Ops:
  7.2 56.5 %all-gather.3.cloned.1.call-start = ((), (), s32[]{:S(2)}) async-start(), calls=%async_computation.8 | async-start | bytes 2064384 | tf_op jit(solution)/shard_map/all_gather | solution.py:364
  10.3 14.1 %copy-start = (bf16[14,2,32,1024]{3,2,1,0:T(8,128)(2,1)S(1)}, bf16[14,2,32,1024]{3,2,1,0:T(8,128)(2,1)}, u32[]{:S(2)}) copy-start(bf16[14,2,32,1024]{3,2,1,0:T(8,128)(2,1)} %block3.1) | copy-start | bytes 5505028
  10.3 62.4 %all-to-all-start = ((bf16[32,128,256]{2,1,0:T(8,128)(2,1)}), bf16[32,128,256]{2,1,0:T(8,128)(2,1)}, u32[]{:S(2)}, u32[]{:S(2)}) async-start(bf16[32,128,256]{2,1,0:T(8,128)(2,1)} %broadcast_in_dim.36), calls=%async_computation | async-start | bytes 4194304 | tf_op jit(solution)/shard_map/all_to_all | solution.py:41
  25.2 100.5 %copy-start.9 = (bf16[14,2,32,256]{3,2,1,0:T(8,128)(2,1)}, bf16[14,2,32,256]{3,2,1,0:T(8,128)(2,1)S(1)}, u32[]{:S(2)}) copy-start(bf16[14,2,32,256]{3,2,1,0:T(8,128)(2,1)S(1)} %get-tuple-element.38.own.refs_0_) | copy-start | bytes 1376260
  25.2 43.8 %copy-start.18 = (s32[224,2]{0,1:T(2,128)S(1)}, s32[224,2]{0,1:T(2,128)}, u32[]{:S(2)}) copy-start(s32[224,2]{0,1:T(2,128)} %param.9) | copy-start | bytes 5380
  25.2 16.4 %collective-permute-start = (bf16[14,32,256]{2,1,0:T(8,128)(2,1)S(1)}, bf16[14,32,256]{2,1,0:T(8,128)(2,1)S(1)}, u32[]{:S(2)}, u32[]{:S(2)}) collective-permute-start(bf16[14,32,256]{2,1,0:T(8,128)(2,1)S(1)} %get-tuple-element.34), channel_id=1, source_target_pairs={{0,1},{1,2},{2,3},{3,0},{4,5},{5,6},{6,7},{7,4},{8,9},{9,10},{10,1... | collective-permute-start | bytes 688136 | tf_op jit(solution)/shard_map/ppermute | solution.py:50
  29.5 20.7 %collective-permute-start.1 = (bf16[14,32,256]{2,1,0:T(8,128)(2,1)S(1)}, bf16[14,32,256]{2,1,0:T(8,128)(2,1)S(1)}, u32[]{:S(2)}, u32[]{:S(2)}) collective-permute-start(bf16[14,32,256]{2,1,0:T(8,128)(2,1)S(1)} %get-tuple-element.36), channel_id=1, source_target_pairs={{0,3},{1,0},{2,1},{3,2},{4,7},{5,4},{6,5},{7,6},{8,11},{9,8},{10,9... | collective-permute-start | bytes 688136 | tf_op jit(solution)/shard_map/ppermute | solution.py:50
  63.7 9.1 %collective-permute-start.2 = (bf16[8,448,256]{2,1,0:T(8,128)(2,1)}, bf16[8,448,256]{2,1,0:T(8,128)(2,1)S(1)}, u32[]{:S(2)}, u32[]{:S(2)}) collective-permute-start(bf16[8,448,256]{2,1,0:T(8,128)(2,1)} %bitcast.11), channel_id=1, source_target_pairs={{0,128},{128,0},{1,129},{129,1},{2,130},{130,2},{3,131},{131,3},{4... | collective-permute-start | bytes 5505032 | tf_op jit(solution)/shard_map/ppermute | solution.py:50
  72.7 5.9 %copy-start.4 = (bf16[8,448,256]{2,1,0:T(8,128)(2,1)}, bf16[8,448,256]{2,1,0:T(8,128)(2,1)S(1)}, u32[]{:S(2)}) copy-start(bf16[8,448,256]{2,1,0:T(8,128)(2,1)S(1)} %collective-permute-done.2.other) | copy-start | bytes 5505028
  72.7 2.2 copy-start.2
  78.6 47.0 %all-to-all-start.1 = ((bf16[32,64,256]{2,1,0:T(8,128)(2,1)}), bf16[32,64,256]{2,1,0:T(8,128)(2,1)S(1)}, u32[]{:S(2)}, u32[]{:S(2)}) async-start(bf16[32,64,256]{2,1,0:T(8,128)(2,1)} %shard_map.94), calls=%async_computation.1 | async-start | bytes 2097152 | tf_op jit(solution)/shard_map/all_to_all | solution.py:41
  87.6 29.1 %collective-permute-start.3 = (bf16[14,3,32,256]{3,2,1,0:T(8,128)(2,1)}, bf16[14,3,32,256]{3,2,1,0:T(8,128)(2,1)S(1)}, u32[]{:S(2)}, u32[]{:S(2)}) collective-permute-start(bf16[14,3,32,256]{3,2,1,0:T(8,128)(2,1)} %pad_maximum_fusion), channel_id=1, source_target_pairs={{0,1},{1,2},{2,3},{3,0},{4,5},{5,6},{6,7},{7,4},{8,9},{9,10},{10,1... | collective-permute-start | bytes 2064392 | tf_op jit(solution)/shard_map/ppermute | solution.py:50
  90.6 35.0 %collective-permute-start.4 = (bf16[14,3,32,256]{3,2,1,0:T(8,128)(2,1)}, bf16[14,3,32,256]{3,2,1,0:T(8,128)(2,1)S(1)}, u32[]{:S(2)}, u32[]{:S(2)}) collective-permute-start(bf16[14,3,32,256]{3,2,1,0:T(8,128)(2,1)} %pad_maximum_fusion.1), channel_id=1, source_target_pairs={{0,3},{1,0},{2,1},{3,2},{4,7},{5,4},{6,5},{7,6},{8,11},{9,8},{10,9... | collective-permute-start | bytes 2064392 | tf_op jit(solution)/shard_map/ppermute | solution.py:50
  95.2 73.3 %copy-start.13 = (s32[14]{0:T(128)}, s32[14]{0:T(128)S(1)}, u32[]{:S(2)}) copy-start(s32[14]{0:T(128)S(1)} %select_reduce_fusion.target) | copy-start | bytes 172
  116.7 51.8 %copy-start.6 = (bf16[14,3,32,256]{3,2,1,0:T(8,128)(2,1)}, bf16[14,3,32,256]{3,2,1,0:T(8,128)(2,1)S(1)}, u32[]{:S(2)}) copy-start(bf16[14,3,32,256]{3,2,1,0:T(8,128)(2,1)S(1)} %collective-permute-done.3.up.refs_1_) | copy-start | bytes 2064388
  125.7 42.8 %copy-start.7 = (bf16[14,3,32,256]{3,2,1,0:T(8,128)(2,1)}, bf16[14,3,32,256]{3,2,1,0:T(8,128)(2,1)S(1)}, u32[]{:S(2)}) copy-start(bf16[14,3,32,256]{3,2,1,0:T(8,128)(2,1)S(1)} %collective-permute-done.4.down.refs_2_) | copy-start | bytes 2064388
  125.7 42.8 %copy-start.1 = (bf16[32,64,256]{2,1,0:T(8,128)(2,1)}, bf16[32,64,256]{2,1,0:T(8,128)(2,1)S(1)}, u32[]{:S(2)}) copy-start(bf16[32,64,256]{2,1,0:T(8,128)(2,1)S(1)} %all-to-all-done.1.arrived.queries) | copy-start | bytes 3145732
  127.3 0.9 copy-start.10
  128.3 40.2 %copy-start.11 = (bf16[448,256]{1,0:T(8,128)(2,1)S(1)}, bf16[448,256]{1,0:T(8,128)(2,1)}, u32[]{:S(2)}) copy-start(bf16[448,256]{1,0:T(8,128)(2,1)} %d_mixed.3) | copy-start | bytes 688132
  128.3 40.2 %copy-start.14 = (f32[256]{0:T(256)S(1)}, f32[256]{0:T(256)}, u32[]{:S(2)}) copy-start(f32[256]{0:T(256)} %param.10) | copy-start | bytes 3076
  230.9 30.2 %copy-start.3 = (bf16[3584,256]{1,0:T(8,128)(2,1)S(1)}, bf16[3584,256]{1,0:T(8,128)(2,1)}, u32[]{:S(2)}) copy-start(bf16[3584,256]{1,0:T(8,128)(2,1)} %all-gather.3.cloned.1.call-done) | copy-start | bytes 5505028
  230.9 30.2 %all-to-all-start.5 = ((bf16[32,64,256]{2,1,0:T(8,128)(2,1)}), bf16[32,64,256]{2,1,0:T(8,128)(2,1)S(1)}, u32[]{:S(2)}, u32[]{:S(2)}) async-start(bf16[32,64,256]{2,1,0:T(8,128)(2,1)} %get-tuple-element.48), calls=%async_computation.5 | async-start | bytes 2097152 | tf_op jit(solution)/shard_map/all_to_all | solution.py:41
  235.0 31.4 %collective-permute-start.5 = (bf16[14,2,32,256]{3,2,1,0:T(8,128)(2,1)}, bf16[14,2,32,256]{3,2,1,0:T(8,128)(2,1)S(1)}, u32[]{:S(2)}, u32[]{:S(2)}) collective-permute-start(bf16[14,2,32,256]{3,2,1,0:T(8,128)(2,1)} %get-tuple-element.52), channel_id=1, source_target_pairs={{0,3},{1,0},{2,1},{3,2},{4,7},{5,4},{6,5},{7,6},{8,11},{9,8},{10,9... | collective-permute-start | bytes 1376264 | tf_op jit(solution)/shard_map/ppermute | solution.py:50
  236.9 29.4 %collective-permute-start.6 = (bf16[14,2,32,256]{3,2,1,0:T(8,128)(2,1)}, bf16[14,2,32,256]{3,2,1,0:T(8,128)(2,1)}, u32[]{:S(2)}, u32[]{:S(2)}) collective-permute-start(bf16[14,2,32,256]{3,2,1,0:T(8,128)(2,1)} %get-tuple-element.53), channel_id=1, source_target_pairs={{0,1},{1,2},{2,3},{3,0},{4,5},{5,6},{6,7},{7,4},{8,9},{9,10},{10,1... | collective-permute-start | bytes 1376264 | tf_op jit(solution)/shard_map/ppermute | solution.py:50
  261.1 1.5 copy-start.5
  265.0 1.4 copy-start.8
  266.4 5.6 %copy-start.17 = (bf16[14,32,256]{2,1,0:T(8,128)(2,1)S(1)}, bf16[14,32,256]{2,1,0:T(8,128)(2,1)}, u32[]{:S(2)}) copy-start(bf16[14,32,256]{2,1,0:T(8,128)(2,1)} %get-tuple-element.58) | copy-start | bytes 688132
  266.4 31.5 %all-to-all-start.6 = ((bf16[32,128,256]{2,1,0:T(8,128)(2,1)}), bf16[32,128,256]{2,1,0:T(8,128)(2,1)S(1)}, u32[]{:S(2)}, u32[]{:S(2)}) async-start(bf16[32,128,256]{2,1,0:T(8,128)(2,1)} %bitcast.14), calls=%async_computation.6 | async-start | bytes 4194304 | tf_op jit(solution)/shard_map/all_to_all | solution.py:41
  270.9 3.1 copy-start.16
  272.0 24.2 %collective-permute-start.8 = (bf16[14,2,32,256]{3,2,1,0:T(8,128)(2,1)S(1)}, bf16[14,2,32,256]{3,2,1,0:T(8,128)(2,1)S(1)}, u32[]{:S(2)}, u32[]{:S(2)}) collective-permute-start(bf16[14,2,32,256]{3,2,1,0:T(8,128)(2,1)S(1)} %pad_maximum_fusion.3), channel_id=1, source_target_pairs={{0,1},{1,2},{2,3},{3,0},{4,5},{5,6},{6,7},{7,4},{8,9},{9,10},{10,1... | collective-permute-start | bytes 1376264 | tf_op jit(solution)/shard_map/ppermute | solution.py:50
  274.1 23.7 %collective-permute-start.7 = (bf16[14,2,32,256]{3,2,1,0:T(8,128)(2,1)S(1)}, bf16[14,2,32,256]{3,2,1,0:T(8,128)(2,1)S(1)}, u32[]{:S(2)}, u32[]{:S(2)}) collective-permute-start(bf16[14,2,32,256]{3,2,1,0:T(8,128)(2,1)S(1)} %pad_maximum_fusion.2), channel_id=1, source_target_pairs={{0,3},{1,0},{2,1},{3,2},{4,7},{5,4},{6,5},{7,6},{8,11},{9,8},{10,9... | collective-permute-start | bytes 1376264 | tf_op jit(solution)/shard_map/ppermute | solution.py:50
  297.8 1.4 copy-start.15
  299.2 6.4 %copy-start.12 = (bf16[14,2,32,256]{3,2,1,0:T(8,128)(2,1)S(1)}, bf16[14,2,32,256]{3,2,1,0:T(8,128)(2,1)}, u32[]{:S(2)}) copy-start(bf16[14,2,32,256]{3,2,1,0:T(8,128)(2,1)} %get-tuple-element.50.own) | copy-start | bytes 1376260
  302.1 18.9 %all-to-all-start.7 = ((bf16[8,128,256]{2,1,0:T(8,128)(2,1)}), bf16[8,128,256]{2,1,0:T(8,128)(2,1)S(1)}, u32[]{:S(2)}, u32[]{:S(2)}) async-start(bf16[8,128,256]{2,1,0:T(8,128)(2,1)} %reduce_sum.34), calls=%async_computation.7 | async-start | bytes 1048576 | tf_op jit(solution)/shard_map/all_to_all | solution.py:41
Sparse Core Ops, SparseCore 0:
  10.1 53.5 all-gather.2

commit v8 on v7

--- a/solution.py
+++ b/solution.py
@@ -118,10 +118,10 @@
     far_values[...] = block2[:, 1]
 
 
-def whole_rows(n, own, up, down):
+def whole_rows(n, own, first, last, far_keys, far_values):
     return [
-        jnp.concatenate([own[n, 0], up[n, 0], up[n, 2], down[n, 0]], axis=0),
-        jnp.concatenate([own[n, 1], up[n, 1], down[n, 2], down[n, 1]], axis=0),
+        jnp.concatenate([own[n, i], first[n, i], far[n], last[n, i]], axis=0)
+        for i, far in enumerate((far_keys, far_values))
     ]
 
 
@@ -150,10 +150,10 @@
         slots[source[k]] = total[c * GROUP_LEN : (c + 1) * GROUP_LEN].astype(BF)
 
 
-def owner_forward_kernel(target, arrived, own, up, down, slots, probs):
+def owner_forward_kernel(target, arrived, own, first, last, far_keys, far_values, slots, probs):
     for n in range(target.shape[0]):
         t = target[n]
-        keys, values = whole_rows(n, own, up, down)
+        keys, values = whole_rows(n, own, first, last, far_keys, far_values)
         scores = dot(keys, by_head(arrived[t]), LAST) * SCALE
         top = jnp.max(scores, axis=0, keepdims=True)
         expo = jnp.exp(scores - top)
@@ -231,7 +231,7 @@
 
 
 def owner_backward_kernel(target, arrived, queries, probs, *refs):
-    kv_refs, (slots, own, up, down, first, last) = refs[:3], refs[3:]
+    kv_refs, (slots, own, up, down, first, last) = refs[:5], refs[5:]
     for n in range(target.shape[0]):
         t = target[n]
         keys, values = whole_rows(n, *kv_refs)
@@ -266,6 +266,13 @@
                 partial[lax.rem(first + i, n_x), lax.div(first + i, n_x)] = product[
                     i * rows : (i + 1) * rows
                 ]
+
+
+def add_kernel(parts, out):
+    total = parts[0].astype(F32)
+    for i in range(1, parts.shape[0]):
+        total = total + parts[i].astype(F32)
+    out[...] = total.astype(BF)
 
 
 def merge_kernel(place, own, up, down, far_up, far_down, out):
@@ -364,11 +371,13 @@
     line = lax.all_gather(hidden, LINE, axis=0)
     own, first, last, far_keys, far_values = split_by_quarter(place, kv_enc)
     weight = exchange(copies(wq, n_dp), DP).reshape(-1, dec_width)
-    up = jnp.concatenate([first, shift(far_keys, "mp", 1)[:, None]], axis=1)
-    down = jnp.concatenate([last, shift(far_values, "mp", -1)[:, None]], axis=1)
-    line, up, down = lax.optimization_barrier((line, up, down))
+    for _ in range(2):
+        far_keys, far_values = shift(far_keys, "mp", 1), shift(far_values, "mp", -1)
+    line, far_keys, far_values, first, last = lax.optimization_barrier(
+        (line, far_keys, far_values, first, last)
+    )
     other = shift(line, "co", 1)
-    kv = (own, shift(up, "mp", 1), shift(down, "mp", -1))
+    kv = (own, shift(first, "mp", 1), shift(last, "mp", -1), far_keys, far_values)
 
     (slots,) = pl.pallas_call(
         functools.partial(query_kernel, sizes),
@@ -427,7 +436,7 @@
     column = exchange(partial.reshape(n_x * n_z, -1, dec_width), "dx").reshape(blocks)
     column, far_up, far_down = lax.optimization_barrier((column, far_up, far_down))
     grad_kv = merge_quarters(place, (own, up, down, far_up, far_down))
-    column = jnp.sum(column, axis=0, dtype=F32).astype(BF)
+    (column,) = call(add_kernel, (), (column,), [(blocks[1:], BF)])
     grad_wq = jnp.sum(exchange(column, "dz"), axis=0, dtype=F32).astype(BF)
     return (mixed, grad_q, grad_kv, grad_wq)
 

time: 332 us -> 326 us (0.982)
  waiting for transfers between devices: 113 us -> 104 us
  other arithmetic: 5.93 us -> 1.17 us
  starting transfers between devices: 69.3 us -> 72.9 us
    all_to_all x5, waiting for transfers between devices: 35.3 us -> 29.6 us  [exchange(): return lax.all_to_all(array, axes, split_axis=0, concat_axis=0, tiled=True)]
    all_gather x1, waiting for transfers between devices: 12.5 us -> 8.06 us  [shards(): line = lax.all_gather(hidden, LINE, axis=0)]
    ppermute x9 -> x11, starting transfers between devices: 34.2 us -> 37.7 us  [shift(): lax.ppermute(array, axis, [(i, (i + step) % size) for i in range(size)])]
    unnamed x39 -> x51, local copies, waits for them, and re-layouts: 7.5 us -> 9.68 us
    pallas_call x5 -> x6, Pallas kernels: 14.6 us -> 15.6 us  [call(): pl.pallas_call(kernel, in_specs=[SMEM] * len(scalars) + [VMEM] * len(arra...]
    ppermute x9 -> x11, waiting for transfers between devices: 64.9 us -> 65.7 us  [shift(): lax.ppermute(array, axis, [(i, (i + step) % size) for i in range(size)])]
  transfers between devices with their start and end apart: 15 -> 17, of which waited for: 10 -> 12; matrix products, arithmetic and copies ran while one was open for 2% -> 1% of each run, Pallas kernels for 2% -> 2%
where the time goes in v8:
time: 326 us; the launch traced here: 322 us
  waiting for transfers between devices  104 us (32%)
  blocking collectives  92.2 us (28%)
  starting transfers between devices  72.9 us (22%)
  Pallas kernels  24.2 us (7%)
  between operations  14.4 us (4%)
  local copies, waits for them, and re-layouts  13.3 us (4%)
    all_to_all x3, blocking collectives, exchange(): return lax.all_to_all(array, axes, split_axis=0, concat_axis=0, tiled=True)  92.2 us
    ppermute x11, waiting for transfers between devices, shift(): lax.ppermute(array, axis, [(i, (i + step) % size) for i in range(size)])  65.7 us
    ppermute x11, starting transfers between devices, shift(): lax.ppermute(array, axis, [(i, (i + step) % size) for i in range(size)])  37.7 us
    all_to_all x5, starting transfers between devices, exchange(): return lax.all_to_all(array, axes, split_axis=0, concat_axis=0, tiled=True)  35.1 us
    all_to_all x5, waiting for transfers between devices, exchange(): return lax.all_to_all(array, axes, split_axis=0, concat_axis=0, tiled=True)  29.6 us
    pallas_call x6, Pallas kernels, call(): pl.pallas_call(kernel, in_specs=[SMEM] * len(scalars) + [VMEM] * len(arra...  15.6 us
    unnamed x51, local copies, waits for them, and re-layouts  9.68 us
    all_gather x1, waiting for transfers between devices, shards(): line = lax.all_gather(hidden, LINE, axis=0)  8.06 us
  transfers between devices with their start and end apart: 17, of which 12 were waited for; matrix products, arithmetic and copies ran while one was open for 1% of the time, Pallas kernels for 2%

profile of v8, /device:TPU:1, one launch (start us, length us, event | category | flops | bytes accessed | tf_op | source)
XLA Modules:
  0.0 322.0 jit_solution(8622678920165617222)
XLA Ops:
  7.2 0.0 all-gather.3.cloned.1.call-start
  7.2 0.7 all-gather.3.cloned.1.call-update
  7.9 2.4 broadcast_in_dim.28
  10.3 14.0 %all-to-all-start = ((bf16[32,128,256]{2,1,0:T(8,128)(2,1)}), bf16[32,128,256]{2,1,0:T(8,128)(2,1)}, u32[]{:S(2)}, u32[]{:S(2)}) async-start(bf16[32,128,256]{2,1,0:T(8,128)(2,1)} %broadcast_in_dim.28), calls=%async_computation | async-start | bytes 4194304 | tf_op jit(solution)/shard_map/all_to_all | solution.py:41
  24.3 0.1 pad_add_fusion.place
  24.4 1.6 shard_map.93
  25.9 4.2 %collective-permute-start = (bf16[14,32,256]{2,1,0:T(8,128)(2,1)S(1)}, bf16[14,32,256]{2,1,0:T(8,128)(2,1)S(1)}, u32[]{:S(2)}, u32[]{:S(2)}) collective-permute-start(bf16[14,32,256]{2,1,0:T(8,128)(2,1)S(1)} %get-tuple-element.35), channel_id=1, source_target_pairs={{0,1},{1,2},{2,3},{3,0},{4,5},{5,6},{6,7},{7,4},{8,9},{9,10},{10,1... | collective-permute-start | bytes 688136 | tf_op jit(solution)/shard_map/ppermute | solution.py:50
  30.1 3.6 %collective-permute-start.2 = (bf16[14,32,256]{2,1,0:T(8,128)(2,1)S(1)}, bf16[14,32,256]{2,1,0:T(8,128)(2,1)S(1)}, u32[]{:S(2)}, u32[]{:S(2)}) collective-permute-start(bf16[14,32,256]{2,1,0:T(8,128)(2,1)S(1)} %get-tuple-element.36), channel_id=1, source_target_pairs={{0,3},{1,0},{2,1},{3,2},{4,7},{5,4},{6,5},{7,6},{8,11},{9,8},{10,9... | collective-permute-start | bytes 688136 | tf_op jit(solution)/shard_map/ppermute | solution.py:50
  33.7 9.6 %collective-permute-done = bf16[14,32,256]{2,1,0:T(8,128)(2,1)S(1)} collective-permute-done((bf16[14,32,256]{2,1,0:T(8,128)(2,1)S(1)}, bf16[14,32,256]{2,1,0:T(8,128)(2,1)S(1)}, u32[]{:S(2)}, u32[]{:S(2)}) %collective-permute-start) | collective-permute-done | bytes 229408 | tf_op jit(solution)/shard_map/ppermute | solution.py:50
  43.4 4.1 %collective-permute-start.1 = (bf16[14,32,256]{2,1,0:T(8,128)(2,1)S(1)}, bf16[14,32,256]{2,1,0:T(8,128)(2,1)S(1)}, u32[]{:S(2)}, u32[]{:S(2)}) collective-permute-start(bf16[14,32,256]{2,1,0:T(8,128)(2,1)S(1)} %collective-permute-done), channel_id=1, source_target_pairs={{0,1},{1,2},{2,3},{3,0},{4,5},{5,6},{6,7},{7,4},{8,9},{9,10},{10,1... | collective-permute-start | bytes 688136 | tf_op jit(solution)/shard_map/ppermute | solution.py:50
  47.5 3.2 collective-permute-done.2
  50.6 1.9 collective-permute-start.3
  52.5 5.0 %collective-permute-done.1.far_keys.refs_3_ = bf16[14,32,256]{2,1,0:T(8,128)(2,1)S(1)} collective-permute-done((bf16[14,32,256]{2,1,0:T(8,128)(2,1)S(1)}, bf16[14,32,256]{2,1,0:T(8,128)(2,1)S(1)}, u32[]{:S(2)}, u32[]{:S(2)}) %collective-permute-start.1) | collective-permute-done | bytes 229408 | tf_op jit(solution)/shard_map/ppermute | solution.py:50
  57.5 6.6 %collective-permute-done.3.far_values.refs_4_ = bf16[14,32,256]{2,1,0:T(8,128)(2,1)S(1)} collective-permute-done((bf16[14,32,256]{2,1,0:T(8,128)(2,1)S(1)}, bf16[14,32,256]{2,1,0:T(8,128)(2,1)S(1)}, u32[]{:S(2)}, u32[]{:S(2)}) %collective-permute-start.3) | collective-permute-done | bytes 229408 | tf_op jit(solution)/shard_map/ppermute | solution.py:50
  64.1 8.1 %all-gather.3.cloned.1.call-done = bf16[3584,256]{1,0:T(8,128)(2,1)} async-done(((bf16[448,256]{1,0:T(8,128)(2,1)}), bf16[3584,256]{1,0:T(8,128)(2,1)}) %all-gather.3.cloned.1.call-update) | async-done | bytes 1835024 | tf_op jit(solution)/shard_map/all_gather | solution.py:371
  72.1 3.0 collective-permute-start.4
  75.1 0.1 copy.11
  75.3 0.1 reshape.43
  75.4 0.1 and_select_fusion.source
  75.5 0.0 all-to-all-done
  75.5 3.2 collective-permute-done.4.other
  78.7 2.2 copy-done.2
  80.9 3.7 %shard_map.94 = bf16[32,64,256]{2,1,0:T(8,128)(2,1)} custom-call(s32[2]{0:T(128)S(1)} %pad_add_fusion.place, s32[14]{0:T(128)S(1)} %and_select_fusion.source, bf16[8,448,256]{2,1,0:T(8,128)(2,1)S(1)} %bitcast.11, bf16[8,448,256]{2,1,0:T(8,128)(2,1)S(1)} %collective-permute-done.4.other, bf16[4096,256]{1,0:T(8,128)(2,1)} %bitcast.3.weight), custom_call_target="tpu_custom_call" | custom-call | tf_op jit(solution)/shard_map/pallas_call | solution.py:382
  84.6 9.0 %all-to-all-start.1 = ((bf16[32,64,256]{2,1,0:T(8,128)(2,1)}), bf16[32,64,256]{2,1,0:T(8,128)(2,1)S(1)}, u32[]{:S(2)}, u32[]{:S(2)}) async-start(bf16[32,64,256]{2,1,0:T(8,128)(2,1)} %shard_map.94), calls=%async_computation.1 | async-start | bytes 2097152 | tf_op jit(solution)/shard_map/all_to_all | solution.py:41
  93.6 4.0 %collective-permute-start.5 = (bf16[14,2,32,256]{3,2,1,0:T(8,128)(2,1)}, bf16[14,2,32,256]{3,2,1,0:T(8,128)(2,1)S(1)}, u32[]{:S(2)}, u32[]{:S(2)}) collective-permute-start(bf16[14,2,32,256]{3,2,1,0:T(8,128)(2,1)} %get-tuple-element.41), channel_id=1, source_target_pairs={{0,1},{1,2},{2,3},{3,0},{4,5},{5,6},{6,7},{7,4},{8,9},{9,10},{10,1... | collective-permute-start | bytes 1376264 | tf_op jit(solution)/shard_map/ppermute | solution.py:50
  97.6 3.4 %collective-permute-start.6 = (bf16[14,2,32,256]{3,2,1,0:T(8,128)(2,1)}, bf16[14,2,32,256]{3,2,1,0:T(8,128)(2,1)S(1)}, u32[]{:S(2)}, u32[]{:S(2)}) collective-permute-start(bf16[14,2,32,256]{3,2,1,0:T(8,128)(2,1)} %copy-done.21), channel_id=1, source_target_pairs={{0,3},{1,0},{2,1},{3,2},{4,7},{5,4},{6,5},{7,6},{8,11},{9,8},{10,9... | collective-permute-start | bytes 1376264 | tf_op jit(solution)/shard_map/ppermute | solution.py:50
  101.0 0.2 select_reduce_fusion.target
  101.2 18.6 %collective-permute-done.5.first.refs_1_ = bf16[14,2,32,256]{3,2,1,0:T(8,128)(2,1)S(1)} collective-permute-done((bf16[14,2,32,256]{3,2,1,0:T(8,128)(2,1)}, bf16[14,2,32,256]{3,2,1,0:T(8,128)(2,1)S(1)}, u32[]{:S(2)}, u32[]{:S(2)}) %collective-permute-start.5) | collective-permute-done | bytes 458784 | tf_op jit(solution)/shard_map/ppermute | solution.py:50
  119.8 2.0 collective-permute-done.6.last.refs_2_
  121.8 0.0 all-to-all-done.1.arrived.queries
  121.9 1.7 shard_map.95
  123.6 0.9 copy-done.10
  124.5 39.8 %all_to_all.40.arrived = bf16[32,16,1152]{2,1,0:T(8,128)(2,1)S(1)} all-to-all(bf16[32,16,1152]{2,1,0:T(8,128)(2,1)S(1)} %get-tuple-element.45), channel_id=1, replica_groups=mesh['yl'=2,'co'=2,'dz'=8,'dx'=4,'mp'=4] {'dz','dx'}, dimensions={0} | all-to-all | bytes 2359296 | tf_op jit(solution)/shard_map/all_to_all | solution.py:41
  164.3 1.6 shard_map.96
  165.9 16.1 %all_to_all.41.moved = f32[16,8,128]{2,1,0:T(8,128)S(1)} all-to-all(f32[16,8,128]{2,1,0:T(8,128)S(1)} %broadcast_in_dim.29), channel_id=1, replica_groups=mesh['yl'=2,'co'=2,'dz'=8,'dx'=4,'mp'=4] {'yl','co','mp'}, dimensions={0} | all-to-all | bytes 131072 | tf_op jit(solution)/shard_map/all_to_all | solution.py:41
  182.1 2.5 shard_map.97
  184.6 36.2 %all_to_all.42.arrived = bf16[32,16,1152]{2,1,0:T(8,128)(2,1)} all-to-all(bf16[32,16,1152]{2,1,0:T(8,128)(2,1)S(1)} %get-tuple-element.50), channel_id=1, replica_groups=mesh['yl'=2,'co'=2,'dz'=8,'dx'=4,'mp'=4] {'dz','dx'}, dimensions={0} | all-to-all | bytes 2359296 | tf_op jit(solution)/shard_map/all_to_all | solution.py:41
  220.7 6.5 %shard_map.98 = (bf16[32,64,256]{2,1,0:T(8,128)(2,1)}, bf16[14,2,32,256]{3,2,1,0:T(8,128)(2,1)}, bf16[14,2,32,256]{3,2,1,0:T(8,128)(2,1)}, bf16[14,2,32,256]{3,2...) custom-call(s32[14]{0:T(128)} %copy-done.19, bf16[32,16,1152]{2,1,0:T(8,128)(2,1)} %all_to_all.42.arrived, ...), custom_call_target="tpu_custom_call" | custom-call | tf_op jit(solution)/shard_map/pallas_call | solution.py:31
  227.2 4.1 %all-to-all-start.5 = ((bf16[32,64,256]{2,1,0:T(8,128)(2,1)}), bf16[32,64,256]{2,1,0:T(8,128)(2,1)S(1)}, u32[]{:S(2)}, u32[]{:S(2)}) async-start(bf16[32,64,256]{2,1,0:T(8,128)(2,1)} %get-tuple-element.52), calls=%async_computation.5 | async-start | bytes 2097152 | tf_op jit(solution)/shard_map/all_to_all | solution.py:41
  231.3 1.9 collective-permute-start.7
  233.2 4.3 %collective-permute-start.8 = (bf16[14,2,32,256]{3,2,1,0:T(8,128)(2,1)}, bf16[14,2,32,256]{3,2,1,0:T(8,128)(2,1)}, u32[]{:S(2)}, u32[]{:S(2)}) collective-permute-start(bf16[14,2,32,256]{3,2,1,0:T(8,128)(2,1)} %get-tuple-element.57), channel_id=1, source_target_pairs={{0,1},{1,2},{2,3},{3,0},{4,5},{5,6},{6,7},{7,4},{8,9},{9,10},{10,1... | collective-permute-start | bytes 1376264 | tf_op jit(solution)/shard_map/ppermute | solution.py:50
  237.5 19.9 %all-to-all-done.5.arrived = bf16[32,64,256]{2,1,0:T(8,128)(2,1)S(1)} async-done(((bf16[32,64,256]{2,1,0:T(8,128)(2,1)}), bf16[32,64,256]{2,1,0:T(8,128)(2,1)S(1)}, u32[]{:S(2)}, u32[]{:S(2)}) %all-to-all-start.5) | async-done | bytes 1048608 | tf_op jit(solution)/shard_map/all_to_all | solution.py:41
  257.4 1.5 copy-done.5
  258.9 2.4 shard_map.99
  261.3 1.3 copy-done.6
  262.6 0.0 collective-permute-done.7.up
  262.6 0.0 collective-permute-done.8.down
  262.6 4.6 %all-to-all-start.6 = ((bf16[32,128,256]{2,1,0:T(8,128)(2,1)}), bf16[32,128,256]{2,1,0:T(8,128)(2,1)S(1)}, u32[]{:S(2)}, u32[]{:S(2)}) async-start(bf16[32,128,256]{2,1,0:T(8,128)(2,1)} %bitcast.13), calls=%async_computation.6 | async-start | bytes 4194304 | tf_op jit(solution)/shard_map/all_to_all | solution.py:41
  267.2 1.0 slice.7
  268.3 2.0 collective-permute-start.10
  270.3 0.1 pad_maximum_fusion
  270.3 5.4 %collective-permute-start.9 = (bf16[14,2,32,256]{3,2,1,0:T(8,128)(2,1)S(1)}, bf16[14,2,32,256]{3,2,1,0:T(8,128)(2,1)S(1)}, u32[]{:S(2)}, u32[]{:S(2)}) collective-permute-start(bf16[14,2,32,256]{3,2,1,0:T(8,128)(2,1)S(1)} %pad_maximum_fusion), channel_id=1, source_target_pairs={{0,3},{1,0},{2,1},{3,2},{4,7},{5,4},{6,5},{7,6},{8,11},{9,8},{10,9... | collective-permute-start | bytes 1376264 | tf_op jit(solution)/shard_map/ppermute | solution.py:50
  275.8 16.7 %collective-permute-done.10.far_down = bf16[14,2,32,256]{3,2,1,0:T(8,128)(2,1)S(1)} collective-permute-done((bf16[14,2,32,256]{3,2,1,0:T(8,128)(2,1)S(1)}, bf16[14,2,32,256]{3,2,1,0:T(8,128)(2,1)S(1)}, u32[]{:S(2)}, u32[]{:S(2)}) %collective-permute-start.10) | collective-permute-done | bytes 458784 | tf_op jit(solution)/shard_map/ppermute | solution.py:50
  292.5 0.8 copy-done.15
  293.3 0.8 collective-permute-done.9.far_up
  294.1 0.8 copy-done.17
  294.8 0.0 all-to-all-done.6
  294.8 1.1 shard_map.101
  295.9 3.5 %all-to-all-start.7 = ((bf16[8,128,256]{2,1,0:T(8,128)(2,1)}), bf16[8,128,256]{2,1,0:T(8,128)(2,1)S(1)}, u32[]{:S(2)}, u32[]{:S(2)}) async-start(bf16[8,128,256]{2,1,0:T(8,128)(2,1)} %shard_map.101), calls=%async_computation.7 | async-start | bytes 1048576 | tf_op jit(solution)/shard_map/all_to_all | solution.py:41
  299.4 1.0 copy-done.16
  300.4 1.0 copy-done.18
  301.5 3.4 %shard_map.100 = bf16[14,2,32,1024]{3,2,1,0:T(8,128)(2,1)} custom-call(s32[2]{0:T(128)S(1)} %pad_add_fusion.place, bf16[14,2,32,256]{3,2,1,0:T(8,128)(2,1)S(1)} %copy-done.14, bf16[14,2,32,256]{3,2,1,0:T(8,128)(2,1)S(1)} %collective-permute-done.7.up, bf16[14,2,32,256]{3,2,1,0:T(8,128)(2,1)} %collective-permute-done.8.down, ...), custom_call_target="tpu_custom_call" | custom-call | tf_op jit(solution)/shard_map/pallas_call | solution.py:330
  304.8 9.7 %all-to-all-done.7 = bf16[8,128,256]{2,1,0:T(8,128)(2,1)S(1)} async-done(((bf16[8,128,256]{2,1,0:T(8,128)(2,1)}), bf16[8,128,256]{2,1,0:T(8,128)(2,1)S(1)}, u32[]{:S(2)}, u32[]{:S(2)}) %all-to-all-start.7) | async-done | bytes 524320 | tf_op jit(solution)/shard_map/all_to_all | solution.py:41
  314.5 0.7 reduce_sum.22
  (47 shorter events, 0.2 us)
Async XLA Ops:
  7.2 65.0 %all-gather.3.cloned.1.call-start = ((), (), s32[]{:S(2)}) async-start(), calls=%async_computation.8 | async-start | bytes 2064384 | tf_op jit(solution)/shard_map/all_gather | solution.py:371
  10.3 14.1 %copy-start = (bf16[14,2,32,1024]{3,2,1,0:T(8,128)(2,1)S(1)}, bf16[14,2,32,1024]{3,2,1,0:T(8,128)(2,1)}, u32[]{:S(2)}) copy-start(bf16[14,2,32,1024]{3,2,1,0:T(8,128)(2,1)} %block3.1) | copy-start | bytes 5505028
  10.3 65.2 %all-to-all-start = ((bf16[32,128,256]{2,1,0:T(8,128)(2,1)}), bf16[32,128,256]{2,1,0:T(8,128)(2,1)}, u32[]{:S(2)}, u32[]{:S(2)}) async-start(bf16[32,128,256]{2,1,0:T(8,128)(2,1)} %broadcast_in_dim.28), calls=%async_computation | async-start | bytes 4194304 | tf_op jit(solution)/shard_map/all_to_all | solution.py:41
  24.4 50.7 %copy-start.24 = (s32[224,2]{0,1:T(2,128)S(1)}, s32[224,2]{0,1:T(2,128)}, u32[]{:S(2)}) copy-start(s32[224,2]{0,1:T(2,128)} %param.9) | copy-start | bytes 5380
  25.9 31.6 %copy-start.21 = (bf16[14,2,32,256]{3,2,1,0:T(8,128)(2,1)}, bf16[14,2,32,256]{3,2,1,0:T(8,128)(2,1)S(1)}, u32[]{:S(2)}) copy-start(bf16[14,2,32,256]{3,2,1,0:T(8,128)(2,1)S(1)} %get-tuple-element.42) | copy-start | bytes 1376260
  25.9 95.9 %copy-start.7 = (bf16[14,2,32,256]{3,2,1,0:T(8,128)(2,1)}, bf16[14,2,32,256]{3,2,1,0:T(8,128)(2,1)S(1)}, u32[]{:S(2)}) copy-start(bf16[14,2,32,256]{3,2,1,0:T(8,128)(2,1)S(1)} %get-tuple-element.40.own.refs_0_) | copy-start | bytes 1376260
  25.9 17.4 %collective-permute-start = (bf16[14,32,256]{2,1,0:T(8,128)(2,1)S(1)}, bf16[14,32,256]{2,1,0:T(8,128)(2,1)S(1)}, u32[]{:S(2)}, u32[]{:S(2)}) collective-permute-start(bf16[14,32,256]{2,1,0:T(8,128)(2,1)S(1)} %get-tuple-element.35), channel_id=1, source_target_pairs={{0,1},{1,2},{2,3},{3,0},{4,5},{5,6},{6,7},{7,4},{8,9},{9,10},{10,1... | collective-permute-start | bytes 688136 | tf_op jit(solution)/shard_map/ppermute | solution.py:50
  30.1 20.5 %collective-permute-start.2 = (bf16[14,32,256]{2,1,0:T(8,128)(2,1)S(1)}, bf16[14,32,256]{2,1,0:T(8,128)(2,1)S(1)}, u32[]{:S(2)}, u32[]{:S(2)}) collective-permute-start(bf16[14,32,256]{2,1,0:T(8,128)(2,1)S(1)} %get-tuple-element.36), channel_id=1, source_target_pairs={{0,3},{1,0},{2,1},{3,2},{4,7},{5,4},{6,5},{7,6},{8,11},{9,8},{10,9... | collective-permute-start | bytes 688136 | tf_op jit(solution)/shard_map/ppermute | solution.py:50
  43.4 14.1 %collective-permute-start.1 = (bf16[14,32,256]{2,1,0:T(8,128)(2,1)S(1)}, bf16[14,32,256]{2,1,0:T(8,128)(2,1)S(1)}, u32[]{:S(2)}, u32[]{:S(2)}) collective-permute-start(bf16[14,32,256]{2,1,0:T(8,128)(2,1)S(1)} %collective-permute-done), channel_id=1, source_target_pairs={{0,1},{1,2},{2,3},{3,0},{4,5},{5,6},{6,7},{7,4},{8,9},{9,10},{10,1... | collective-permute-start | bytes 688136 | tf_op jit(solution)/shard_map/ppermute | solution.py:50
  50.6 13.5 %collective-permute-start.3 = (bf16[14,32,256]{2,1,0:T(8,128)(2,1)S(1)}, bf16[14,32,256]{2,1,0:T(8,128)(2,1)S(1)}, u32[]{:S(2)}, u32[]{:S(2)}) collective-permute-start(bf16[14,32,256]{2,1,0:T(8,128)(2,1)S(1)} %collective-permute-done.2), channel_id=1, source_target_pairs={{0,3},{1,0},{2,1},{3,2},{4,7},{5,4},{6,5},{7,6},{8,11},{9,8},{10,9... | collective-permute-start | bytes 688136 | tf_op jit(solution)/shard_map/ppermute | solution.py:50
  57.5 64.3 %copy-start.11 = (bf16[14,32,256]{2,1,0:T(8,128)(2,1)}, bf16[14,32,256]{2,1,0:T(8,128)(2,1)S(1)}, u32[]{:S(2)}) copy-start(bf16[14,32,256]{2,1,0:T(8,128)(2,1)S(1)} %collective-permute-done.1.far_keys.refs_3_) | copy-start | bytes 688132
  64.1 57.8 %copy-start.12 = (bf16[14,32,256]{2,1,0:T(8,128)(2,1)}, bf16[14,32,256]{2,1,0:T(8,128)(2,1)S(1)}, u32[]{:S(2)}) copy-start(bf16[14,32,256]{2,1,0:T(8,128)(2,1)S(1)} %collective-permute-done.3.far_values.refs_4_) | copy-start | bytes 688132
  72.1 6.6 %collective-permute-start.4 = (bf16[8,448,256]{2,1,0:T(8,128)(2,1)}, bf16[8,448,256]{2,1,0:T(8,128)(2,1)S(1)}, u32[]{:S(2)}, u32[]{:S(2)}) collective-permute-start(bf16[8,448,256]{2,1,0:T(8,128)(2,1)} %bitcast.10), channel_id=1, source_target_pairs={{0,128},{128,0},{1,129},{129,1},{2,130},{130,2},{3,131},{131,3},{4... | collective-permute-start | bytes 5505032 | tf_op jit(solution)/shard_map/ppermute | solution.py:50
  78.7 5.9 %copy-start.4 = (bf16[8,448,256]{2,1,0:T(8,128)(2,1)}, bf16[8,448,256]{2,1,0:T(8,128)(2,1)S(1)}, u32[]{:S(2)}) copy-start(bf16[8,448,256]{2,1,0:T(8,128)(2,1)S(1)} %collective-permute-done.4.other) | copy-start | bytes 5505028
  78.7 2.2 copy-start.2
  84.6 37.3 %all-to-all-start.1 = ((bf16[32,64,256]{2,1,0:T(8,128)(2,1)}), bf16[32,64,256]{2,1,0:T(8,128)(2,1)S(1)}, u32[]{:S(2)}, u32[]{:S(2)}) async-start(bf16[32,64,256]{2,1,0:T(8,128)(2,1)} %shard_map.94), calls=%async_computation.1 | async-start | bytes 2097152 | tf_op jit(solution)/shard_map/all_to_all | solution.py:41
  93.6 26.2 %collective-permute-start.5 = (bf16[14,2,32,256]{3,2,1,0:T(8,128)(2,1)}, bf16[14,2,32,256]{3,2,1,0:T(8,128)(2,1)S(1)}, u32[]{:S(2)}, u32[]{:S(2)}) collective-permute-start(bf16[14,2,32,256]{3,2,1,0:T(8,128)(2,1)} %get-tuple-element.41), channel_id=1, source_target_pairs={{0,1},{1,2},{2,3},{3,0},{4,5},{5,6},{6,7},{7,4},{8,9},{9,10},{10,1... | collective-permute-start | bytes 1376264 | tf_op jit(solution)/shard_map/ppermute | solution.py:50
  97.6 24.3 %collective-permute-start.6 = (bf16[14,2,32,256]{3,2,1,0:T(8,128)(2,1)}, bf16[14,2,32,256]{3,2,1,0:T(8,128)(2,1)S(1)}, u32[]{:S(2)}, u32[]{:S(2)}) collective-permute-start(bf16[14,2,32,256]{3,2,1,0:T(8,128)(2,1)} %copy-done.21), channel_id=1, source_target_pairs={{0,3},{1,0},{2,1},{3,2},{4,7},{5,4},{6,5},{7,6},{8,11},{9,8},{10,9... | collective-permute-start | bytes 1376264 | tf_op jit(solution)/shard_map/ppermute | solution.py:50
  101.2 63.1 %copy-start.19 = (s32[14]{0:T(128)}, s32[14]{0:T(128)S(1)}, u32[]{:S(2)}) copy-start(s32[14]{0:T(128)S(1)} %select_reduce_fusion.target) | copy-start | bytes 172
  119.8 44.5 %copy-start.8 = (bf16[14,2,32,256]{3,2,1,0:T(8,128)(2,1)}, bf16[14,2,32,256]{3,2,1,0:T(8,128)(2,1)S(1)}, u32[]{:S(2)}) copy-start(bf16[14,2,32,256]{3,2,1,0:T(8,128)(2,1)S(1)} %collective-permute-done.5.first.refs_1_) | copy-start | bytes 1376260
  121.8 42.5 %copy-start.9 = (bf16[14,2,32,256]{3,2,1,0:T(8,128)(2,1)}, bf16[14,2,32,256]{3,2,1,0:T(8,128)(2,1)S(1)}, u32[]{:S(2)}) copy-start(bf16[14,2,32,256]{3,2,1,0:T(8,128)(2,1)S(1)} %collective-permute-done.6.last.refs_2_) | copy-start | bytes 1376260
  121.9 42.5 %copy-start.1 = (bf16[32,64,256]{2,1,0:T(8,128)(2,1)}, bf16[32,64,256]{2,1,0:T(8,128)(2,1)S(1)}, u32[]{:S(2)}) copy-start(bf16[32,64,256]{2,1,0:T(8,128)(2,1)S(1)} %all-to-all-done.1.arrived.queries) | copy-start | bytes 3145732
  123.6 0.9 copy-start.10
  124.5 39.9 %copy-start.13 = (bf16[448,256]{1,0:T(8,128)(2,1)S(1)}, bf16[448,256]{1,0:T(8,128)(2,1)}, u32[]{:S(2)}) copy-start(bf16[448,256]{1,0:T(8,128)(2,1)} %d_mixed.3) | copy-start | bytes 688132
  124.5 39.9 %copy-start.20 = (f32[256]{0:T(256)S(1)}, f32[256]{0:T(256)}, u32[]{:S(2)}) copy-start(f32[256]{0:T(256)} %param.10) | copy-start | bytes 3076
  227.2 30.2 %copy-start.3 = (bf16[3584,256]{1,0:T(8,128)(2,1)S(1)}, bf16[3584,256]{1,0:T(8,128)(2,1)}, u32[]{:S(2)}) copy-start(bf16[3584,256]{1,0:T(8,128)(2,1)} %all-gather.3.cloned.1.call-done) | copy-start | bytes 5505028
  227.2 30.2 %all-to-all-start.5 = ((bf16[32,64,256]{2,1,0:T(8,128)(2,1)}), bf16[32,64,256]{2,1,0:T(8,128)(2,1)S(1)}, u32[]{:S(2)}, u32[]{:S(2)}) async-start(bf16[32,64,256]{2,1,0:T(8,128)(2,1)} %get-tuple-element.52), calls=%async_computation.5 | async-start | bytes 2097152 | tf_op jit(solution)/shard_map/all_to_all | solution.py:41
  231.3 31.3 %collective-permute-start.7 = (bf16[14,2,32,256]{3,2,1,0:T(8,128)(2,1)}, bf16[14,2,32,256]{3,2,1,0:T(8,128)(2,1)S(1)}, u32[]{:S(2)}, u32[]{:S(2)}) collective-permute-start(bf16[14,2,32,256]{3,2,1,0:T(8,128)(2,1)} %get-tuple-element.56), channel_id=1, source_target_pairs={{0,3},{1,0},{2,1},{3,2},{4,7},{5,4},{6,5},{7,6},{8,11},{9,8},{10,9... | collective-permute-start | bytes 1376264 | tf_op jit(solution)/shard_map/ppermute | solution.py:50
  233.2 29.4 %collective-permute-start.8 = (bf16[14,2,32,256]{3,2,1,0:T(8,128)(2,1)}, bf16[14,2,32,256]{3,2,1,0:T(8,128)(2,1)}, u32[]{:S(2)}, u32[]{:S(2)}) collective-permute-start(bf16[14,2,32,256]{3,2,1,0:T(8,128)(2,1)} %get-tuple-element.57), channel_id=1, source_target_pairs={{0,1},{1,2},{2,3},{3,0},{4,5},{5,6},{6,7},{7,4},{8,9},{9,10},{10,1... | collective-permute-start | bytes 1376264 | tf_op jit(solution)/shard_map/ppermute | solution.py:50
  257.4 1.5 copy-start.5
  261.3 1.3 copy-start.6
  262.6 5.6 %copy-start.23 = (bf16[14,32,256]{2,1,0:T(8,128)(2,1)S(1)}, bf16[14,32,256]{2,1,0:T(8,128)(2,1)}, u32[]{:S(2)}) copy-start(bf16[14,32,256]{2,1,0:T(8,128)(2,1)} %get-tuple-element.62) | copy-start | bytes 688132
  262.6 32.2 %all-to-all-start.6 = ((bf16[32,128,256]{2,1,0:T(8,128)(2,1)}), bf16[32,128,256]{2,1,0:T(8,128)(2,1)S(1)}, u32[]{:S(2)}, u32[]{:S(2)}) async-start(bf16[32,128,256]{2,1,0:T(8,128)(2,1)} %bitcast.13), calls=%async_computation.6 | async-start | bytes 4194304 | tf_op jit(solution)/shard_map/all_to_all | solution.py:41
  267.2 3.1 copy-start.22
  268.3 24.2 %collective-permute-start.10 = (bf16[14,2,32,256]{3,2,1,0:T(8,128)(2,1)S(1)}, bf16[14,2,32,256]{3,2,1,0:T(8,128)(2,1)S(1)}, u32[]{:S(2)}, u32[]{:S(2)}) collective-permute-start(bf16[14,2,32,256]{3,2,1,0:T(8,128)(2,1)S(1)} %pad_maximum_fusion.1), channel_id=1, source_target_pairs={{0,1},{1,2},{2,3},{3,0},{4,5},{5,6},{6,7},{7,4},{8,9},{9,10},{10,1... | collective-permute-start | bytes 1376264 | tf_op jit(solution)/shard_map/ppermute | solution.py:50
  270.3 23.7 %collective-permute-start.9 = (bf16[14,2,32,256]{3,2,1,0:T(8,128)(2,1)S(1)}, bf16[14,2,32,256]{3,2,1,0:T(8,128)(2,1)S(1)}, u32[]{:S(2)}, u32[]{:S(2)}) collective-permute-start(bf16[14,2,32,256]{3,2,1,0:T(8,128)(2,1)S(1)} %pad_maximum_fusion), channel_id=1, source_target_pairs={{0,3},{1,0},{2,1},{3,2},{4,7},{5,4},{6,5},{7,6},{8,11},{9,8},{10,9... | collective-permute-start | bytes 1376264 | tf_op jit(solution)/shard_map/ppermute | solution.py:50
  292.5 0.8 copy-start.15
  294.1 0.8 copy-start.17
  294.8 4.6 %copy-start.14 = (bf16[14,2,32,256]{3,2,1,0:T(8,128)(2,1)S(1)}, bf16[14,2,32,256]{3,2,1,0:T(8,128)(2,1)}, u32[]{:S(2)}) copy-start(bf16[14,2,32,256]{3,2,1,0:T(8,128)(2,1)} %get-tuple-element.54.own) | copy-start | bytes 1376260
  295.9 18.6 %all-to-all-start.7 = ((bf16[8,128,256]{2,1,0:T(8,128)(2,1)}), bf16[8,128,256]{2,1,0:T(8,128)(2,1)S(1)}, u32[]{:S(2)}, u32[]{:S(2)}) async-start(bf16[8,128,256]{2,1,0:T(8,128)(2,1)} %shard_map.101), calls=%async_computation.7 | async-start | bytes 1048576 | tf_op jit(solution)/shard_map/all_to_all | solution.py:41
  299.4 1.0 copy-start.16
  300.4 1.0 copy-start.18
Sparse Core Ops, SparseCore 0:
  10.1 62.0 all-gather.2

commit v9 on v8

--- a/solution.py
+++ b/solution.py
@@ -79,35 +79,36 @@
     return jnp.concatenate([both[:half, :HEAD_DIM], both[half:, HEAD_DIM:]], axis=1)
 
 
-def pieces(row, count):
-    index = lax.broadcasted_iota(jnp.int32, (EXTRA, row.shape[1]), 0)
-    tile = jnp.zeros((EXTRA, row.shape[1]), F32)
-    rest = row
-    for i in range(count):
-        part = rest.astype(BF).astype(F32)
-        tile = jnp.where(index == i, part, tile)
-        rest = rest - part
+def pieces(rows):
+    index = lax.broadcasted_iota(jnp.int32, (EXTRA, rows[0].shape[1]), 0)
+    tile = jnp.zeros((EXTRA, rows[0].shape[1]), F32)
+    for k, rest in enumerate(rows):
+        for i in range(3):
+            part = rest.astype(BF).astype(F32)
+            tile = jnp.where(index == 3 * k + i, part, tile)
+            rest = rest - part
     return tile.astype(BF)
 
 
-def write_slot(slots, slot, block, row, count):
+def joined(tile, k):
+    index = lax.broadcasted_iota(jnp.int32, tile.shape, 0)
+    ours = (index >= 3 * k) & (index < 3 * k + 3)
+    return jnp.sum(jnp.where(ours, tile, 0.0), axis=0, keepdims=True)
+
+
+def write_slot(slots, slot, block, rows):
     width = block.shape[1]
     for i in range(GROUP_LEN // EXTRA):
         slots[slot, :, i * width : (i + 1) * width] = block[i * EXTRA : (i + 1) * EXTRA]
-    slots[slot, :, GROUP_LEN // EXTRA * width :] = pieces(row, count)
-
-
-def read_slot(slots, slot, width, count):
+    slots[slot, :, GROUP_LEN // EXTRA * width :] = pieces(rows)
+
+
+def read_slot(slots, slot, width):
     folds = GROUP_LEN // EXTRA
     tile = slots[slot]
     block = jnp.concatenate([tile[:, i * width : (i + 1) * width] for i in range(folds)], axis=0)
-    return block, joined(tile[:, folds * width :], count)
-
-
-def joined(tile, count):
-    tile = tile.astype(F32)
-    index = lax.broadcasted_iota(jnp.int32, tile.shape, 0)
-    return jnp.sum(jnp.where(index < count, tile, 0.0), axis=0, keepdims=True)
+    extra = tile[:, folds * width :].astype(F32)
+    return block, joined(extra, 0), joined(extra, 1)
 
 
 def split_kernel(place, block0, block1, block2, block3, own, first, last, far_keys, far_values):
@@ -161,7 +162,7 @@
         prob = expo / total
         probs[n] = prob
         out = own_head(dot(prob.astype(BF), values, FIRST))
-        write_slot(slots, t, out.astype(BF), top + jnp.log(total), 3)
+        write_slot(slots, t, out.astype(BF), [top, total])
 
 
 def combine_kernel(source, arrived, d_mixed, gain, attended, shares, stats):
@@ -170,11 +171,11 @@
     width = attended.shape[1]
     for c in range(source.shape[0] // NEIGHBOURS):
         here = slice(c * GROUP_LEN, (c + 1) * GROUP_LEN)
-        values, logs = zip(
-            *[read_slot(arrived, source[NEIGHBOURS * c + k], width, 3) for k in range(NEIGHBOURS)]
+        values, tops, totals = zip(
+            *[read_slot(arrived, source[NEIGHBOURS * c + k], width) for k in range(NEIGHBOURS)]
         )
-        top = jnp.maximum(logs[0], logs[1])
-        expos = [jnp.exp(log - top) for log in logs]
+        top = jnp.maximum(tops[0], tops[1])
+        expos = [total * jnp.exp(part - top) for part, total in zip(tops, totals)]
         rest = 1.0 / (expos[0] + expos[1])
         out = jnp.zeros((GROUP_LEN, 2 * HEAD_DIM), F32)
         for k in range(NEIGHBOURS):
@@ -220,14 +221,10 @@
             ],
             axis=0,
         )
+        delta = as_row(delta)
         for k in range(NEIGHBOURS):
-            slot = source[NEIGHBOURS * c + k]
-            share = as_column(shares[NEIGHBOURS * c + k : NEIGHBOURS * c + k + 1, :])
-            scaled = jnp.concatenate(
-                [grad[:, :HEAD_DIM] * share[:GROUP_LEN], grad[:, HEAD_DIM:] * share[GROUP_LEN:]],
-                axis=1,
-            )
-            write_slot(slots, slot, scaled.astype(BF), as_row(delta * share), 2)
+            share = shares[NEIGHBOURS * c + k : NEIGHBOURS * c + k + 1, :]
+            write_slot(slots, source[NEIGHBOURS * c + k], grad.astype(BF), [share, delta])
 
 
 def owner_backward_kernel(target, arrived, queries, probs, *refs):
@@ -235,10 +232,10 @@
     for n in range(target.shape[0]):
         t = target[n]
         keys, values = whole_rows(n, *kv_refs)
-        block, delta = read_slot(arrived, t, keys.shape[1], 2)
+        block, share, delta = read_slot(arrived, t, keys.shape[1])
         grad = by_head(block)
         query = by_head(queries[t])
-        prob = probs[n]
+        prob = probs[n] * share
         grad_scores = (prob * (dot(values, grad, LAST) - delta)).astype(BF)
         slots[t] = (own_head(dot(grad_scores, keys, FIRST)) * SCALE).astype(BF)
         grad_keys = (dot(grad_scores, query, PLAIN) * SCALE).astype(BF)

time: 326 us -> 325 us (level)
  no operation moved by 1% of the time
where the time goes in v9:
time: 325 us; the launch traced here: 322 us
  waiting for transfers between devices  104 us (32%)
  blocking collectives  92.2 us (28%)
  starting transfers between devices  72.9 us (22%)
  Pallas kernels  23.8 us (7%)
  between operations  14.4 us (4%)
  local copies, waits for them, and re-layouts  13.3 us (4%)
    all_to_all x3, blocking collectives, exchange(): return lax.all_to_all(array, axes, split_axis=0, concat_axis=0, tiled=True)  92.2 us
    ppermute x11, waiting for transfers between devices, shift(): lax.ppermute(array, axis, [(i, (i + step) % size) for i in range(size)])  65.7 us
    ppermute x11, starting transfers between devices, shift(): lax.ppermute(array, axis, [(i, (i + step) % size) for i in range(size)])  37.7 us
    all_to_all x5, starting transfers between devices, exchange(): return lax.all_to_all(array, axes, split_axis=0, concat_axis=0, tiled=True)  35.1 us
    all_to_all x5, waiting for transfers between devices, exchange(): return lax.all_to_all(array, axes, split_axis=0, concat_axis=0, tiled=True)  29.6 us
    pallas_call x6, Pallas kernels, call(): pl.pallas_call(kernel, in_specs=[SMEM] * len(scalars) + [VMEM] * len(arra...  15.2 us
    unnamed x51, local copies, waits for them, and re-layouts  9.68 us
    all_gather x1, waiting for transfers between devices, shards(): line = lax.all_gather(hidden, LINE, axis=0)  8.06 us
  transfers between devices with their start and end apart: 17, of which 12 were waited for; matrix products, arithmetic and copies ran while one was open for 1% of the time, Pallas kernels for 2%

profile of v9, /device:TPU:1, one launch (start us, length us, event | category | flops | bytes accessed | tf_op | source)
XLA Modules:
  0.0 321.6 jit_solution(11013175940750159883)
XLA Ops:
  7.2 0.0 all-gather.3.cloned.1.call-start
  7.2 0.7 all-gather.3.cloned.1.call-update
  7.9 2.4 broadcast_in_dim.28
  10.3 14.0 %all-to-all-start = ((bf16[32,128,256]{2,1,0:T(8,128)(2,1)}), bf16[32,128,256]{2,1,0:T(8,128)(2,1)}, u32[]{:S(2)}, u32[]{:S(2)}) async-start(bf16[32,128,256]{2,1,0:T(8,128)(2,1)} %broadcast_in_dim.28), calls=%async_computation | async-start | bytes 4194304 | tf_op jit(solution)/shard_map/all_to_all | solution.py:41
  24.3 0.1 pad_add_fusion.place
  24.4 1.6 shard_map.93
  25.9 4.2 %collective-permute-start = (bf16[14,32,256]{2,1,0:T(8,128)(2,1)S(1)}, bf16[14,32,256]{2,1,0:T(8,128)(2,1)S(1)}, u32[]{:S(2)}, u32[]{:S(2)}) collective-permute-start(bf16[14,32,256]{2,1,0:T(8,128)(2,1)S(1)} %get-tuple-element.35), channel_id=1, source_target_pairs={{0,1},{1,2},{2,3},{3,0},{4,5},{5,6},{6,7},{7,4},{8,9},{9,10},{10,1... | collective-permute-start | bytes 688136 | tf_op jit(solution)/shard_map/ppermute | solution.py:50
  30.1 3.6 %collective-permute-start.2 = (bf16[14,32,256]{2,1,0:T(8,128)(2,1)S(1)}, bf16[14,32,256]{2,1,0:T(8,128)(2,1)S(1)}, u32[]{:S(2)}, u32[]{:S(2)}) collective-permute-start(bf16[14,32,256]{2,1,0:T(8,128)(2,1)S(1)} %get-tuple-element.36), channel_id=1, source_target_pairs={{0,3},{1,0},{2,1},{3,2},{4,7},{5,4},{6,5},{7,6},{8,11},{9,8},{10,9... | collective-permute-start | bytes 688136 | tf_op jit(solution)/shard_map/ppermute | solution.py:50
  33.7 9.6 %collective-permute-done = bf16[14,32,256]{2,1,0:T(8,128)(2,1)S(1)} collective-permute-done((bf16[14,32,256]{2,1,0:T(8,128)(2,1)S(1)}, bf16[14,32,256]{2,1,0:T(8,128)(2,1)S(1)}, u32[]{:S(2)}, u32[]{:S(2)}) %collective-permute-start) | collective-permute-done | bytes 229408 | tf_op jit(solution)/shard_map/ppermute | solution.py:50
  43.4 4.1 %collective-permute-start.1 = (bf16[14,32,256]{2,1,0:T(8,128)(2,1)S(1)}, bf16[14,32,256]{2,1,0:T(8,128)(2,1)S(1)}, u32[]{:S(2)}, u32[]{:S(2)}) collective-permute-start(bf16[14,32,256]{2,1,0:T(8,128)(2,1)S(1)} %collective-permute-done), channel_id=1, source_target_pairs={{0,1},{1,2},{2,3},{3,0},{4,5},{5,6},{6,7},{7,4},{8,9},{9,10},{10,1... | collective-permute-start | bytes 688136 | tf_op jit(solution)/shard_map/ppermute | solution.py:50
  47.5 3.2 collective-permute-done.2
  50.6 1.9 collective-permute-start.3
  52.5 5.0 %collective-permute-done.1.far_keys.refs_3_ = bf16[14,32,256]{2,1,0:T(8,128)(2,1)S(1)} collective-permute-done((bf16[14,32,256]{2,1,0:T(8,128)(2,1)S(1)}, bf16[14,32,256]{2,1,0:T(8,128)(2,1)S(1)}, u32[]{:S(2)}, u32[]{:S(2)}) %collective-permute-start.1) | collective-permute-done | bytes 229408 | tf_op jit(solution)/shard_map/ppermute | solution.py:50
  57.5 6.6 %collective-permute-done.3.far_values.refs_4_ = bf16[14,32,256]{2,1,0:T(8,128)(2,1)S(1)} collective-permute-done((bf16[14,32,256]{2,1,0:T(8,128)(2,1)S(1)}, bf16[14,32,256]{2,1,0:T(8,128)(2,1)S(1)}, u32[]{:S(2)}, u32[]{:S(2)}) %collective-permute-start.3) | collective-permute-done | bytes 229408 | tf_op jit(solution)/shard_map/ppermute | solution.py:50
  64.1 8.1 %all-gather.3.cloned.1.call-done = bf16[3584,256]{1,0:T(8,128)(2,1)} async-done(((bf16[448,256]{1,0:T(8,128)(2,1)}), bf16[3584,256]{1,0:T(8,128)(2,1)}) %all-gather.3.cloned.1.call-update) | async-done | bytes 1835024 | tf_op jit(solution)/shard_map/all_gather | solution.py:368
  72.1 3.0 collective-permute-start.4
  75.1 0.1 copy.11
  75.3 0.1 reshape.43
  75.4 0.1 and_select_fusion.source
  75.5 0.0 all-to-all-done
  75.5 3.2 collective-permute-done.4.other
  78.7 2.2 copy-done.2
  80.9 3.7 %shard_map.94 = bf16[32,64,256]{2,1,0:T(8,128)(2,1)} custom-call(s32[2]{0:T(128)S(1)} %pad_add_fusion.place, s32[14]{0:T(128)S(1)} %and_select_fusion.source, bf16[8,448,256]{2,1,0:T(8,128)(2,1)S(1)} %bitcast.11, bf16[8,448,256]{2,1,0:T(8,128)(2,1)S(1)} %collective-permute-done.4.other, bf16[4096,256]{1,0:T(8,128)(2,1)} %bitcast.3.weight), custom_call_target="tpu_custom_call" | custom-call | tf_op jit(solution)/shard_map/pallas_call | solution.py:379
  84.6 9.0 %all-to-all-start.1 = ((bf16[32,64,256]{2,1,0:T(8,128)(2,1)}), bf16[32,64,256]{2,1,0:T(8,128)(2,1)S(1)}, u32[]{:S(2)}, u32[]{:S(2)}) async-start(bf16[32,64,256]{2,1,0:T(8,128)(2,1)} %shard_map.94), calls=%async_computation.1 | async-start | bytes 2097152 | tf_op jit(solution)/shard_map/all_to_all | solution.py:41
  93.6 4.0 %collective-permute-start.5 = (bf16[14,2,32,256]{3,2,1,0:T(8,128)(2,1)}, bf16[14,2,32,256]{3,2,1,0:T(8,128)(2,1)S(1)}, u32[]{:S(2)}, u32[]{:S(2)}) collective-permute-start(bf16[14,2,32,256]{3,2,1,0:T(8,128)(2,1)} %get-tuple-element.41), channel_id=1, source_target_pairs={{0,1},{1,2},{2,3},{3,0},{4,5},{5,6},{6,7},{7,4},{8,9},{9,10},{10,1... | collective-permute-start | bytes 1376264 | tf_op jit(solution)/shard_map/ppermute | solution.py:50
  97.6 3.4 %collective-permute-start.6 = (bf16[14,2,32,256]{3,2,1,0:T(8,128)(2,1)}, bf16[14,2,32,256]{3,2,1,0:T(8,128)(2,1)S(1)}, u32[]{:S(2)}, u32[]{:S(2)}) collective-permute-start(bf16[14,2,32,256]{3,2,1,0:T(8,128)(2,1)} %copy-done.21), channel_id=1, source_target_pairs={{0,3},{1,0},{2,1},{3,2},{4,7},{5,4},{6,5},{7,6},{8,11},{9,8},{10,9... | collective-permute-start | bytes 1376264 | tf_op jit(solution)/shard_map/ppermute | solution.py:50
  101.0 0.2 select_reduce_fusion.target
  101.2 18.6 %collective-permute-done.5.first.refs_1_ = bf16[14,2,32,256]{3,2,1,0:T(8,128)(2,1)S(1)} collective-permute-done((bf16[14,2,32,256]{3,2,1,0:T(8,128)(2,1)}, bf16[14,2,32,256]{3,2,1,0:T(8,128)(2,1)S(1)}, u32[]{:S(2)}, u32[]{:S(2)}) %collective-permute-start.5) | collective-permute-done | bytes 458784 | tf_op jit(solution)/shard_map/ppermute | solution.py:50
  119.8 2.0 collective-permute-done.6.last.refs_2_
  121.8 0.0 all-to-all-done.1.arrived.queries
  121.9 1.7 shard_map.95
  123.6 0.9 copy-done.10
  124.5 39.8 %all_to_all.40.arrived = bf16[32,16,1152]{2,1,0:T(8,128)(2,1)S(1)} all-to-all(bf16[32,16,1152]{2,1,0:T(8,128)(2,1)S(1)} %get-tuple-element.45), channel_id=1, replica_groups=mesh['yl'=2,'co'=2,'dz'=8,'dx'=4,'mp'=4] {'dz','dx'}, dimensions={0} | all-to-all | bytes 2359296 | tf_op jit(solution)/shard_map/all_to_all | solution.py:41
  164.3 1.6 shard_map.96
  165.9 16.1 %all_to_all.41.moved = f32[16,8,128]{2,1,0:T(8,128)S(1)} all-to-all(f32[16,8,128]{2,1,0:T(8,128)S(1)} %broadcast_in_dim.29), channel_id=1, replica_groups=mesh['yl'=2,'co'=2,'dz'=8,'dx'=4,'mp'=4] {'yl','co','mp'}, dimensions={0} | all-to-all | bytes 131072 | tf_op jit(solution)/shard_map/all_to_all | solution.py:41
  182.1 2.0 shard_map.97
  184.1 36.2 %all_to_all.42.arrived = bf16[32,16,1152]{2,1,0:T(8,128)(2,1)} all-to-all(bf16[32,16,1152]{2,1,0:T(8,128)(2,1)S(1)} %get-tuple-element.50), channel_id=1, replica_groups=mesh['yl'=2,'co'=2,'dz'=8,'dx'=4,'mp'=4] {'dz','dx'}, dimensions={0} | all-to-all | bytes 2359296 | tf_op jit(solution)/shard_map/all_to_all | solution.py:41
  220.3 6.5 %shard_map.98 = (bf16[32,64,256]{2,1,0:T(8,128)(2,1)}, bf16[14,2,32,256]{3,2,1,0:T(8,128)(2,1)}, bf16[14,2,32,256]{3,2,1,0:T(8,128)(2,1)}, bf16[14,2,32,256]{3,2...) custom-call(s32[14]{0:T(128)} %copy-done.19, bf16[32,16,1152]{2,1,0:T(8,128)(2,1)} %all_to_all.42.arrived, ...), custom_call_target="tpu_custom_call" | custom-call | tf_op jit(solution)/shard_map/pallas_call | solution.py:31
  226.8 4.1 %all-to-all-start.5 = ((bf16[32,64,256]{2,1,0:T(8,128)(2,1)}), bf16[32,64,256]{2,1,0:T(8,128)(2,1)S(1)}, u32[]{:S(2)}, u32[]{:S(2)}) async-start(bf16[32,64,256]{2,1,0:T(8,128)(2,1)} %get-tuple-element.52), calls=%async_computation.5 | async-start | bytes 2097152 | tf_op jit(solution)/shard_map/all_to_all | solution.py:41
  230.9 1.9 collective-permute-start.7
  232.8 4.3 %collective-permute-start.8 = (bf16[14,2,32,256]{3,2,1,0:T(8,128)(2,1)}, bf16[14,2,32,256]{3,2,1,0:T(8,128)(2,1)}, u32[]{:S(2)}, u32[]{:S(2)}) collective-permute-start(bf16[14,2,32,256]{3,2,1,0:T(8,128)(2,1)} %get-tuple-element.57), channel_id=1, source_target_pairs={{0,1},{1,2},{2,3},{3,0},{4,5},{5,6},{6,7},{7,4},{8,9},{9,10},{10,1... | collective-permute-start | bytes 1376264 | tf_op jit(solution)/shard_map/ppermute | solution.py:50
  237.1 19.9 %all-to-all-done.5.arrived = bf16[32,64,256]{2,1,0:T(8,128)(2,1)S(1)} async-done(((bf16[32,64,256]{2,1,0:T(8,128)(2,1)}), bf16[32,64,256]{2,1,0:T(8,128)(2,1)S(1)}, u32[]{:S(2)}, u32[]{:S(2)}) %all-to-all-start.5) | async-done | bytes 1048608 | tf_op jit(solution)/shard_map/all_to_all | solution.py:41
  256.9 1.5 copy-done.5
  258.4 2.4 shard_map.99
  260.8 1.3 copy-done.6
  262.2 0.0 collective-permute-done.7.up
  262.2 0.0 collective-permute-done.8.down
  262.2 4.6 %all-to-all-start.6 = ((bf16[32,128,256]{2,1,0:T(8,128)(2,1)}), bf16[32,128,256]{2,1,0:T(8,128)(2,1)S(1)}, u32[]{:S(2)}, u32[]{:S(2)}) async-start(bf16[32,128,256]{2,1,0:T(8,128)(2,1)} %bitcast.13), calls=%async_computation.6 | async-start | bytes 4194304 | tf_op jit(solution)/shard_map/all_to_all | solution.py:41
  266.8 1.0 slice.7
  267.9 2.0 collective-permute-start.10
  269.8 0.1 pad_maximum_fusion
  269.9 5.4 %collective-permute-start.9 = (bf16[14,2,32,256]{3,2,1,0:T(8,128)(2,1)S(1)}, bf16[14,2,32,256]{3,2,1,0:T(8,128)(2,1)S(1)}, u32[]{:S(2)}, u32[]{:S(2)}) collective-permute-start(bf16[14,2,32,256]{3,2,1,0:T(8,128)(2,1)S(1)} %pad_maximum_fusion), channel_id=1, source_target_pairs={{0,3},{1,0},{2,1},{3,2},{4,7},{5,4},{6,5},{7,6},{8,11},{9,8},{10,9... | collective-permute-start | bytes 1376264 | tf_op jit(solution)/shard_map/ppermute | solution.py:50
  275.3 16.7 %collective-permute-done.10.far_down = bf16[14,2,32,256]{3,2,1,0:T(8,128)(2,1)S(1)} collective-permute-done((bf16[14,2,32,256]{3,2,1,0:T(8,128)(2,1)S(1)}, bf16[14,2,32,256]{3,2,1,0:T(8,128)(2,1)S(1)}, u32[]{:S(2)}, u32[]{:S(2)}) %collective-permute-start.10) | collective-permute-done | bytes 458784 | tf_op jit(solution)/shard_map/ppermute | solution.py:50
  292.1 0.8 copy-done.15
  292.8 0.8 collective-permute-done.9.far_up
  293.6 0.8 copy-done.17
  294.4 0.0 all-to-all-done.6
  294.4 1.1 shard_map.101
  295.5 3.5 %all-to-all-start.7 = ((bf16[8,128,256]{2,1,0:T(8,128)(2,1)}), bf16[8,128,256]{2,1,0:T(8,128)(2,1)S(1)}, u32[]{:S(2)}, u32[]{:S(2)}) async-start(bf16[8,128,256]{2,1,0:T(8,128)(2,1)} %shard_map.101), calls=%async_computation.7 | async-start | bytes 1048576 | tf_op jit(solution)/shard_map/all_to_all | solution.py:41
  299.0 1.0 copy-done.16
  300.0 1.0 copy-done.18
  301.0 3.4 %shard_map.100 = bf16[14,2,32,1024]{3,2,1,0:T(8,128)(2,1)} custom-call(s32[2]{0:T(128)S(1)} %pad_add_fusion.place, bf16[14,2,32,256]{3,2,1,0:T(8,128)(2,1)S(1)} %copy-done.14, bf16[14,2,32,256]{3,2,1,0:T(8,128)(2,1)S(1)} %collective-permute-done.7.up, bf16[14,2,32,256]{3,2,1,0:T(8,128)(2,1)} %collective-permute-done.8.down, ...), custom_call_target="tpu_custom_call" | custom-call | tf_op jit(solution)/shard_map/pallas_call | solution.py:327
  304.4 9.7 %all-to-all-done.7 = bf16[8,128,256]{2,1,0:T(8,128)(2,1)S(1)} async-done(((bf16[8,128,256]{2,1,0:T(8,128)(2,1)}), bf16[8,128,256]{2,1,0:T(8,128)(2,1)S(1)}, u32[]{:S(2)}, u32[]{:S(2)}) %all-to-all-start.7) | async-done | bytes 524320 | tf_op jit(solution)/shard_map/all_to_all | solution.py:41
  314.1 0.7 reduce_sum.22
  (47 shorter events, 0.2 us)
Async XLA Ops:
  7.2 65.0 %all-gather.3.cloned.1.call-start = ((), (), s32[]{:S(2)}) async-start(), calls=%async_computation.8 | async-start | bytes 2064384 | tf_op jit(solution)/shard_map/all_gather | solution.py:368
  10.3 14.1 %copy-start = (bf16[14,2,32,1024]{3,2,1,0:T(8,128)(2,1)S(1)}, bf16[14,2,32,1024]{3,2,1,0:T(8,128)(2,1)}, u32[]{:S(2)}) copy-start(bf16[14,2,32,1024]{3,2,1,0:T(8,128)(2,1)} %block3.1) | copy-start | bytes 5505028
  10.3 65.2 %all-to-all-start = ((bf16[32,128,256]{2,1,0:T(8,128)(2,1)}), bf16[32,128,256]{2,1,0:T(8,128)(2,1)}, u32[]{:S(2)}, u32[]{:S(2)}) async-start(bf16[32,128,256]{2,1,0:T(8,128)(2,1)} %broadcast_in_dim.28), calls=%async_computation | async-start | bytes 4194304 | tf_op jit(solution)/shard_map/all_to_all | solution.py:41
  24.4 50.7 %copy-start.24 = (s32[224,2]{0,1:T(2,128)S(1)}, s32[224,2]{0,1:T(2,128)}, u32[]{:S(2)}) copy-start(s32[224,2]{0,1:T(2,128)} %param.9) | copy-start | bytes 5380
  25.9 31.6 %copy-start.21 = (bf16[14,2,32,256]{3,2,1,0:T(8,128)(2,1)}, bf16[14,2,32,256]{3,2,1,0:T(8,128)(2,1)S(1)}, u32[]{:S(2)}) copy-start(bf16[14,2,32,256]{3,2,1,0:T(8,128)(2,1)S(1)} %get-tuple-element.42) | copy-start | bytes 1376260
  25.9 95.9 %copy-start.7 = (bf16[14,2,32,256]{3,2,1,0:T(8,128)(2,1)}, bf16[14,2,32,256]{3,2,1,0:T(8,128)(2,1)S(1)}, u32[]{:S(2)}) copy-start(bf16[14,2,32,256]{3,2,1,0:T(8,128)(2,1)S(1)} %get-tuple-element.40.own.refs_0_) | copy-start | bytes 1376260
  25.9 17.4 %collective-permute-start = (bf16[14,32,256]{2,1,0:T(8,128)(2,1)S(1)}, bf16[14,32,256]{2,1,0:T(8,128)(2,1)S(1)}, u32[]{:S(2)}, u32[]{:S(2)}) collective-permute-start(bf16[14,32,256]{2,1,0:T(8,128)(2,1)S(1)} %get-tuple-element.35), channel_id=1, source_target_pairs={{0,1},{1,2},{2,3},{3,0},{4,5},{5,6},{6,7},{7,4},{8,9},{9,10},{10,1... | collective-permute-start | bytes 688136 | tf_op jit(solution)/shard_map/ppermute | solution.py:50
  30.1 20.5 %collective-permute-start.2 = (bf16[14,32,256]{2,1,0:T(8,128)(2,1)S(1)}, bf16[14,32,256]{2,1,0:T(8,128)(2,1)S(1)}, u32[]{:S(2)}, u32[]{:S(2)}) collective-permute-start(bf16[14,32,256]{2,1,0:T(8,128)(2,1)S(1)} %get-tuple-element.36), channel_id=1, source_target_pairs={{0,3},{1,0},{2,1},{3,2},{4,7},{5,4},{6,5},{7,6},{8,11},{9,8},{10,9... | collective-permute-start | bytes 688136 | tf_op jit(solution)/shard_map/ppermute | solution.py:50
  43.4 14.1 %collective-permute-start.1 = (bf16[14,32,256]{2,1,0:T(8,128)(2,1)S(1)}, bf16[14,32,256]{2,1,0:T(8,128)(2,1)S(1)}, u32[]{:S(2)}, u32[]{:S(2)}) collective-permute-start(bf16[14,32,256]{2,1,0:T(8,128)(2,1)S(1)} %collective-permute-done), channel_id=1, source_target_pairs={{0,1},{1,2},{2,3},{3,0},{4,5},{5,6},{6,7},{7,4},{8,9},{9,10},{10,1... | collective-permute-start | bytes 688136 | tf_op jit(solution)/shard_map/ppermute | solution.py:50
  50.6 13.5 %collective-permute-start.3 = (bf16[14,32,256]{2,1,0:T(8,128)(2,1)S(1)}, bf16[14,32,256]{2,1,0:T(8,128)(2,1)S(1)}, u32[]{:S(2)}, u32[]{:S(2)}) collective-permute-start(bf16[14,32,256]{2,1,0:T(8,128)(2,1)S(1)} %collective-permute-done.2), channel_id=1, source_target_pairs={{0,3},{1,0},{2,1},{3,2},{4,7},{5,4},{6,5},{7,6},{8,11},{9,8},{10,9... | collective-permute-start | bytes 688136 | tf_op jit(solution)/shard_map/ppermute | solution.py:50
  57.5 64.3 %copy-start.11 = (bf16[14,32,256]{2,1,0:T(8,128)(2,1)}, bf16[14,32,256]{2,1,0:T(8,128)(2,1)S(1)}, u32[]{:S(2)}) copy-start(bf16[14,32,256]{2,1,0:T(8,128)(2,1)S(1)} %collective-permute-done.1.far_keys.refs_3_) | copy-start | bytes 688132
  64.1 57.8 %copy-start.12 = (bf16[14,32,256]{2,1,0:T(8,128)(2,1)}, bf16[14,32,256]{2,1,0:T(8,128)(2,1)S(1)}, u32[]{:S(2)}) copy-start(bf16[14,32,256]{2,1,0:T(8,128)(2,1)S(1)} %collective-permute-done.3.far_values.refs_4_) | copy-start | bytes 688132
  72.1 6.6 %collective-permute-start.4 = (bf16[8,448,256]{2,1,0:T(8,128)(2,1)}, bf16[8,448,256]{2,1,0:T(8,128)(2,1)S(1)}, u32[]{:S(2)}, u32[]{:S(2)}) collective-permute-start(bf16[8,448,256]{2,1,0:T(8,128)(2,1)} %bitcast.10), channel_id=1, source_target_pairs={{0,128},{128,0},{1,129},{129,1},{2,130},{130,2},{3,131},{131,3},{4... | collective-permute-start | bytes 5505032 | tf_op jit(solution)/shard_map/ppermute | solution.py:50
  78.7 5.9 %copy-start.4 = (bf16[8,448,256]{2,1,0:T(8,128)(2,1)}, bf16[8,448,256]{2,1,0:T(8,128)(2,1)S(1)}, u32[]{:S(2)}) copy-start(bf16[8,448,256]{2,1,0:T(8,128)(2,1)S(1)} %collective-permute-done.4.other) | copy-start | bytes 5505028
  78.7 2.2 copy-start.2
  84.6 37.3 %all-to-all-start.1 = ((bf16[32,64,256]{2,1,0:T(8,128)(2,1)}), bf16[32,64,256]{2,1,0:T(8,128)(2,1)S(1)}, u32[]{:S(2)}, u32[]{:S(2)}) async-start(bf16[32,64,256]{2,1,0:T(8,128)(2,1)} %shard_map.94), calls=%async_computation.1 | async-start | bytes 2097152 | tf_op jit(solution)/shard_map/all_to_all | solution.py:41
  93.6 26.2 %collective-permute-start.5 = (bf16[14,2,32,256]{3,2,1,0:T(8,128)(2,1)}, bf16[14,2,32,256]{3,2,1,0:T(8,128)(2,1)S(1)}, u32[]{:S(2)}, u32[]{:S(2)}) collective-permute-start(bf16[14,2,32,256]{3,2,1,0:T(8,128)(2,1)} %get-tuple-element.41), channel_id=1, source_target_pairs={{0,1},{1,2},{2,3},{3,0},{4,5},{5,6},{6,7},{7,4},{8,9},{9,10},{10,1... | collective-permute-start | bytes 1376264 | tf_op jit(solution)/shard_map/ppermute | solution.py:50
  97.6 24.3 %collective-permute-start.6 = (bf16[14,2,32,256]{3,2,1,0:T(8,128)(2,1)}, bf16[14,2,32,256]{3,2,1,0:T(8,128)(2,1)S(1)}, u32[]{:S(2)}, u32[]{:S(2)}) collective-permute-start(bf16[14,2,32,256]{3,2,1,0:T(8,128)(2,1)} %copy-done.21), channel_id=1, source_target_pairs={{0,3},{1,0},{2,1},{3,2},{4,7},{5,4},{6,5},{7,6},{8,11},{9,8},{10,9... | collective-permute-start | bytes 1376264 | tf_op jit(solution)/shard_map/ppermute | solution.py:50
  101.2 63.1 %copy-start.19 = (s32[14]{0:T(128)}, s32[14]{0:T(128)S(1)}, u32[]{:S(2)}) copy-start(s32[14]{0:T(128)S(1)} %select_reduce_fusion.target) | copy-start | bytes 172
  119.8 44.5 %copy-start.8 = (bf16[14,2,32,256]{3,2,1,0:T(8,128)(2,1)}, bf16[14,2,32,256]{3,2,1,0:T(8,128)(2,1)S(1)}, u32[]{:S(2)}) copy-start(bf16[14,2,32,256]{3,2,1,0:T(8,128)(2,1)S(1)} %collective-permute-done.5.first.refs_1_) | copy-start | bytes 1376260
  121.8 42.5 %copy-start.9 = (bf16[14,2,32,256]{3,2,1,0:T(8,128)(2,1)}, bf16[14,2,32,256]{3,2,1,0:T(8,128)(2,1)S(1)}, u32[]{:S(2)}) copy-start(bf16[14,2,32,256]{3,2,1,0:T(8,128)(2,1)S(1)} %collective-permute-done.6.last.refs_2_) | copy-start | bytes 1376260
  121.9 42.5 %copy-start.1 = (bf16[32,64,256]{2,1,0:T(8,128)(2,1)}, bf16[32,64,256]{2,1,0:T(8,128)(2,1)S(1)}, u32[]{:S(2)}) copy-start(bf16[32,64,256]{2,1,0:T(8,128)(2,1)S(1)} %all-to-all-done.1.arrived.queries) | copy-start | bytes 3145732
  123.6 0.9 copy-start.10
  124.5 39.9 %copy-start.13 = (bf16[448,256]{1,0:T(8,128)(2,1)S(1)}, bf16[448,256]{1,0:T(8,128)(2,1)}, u32[]{:S(2)}) copy-start(bf16[448,256]{1,0:T(8,128)(2,1)} %d_mixed.3) | copy-start | bytes 688132
  124.5 39.9 %copy-start.20 = (f32[256]{0:T(256)S(1)}, f32[256]{0:T(256)}, u32[]{:S(2)}) copy-start(f32[256]{0:T(256)} %param.10) | copy-start | bytes 3076
  226.8 30.2 %copy-start.3 = (bf16[3584,256]{1,0:T(8,128)(2,1)S(1)}, bf16[3584,256]{1,0:T(8,128)(2,1)}, u32[]{:S(2)}) copy-start(bf16[3584,256]{1,0:T(8,128)(2,1)} %all-gather.3.cloned.1.call-done) | copy-start | bytes 5505028
  226.8 30.2 %all-to-all-start.5 = ((bf16[32,64,256]{2,1,0:T(8,128)(2,1)}), bf16[32,64,256]{2,1,0:T(8,128)(2,1)S(1)}, u32[]{:S(2)}, u32[]{:S(2)}) async-start(bf16[32,64,256]{2,1,0:T(8,128)(2,1)} %get-tuple-element.52), calls=%async_computation.5 | async-start | bytes 2097152 | tf_op jit(solution)/shard_map/all_to_all | solution.py:41
  230.9 31.3 %collective-permute-start.7 = (bf16[14,2,32,256]{3,2,1,0:T(8,128)(2,1)}, bf16[14,2,32,256]{3,2,1,0:T(8,128)(2,1)S(1)}, u32[]{:S(2)}, u32[]{:S(2)}) collective-permute-start(bf16[14,2,32,256]{3,2,1,0:T(8,128)(2,1)} %get-tuple-element.56), channel_id=1, source_target_pairs={{0,3},{1,0},{2,1},{3,2},{4,7},{5,4},{6,5},{7,6},{8,11},{9,8},{10,9... | collective-permute-start | bytes 1376264 | tf_op jit(solution)/shard_map/ppermute | solution.py:50
  232.8 29.4 %collective-permute-start.8 = (bf16[14,2,32,256]{3,2,1,0:T(8,128)(2,1)}, bf16[14,2,32,256]{3,2,1,0:T(8,128)(2,1)}, u32[]{:S(2)}, u32[]{:S(2)}) collective-permute-start(bf16[14,2,32,256]{3,2,1,0:T(8,128)(2,1)} %get-tuple-element.57), channel_id=1, source_target_pairs={{0,1},{1,2},{2,3},{3,0},{4,5},{5,6},{6,7},{7,4},{8,9},{9,10},{10,1... | collective-permute-start | bytes 1376264 | tf_op jit(solution)/shard_map/ppermute | solution.py:50
  256.9 1.5 copy-start.5
  260.8 1.3 copy-start.6
  262.2 5.6 %copy-start.23 = (bf16[14,32,256]{2,1,0:T(8,128)(2,1)S(1)}, bf16[14,32,256]{2,1,0:T(8,128)(2,1)}, u32[]{:S(2)}) copy-start(bf16[14,32,256]{2,1,0:T(8,128)(2,1)} %get-tuple-element.62) | copy-start | bytes 688132
  262.2 32.2 %all-to-all-start.6 = ((bf16[32,128,256]{2,1,0:T(8,128)(2,1)}), bf16[32,128,256]{2,1,0:T(8,128)(2,1)S(1)}, u32[]{:S(2)}, u32[]{:S(2)}) async-start(bf16[32,128,256]{2,1,0:T(8,128)(2,1)} %bitcast.13), calls=%async_computation.6 | async-start | bytes 4194304 | tf_op jit(solution)/shard_map/all_to_all | solution.py:41
  266.8 3.1 copy-start.22
  267.9 24.2 %collective-permute-start.10 = (bf16[14,2,32,256]{3,2,1,0:T(8,128)(2,1)S(1)}, bf16[14,2,32,256]{3,2,1,0:T(8,128)(2,1)S(1)}, u32[]{:S(2)}, u32[]{:S(2)}) collective-permute-start(bf16[14,2,32,256]{3,2,1,0:T(8,128)(2,1)S(1)} %pad_maximum_fusion.1), channel_id=1, source_target_pairs={{0,1},{1,2},{2,3},{3,0},{4,5},{5,6},{6,7},{7,4},{8,9},{9,10},{10,1... | collective-permute-start | bytes 1376264 | tf_op jit(solution)/shard_map/ppermute | solution.py:50
  269.9 23.7 %collective-permute-start.9 = (bf16[14,2,32,256]{3,2,1,0:T(8,128)(2,1)S(1)}, bf16[14,2,32,256]{3,2,1,0:T(8,128)(2,1)S(1)}, u32[]{:S(2)}, u32[]{:S(2)}) collective-permute-start(bf16[14,2,32,256]{3,2,1,0:T(8,128)(2,1)S(1)} %pad_maximum_fusion), channel_id=1, source_target_pairs={{0,3},{1,0},{2,1},{3,2},{4,7},{5,4},{6,5},{7,6},{8,11},{9,8},{10,9... | collective-permute-start | bytes 1376264 | tf_op jit(solution)/shard_map/ppermute | solution.py:50
  292.1 0.8 copy-start.15
  293.6 0.8 copy-start.17
  294.4 4.6 %copy-start.14 = (bf16[14,2,32,256]{3,2,1,0:T(8,128)(2,1)S(1)}, bf16[14,2,32,256]{3,2,1,0:T(8,128)(2,1)}, u32[]{:S(2)}) copy-start(bf16[14,2,32,256]{3,2,1,0:T(8,128)(2,1)} %get-tuple-element.54.own) | copy-start | bytes 1376260
  295.5 18.6 %all-to-all-start.7 = ((bf16[8,128,256]{2,1,0:T(8,128)(2,1)}), bf16[8,128,256]{2,1,0:T(8,128)(2,1)S(1)}, u32[]{:S(2)}, u32[]{:S(2)}) async-start(bf16[8,128,256]{2,1,0:T(8,128)(2,1)} %shard_map.101), calls=%async_computation.7 | async-start | bytes 1048576 | tf_op jit(solution)/shard_map/all_to_all | solution.py:41
  299.0 1.0 copy-start.16
  300.0 1.0 copy-start.18
Sparse Core Ops, SparseCore 0:
  10.1 62.0 all-gather.2

commit v10 on v9

--- a/solution.py
+++ b/solution.py
@@ -22,6 +22,7 @@
 SMEM = pl.BlockSpec(memory_space=pltpu.SMEM)
 VMEM = pl.BlockSpec(memory_space=pltpu.VMEM)
 PARAMS = pltpu.CompilerParams(vmem_limit_bytes=24 << 20)
+LARGE = pltpu.CompilerParams(vmem_limit_bytes=60 << 20)
 LAST = (((1,), (1,)), ((), ()))
 FIRST = (((0,), (0,)), ((), ()))
 PLAIN = (((1,), (0,)), ((), ()))
@@ -337,7 +338,7 @@
             ),
         ),
         out_shape=jax.ShapeDtypeStruct((n, 2, quarter, 4 * part), parts[0].dtype),
-        compiler_params=PARAMS,
+        compiler_params=LARGE,
     )(place, *parts)
 
 
@@ -416,7 +417,7 @@
         [((n_dp, GROUP_LEN, dec_width), BF)]
         + [(own.shape, BF)] * 3
         + [(far_keys.shape, BF)] * 2,
-        pltpu.CompilerParams(vmem_limit_bytes=60 << 20),
+        LARGE,
     )
     up, down = shift(up, "mp", -1), shift(down, "mp", 1)
     arrived = exchange(slots, DP)

time: 325 us -> 325 us (level)
    unnamed x51 -> x47, local copies, waits for them, and re-layouts: 9.68 us -> 6.12 us
  transfers between devices with their start and end apart: 17 -> 17, of which waited for: 12 -> 12; matrix products, arithmetic and copies ran while one was open for 1% -> 2% of each run, Pallas kernels for 2% -> 2%
where the time goes in v10:
time: 325 us; the launch traced here: 322 us
  waiting for transfers between devices  107 us (33%)
  blocking collectives  92.1 us (28%)
  starting transfers between devices  72.8 us (22%)
  Pallas kernels  24.4 us (8%)
  between operations  14.3 us (4%)
  local copies, waits for them, and re-layouts  10.6 us (3%)
    all_to_all x3, blocking collectives, exchange(): return lax.all_to_all(array, axes, split_axis=0, concat_axis=0, tiled=True)  92.1 us
    ppermute x11, waiting for transfers between devices, shift(): lax.ppermute(array, axis, [(i, (i + step) % size) for i in range(size)])  67.3 us
    ppermute x11, starting transfers between devices, shift(): lax.ppermute(array, axis, [(i, (i + step) % size) for i in range(size)])  37.7 us
    all_to_all x5, starting transfers between devices, exchange(): return lax.all_to_all(array, axes, split_axis=0, concat_axis=0, tiled=True)  35.1 us
    all_to_all x5, waiting for transfers between devices, exchange(): return lax.all_to_all(array, axes, split_axis=0, concat_axis=0, tiled=True)  31.1 us
    pallas_call x6, Pallas kernels, call(): pl.pallas_call(kernel, in_specs=[SMEM] * len(scalars) + [VMEM] * len(arra...  15.1 us
    all_gather x1, waiting for transfers between devices, shards(): line = lax.all_gather(hidden, LINE, axis=0)  7.43 us
  transfers between devices with their start and end apart: 17, of which 12 were waited for; matrix products, arithmetic and copies ran while one was open for 2% of the time, Pallas kernels for 2%

profile of v10, /device:TPU:1, one launch (start us, length us, event | category | flops | bytes accessed | tf_op | source)
XLA Modules:
  0.0 321.9 jit_solution(14519743240614994210)
XLA Ops:
  7.2 0.0 all-gather.3.cloned.1.call-start
  7.2 0.7 all-gather.3.cloned.1.call-update
  7.9 2.4 broadcast_in_dim.28
  10.3 14.0 %all-to-all-start = ((bf16[32,128,256]{2,1,0:T(8,128)(2,1)}), bf16[32,128,256]{2,1,0:T(8,128)(2,1)}, u32[]{:S(2)}, u32[]{:S(2)}) async-start(bf16[32,128,256]{2,1,0:T(8,128)(2,1)} %broadcast_in_dim.28), calls=%async_computation | async-start | bytes 4194304 | tf_op jit(solution)/shard_map/all_to_all | solution.py:42
  24.3 0.1 pad_add_fusion.place
  24.4 0.0 copy-done
  24.4 1.5 shard_map.93
  25.9 4.2 %collective-permute-start = (bf16[14,32,256]{2,1,0:T(8,128)(2,1)S(1)}, bf16[14,32,256]{2,1,0:T(8,128)(2,1)S(1)}, u32[]{:S(2)}, u32[]{:S(2)}) collective-permute-start(bf16[14,32,256]{2,1,0:T(8,128)(2,1)S(1)} %get-tuple-element.35), channel_id=1, source_target_pairs={{0,1},{1,2},{2,3},{3,0},{4,5},{5,6},{6,7},{7,4},{8,9},{9,10},{10,1... | collective-permute-start | bytes 688136 | tf_op jit(solution)/shard_map/ppermute | solution.py:51
  30.2 3.6 %collective-permute-start.2 = (bf16[14,32,256]{2,1,0:T(8,128)(2,1)S(1)}, bf16[14,32,256]{2,1,0:T(8,128)(2,1)S(1)}, u32[]{:S(2)}, u32[]{:S(2)}) collective-permute-start(bf16[14,32,256]{2,1,0:T(8,128)(2,1)S(1)} %get-tuple-element.36), channel_id=1, source_target_pairs={{0,3},{1,0},{2,1},{3,2},{4,7},{5,4},{6,5},{7,6},{8,11},{9,8},{10,9... | collective-permute-start | bytes 688136 | tf_op jit(solution)/shard_map/ppermute | solution.py:51
  33.8 9.7 %collective-permute-done = bf16[14,32,256]{2,1,0:T(8,128)(2,1)S(1)} collective-permute-done((bf16[14,32,256]{2,1,0:T(8,128)(2,1)S(1)}, bf16[14,32,256]{2,1,0:T(8,128)(2,1)S(1)}, u32[]{:S(2)}, u32[]{:S(2)}) %collective-permute-start) | collective-permute-done | bytes 229408 | tf_op jit(solution)/shard_map/ppermute | solution.py:51
  43.4 4.1 %collective-permute-start.1 = (bf16[14,32,256]{2,1,0:T(8,128)(2,1)S(1)}, bf16[14,32,256]{2,1,0:T(8,128)(2,1)S(1)}, u32[]{:S(2)}, u32[]{:S(2)}) collective-permute-start(bf16[14,32,256]{2,1,0:T(8,128)(2,1)S(1)} %collective-permute-done), channel_id=1, source_target_pairs={{0,1},{1,2},{2,3},{3,0},{4,5},{5,6},{6,7},{7,4},{8,9},{9,10},{10,1... | collective-permute-start | bytes 688136 | tf_op jit(solution)/shard_map/ppermute | solution.py:51
  47.5 3.1 collective-permute-done.2
  50.6 1.9 collective-permute-start.3
  52.6 5.3 %collective-permute-done.1.far_keys.refs_3_ = bf16[14,32,256]{2,1,0:T(8,128)(2,1)S(1)} collective-permute-done((bf16[14,32,256]{2,1,0:T(8,128)(2,1)S(1)}, bf16[14,32,256]{2,1,0:T(8,128)(2,1)S(1)}, u32[]{:S(2)}, u32[]{:S(2)}) %collective-permute-start.1) | collective-permute-done | bytes 229408 | tf_op jit(solution)/shard_map/ppermute | solution.py:51
  57.8 0.0 copy-done.17
  57.8 6.9 %collective-permute-done.3.far_values.refs_4_ = bf16[14,32,256]{2,1,0:T(8,128)(2,1)S(1)} collective-permute-done((bf16[14,32,256]{2,1,0:T(8,128)(2,1)S(1)}, bf16[14,32,256]{2,1,0:T(8,128)(2,1)S(1)}, u32[]{:S(2)}, u32[]{:S(2)}) %collective-permute-start.3) | collective-permute-done | bytes 229408 | tf_op jit(solution)/shard_map/ppermute | solution.py:51
  64.7 7.4 %all-gather.3.cloned.1.call-done = bf16[3584,256]{1,0:T(8,128)(2,1)} async-done(((bf16[448,256]{1,0:T(8,128)(2,1)}), bf16[3584,256]{1,0:T(8,128)(2,1)}) %all-gather.3.cloned.1.call-update) | async-done | bytes 1835024 | tf_op jit(solution)/shard_map/all_gather | solution.py:369
  72.2 2.9 collective-permute-start.4
  75.1 0.1 copy.11
  75.3 0.1 reshape.43
  75.4 0.1 and_select_fusion.source
  75.5 0.0 all-to-all-done
  75.5 3.2 collective-permute-done.4.other
  78.7 2.2 copy-done.2
  80.9 3.7 %shard_map.94 = bf16[32,64,256]{2,1,0:T(8,128)(2,1)} custom-call(s32[2]{0:T(128)S(1)} %pad_add_fusion.place, s32[14]{0:T(128)S(1)} %and_select_fusion.source, bf16[8,448,256]{2,1,0:T(8,128)(2,1)S(1)} %bitcast.11, bf16[8,448,256]{2,1,0:T(8,128)(2,1)S(1)} %collective-permute-done.4.other, bf16[4096,256]{1,0:T(8,128)(2,1)} %bitcast.3.weight), custom_call_target="tpu_custom_call" | custom-call | tf_op jit(solution)/shard_map/pallas_call | solution.py:380
  84.6 0.0 copy-done.4
  84.6 9.0 %all-to-all-start.1 = ((bf16[32,64,256]{2,1,0:T(8,128)(2,1)}), bf16[32,64,256]{2,1,0:T(8,128)(2,1)S(1)}, u32[]{:S(2)}, u32[]{:S(2)}) async-start(bf16[32,64,256]{2,1,0:T(8,128)(2,1)} %shard_map.94), calls=%async_computation.1 | async-start | bytes 2097152 | tf_op jit(solution)/shard_map/all_to_all | solution.py:42
  93.6 4.0 %collective-permute-start.5 = (bf16[14,2,32,256]{3,2,1,0:T(8,128)(2,1)}, bf16[14,2,32,256]{3,2,1,0:T(8,128)(2,1)S(1)}, u32[]{:S(2)}, u32[]{:S(2)}) collective-permute-start(bf16[14,2,32,256]{3,2,1,0:T(8,128)(2,1)} %get-tuple-element.41), channel_id=1, source_target_pairs={{0,1},{1,2},{2,3},{3,0},{4,5},{5,6},{6,7},{7,4},{8,9},{9,10},{10,1... | collective-permute-start | bytes 1376264 | tf_op jit(solution)/shard_map/ppermute | solution.py:51
  97.6 3.4 %collective-permute-start.6 = (bf16[14,2,32,256]{3,2,1,0:T(8,128)(2,1)}, bf16[14,2,32,256]{3,2,1,0:T(8,128)(2,1)S(1)}, u32[]{:S(2)}, u32[]{:S(2)}) collective-permute-start(bf16[14,2,32,256]{3,2,1,0:T(8,128)(2,1)} %copy-done.17), channel_id=1, source_target_pairs={{0,3},{1,0},{2,1},{3,2},{4,7},{5,4},{6,5},{7,6},{8,11},{9,8},{10,9... | collective-permute-start | bytes 1376264 | tf_op jit(solution)/shard_map/ppermute | solution.py:51
  101.0 0.2 select_reduce_fusion.target
  101.2 18.5 %collective-permute-done.5.first.refs_1_ = bf16[14,2,32,256]{3,2,1,0:T(8,128)(2,1)S(1)} collective-permute-done((bf16[14,2,32,256]{3,2,1,0:T(8,128)(2,1)}, bf16[14,2,32,256]{3,2,1,0:T(8,128)(2,1)S(1)}, u32[]{:S(2)}, u32[]{:S(2)}) %collective-permute-start.5) | collective-permute-done | bytes 458784 | tf_op jit(solution)/shard_map/ppermute | solution.py:51
  119.7 2.2 collective-permute-done.6.last.refs_2_
  121.9 0.0 all-to-all-done.1.arrived.queries
  122.0 1.7 shard_map.95
  123.7 0.9 copy-done.10
  124.6 39.8 %all_to_all.40.arrived = bf16[32,16,1152]{2,1,0:T(8,128)(2,1)S(1)} all-to-all(bf16[32,16,1152]{2,1,0:T(8,128)(2,1)S(1)} %get-tuple-element.45), channel_id=1, replica_groups=mesh['yl'=2,'co'=2,'dz'=8,'dx'=4,'mp'=4] {'dz','dx'}, dimensions={0} | all-to-all | bytes 2359296 | tf_op jit(solution)/shard_map/all_to_all | solution.py:42
  164.5 1.6 shard_map.96
  166.1 16.0 %all_to_all.41.moved = f32[16,8,128]{2,1,0:T(8,128)S(1)} all-to-all(f32[16,8,128]{2,1,0:T(8,128)S(1)} %broadcast_in_dim.29), channel_id=1, replica_groups=mesh['yl'=2,'co'=2,'dz'=8,'dx'=4,'mp'=4] {'yl','co','mp'}, dimensions={0} | all-to-all | bytes 131072 | tf_op jit(solution)/shard_map/all_to_all | solution.py:42
  182.1 2.0 shard_map.97
  184.1 36.2 %all_to_all.42.arrived = bf16[32,16,1152]{2,1,0:T(8,128)(2,1)} all-to-all(bf16[32,16,1152]{2,1,0:T(8,128)(2,1)S(1)} %get-tuple-element.50), channel_id=1, replica_groups=mesh['yl'=2,'co'=2,'dz'=8,'dx'=4,'mp'=4] {'dz','dx'}, dimensions={0} | all-to-all | bytes 2359296 | tf_op jit(solution)/shard_map/all_to_all | solution.py:42
  220.3 6.4 %shard_map.98 = (bf16[32,64,256]{2,1,0:T(8,128)(2,1)}, bf16[14,2,32,256]{3,2,1,0:T(8,128)(2,1)}, bf16[14,2,32,256]{3,2,1,0:T(8,128)(2,1)}, bf16[14,2,32,256]{3,2...) custom-call(s32[14]{0:T(128)} %copy-done.15, bf16[32,16,1152]{2,1,0:T(8,128)(2,1)} %all_to_all.42.arrived, ...), custom_call_target="tpu_custom_call" | custom-call | tf_op jit(solution)/shard_map/pallas_call | solution.py:32
  226.7 4.1 %all-to-all-start.5 = ((bf16[32,64,256]{2,1,0:T(8,128)(2,1)}), bf16[32,64,256]{2,1,0:T(8,128)(2,1)S(1)}, u32[]{:S(2)}, u32[]{:S(2)}) async-start(bf16[32,64,256]{2,1,0:T(8,128)(2,1)} %get-tuple-element.52), calls=%async_computation.5 | async-start | bytes 2097152 | tf_op jit(solution)/shard_map/all_to_all | solution.py:42
  230.8 1.9 collective-permute-start.7
  232.7 4.3 %collective-permute-start.8 = (bf16[14,2,32,256]{3,2,1,0:T(8,128)(2,1)}, bf16[14,2,32,256]{3,2,1,0:T(8,128)(2,1)}, u32[]{:S(2)}, u32[]{:S(2)}) collective-permute-start(bf16[14,2,32,256]{3,2,1,0:T(8,128)(2,1)} %get-tuple-element.57), channel_id=1, source_target_pairs={{0,1},{1,2},{2,3},{3,0},{4,5},{5,6},{6,7},{7,4},{8,9},{9,10},{10,1... | collective-permute-start | bytes 1376264 | tf_op jit(solution)/shard_map/ppermute | solution.py:51
  237.0 19.9 %all-to-all-done.5.arrived = bf16[32,64,256]{2,1,0:T(8,128)(2,1)S(1)} async-done(((bf16[32,64,256]{2,1,0:T(8,128)(2,1)}), bf16[32,64,256]{2,1,0:T(8,128)(2,1)S(1)}, u32[]{:S(2)}, u32[]{:S(2)}) %all-to-all-start.5) | async-done | bytes 1048608 | tf_op jit(solution)/shard_map/all_to_all | solution.py:42
  256.9 0.0 copy-done.3
  256.9 1.5 copy-done.5
  258.4 2.4 shard_map.99
  260.8 1.3 copy-done.6
  262.1 0.0 collective-permute-done.7.up
  262.1 0.0 collective-permute-done.8.down
  262.1 4.6 %all-to-all-start.6 = ((bf16[32,128,256]{2,1,0:T(8,128)(2,1)}), bf16[32,128,256]{2,1,0:T(8,128)(2,1)S(1)}, u32[]{:S(2)}, u32[]{:S(2)}) async-start(bf16[32,128,256]{2,1,0:T(8,128)(2,1)} %bitcast.13), calls=%async_computation.6 | async-start | bytes 4194304 | tf_op jit(solution)/shard_map/all_to_all | solution.py:42
  266.7 1.0 slice.6
  267.7 1.0 slice.7
  268.7 2.0 collective-permute-start.10
  270.8 5.4 %collective-permute-start.9 = (bf16[14,2,32,256]{3,2,1,0:T(8,128)(2,1)S(1)}, bf16[14,2,32,256]{3,2,1,0:T(8,128)(2,1)S(1)}, u32[]{:S(2)}, u32[]{:S(2)}) collective-permute-start(bf16[14,2,32,256]{3,2,1,0:T(8,128)(2,1)S(1)} %pad_maximum_fusion), channel_id=1, source_target_pairs={{0,3},{1,0},{2,1},{3,2},{4,7},{5,4},{6,5},{7,6},{8,11},{9,8},{10,9... | collective-permute-start | bytes 1376264 | tf_op jit(solution)/shard_map/ppermute | solution.py:51
  276.2 16.7 %collective-permute-done.10.far_down = bf16[14,2,32,256]{3,2,1,0:T(8,128)(2,1)S(1)} collective-permute-done((bf16[14,2,32,256]{3,2,1,0:T(8,128)(2,1)S(1)}, bf16[14,2,32,256]{3,2,1,0:T(8,128)(2,1)S(1)}, u32[]{:S(2)}, u32[]{:S(2)}) %collective-permute-start.10) | collective-permute-done | bytes 458784 | tf_op jit(solution)/shard_map/ppermute | solution.py:51
  292.9 1.6 collective-permute-done.9.far_up
  294.5 0.0 all-to-all-done.6
  294.5 1.1 shard_map.101
  295.6 3.5 %all-to-all-start.7 = ((bf16[8,128,256]{2,1,0:T(8,128)(2,1)}), bf16[8,128,256]{2,1,0:T(8,128)(2,1)S(1)}, u32[]{:S(2)}, u32[]{:S(2)}) async-start(bf16[8,128,256]{2,1,0:T(8,128)(2,1)} %shard_map.101), calls=%async_computation.7 | async-start | bytes 1048576 | tf_op jit(solution)/shard_map/all_to_all | solution.py:42
  299.1 4.0 %shard_map.100 = bf16[14,2,32,1024]{3,2,1,0:T(8,128)(2,1)} custom-call(s32[2]{0:T(128)} %copy-done.14, bf16[14,2,32,256]{3,2,1,0:T(8,128)(2,1)} %get-tuple-element.54.own, bf16[14,2,32,256]{3,2,1,0:T(8,128)(2,1)} %collective-permute-done.7.up, bf16[14,2,32,256]{3,2,1,0:T(8,128)(2,1)} %collective-permute-done.8.down, bf16[14,2,32,256]{3,2,1,0:T(8,128)(2,1)} %copy-done.19, ...), custom_call_target="tpu_custom_call" | custom-call | tf_op jit(solution)/shard_map/pallas_call | solution.py:328
  303.1 11.2 %all-to-all-done.7 = bf16[8,128,256]{2,1,0:T(8,128)(2,1)S(1)} async-done(((bf16[8,128,256]{2,1,0:T(8,128)(2,1)}), bf16[8,128,256]{2,1,0:T(8,128)(2,1)S(1)}, u32[]{:S(2)}, u32[]{:S(2)}) %all-to-all-start.7) | async-done | bytes 524320 | tf_op jit(solution)/shard_map/all_to_all | solution.py:42
  314.4 0.7 reduce_sum.22
  (43 shorter events, 0.2 us)
Async XLA Ops:
  7.2 65.0 %all-gather.3.cloned.1.call-start = ((), (), s32[]{:S(2)}) async-start(), calls=%async_computation.8 | async-start | bytes 2064384 | tf_op jit(solution)/shard_map/all_gather | solution.py:369
  10.3 14.1 %copy-start = (bf16[14,2,32,1024]{3,2,1,0:T(8,128)(2,1)S(1)}, bf16[14,2,32,1024]{3,2,1,0:T(8,128)(2,1)}, u32[]{:S(2)}) copy-start(bf16[14,2,32,1024]{3,2,1,0:T(8,128)(2,1)} %block3.1) | copy-start | bytes 5505028
  10.3 65.2 %all-to-all-start = ((bf16[32,128,256]{2,1,0:T(8,128)(2,1)}), bf16[32,128,256]{2,1,0:T(8,128)(2,1)}, u32[]{:S(2)}, u32[]{:S(2)}) async-start(bf16[32,128,256]{2,1,0:T(8,128)(2,1)} %broadcast_in_dim.28), calls=%async_computation | async-start | bytes 4194304 | tf_op jit(solution)/shard_map/all_to_all | solution.py:42
  24.4 232.5 %copy-start.14 = (s32[2]{0:T(128)}, s32[2]{0:T(128)S(1)}, u32[]{:S(2)}) copy-start(s32[2]{0:T(128)S(1)} %pad_add_fusion.place) | copy-start | bytes 28
  24.4 50.7 %copy-start.22 = (s32[224,2]{0,1:T(2,128)S(1)}, s32[224,2]{0,1:T(2,128)}, u32[]{:S(2)}) copy-start(s32[224,2]{0,1:T(2,128)} %param.9) | copy-start | bytes 5380
  25.9 31.9 %copy-start.17 = (bf16[14,2,32,256]{3,2,1,0:T(8,128)(2,1)}, bf16[14,2,32,256]{3,2,1,0:T(8,128)(2,1)S(1)}, u32[]{:S(2)}) copy-start(bf16[14,2,32,256]{3,2,1,0:T(8,128)(2,1)S(1)} %get-tuple-element.42) | copy-start | bytes 1376260
  25.9 96.0 %copy-start.7 = (bf16[14,2,32,256]{3,2,1,0:T(8,128)(2,1)}, bf16[14,2,32,256]{3,2,1,0:T(8,128)(2,1)S(1)}, u32[]{:S(2)}) copy-start(bf16[14,2,32,256]{3,2,1,0:T(8,128)(2,1)S(1)} %get-tuple-element.40.own.refs_0_) | copy-start | bytes 1376260
  25.9 17.5 %collective-permute-start = (bf16[14,32,256]{2,1,0:T(8,128)(2,1)S(1)}, bf16[14,32,256]{2,1,0:T(8,128)(2,1)S(1)}, u32[]{:S(2)}, u32[]{:S(2)}) collective-permute-start(bf16[14,32,256]{2,1,0:T(8,128)(2,1)S(1)} %get-tuple-element.35), channel_id=1, source_target_pairs={{0,1},{1,2},{2,3},{3,0},{4,5},{5,6},{6,7},{7,4},{8,9},{9,10},{10,1... | collective-permute-start | bytes 688136 | tf_op jit(solution)/shard_map/ppermute | solution.py:51
  30.2 20.5 %collective-permute-start.2 = (bf16[14,32,256]{2,1,0:T(8,128)(2,1)S(1)}, bf16[14,32,256]{2,1,0:T(8,128)(2,1)S(1)}, u32[]{:S(2)}, u32[]{:S(2)}) collective-permute-start(bf16[14,32,256]{2,1,0:T(8,128)(2,1)S(1)} %get-tuple-element.36), channel_id=1, source_target_pairs={{0,3},{1,0},{2,1},{3,2},{4,7},{5,4},{6,5},{7,6},{8,11},{9,8},{10,9... | collective-permute-start | bytes 688136 | tf_op jit(solution)/shard_map/ppermute | solution.py:51
  43.4 14.4 %collective-permute-start.1 = (bf16[14,32,256]{2,1,0:T(8,128)(2,1)S(1)}, bf16[14,32,256]{2,1,0:T(8,128)(2,1)S(1)}, u32[]{:S(2)}, u32[]{:S(2)}) collective-permute-start(bf16[14,32,256]{2,1,0:T(8,128)(2,1)S(1)} %collective-permute-done), channel_id=1, source_target_pairs={{0,1},{1,2},{2,3},{3,0},{4,5},{5,6},{6,7},{7,4},{8,9},{9,10},{10,1... | collective-permute-start | bytes 688136 | tf_op jit(solution)/shard_map/ppermute | solution.py:51
  50.6 14.1 %collective-permute-start.3 = (bf16[14,32,256]{2,1,0:T(8,128)(2,1)S(1)}, bf16[14,32,256]{2,1,0:T(8,128)(2,1)S(1)}, u32[]{:S(2)}, u32[]{:S(2)}) collective-permute-start(bf16[14,32,256]{2,1,0:T(8,128)(2,1)S(1)} %collective-permute-done.2), channel_id=1, source_target_pairs={{0,3},{1,0},{2,1},{3,2},{4,7},{5,4},{6,5},{7,6},{8,11},{9,8},{10,9... | collective-permute-start | bytes 688136 | tf_op jit(solution)/shard_map/ppermute | solution.py:51
  57.8 64.1 %copy-start.11 = (bf16[14,32,256]{2,1,0:T(8,128)(2,1)}, bf16[14,32,256]{2,1,0:T(8,128)(2,1)S(1)}, u32[]{:S(2)}) copy-start(bf16[14,32,256]{2,1,0:T(8,128)(2,1)S(1)} %collective-permute-done.1.far_keys.refs_3_) | copy-start | bytes 688132
  64.7 57.2 %copy-start.12 = (bf16[14,32,256]{2,1,0:T(8,128)(2,1)}, bf16[14,32,256]{2,1,0:T(8,128)(2,1)S(1)}, u32[]{:S(2)}) copy-start(bf16[14,32,256]{2,1,0:T(8,128)(2,1)S(1)} %collective-permute-done.3.far_values.refs_4_) | copy-start | bytes 688132
  72.2 6.6 %collective-permute-start.4 = (bf16[8,448,256]{2,1,0:T(8,128)(2,1)}, bf16[8,448,256]{2,1,0:T(8,128)(2,1)S(1)}, u32[]{:S(2)}, u32[]{:S(2)}) collective-permute-start(bf16[8,448,256]{2,1,0:T(8,128)(2,1)} %bitcast.10), channel_id=1, source_target_pairs={{0,128},{128,0},{1,129},{129,1},{2,130},{130,2},{3,131},{131,3},{4... | collective-permute-start | bytes 5505032 | tf_op jit(solution)/shard_map/ppermute | solution.py:51
  78.7 5.9 %copy-start.4 = (bf16[8,448,256]{2,1,0:T(8,128)(2,1)}, bf16[8,448,256]{2,1,0:T(8,128)(2,1)S(1)}, u32[]{:S(2)}) copy-start(bf16[8,448,256]{2,1,0:T(8,128)(2,1)S(1)} %collective-permute-done.4.other) | copy-start | bytes 5505028
  78.7 2.2 copy-start.2
  84.6 37.4 %all-to-all-start.1 = ((bf16[32,64,256]{2,1,0:T(8,128)(2,1)}), bf16[32,64,256]{2,1,0:T(8,128)(2,1)S(1)}, u32[]{:S(2)}, u32[]{:S(2)}) async-start(bf16[32,64,256]{2,1,0:T(8,128)(2,1)} %shard_map.94), calls=%async_computation.1 | async-start | bytes 2097152 | tf_op jit(solution)/shard_map/all_to_all | solution.py:42
  93.6 26.2 %collective-permute-start.5 = (bf16[14,2,32,256]{3,2,1,0:T(8,128)(2,1)}, bf16[14,2,32,256]{3,2,1,0:T(8,128)(2,1)S(1)}, u32[]{:S(2)}, u32[]{:S(2)}) collective-permute-start(bf16[14,2,32,256]{3,2,1,0:T(8,128)(2,1)} %get-tuple-element.41), channel_id=1, source_target_pairs={{0,1},{1,2},{2,3},{3,0},{4,5},{5,6},{6,7},{7,4},{8,9},{9,10},{10,1... | collective-permute-start | bytes 1376264 | tf_op jit(solution)/shard_map/ppermute | solution.py:51
  97.6 24.4 %collective-permute-start.6 = (bf16[14,2,32,256]{3,2,1,0:T(8,128)(2,1)}, bf16[14,2,32,256]{3,2,1,0:T(8,128)(2,1)S(1)}, u32[]{:S(2)}, u32[]{:S(2)}) collective-permute-start(bf16[14,2,32,256]{3,2,1,0:T(8,128)(2,1)} %copy-done.17), channel_id=1, source_target_pairs={{0,3},{1,0},{2,1},{3,2},{4,7},{5,4},{6,5},{7,6},{8,11},{9,8},{10,9... | collective-permute-start | bytes 1376264 | tf_op jit(solution)/shard_map/ppermute | solution.py:51
  101.2 63.2 %copy-start.15 = (s32[14]{0:T(128)}, s32[14]{0:T(128)S(1)}, u32[]{:S(2)}) copy-start(s32[14]{0:T(128)S(1)} %select_reduce_fusion.target) | copy-start | bytes 172
  119.7 44.7 %copy-start.8 = (bf16[14,2,32,256]{3,2,1,0:T(8,128)(2,1)}, bf16[14,2,32,256]{3,2,1,0:T(8,128)(2,1)S(1)}, u32[]{:S(2)}) copy-start(bf16[14,2,32,256]{3,2,1,0:T(8,128)(2,1)S(1)} %collective-permute-done.5.first.refs_1_) | copy-start | bytes 1376260
  121.9 42.5 %copy-start.9 = (bf16[14,2,32,256]{3,2,1,0:T(8,128)(2,1)}, bf16[14,2,32,256]{3,2,1,0:T(8,128)(2,1)S(1)}, u32[]{:S(2)}) copy-start(bf16[14,2,32,256]{3,2,1,0:T(8,128)(2,1)S(1)} %collective-permute-done.6.last.refs_2_) | copy-start | bytes 1376260
  121.9 42.5 %copy-start.1 = (bf16[32,64,256]{2,1,0:T(8,128)(2,1)}, bf16[32,64,256]{2,1,0:T(8,128)(2,1)S(1)}, u32[]{:S(2)}) copy-start(bf16[32,64,256]{2,1,0:T(8,128)(2,1)S(1)} %all-to-all-done.1.arrived.queries) | copy-start | bytes 3145732
  123.7 0.9 copy-start.10
  124.6 39.9 %copy-start.13 = (bf16[448,256]{1,0:T(8,128)(2,1)S(1)}, bf16[448,256]{1,0:T(8,128)(2,1)}, u32[]{:S(2)}) copy-start(bf16[448,256]{1,0:T(8,128)(2,1)} %d_mixed.3) | copy-start | bytes 688132
  124.6 39.9 %copy-start.16 = (f32[256]{0:T(256)S(1)}, f32[256]{0:T(256)}, u32[]{:S(2)}) copy-start(f32[256]{0:T(256)} %param.10) | copy-start | bytes 3076
  226.7 30.2 %copy-start.3 = (bf16[3584,256]{1,0:T(8,128)(2,1)S(1)}, bf16[3584,256]{1,0:T(8,128)(2,1)}, u32[]{:S(2)}) copy-start(bf16[3584,256]{1,0:T(8,128)(2,1)} %all-gather.3.cloned.1.call-done) | copy-start | bytes 5505028
  226.7 30.2 %all-to-all-start.5 = ((bf16[32,64,256]{2,1,0:T(8,128)(2,1)}), bf16[32,64,256]{2,1,0:T(8,128)(2,1)S(1)}, u32[]{:S(2)}, u32[]{:S(2)}) async-start(bf16[32,64,256]{2,1,0:T(8,128)(2,1)} %get-tuple-element.52), calls=%async_computation.5 | async-start | bytes 2097152 | tf_op jit(solution)/shard_map/all_to_all | solution.py:42
  230.8 31.3 %collective-permute-start.7 = (bf16[14,2,32,256]{3,2,1,0:T(8,128)(2,1)}, bf16[14,2,32,256]{3,2,1,0:T(8,128)(2,1)}, u32[]{:S(2)}, u32[]{:S(2)}) collective-permute-start(bf16[14,2,32,256]{3,2,1,0:T(8,128)(2,1)} %get-tuple-element.56), channel_id=1, source_target_pairs={{0,3},{1,0},{2,1},{3,2},{4,7},{5,4},{6,5},{7,6},{8,11},{9,8},{10,9... | collective-permute-start | bytes 1376264 | tf_op jit(solution)/shard_map/ppermute | solution.py:51
  232.7 29.4 %collective-permute-start.8 = (bf16[14,2,32,256]{3,2,1,0:T(8,128)(2,1)}, bf16[14,2,32,256]{3,2,1,0:T(8,128)(2,1)}, u32[]{:S(2)}, u32[]{:S(2)}) collective-permute-start(bf16[14,2,32,256]{3,2,1,0:T(8,128)(2,1)} %get-tuple-element.57), channel_id=1, source_target_pairs={{0,1},{1,2},{2,3},{3,0},{4,5},{5,6},{6,7},{7,4},{8,9},{9,10},{10,1... | collective-permute-start | bytes 1376264 | tf_op jit(solution)/shard_map/ppermute | solution.py:51
  256.9 1.5 copy-start.5
  260.8 1.3 copy-start.6
  262.1 6.6 %copy-start.21 = (bf16[14,32,256]{2,1,0:T(8,128)(2,1)S(1)}, bf16[14,32,256]{2,1,0:T(8,128)(2,1)}, u32[]{:S(2)}) copy-start(bf16[14,32,256]{2,1,0:T(8,128)(2,1)} %get-tuple-element.62) | copy-start | bytes 688132
  262.1 32.4 %all-to-all-start.6 = ((bf16[32,128,256]{2,1,0:T(8,128)(2,1)}), bf16[32,128,256]{2,1,0:T(8,128)(2,1)S(1)}, u32[]{:S(2)}, u32[]{:S(2)}) async-start(bf16[32,128,256]{2,1,0:T(8,128)(2,1)} %bitcast.13), calls=%async_computation.6 | async-start | bytes 4194304 | tf_op jit(solution)/shard_map/all_to_all | solution.py:42
  266.7 4.0 %copy-start.20 = (bf16[14,32,256]{2,1,0:T(8,128)(2,1)S(1)}, bf16[14,32,256]{2,1,0:T(8,128)(2,1)}, u32[]{:S(2)}) copy-start(bf16[14,32,256]{2,1,0:T(8,128)(2,1)} %get-tuple-element.61) | copy-start | bytes 688132
  268.7 24.2 %collective-permute-start.10 = (bf16[14,2,32,256]{3,2,1,0:T(8,128)(2,1)S(1)}, bf16[14,2,32,256]{3,2,1,0:T(8,128)(2,1)S(1)}, u32[]{:S(2)}, u32[]{:S(2)}) collective-permute-start(bf16[14,2,32,256]{3,2,1,0:T(8,128)(2,1)S(1)} %pad_maximum_fusion.1), channel_id=1, source_target_pairs={{0,1},{1,2},{2,3},{3,0},{4,5},{5,6},{6,7},{7,4},{8,9},{9,10},{10,1... | collective-permute-start | bytes 1376264 | tf_op jit(solution)/shard_map/ppermute | solution.py:51
  270.8 23.7 %collective-permute-start.9 = (bf16[14,2,32,256]{3,2,1,0:T(8,128)(2,1)S(1)}, bf16[14,2,32,256]{3,2,1,0:T(8,128)(2,1)S(1)}, u32[]{:S(2)}, u32[]{:S(2)}) collective-permute-start(bf16[14,2,32,256]{3,2,1,0:T(8,128)(2,1)S(1)} %pad_maximum_fusion), channel_id=1, source_target_pairs={{0,3},{1,0},{2,1},{3,2},{4,7},{5,4},{6,5},{7,6},{8,11},{9,8},{10,9... | collective-permute-start | bytes 1376264 | tf_op jit(solution)/shard_map/ppermute | solution.py:51
  292.9 2.6 copy-start.18
  294.5 1.1 copy-start.19
  295.6 18.8 %all-to-all-start.7 = ((bf16[8,128,256]{2,1,0:T(8,128)(2,1)}), bf16[8,128,256]{2,1,0:T(8,128)(2,1)S(1)}, u32[]{:S(2)}, u32[]{:S(2)}) async-start(bf16[8,128,256]{2,1,0:T(8,128)(2,1)} %shard_map.101), calls=%async_computation.7 | async-start | bytes 1048576 | tf_op jit(solution)/shard_map/all_to_all | solution.py:42
Sparse Core Ops, SparseCore 0:
  10.1 62.0 all-gather.2

commit v11 on v10

--- a/solution.py
+++ b/solution.py
@@ -248,8 +248,16 @@
         down[n, 0], last[n] = grad_keys[3 * rows :], grad_values[3 * rows :]
 
 
-def weight_kernel(sizes, place, source, arrived, mine, other, grad_q, partial):
+def weight_kernel(
+    sizes, place, source, arrived, mine_far, other_far, grad_q, partial, mine, other, sems
+):
     n_yl, n_co, n_mp, n_x = sizes
+    fetches = [
+        pltpu.make_async_copy(mine_far, mine, sems.at[0]),
+        pltpu.make_async_copy(other_far, other, sems.at[1]),
+    ]
+    for fetch in fetches:
+        fetch.start()
     for c in range(source.shape[0] // NEIGHBOURS):
         both = sum(arrived[source[NEIGHBOURS * c + k]].astype(F32) for k in range(NEIGHBOURS))
         grad_q[c * GROUP_LEN : (c + 1) * GROUP_LEN, :] = both.astype(BF)
@@ -257,6 +265,7 @@
     per = mine.shape[2] // rows
     for part, block in enumerate((mine, other)):
         co = lax.rem(place[1] + part, n_co)
+        fetches[part].wait()
         for line in range(mine.shape[0]):
             first = weight_rows(line, co, n_yl, n_co, n_mp) * per
             product = dot(block[line], grad_q[...], FIRST).astype(BF)
@@ -422,12 +431,22 @@
     up, down = shift(up, "mp", -1), shift(down, "mp", 1)
     arrived = exchange(slots, DP)
     blocks = (n_x, n_z, wq.shape[0], dec_width)
-    grad_q, partial = call(
+    far = pl.BlockSpec(memory_space=pl.ANY)
+    grad_q, partial = pl.pallas_call(
         functools.partial(weight_kernel, sizes),
-        (place, source),
-        (arrived, line, other),
-        [((tok_dev, dec_width), BF), (blocks, BF)],
-    )
+        in_specs=[SMEM, SMEM, VMEM, far, far],
+        out_specs=[VMEM, VMEM],
+        out_shape=[
+            jax.ShapeDtypeStruct((tok_dev, dec_width), BF),
+            jax.ShapeDtypeStruct(blocks, BF),
+        ],
+        scratch_shapes=[
+            pltpu.VMEM(line.shape, line.dtype),
+            pltpu.VMEM(line.shape, line.dtype),
+            pltpu.SemaphoreType.DMA((2,)),
+        ],
+        compiler_params=LARGE,
+    )(place, source, arrived, line, other)
     partial, up, down = lax.optimization_barrier((partial, up, down))
     far_up = shift(second_step(first, up), "mp", -1)
     far_down = shift(second_step(last, down), "mp", 1)

time: 325 us -> 325 us (level)
    pallas_call x0 -> x1, Pallas kernels: none -> 5.65 us  [shards(): pl.pallas_call(functools.partial(weight_kernel, sizes), in_specs=[SMEM, S...]
    pallas_call x6 -> x5, Pallas kernels: 15.1 us -> 12.9 us  [call(): pl.pallas_call(kernel, in_specs=[SMEM] * len(scalars) + [VMEM] * len(arra...]
  transfers between devices with their start and end apart: 17 -> 17, of which waited for: 12 -> 12; matrix products, arithmetic and copies ran while one was open for 2% -> 1% of each run, Pallas kernels for 2% -> 3%
where the time goes in v11:
time: 325 us; the launch traced here: 322 us
  waiting for transfers between devices  107 us (33%)
  blocking collectives  92.1 us (28%)
  starting transfers between devices  72.7 us (22%)
  Pallas kernels  27.1 us (8%)
  between operations  14.4 us (4%)
  local copies, waits for them, and re-layouts  7.61 us (2%)
    all_to_all x3, blocking collectives, exchange(): return lax.all_to_all(array, axes, split_axis=0, concat_axis=0, tiled=True)  92.1 us
    ppermute x11, waiting for transfers between devices, shift(): lax.ppermute(array, axis, [(i, (i + step) % size) for i in range(size)])  66.9 us
    ppermute x11, starting transfers between devices, shift(): lax.ppermute(array, axis, [(i, (i + step) % size) for i in range(size)])  37.6 us
    all_to_all x5, starting transfers between devices, exchange(): return lax.all_to_all(array, axes, split_axis=0, concat_axis=0, tiled=True)  35.1 us
    all_to_all x5, waiting for transfers between devices, exchange(): return lax.all_to_all(array, axes, split_axis=0, concat_axis=0, tiled=True)  31.4 us
    pallas_call x5, Pallas kernels, call(): pl.pallas_call(kernel, in_specs=[SMEM] * len(scalars) + [VMEM] * len(arra...  12.9 us
    all_gather x1, waiting for transfers between devices, shards(): line = lax.all_gather(hidden, LINE, axis=0)  7.52 us
  transfers between devices with their start and end apart: 17, of which 12 were waited for; matrix products, arithmetic and copies ran while one was open for 1% of the time, Pallas kernels for 3%

profile of v11, /device:TPU:1, one launch (start us, length us, event | category | flops | bytes accessed | tf_op | source)
XLA Modules:
  0.0 321.7 jit_solution(12866418606272535677)
XLA Ops:
  7.2 0.0 all-gather.3.cloned.1.call-start
  7.2 0.7 all-gather.3.cloned.1.call-update
  7.9 2.4 broadcast_in_dim.28
  10.3 14.0 %all-to-all-start = ((bf16[32,128,256]{2,1,0:T(8,128)(2,1)}), bf16[32,128,256]{2,1,0:T(8,128)(2,1)}, u32[]{:S(2)}, u32[]{:S(2)}) async-start(bf16[32,128,256]{2,1,0:T(8,128)(2,1)} %broadcast_in_dim.28), calls=%async_computation | async-start | bytes 4194304 | tf_op jit(solution)/shard_map/all_to_all | solution.py:42
  24.3 0.1 pad_add_fusion.place
  24.4 0.0 copy-done
  24.4 0.8 shard_map.93
  25.2 0.8 copy-done.15
  26.0 4.2 %collective-permute-start = (bf16[14,32,256]{2,1,0:T(8,128)(2,1)S(1)}, bf16[14,32,256]{2,1,0:T(8,128)(2,1)S(1)}, u32[]{:S(2)}, u32[]{:S(2)}) collective-permute-start(bf16[14,32,256]{2,1,0:T(8,128)(2,1)S(1)} %get-tuple-element.35), channel_id=1, source_target_pairs={{0,1},{1,2},{2,3},{3,0},{4,5},{5,6},{6,7},{7,4},{8,9},{9,10},{10,1... | collective-permute-start | bytes 688136 | tf_op jit(solution)/shard_map/ppermute | solution.py:51
  30.2 3.6 %collective-permute-start.2 = (bf16[14,32,256]{2,1,0:T(8,128)(2,1)S(1)}, bf16[14,32,256]{2,1,0:T(8,128)(2,1)S(1)}, u32[]{:S(2)}, u32[]{:S(2)}) collective-permute-start(bf16[14,32,256]{2,1,0:T(8,128)(2,1)S(1)} %get-tuple-element.36), channel_id=1, source_target_pairs={{0,3},{1,0},{2,1},{3,2},{4,7},{5,4},{6,5},{7,6},{8,11},{9,8},{10,9... | collective-permute-start | bytes 688136 | tf_op jit(solution)/shard_map/ppermute | solution.py:51
  33.8 9.8 %collective-permute-done = bf16[14,32,256]{2,1,0:T(8,128)(2,1)S(1)} collective-permute-done((bf16[14,32,256]{2,1,0:T(8,128)(2,1)S(1)}, bf16[14,32,256]{2,1,0:T(8,128)(2,1)S(1)}, u32[]{:S(2)}, u32[]{:S(2)}) %collective-permute-start) | collective-permute-done | bytes 229408 | tf_op jit(solution)/shard_map/ppermute | solution.py:51
  43.5 4.0 %collective-permute-start.1 = (bf16[14,32,256]{2,1,0:T(8,128)(2,1)S(1)}, bf16[14,32,256]{2,1,0:T(8,128)(2,1)S(1)}, u32[]{:S(2)}, u32[]{:S(2)}) collective-permute-start(bf16[14,32,256]{2,1,0:T(8,128)(2,1)S(1)} %collective-permute-done), channel_id=1, source_target_pairs={{0,1},{1,2},{2,3},{3,0},{4,5},{5,6},{6,7},{7,4},{8,9},{9,10},{10,1... | collective-permute-start | bytes 688136 | tf_op jit(solution)/shard_map/ppermute | solution.py:51
  47.5 3.2 collective-permute-done.2
  50.7 1.9 collective-permute-start.3
  52.6 5.8 %collective-permute-done.1.far_keys.refs_3_ = bf16[14,32,256]{2,1,0:T(8,128)(2,1)S(1)} collective-permute-done((bf16[14,32,256]{2,1,0:T(8,128)(2,1)S(1)}, bf16[14,32,256]{2,1,0:T(8,128)(2,1)S(1)}, u32[]{:S(2)}, u32[]{:S(2)}) %collective-permute-start.1) | collective-permute-done | bytes 229408 | tf_op jit(solution)/shard_map/ppermute | solution.py:51
  58.4 6.3 %collective-permute-done.3.far_values.refs_4_ = bf16[14,32,256]{2,1,0:T(8,128)(2,1)S(1)} collective-permute-done((bf16[14,32,256]{2,1,0:T(8,128)(2,1)S(1)}, bf16[14,32,256]{2,1,0:T(8,128)(2,1)S(1)}, u32[]{:S(2)}, u32[]{:S(2)}) %collective-permute-start.3) | collective-permute-done | bytes 229408 | tf_op jit(solution)/shard_map/ppermute | solution.py:51
  64.6 7.5 %all-gather.3.cloned.1.call-done = bf16[3584,256]{1,0:T(8,128)(2,1)} async-done(((bf16[448,256]{1,0:T(8,128)(2,1)}), bf16[3584,256]{1,0:T(8,128)(2,1)}) %all-gather.3.cloned.1.call-update) | async-done | bytes 1835024 | tf_op jit(solution)/shard_map/all_gather | solution.py:378
  72.2 3.0 collective-permute-start.4
  75.2 0.1 copy.11
  75.3 0.1 reshape.43
  75.4 0.1 and_select_fusion.source
  75.5 0.0 all-to-all-done
  75.5 3.2 collective-permute-done.4.other.other_far
  78.7 0.0 copy-done.12
  78.7 2.2 copy-done.2
  80.9 3.7 %shard_map.94 = bf16[32,64,256]{2,1,0:T(8,128)(2,1)} custom-call(s32[2]{0:T(128)S(1)} %pad_add_fusion.place, s32[14]{0:T(128)S(1)} %and_select_fusion.source, bf16[8,448,256]{2,1,0:T(8,128)(2,1)S(1)} %bitcast.12, bf16[8,448,256]{2,1,0:T(8,128)(2,1)S(1)} %collective-permute-done.4.other.other_far, bf16[4096,256]{1,0:T(8,128)(2,1)} %bitcast.3.weight), custom_call_target="tpu_custom_call" | custom-call | tf_op jit(solution)/shard_map/pallas_call | solution.py:389
  84.6 0.0 copy-done.3
  84.6 9.0 %all-to-all-start.1 = ((bf16[32,64,256]{2,1,0:T(8,128)(2,1)}), bf16[32,64,256]{2,1,0:T(8,128)(2,1)S(1)}, u32[]{:S(2)}, u32[]{:S(2)}) async-start(bf16[32,64,256]{2,1,0:T(8,128)(2,1)} %shard_map.94), calls=%async_computation.1 | async-start | bytes 2097152 | tf_op jit(solution)/shard_map/all_to_all | solution.py:42
  93.6 4.0 %collective-permute-start.5 = (bf16[14,2,32,256]{3,2,1,0:T(8,128)(2,1)}, bf16[14,2,32,256]{3,2,1,0:T(8,128)(2,1)S(1)}, u32[]{:S(2)}, u32[]{:S(2)}) collective-permute-start(bf16[14,2,32,256]{3,2,1,0:T(8,128)(2,1)} %copy-done.15), channel_id=1, source_target_pairs={{0,1},{1,2},{2,3},{3,0},{4,5},{5,6},{6,7},{7,4},{8,9},{9,10},{10,1... | collective-permute-start | bytes 1376264 | tf_op jit(solution)/shard_map/ppermute | solution.py:51
  97.6 3.4 %collective-permute-start.6 = (bf16[14,2,32,256]{3,2,1,0:T(8,128)(2,1)S(1)}, bf16[14,2,32,256]{3,2,1,0:T(8,128)(2,1)S(1)}, u32[]{:S(2)}, u32[]{:S(2)}) collective-permute-start(bf16[14,2,32,256]{3,2,1,0:T(8,128)(2,1)S(1)} %get-tuple-element.42), channel_id=1, source_target_pairs={{0,3},{1,0},{2,1},{3,2},{4,7},{5,4},{6,5},{7,6},{8,11},{9,8},{10,9... | collective-permute-start | bytes 1376264 | tf_op jit(solution)/shard_map/ppermute | solution.py:51
  101.0 0.2 select_reduce_fusion.target
  101.2 18.5 %collective-permute-done.5.first.refs_1_ = bf16[14,2,32,256]{3,2,1,0:T(8,128)(2,1)S(1)} collective-permute-done((bf16[14,2,32,256]{3,2,1,0:T(8,128)(2,1)}, bf16[14,2,32,256]{3,2,1,0:T(8,128)(2,1)S(1)}, u32[]{:S(2)}, u32[]{:S(2)}) %collective-permute-start.5) | collective-permute-done | bytes 458784 | tf_op jit(solution)/shard_map/ppermute | solution.py:51
  119.7 2.0 collective-permute-done.6.last.refs_2_
  121.7 0.0 all-to-all-done.1.arrived.queries
  121.7 0.0 copy-done.8
  121.7 0.0 copy-done.9
  121.7 1.7 shard_map.95
  123.4 0.9 copy-done.7
  124.3 39.8 %all_to_all.40.arrived = bf16[32,16,1152]{2,1,0:T(8,128)(2,1)S(1)} all-to-all(bf16[32,16,1152]{2,1,0:T(8,128)(2,1)S(1)} %get-tuple-element.45), channel_id=1, replica_groups=mesh['yl'=2,'co'=2,'dz'=8,'dx'=4,'mp'=4] {'dz','dx'}, dimensions={0} | all-to-all | bytes 2359296 | tf_op jit(solution)/shard_map/all_to_all | solution.py:42
  164.2 0.0 copy-done.13
  164.2 1.6 shard_map.96
  165.8 16.1 %all_to_all.41.moved = f32[16,8,128]{2,1,0:T(8,128)S(1)} all-to-all(f32[16,8,128]{2,1,0:T(8,128)S(1)} %broadcast_in_dim.29), channel_id=1, replica_groups=mesh['yl'=2,'co'=2,'dz'=8,'dx'=4,'mp'=4] {'yl','co','mp'}, dimensions={0} | all-to-all | bytes 131072 | tf_op jit(solution)/shard_map/all_to_all | solution.py:42
  181.9 2.0 shard_map.97
  184.0 36.2 %all_to_all.42.arrived = bf16[32,16,1152]{2,1,0:T(8,128)(2,1)} all-to-all(bf16[32,16,1152]{2,1,0:T(8,128)(2,1)S(1)} %get-tuple-element.50), channel_id=1, replica_groups=mesh['yl'=2,'co'=2,'dz'=8,'dx'=4,'mp'=4] {'dz','dx'}, dimensions={0} | all-to-all | bytes 2359296 | tf_op jit(solution)/shard_map/all_to_all | solution.py:42
  220.1 6.5 %shard_map.98 = (bf16[32,64,256]{2,1,0:T(8,128)(2,1)}, bf16[14,2,32,256]{3,2,1,0:T(8,128)(2,1)}, bf16[14,2,32,256]{3,2,1,0:T(8,128)(2,1)}, bf16[14,2,32,256]{3,2...) custom-call(s32[14]{0:T(128)} %copy-done.13, bf16[32,16,1152]{2,1,0:T(8,128)(2,1)} %all_to_all.42.arrived, ...), custom_call_target="tpu_custom_call" | custom-call | tf_op jit(solution)/shard_map/pallas_call | solution.py:32
  226.7 4.1 %all-to-all-start.5 = ((bf16[32,64,256]{2,1,0:T(8,128)(2,1)}), bf16[32,64,256]{2,1,0:T(8,128)(2,1)S(1)}, u32[]{:S(2)}, u32[]{:S(2)}) async-start(bf16[32,64,256]{2,1,0:T(8,128)(2,1)} %get-tuple-element.52), calls=%async_computation.5 | async-start | bytes 2097152 | tf_op jit(solution)/shard_map/all_to_all | solution.py:42
  230.8 1.9 collective-permute-start.7
  232.7 4.3 %collective-permute-start.8 = (bf16[14,2,32,256]{3,2,1,0:T(8,128)(2,1)S(1)}, bf16[14,2,32,256]{3,2,1,0:T(8,128)(2,1)S(1)}, u32[]{:S(2)}, u32[]{:S(2)}) collective-permute-start(bf16[14,2,32,256]{3,2,1,0:T(8,128)(2,1)S(1)} %copy-done.24), channel_id=1, source_target_pairs={{0,1},{1,2},{2,3},{3,0},{4,5},{5,6},{6,7},{7,4},{8,9},{9,10},{10,1... | collective-permute-start | bytes 1376264 | tf_op jit(solution)/shard_map/ppermute | solution.py:51
  237.0 19.9 %all-to-all-done.5.arrived = bf16[32,64,256]{2,1,0:T(8,128)(2,1)S(1)} async-done(((bf16[32,64,256]{2,1,0:T(8,128)(2,1)}), bf16[32,64,256]{2,1,0:T(8,128)(2,1)S(1)}, u32[]{:S(2)}, u32[]{:S(2)}) %all-to-all-start.5) | async-done | bytes 1048608 | tf_op jit(solution)/shard_map/all_to_all | solution.py:42
  256.9 1.0 copy-done.16
  257.8 5.7 %shard_map.99 = (bf16[448,256]{1,0:T(8,128)(2,1)}, bf16[4,8,128,256]{3,2,1,0:T(8,128)(2,1)}) custom-call(s32[2]{0:T(128)} %copy-done.12, s32[14]{0:T(128)} %copy-done.11, bf16[32,64,256]{2,1,0:T(8,128)(2,1)} %copy-done.16, bf16[8,448,256]{2,1,0:T(8,128)(2,1)} %bitcast.11, bf16[8,448,256]{2,1,0:T(8,128)(2,1)} %copy-done.3), custom_call_target="tpu_custom_call" | custom-call | tf_op jit(solution)/shard_map/pallas_call | solution.py:435
  263.5 0.0 collective-permute-done.7.up
  263.5 0.0 collective-permute-done.8.down
  263.5 4.6 %all-to-all-start.6 = ((bf16[32,128,256]{2,1,0:T(8,128)(2,1)}), bf16[32,128,256]{2,1,0:T(8,128)(2,1)S(1)}, u32[]{:S(2)}, u32[]{:S(2)}) async-start(bf16[32,128,256]{2,1,0:T(8,128)(2,1)} %bitcast.15), calls=%async_computation.6 | async-start | bytes 4194304 | tf_op jit(solution)/shard_map/all_to_all | solution.py:42
  268.2 1.9 collective-permute-start.10
  270.2 5.5 %collective-permute-start.9 = (bf16[14,2,32,256]{3,2,1,0:T(8,128)(2,1)S(1)}, bf16[14,2,32,256]{3,2,1,0:T(8,128)(2,1)S(1)}, u32[]{:S(2)}, u32[]{:S(2)}) collective-permute-start(bf16[14,2,32,256]{3,2,1,0:T(8,128)(2,1)S(1)} %pad_maximum_fusion), channel_id=1, source_target_pairs={{0,3},{1,0},{2,1},{3,2},{4,7},{5,4},{6,5},{7,6},{8,11},{9,8},{10,9... | collective-permute-start | bytes 1376264 | tf_op jit(solution)/shard_map/ppermute | solution.py:51
  275.7 16.7 %collective-permute-done.10.far_down = bf16[14,2,32,256]{3,2,1,0:T(8,128)(2,1)S(1)} collective-permute-done((bf16[14,2,32,256]{3,2,1,0:T(8,128)(2,1)S(1)}, bf16[14,2,32,256]{3,2,1,0:T(8,128)(2,1)S(1)}, u32[]{:S(2)}, u32[]{:S(2)}) %collective-permute-start.10) | collective-permute-done | bytes 458784 | tf_op jit(solution)/shard_map/ppermute | solution.py:51
  292.4 1.5 collective-permute-done.9.far_up
  294.0 0.0 all-to-all-done.6
  294.0 1.1 shard_map.101
  295.0 3.5 %all-to-all-start.7 = ((bf16[8,128,256]{2,1,0:T(8,128)(2,1)}), bf16[8,128,256]{2,1,0:T(8,128)(2,1)S(1)}, u32[]{:S(2)}, u32[]{:S(2)}) async-start(bf16[8,128,256]{2,1,0:T(8,128)(2,1)} %shard_map.101), calls=%async_computation.7 | async-start | bytes 1048576 | tf_op jit(solution)/shard_map/all_to_all | solution.py:42
  298.5 4.0 %shard_map.100 = bf16[14,2,32,1024]{3,2,1,0:T(8,128)(2,1)} custom-call(s32[2]{0:T(128)} %copy-done.12, bf16[14,2,32,256]{3,2,1,0:T(8,128)(2,1)} %get-tuple-element.54.own, bf16[14,2,32,256]{3,2,1,0:T(8,128)(2,1)} %copy-done.17, bf16[14,2,32,256]{3,2,1,0:T(8,128)(2,1)} %copy-done.18, bf16[14,2,32,256]{3,2,1,0:T(8,128)(2,1)} %copy-done.20, ...), custom_call_target="tpu_custom_call" | custom-call | tf_op jit(solution)/shard_map/pallas_call | solution.py:337
  302.6 11.6 %all-to-all-done.7 = bf16[8,128,256]{2,1,0:T(8,128)(2,1)S(1)} async-done(((bf16[8,128,256]{2,1,0:T(8,128)(2,1)}), bf16[8,128,256]{2,1,0:T(8,128)(2,1)S(1)}, u32[]{:S(2)}, u32[]{:S(2)}) %all-to-all-start.7) | async-done | bytes 524320 | tf_op jit(solution)/shard_map/all_to_all | solution.py:42
  314.1 0.7 reduce_sum.22
  (49 shorter events, 0.2 us)
Async XLA Ops:
  7.2 65.0 %all-gather.3.cloned.1.call-start = ((), (), s32[]{:S(2)}) async-start(), calls=%async_computation.8 | async-start | bytes 2064384 | tf_op jit(solution)/shard_map/all_gather | solution.py:378
  10.3 14.1 %copy-start = (bf16[14,2,32,1024]{3,2,1,0:T(8,128)(2,1)S(1)}, bf16[14,2,32,1024]{3,2,1,0:T(8,128)(2,1)}, u32[]{:S(2)}) copy-start(bf16[14,2,32,1024]{3,2,1,0:T(8,128)(2,1)} %block3.1) | copy-start | bytes 5505028
  10.3 65.2 %all-to-all-start = ((bf16[32,128,256]{2,1,0:T(8,128)(2,1)}), bf16[32,128,256]{2,1,0:T(8,128)(2,1)}, u32[]{:S(2)}, u32[]{:S(2)}) async-start(bf16[32,128,256]{2,1,0:T(8,128)(2,1)} %broadcast_in_dim.28), calls=%async_computation | async-start | bytes 4194304 | tf_op jit(solution)/shard_map/all_to_all | solution.py:42
  24.4 54.4 %copy-start.12 = (s32[2]{0:T(128)}, s32[2]{0:T(128)S(1)}, u32[]{:S(2)}) copy-start(s32[2]{0:T(128)S(1)} %pad_add_fusion.place) | copy-start | bytes 28
  24.4 50.8 %copy-start.23 = (s32[224,2]{0,1:T(2,128)S(1)}, s32[224,2]{0,1:T(2,128)}, u32[]{:S(2)}) copy-start(s32[224,2]{0,1:T(2,128)} %param.9) | copy-start | bytes 5380
  25.2 0.8 copy-start.15
  26.0 95.7 %copy-start.4 = (bf16[14,2,32,256]{3,2,1,0:T(8,128)(2,1)}, bf16[14,2,32,256]{3,2,1,0:T(8,128)(2,1)S(1)}, u32[]{:S(2)}) copy-start(bf16[14,2,32,256]{3,2,1,0:T(8,128)(2,1)S(1)} %get-tuple-element.40.own.refs_0_) | copy-start | bytes 1376260
  26.0 17.6 %collective-permute-start = (bf16[14,32,256]{2,1,0:T(8,128)(2,1)S(1)}, bf16[14,32,256]{2,1,0:T(8,128)(2,1)S(1)}, u32[]{:S(2)}, u32[]{:S(2)}) collective-permute-start(bf16[14,32,256]{2,1,0:T(8,128)(2,1)S(1)} %get-tuple-element.35), channel_id=1, source_target_pairs={{0,1},{1,2},{2,3},{3,0},{4,5},{5,6},{6,7},{7,4},{8,9},{9,10},{10,1... | collective-permute-start | bytes 688136 | tf_op jit(solution)/shard_map/ppermute | solution.py:51
  30.2 20.5 %collective-permute-start.2 = (bf16[14,32,256]{2,1,0:T(8,128)(2,1)S(1)}, bf16[14,32,256]{2,1,0:T(8,128)(2,1)S(1)}, u32[]{:S(2)}, u32[]{:S(2)}) collective-permute-start(bf16[14,32,256]{2,1,0:T(8,128)(2,1)S(1)} %get-tuple-element.36), channel_id=1, source_target_pairs={{0,3},{1,0},{2,1},{3,2},{4,7},{5,4},{6,5},{7,6},{8,11},{9,8},{10,9... | collective-permute-start | bytes 688136 | tf_op jit(solution)/shard_map/ppermute | solution.py:51
  43.5 14.9 %collective-permute-start.1 = (bf16[14,32,256]{2,1,0:T(8,128)(2,1)S(1)}, bf16[14,32,256]{2,1,0:T(8,128)(2,1)S(1)}, u32[]{:S(2)}, u32[]{:S(2)}) collective-permute-start(bf16[14,32,256]{2,1,0:T(8,128)(2,1)S(1)} %collective-permute-done), channel_id=1, source_target_pairs={{0,1},{1,2},{2,3},{3,0},{4,5},{5,6},{6,7},{7,4},{8,9},{9,10},{10,1... | collective-permute-start | bytes 688136 | tf_op jit(solution)/shard_map/ppermute | solution.py:51
  50.7 13.9 %collective-permute-start.3 = (bf16[14,32,256]{2,1,0:T(8,128)(2,1)S(1)}, bf16[14,32,256]{2,1,0:T(8,128)(2,1)S(1)}, u32[]{:S(2)}, u32[]{:S(2)}) collective-permute-start(bf16[14,32,256]{2,1,0:T(8,128)(2,1)S(1)} %collective-permute-done.2), channel_id=1, source_target_pairs={{0,3},{1,0},{2,1},{3,2},{4,7},{5,4},{6,5},{7,6},{8,11},{9,8},{10,9... | collective-permute-start | bytes 688136 | tf_op jit(solution)/shard_map/ppermute | solution.py:51
  58.4 63.3 %copy-start.8 = (bf16[14,32,256]{2,1,0:T(8,128)(2,1)}, bf16[14,32,256]{2,1,0:T(8,128)(2,1)S(1)}, u32[]{:S(2)}) copy-start(bf16[14,32,256]{2,1,0:T(8,128)(2,1)S(1)} %collective-permute-done.1.far_keys.refs_3_) | copy-start | bytes 688132
  64.6 57.1 %copy-start.9 = (bf16[14,32,256]{2,1,0:T(8,128)(2,1)}, bf16[14,32,256]{2,1,0:T(8,128)(2,1)S(1)}, u32[]{:S(2)}) copy-start(bf16[14,32,256]{2,1,0:T(8,128)(2,1)S(1)} %collective-permute-done.3.far_values.refs_4_) | copy-start | bytes 688132
  72.2 6.6 %collective-permute-start.4 = (bf16[8,448,256]{2,1,0:T(8,128)(2,1)}, bf16[8,448,256]{2,1,0:T(8,128)(2,1)S(1)}, u32[]{:S(2)}, u32[]{:S(2)}) collective-permute-start(bf16[8,448,256]{2,1,0:T(8,128)(2,1)} %bitcast.10), channel_id=1, source_target_pairs={{0,128},{128,0},{1,129},{129,1},{2,130},{130,2},{3,131},{131,3},{4... | collective-permute-start | bytes 5505032 | tf_op jit(solution)/shard_map/ppermute | solution.py:51
  75.5 106.4 %copy-start.11 = (s32[14]{0:T(128)}, s32[14]{0:T(128)S(1)}, u32[]{:S(2)}) copy-start(s32[14]{0:T(128)S(1)} %and_select_fusion.source) | copy-start | bytes 172
  78.7 5.9 %copy-start.3 = (bf16[8,448,256]{2,1,0:T(8,128)(2,1)}, bf16[8,448,256]{2,1,0:T(8,128)(2,1)S(1)}, u32[]{:S(2)}) copy-start(bf16[8,448,256]{2,1,0:T(8,128)(2,1)S(1)} %collective-permute-done.4.other.other_far) | copy-start | bytes 5505028
  78.7 2.2 copy-start.2
  84.6 37.1 %all-to-all-start.1 = ((bf16[32,64,256]{2,1,0:T(8,128)(2,1)}), bf16[32,64,256]{2,1,0:T(8,128)(2,1)S(1)}, u32[]{:S(2)}, u32[]{:S(2)}) async-start(bf16[32,64,256]{2,1,0:T(8,128)(2,1)} %shard_map.94), calls=%async_computation.1 | async-start | bytes 2097152 | tf_op jit(solution)/shard_map/all_to_all | solution.py:42
  93.6 26.1 %collective-permute-start.5 = (bf16[14,2,32,256]{3,2,1,0:T(8,128)(2,1)}, bf16[14,2,32,256]{3,2,1,0:T(8,128)(2,1)S(1)}, u32[]{:S(2)}, u32[]{:S(2)}) collective-permute-start(bf16[14,2,32,256]{3,2,1,0:T(8,128)(2,1)} %copy-done.15), channel_id=1, source_target_pairs={{0,1},{1,2},{2,3},{3,0},{4,5},{5,6},{6,7},{7,4},{8,9},{9,10},{10,1... | collective-permute-start | bytes 1376264 | tf_op jit(solution)/shard_map/ppermute | solution.py:51
  97.6 24.1 %collective-permute-start.6 = (bf16[14,2,32,256]{3,2,1,0:T(8,128)(2,1)S(1)}, bf16[14,2,32,256]{3,2,1,0:T(8,128)(2,1)S(1)}, u32[]{:S(2)}, u32[]{:S(2)}) collective-permute-start(bf16[14,2,32,256]{3,2,1,0:T(8,128)(2,1)S(1)} %get-tuple-element.42), channel_id=1, source_target_pairs={{0,3},{1,0},{2,1},{3,2},{4,7},{5,4},{6,5},{7,6},{8,11},{9,8},{10,9... | collective-permute-start | bytes 1376264 | tf_op jit(solution)/shard_map/ppermute | solution.py:51
  101.2 62.9 %copy-start.13 = (s32[14]{0:T(128)}, s32[14]{0:T(128)S(1)}, u32[]{:S(2)}) copy-start(s32[14]{0:T(128)S(1)} %select_reduce_fusion.target) | copy-start | bytes 172
  119.7 44.4 %copy-start.5 = (bf16[14,2,32,256]{3,2,1,0:T(8,128)(2,1)}, bf16[14,2,32,256]{3,2,1,0:T(8,128)(2,1)S(1)}, u32[]{:S(2)}) copy-start(bf16[14,2,32,256]{3,2,1,0:T(8,128)(2,1)S(1)} %collective-permute-done.5.first.refs_1_) | copy-start | bytes 1376260
  121.7 42.5 %copy-start.6 = (bf16[14,2,32,256]{3,2,1,0:T(8,128)(2,1)}, bf16[14,2,32,256]{3,2,1,0:T(8,128)(2,1)S(1)}, u32[]{:S(2)}) copy-start(bf16[14,2,32,256]{3,2,1,0:T(8,128)(2,1)S(1)} %collective-permute-done.6.last.refs_2_) | copy-start | bytes 1376260
  121.7 42.5 %copy-start.1 = (bf16[32,64,256]{2,1,0:T(8,128)(2,1)}, bf16[32,64,256]{2,1,0:T(8,128)(2,1)S(1)}, u32[]{:S(2)}) copy-start(bf16[32,64,256]{2,1,0:T(8,128)(2,1)S(1)} %all-to-all-done.1.arrived.queries) | copy-start | bytes 3145732
  123.4 0.9 copy-start.7
  124.3 39.9 %copy-start.10 = (bf16[448,256]{1,0:T(8,128)(2,1)S(1)}, bf16[448,256]{1,0:T(8,128)(2,1)}, u32[]{:S(2)}) copy-start(bf16[448,256]{1,0:T(8,128)(2,1)} %d_mixed.3) | copy-start | bytes 688132
  124.3 39.9 %copy-start.14 = (f32[256]{0:T(256)S(1)}, f32[256]{0:T(256)}, u32[]{:S(2)}) copy-start(f32[256]{0:T(256)} %param.10) | copy-start | bytes 3076
  226.7 4.1 %copy-start.25 = (bf16[14,2,32,256]{3,2,1,0:T(8,128)(2,1)S(1)}, bf16[14,2,32,256]{3,2,1,0:T(8,128)(2,1)}, u32[]{:S(2)}) copy-start(bf16[14,2,32,256]{3,2,1,0:T(8,128)(2,1)} %get-tuple-element.56) | copy-start | bytes 1376260
  226.7 6.0 %copy-start.24 = (bf16[14,2,32,256]{3,2,1,0:T(8,128)(2,1)S(1)}, bf16[14,2,32,256]{3,2,1,0:T(8,128)(2,1)}, u32[]{:S(2)}) copy-start(bf16[14,2,32,256]{3,2,1,0:T(8,128)(2,1)} %get-tuple-element.57) | copy-start | bytes 1376260
  226.7 30.2 %all-to-all-start.5 = ((bf16[32,64,256]{2,1,0:T(8,128)(2,1)}), bf16[32,64,256]{2,1,0:T(8,128)(2,1)S(1)}, u32[]{:S(2)}, u32[]{:S(2)}) async-start(bf16[32,64,256]{2,1,0:T(8,128)(2,1)} %get-tuple-element.52), calls=%async_computation.5 | async-start | bytes 2097152 | tf_op jit(solution)/shard_map/all_to_all | solution.py:42
  230.8 32.7 %collective-permute-start.7 = (bf16[14,2,32,256]{3,2,1,0:T(8,128)(2,1)S(1)}, bf16[14,2,32,256]{3,2,1,0:T(8,128)(2,1)S(1)}, u32[]{:S(2)}, u32[]{:S(2)}) collective-permute-start(bf16[14,2,32,256]{3,2,1,0:T(8,128)(2,1)S(1)} %copy-done.25), channel_id=1, source_target_pairs={{0,3},{1,0},{2,1},{3,2},{4,7},{5,4},{6,5},{7,6},{8,11},{9,8},{10,9... | collective-permute-start | bytes 1376264 | tf_op jit(solution)/shard_map/ppermute | solution.py:51
  232.7 30.8 %collective-permute-start.8 = (bf16[14,2,32,256]{3,2,1,0:T(8,128)(2,1)S(1)}, bf16[14,2,32,256]{3,2,1,0:T(8,128)(2,1)S(1)}, u32[]{:S(2)}, u32[]{:S(2)}) collective-permute-start(bf16[14,2,32,256]{3,2,1,0:T(8,128)(2,1)S(1)} %copy-done.24), channel_id=1, source_target_pairs={{0,1},{1,2},{2,3},{3,0},{4,5},{5,6},{6,7},{7,4},{8,9},{9,10},{10,1... | collective-permute-start | bytes 1376264 | tf_op jit(solution)/shard_map/ppermute | solution.py:51
  256.9 1.0 copy-start.16
  263.5 4.6 %copy-start.17 = (bf16[14,2,32,256]{3,2,1,0:T(8,128)(2,1)}, bf16[14,2,32,256]{3,2,1,0:T(8,128)(2,1)S(1)}, u32[]{:S(2)}) copy-start(bf16[14,2,32,256]{3,2,1,0:T(8,128)(2,1)S(1)} %collective-permute-done.7.up) | copy-start | bytes 1376260
  263.5 4.6 %copy-start.18 = (bf16[14,2,32,256]{3,2,1,0:T(8,128)(2,1)}, bf16[14,2,32,256]{3,2,1,0:T(8,128)(2,1)S(1)}, u32[]{:S(2)}) copy-start(bf16[14,2,32,256]{3,2,1,0:T(8,128)(2,1)S(1)} %collective-permute-done.8.down) | copy-start | bytes 1376260
  263.5 4.7 %copy-start.22 = (bf16[14,32,256]{2,1,0:T(8,128)(2,1)S(1)}, bf16[14,32,256]{2,1,0:T(8,128)(2,1)}, u32[]{:S(2)}) copy-start(bf16[14,32,256]{2,1,0:T(8,128)(2,1)} %get-tuple-element.62) | copy-start | bytes 688132
  263.5 30.4 %all-to-all-start.6 = ((bf16[32,128,256]{2,1,0:T(8,128)(2,1)}), bf16[32,128,256]{2,1,0:T(8,128)(2,1)S(1)}, u32[]{:S(2)}, u32[]{:S(2)}) async-start(bf16[32,128,256]{2,1,0:T(8,128)(2,1)} %bitcast.15), calls=%async_computation.6 | async-start | bytes 4194304 | tf_op jit(solution)/shard_map/all_to_all | solution.py:42
  268.1 2.0 copy-start.21
  268.2 24.2 %collective-permute-start.10 = (bf16[14,2,32,256]{3,2,1,0:T(8,128)(2,1)S(1)}, bf16[14,2,32,256]{3,2,1,0:T(8,128)(2,1)S(1)}, u32[]{:S(2)}, u32[]{:S(2)}) collective-permute-start(bf16[14,2,32,256]{3,2,1,0:T(8,128)(2,1)S(1)} %pad_maximum_fusion.1), channel_id=1, source_target_pairs={{0,1},{1,2},{2,3},{3,0},{4,5},{5,6},{6,7},{7,4},{8,9},{9,10},{10,1... | collective-permute-start | bytes 1376264 | tf_op jit(solution)/shard_map/ppermute | solution.py:51
  270.2 23.7 %collective-permute-start.9 = (bf16[14,2,32,256]{3,2,1,0:T(8,128)(2,1)S(1)}, bf16[14,2,32,256]{3,2,1,0:T(8,128)(2,1)S(1)}, u32[]{:S(2)}, u32[]{:S(2)}) collective-permute-start(bf16[14,2,32,256]{3,2,1,0:T(8,128)(2,1)S(1)} %pad_maximum_fusion), channel_id=1, source_target_pairs={{0,3},{1,0},{2,1},{3,2},{4,7},{5,4},{6,5},{7,6},{8,11},{9,8},{10,9... | collective-permute-start | bytes 1376264 | tf_op jit(solution)/shard_map/ppermute | solution.py:51
  292.4 2.6 copy-start.19
  294.0 1.1 copy-start.20
  295.0 19.1 %all-to-all-start.7 = ((bf16[8,128,256]{2,1,0:T(8,128)(2,1)}), bf16[8,128,256]{2,1,0:T(8,128)(2,1)S(1)}, u32[]{:S(2)}, u32[]{:S(2)}) async-start(bf16[8,128,256]{2,1,0:T(8,128)(2,1)} %shard_map.101), calls=%async_computation.7 | async-start | bytes 1048576 | tf_op jit(solution)/shard_map/all_to_all | solution.py:42
Sparse Core Ops, SparseCore 0:
  10.1 62.0 all-gather.2
